TPU v7x, 32 devices: a whole 2x2x4 slice. The times are simulated.
32 devices in a mesh: gx: 2 (over x), gy: 4 (over z), gz: 4 (over y, core).
Axes of the slice: x: 2, y: 2, z: 4, core: 2. Of those that a mesh axis runs over, the one named last changes fastest.
Arguments:
- load_cases: float32 [2, 4, 4, 1158, 128], P('gx', 'gy', 'gz'), may hold values from -6 to 6
- schur_matrix: bfloat16 [2, 4, 4, 1158, 1158], P('gx', 'gy', 'gz'), may hold values from -0.25 to 3.25, as said below
- local_inverse: bfloat16 [2, 4, 4, 1158, 1158], P('gx', 'gy', 'gz'), may hold values from -0.05 to 0.45, as said below
- coarse_basis: bfloat16 [2, 4, 4, 6, 1158], P('gx', 'gy', 'gz'), may hold values from -0.25 to 0.25
- coarse_inverse: float32 [192, 192], P(('gx', 'gy', 'gz')), may hold values from -0.4 to 2.9, as said below
- canon_rows: int32 [2, 4, 4, 1158], P('gx', 'gy', 'gz'), may hold values from 0 to 1157, each once within a row
Outputs:
- solution: float32 [2, 4, 4, 1158, 128], P('gx', 'gy', 'gz')
- residual: float32 [2, 4, 4, 1158, 128], P('gx', 'gy', 'gz')
Inputs may be any that keep to these rules, and one draw needn't show every extreme that they name: `schur_matrix`: symmetric for every subdomain. `local_inverse`: symmetric for every subdomain. `coarse_inverse`: symmetric. `canon_rows`: each subdomain's row is a permutation of 0 to 1157.
All inputs are finite; a program needn't handle non-finite values.
Results may differ from a plain program's by a relative error of at most 0.0044.
Values sent between devices are 32-bit elements; how exact they have to be, the bound alone decides.
No kernel may reach another device: no remote copies, remote signals or barrier semaphores. Data moves between devices by JAX's collectives and lax.ppermute only.
A program may use at most 128 MiB of HBM per device.

v0:
```python
import functools
import itertools

import jax
import jax.numpy as jnp
from jax import lax
from jax.experimental import pallas as pl
from jax.experimental.pallas import tpu as pltpu
from jax.sharding import PartitionSpec as P

NODES = 7
DOF = 3
ITERS = 3
AXES = ("gx", "gy", "gz")
STAGES = ((2,), (0, 1))
PAD = 8
TILE = 256
F32 = jnp.float32
BF16 = jnp.bfloat16


def piece_length(placed):
    return DOF * NODES ** sum(1 for c in placed if c == 1)


PLACES = [p for p in itertools.product(range(3), repeat=3) if p != (1, 1, 1)]
CANON_OFFSET = {}
_at = 0
for _p in PLACES:
    CANON_OFFSET[_p] = _at
    _at += piece_length(_p)
IFACE = _at
SLOT_OFFSET = {}
SLOT_ROWS = {}
_at = 0
for _p in PLACES:
    SLOT_OFFSET[_p] = _at
    SLOT_ROWS[_p] = -(-piece_length(_p) // PAD) * PAD
    _at += SLOT_ROWS[_p]
COARSE_AT = _at
ROWS = -(-(COARSE_AT + 16) // TILE) * TILE


class Message:
    def __init__(self, moves, sizes):
        self.moves = moves
        self.sizes = sizes
        self.faces = "C" not in moves
        self.slots = []
        if self.faces:
            for place in PLACES:
                if all(m is None or c == (0 if m == "A" else 2) for m, c in zip(moves, place)):
                    self.slots.append(place)
        self.rows = sum(SLOT_ROWS[s] for s in self.slots)

    def xor(self):
        code = 0
        for move, size in zip(self.moves, self.sizes):
            code = code * size + {None: 0, "A": 1, "B": 3, "C": 2}[move]
        return code

    def pairs(self):
        out = []
        for place in itertools.product(*(range(s) for s in self.sizes)):
            to = []
            for at, move, size in zip(place, self.moves, self.sizes):
                if move == "A":
                    at = at ^ 1
                elif move == "B":
                    at = (at - 1) % size if at % 2 == 0 else (at + 1) % size
                elif move == "C":
                    at = at ^ 2
                to.append(at)
            flat = [0, 0]
            for a, b, size in zip(place, to, self.sizes):
                flat = [flat[0] * size + a, flat[1] * size + b]
            out.append(tuple(flat))
        return out


def ports(size):
    return ("A",) if size == 2 else ("A", "B")


def stage_messages(dims, sizes, coarse):
    choices = []
    for d in range(3):
        if d not in dims:
            choices.append((None,))
        else:
            extra = ("C",) if coarse and sizes[d] == 4 else ()
            choices.append((None,) + ports(sizes[d]) + extra)
    return [Message(m, sizes) for m in itertools.product(*choices) if any(c is not None for c in m)]


class Plan:
    def __init__(self, sizes):
        self.sizes = sizes
        self.subs = sizes[0] * sizes[1] * sizes[2]
        self.ride = all(s in (2, 4) for s in sizes)
        self.plain = [stage_messages(d, sizes, False) for d in STAGES]
        self.coarse = [stage_messages(d, sizes, True) for d in STAGES]
        self.wide = self.subs * 8

    def messages(self, coarse):
        return self.coarse if coarse and self.ride else self.plain


def position():
    return [lax.axis_index(a) for a in AXES]


def has_b(index, size):
    if size == 2:
        return None
    return jnp.logical_and(index > 0, index < size - 1)


def pick(slot, index, of):
    def choose(d, place):
        if d == 3:
            return of(tuple(place))
        if slot[d] == 1:
            return choose(d + 1, place + [1])
        even, odd = (2, 0) if slot[d] == 0 else (0, 2)
        return jnp.where(index[d] % 2 == 0, choose(d + 1, place + [even]), choose(d + 1, place + [odd]))

    return choose(0, [])


def add_received(plan, index, messages, received, acc, width):
    for message, ref in zip(messages, received):
        if not message.faces:
            continue
        ok = None
        for d, move in enumerate(message.moves):
            if move == "B":
                here = has_b(index[d], plan.sizes[d])
                ok = here if ok is None else jnp.logical_and(ok, here)
        at = 0
        for slot in message.slots:
            rows, to = SLOT_ROWS[slot], SLOT_OFFSET[slot]
            value = ref[at : at + rows, :width]
            if ok is not None:
                value = jnp.where(ok, value, 0.0)
            acc[to : to + rows, :width] += value
            at += rows


def write_payloads(messages, outs, acc, blocks):
    for message, out in zip(messages, outs):
        at = 0
        for slot in message.slots:
            rows, frm = SLOT_ROWS[slot], SLOT_OFFSET[slot]
            out[at : at + rows, :] = acc[frm : frm + rows, :]
            at += rows
        for block in blocks:
            out[at : at + 8, :128] = block
            if out.shape[1] > 128:
                out[at : at + 8, 128:] = jnp.zeros((8, out.shape[1] - 128), F32)
            at += 8


def payload_shapes(messages, blocks, width):
    return [jax.ShapeDtypeStruct((m.rows + 8 * blocks, width), F32) for m in messages]


def transfer(messages, payloads):
    return [lax.ppermute(p, AXES, m.pairs()) for m, p in zip(messages, payloads)]


def vm():
    return pl.BlockSpec(memory_space=pltpu.VMEM)


def call(kernel, outs, operands, specs=None, scratch=(), limit=20, flops=0):
    nbytes = sum(o.size * o.dtype.itemsize for o in list(outs) + list(operands))
    return pl.pallas_call(
        kernel,
        out_shape=tuple(outs),
        in_specs=specs or [vm()] * len(operands),
        out_specs=tuple(vm() for _ in outs),
        scratch_shapes=list(scratch),
        compiler_params=pltpu.CompilerParams(vmem_limit_bytes=limit << 20),
        cost_estimate=pl.CostEstimate(flops=flops, bytes_accessed=nbytes, transcendentals=0),
    )(*operands)


def gather_rows(index, canon, load, acc):
    for slot in PLACES:
        rows, at = SLOT_ROWS[slot], SLOT_OFFSET[slot]
        acc[at + rows - 8 : at + rows, :] = jnp.zeros((8, acc.shape[1]), F32)
    acc[COARSE_AT:, :] = jnp.zeros((ROWS - COARSE_AT, acc.shape[1]), F32)
    for slot in PLACES:
        length, at = piece_length(slot), SLOT_OFFSET[slot]
        off = pick(slot, index, lambda place: jnp.int32(CANON_OFFSET[place]))
        step = 7 if length % 7 == 0 else 3

        def body(i, _, off=off, at=at, step=step):
            for j in range(step):
                row = i * step + j
                acc[pl.ds(at + row, 1), :] = load[canon[off + row], :, :]
            return 0

        lax.fori_loop(0, length // step, body, 0)


def input_kernel(plan, canon, load, acc, *outs):
    gather_rows(position(), canon, load, acc)
    write_payloads(plan.plain[0], outs, acc, [])


def scatter_rows(index, canon, pairs):
    for slot in PLACES:
        length, at = piece_length(slot), SLOT_OFFSET[slot]
        off = pick(slot, index, lambda place: jnp.int32(CANON_OFFSET[place]))
        step = 7 if length % 7 == 0 else 3

        def body(i, _, off=off, at=at, step=step):
            for j in range(step):
                row = i * step + j
                to = canon[off + row]
                for acc, out in pairs:
                    out[to, :, :] = acc[pl.ds(at + row, 1), :]
            return 0

        lax.fori_loop(0, length // step, body, 0)


def split(value, parts):
    out = []
    for _ in range(parts):
        piece = value.astype(BF16)
        out.append(piece)
        value = value - piece.astype(F32)
    return out


def dot(a, b):
    return jnp.dot(a, b, preferred_element_type=F32)


def dot_last(a, b):
    return lax.dot_general(a, b, (((1,), (1,)), ((), ())), preferred_element_type=F32)


def prepare_kernel(plan, canon, inverse, schur, basis, cinv, inverse_out, schur_out, k_out, src, wgt, one, one_w, mid):
    index = position()
    src[...] = jnp.full(src.shape, -1, jnp.int32)
    wgt[...] = jnp.zeros(wgt.shape, F32)
    for slot in PLACES:
        at, length = SLOT_OFFSET[slot], piece_length(slot)
        src[at : at + length, :] = pick(
            slot, index, lambda place, length=length: canon[CANON_OFFSET[place] : CANON_OFFSET[place] + length, :]
        )
        weight = jnp.float32(1.0)
        for d in range(3):
            if slot[d] == 0:
                weight = weight * 0.5
            elif slot[d] == 2 and plan.sizes[d] > 2:
                weight = weight * jnp.where(has_b(index[d], plan.sizes[d]), 0.5, 1.0)
        wgt[at : at + length, :] = jnp.full((length, 1), 1.0, F32) * weight

    if plan.ride:
        nc = cinv.shape[1]
        row = lax.broadcasted_iota(jnp.int32, (nc, plan.wide), 0)
        col = lax.broadcasted_iota(jnp.int32, (nc, plan.wide), 1)
        spread = jnp.where(jnp.logical_and((col >> 3) * 6 + (col & 7) == row, (col & 7) < 6), 1.0, 0.0).astype(BF16)
        spread_inverse = [dot(part, spread).astype(BF16) for part in split(cinv[...], 3)]

    def tile(t):
        return pl.ds(pl.multiple_of(t * TILE, TILE), TILE)

    def build(t, _):
        hit = src[tile(t), :] == lax.broadcasted_iota(jnp.int32, (TILE, IFACE), 1)
        one[tile(t), :] = jnp.where(hit, 1.0, 0.0).astype(BF16)
        one_w[tile(t), :] = jnp.where(hit, wgt[tile(t), :], 0.0).astype(BF16)
        return 0

    lax.fori_loop(0, ROWS // TILE, build, 0)

    def left(t, _):
        mid[tile(t), :] = dot(one_w[tile(t), :], inverse[...]).astype(BF16)
        return 0

    lax.fori_loop(0, ROWS // TILE, left, 0)
    mid[COARSE_AT : COARSE_AT + 16, :] = basis[...]

    def right(t, _):
        inverse_out[tile(t), :] = dot_last(mid[tile(t), :], one_w[...]).astype(BF16)
        turned = dot_last(one_w[tile(t), :], basis[...])
        if plan.ride:
            turned = turned.astype(BF16)
            k_out[tile(t), :] = sum(dot(turned, part) for part in spread_inverse)
        else:
            k_out[tile(t), :] = turned
        return 0

    lax.fori_loop(0, ROWS // TILE, right, 0)

    def left_s(t, _):
        mid[tile(t), :] = dot(one[tile(t), :], schur[...]).astype(BF16)
        return 0

    lax.fori_loop(0, ROWS // TILE, left_s, 0)

    def right_s(t, _):
        schur_out[tile(t), :] = dot_last(mid[tile(t), :], one[...]).astype(BF16)
        return 0

    lax.fori_loop(0, ROWS // TILE, right_s, 0)


def middle_kernel(plan, coarse, width, *refs):
    first, second = plan.messages(coarse)
    ride = coarse and plan.ride
    base, received = refs[0], refs[1 : 1 + len(first)]
    outs, acc = refs[1 + len(first) : -1], refs[-1]
    acc[...] = base[...]
    add_received(plan, position(), first, received, acc, width)
    blocks = []
    if ride:
        blocks.append(base[COARSE_AT : COARSE_AT + 8, :128])
        for message, ref in zip(first, received):
            blocks.append(ref[message.rows : message.rows + 8, :128])
    write_payloads(second, outs, acc, blocks)


def multiply(matrix, vector, out):
    for t in range(ROWS // TILE):
        out[t * TILE : (t + 1) * TILE, :128] = dot(matrix[t * TILE : (t + 1) * TILE, :], vector)


def inverse_kernel(plan, opening, *refs):
    first, second = plan.plain
    refs = list(refs)
    base = refs.pop(0)
    got = [refs.pop(0) for _ in range(len(first) + len(second))]
    matrix = refs.pop(0)
    third = refs.pop(0) if plan.ride or not opening else None
    residual, out = refs.pop(0), refs.pop(0)
    acc = refs.pop(-1)
    outs = refs
    index = position()
    acc[...] = base[...]
    add_received(plan, index, first, got[: len(first)], acc, 128)
    add_received(plan, index, second, got[len(first) :], acc, 128)
    value = acc[...] if opening else third[...] - acc[...]
    residual[...] = value
    multiply(matrix, value.astype(BF16), out)
    if plan.ride:
        if opening:
            out[:, 128:] = third[...]
        write_payloads(plan.coarse[0], outs, out, [out[COARSE_AT : COARSE_AT + 8, :128]])


def lift_kernel(plan, base, turned, correction, out, *outs):
    lifted = turned[...].astype(BF16)
    out[...] = base[...] + sum(dot(lifted, part) for part in split(correction[...], 3))
    write_payloads(plan.plain[0], outs, out, [])


def schur_kernel(plan, opening, *refs):
    first, second = plan.messages(True)
    refs = list(refs)
    base = refs.pop(0)
    got = [refs.pop(0) for _ in range(len(first) + len(second))]
    matrix = refs.pop(0)
    width = base.shape[1]
    sol_in = None if opening else refs.pop(0)
    if plan.ride and not opening:
        h_high, h_low = refs.pop(0), refs.pop(0)
    sol, out = refs.pop(0), refs.pop(0)
    outs = refs[: len(plan.plain[0])]
    refs = refs[len(plan.plain[0]) :]
    if plan.ride and opening:
        h_high, h_low = refs.pop(0), refs.pop(0)
    acc, stack = refs
    index = position()
    acc[...] = base[...]
    add_received(plan, index, first, got[: len(first)], acc, width)
    add_received(plan, index, second, got[len(first) :], acc, width)
    if plan.ride and opening:
        high = acc[:, 128:].astype(BF16)
        h_high[...] = high
        h_low[...] = (acc[:, 128:] - high.astype(F32)).astype(BF16)
    if plan.ride:
        me = (index[0] * plan.sizes[1] + index[1]) * plan.sizes[2] + index[2]
        near = [0] + [m.xor() for m in first]
        values = [base[COARSE_AT : COARSE_AT + 8, :128]]
        values += [ref[m.rows : m.rows + 8, :128] for m, ref in zip(first, got)]
        for code, value in zip(near, values):
            stack[pl.ds(pl.multiple_of((me ^ code) * 8, 8), 8), :] = value
        for m, ref in zip(second, got[len(first) :]):
            for i, code in enumerate(near):
                at = m.rows + 8 * i
                to = pl.multiple_of((me ^ code ^ m.xor()) * 8, 8)
                stack[pl.ds(to, 8), :] = ref[at : at + 8, :128]
        r_high, r_low = split(stack[...], 2)
        update = acc[:, :128] + dot(h_high[...], r_high) + dot(h_high[...], r_low) + dot(h_low[...], r_high)
    else:
        update = acc[...]
    sol[...] = update if opening else sol_in[...] + update
    multiply(matrix, update.astype(BF16), out)
    write_payloads(plan.plain[0], outs, out, [])


def output_kernel(plan, canon, base, *refs):
    first, second = plan.plain
    count = len(first) + len(second)
    got = refs[:count]
    residual, sol, sol_out, residual_out, acc = refs[count:]
    index = position()
    acc[...] = base[...]
    add_received(plan, index, first, got[: len(first)], acc, 128)
    add_received(plan, index, second, got[len(first) :], acc, 128)
    acc[...] = residual[...] - acc[...]
    scatter_rows(index, canon, [(sol, sol_out), (acc, residual_out)])


def shape(rows, cols, dtype=F32):
    return jax.ShapeDtypeStruct((rows, cols), dtype)


def local(plan, load_cases, schur_matrix, local_inverse, coarse_basis, coarse_inverse, canon_rows):
    smem = pl.BlockSpec(memory_space=pltpu.SMEM)
    loads = load_cases.shape[-1]
    canon = canon_rows.reshape(IFACE)
    load = load_cases.reshape(IFACE, 1, loads)
    basis = jnp.pad(coarse_basis[0, 0, 0], ((0, 10), (0, 0)))
    cinv = jnp.pad(coarse_inverse, ((0, 10), (0, 0)))
    plain, coarse = plan.plain, plan.messages(True)
    acc = pltpu.VMEM((ROWS, 128), F32)

    def middle(is_coarse, base, got):
        width = base.shape[1]
        first, second = plan.messages(is_coarse)
        blocks = len(first) + 1 if is_coarse and plan.ride else 0
        return call(
            functools.partial(middle_kernel, plan, is_coarse, width),
            payload_shapes(second, blocks, width),
            [base] + got,
            scratch=[pltpu.VMEM((ROWS, width), F32)],
            limit=40 if width > 512 else 20,
        )

    def assemble(is_coarse, base, payloads):
        first, second = plan.messages(is_coarse)
        got = transfer(first, payloads)
        return got + transfer(second, middle(is_coarse, base, got))

    base, *payloads = call(
        functools.partial(input_kernel, plan),
        [shape(ROWS, 128)] + payload_shapes(plain[0], 0, 128),
        [canon, load],
        specs=[smem, vm()],
    )
    inverse, schur, third = call(
        functools.partial(prepare_kernel, plan),
        [shape(ROWS, ROWS, BF16), shape(ROWS, ROWS, BF16), shape(ROWS, plan.wide if plan.ride else 16)],
        [canon_rows.reshape(IFACE, 1), local_inverse[0, 0, 0], schur_matrix[0, 0, 0], basis, cinv],
        scratch=[
            pltpu.VMEM((ROWS, 1), jnp.int32),
            pltpu.VMEM((ROWS, 1), F32),
            pltpu.VMEM((ROWS, IFACE), BF16),
            pltpu.VMEM((ROWS, IFACE), BF16),
            pltpu.VMEM((ROWS, IFACE), BF16),
        ],
        limit=56,
        flops=4 * 2 * ROWS * IFACE * IFACE,
    )
    got = assemble(False, base, payloads)
    sol, turned = None, third
    flops = 2 * ROWS * ROWS * 128
    for iteration in range(ITERS):
        opening = iteration == 0
        width = 128 + plan.wide if opening and plan.ride else 128
        residual, base, *payloads = call(
            functools.partial(inverse_kernel, plan, opening),
            [shape(ROWS, 128), shape(ROWS, width)] + (payload_shapes(coarse[0], 1, width) if plan.ride else []),
            [base] + got + [inverse] + ([third] if plan.ride or not opening else []),
            scratch=[acc],
            flops=flops,
        )
        if not plan.ride:
            rows = lax.all_gather(base[COARSE_AT : COARSE_AT + 6], AXES, axis=0, tiled=True)
            correction = jnp.dot(cinv, rows, precision=lax.Precision.HIGHEST, preferred_element_type=F32)
            base, *payloads = call(
                functools.partial(lift_kernel, plan),
                [shape(ROWS, 128)] + payload_shapes(plain[0], 0, 128),
                [base, turned, correction],
            )
        got = assemble(True, base, payloads)
        kept = []
        if plan.ride:
            kept = [shape(ROWS, plan.wide, BF16)] * 2 if opening else [h_high, h_low]
        results = call(
            functools.partial(schur_kernel, plan, opening),
            [shape(ROWS, 128), shape(ROWS, 128)] + payload_shapes(plain[0], 0, 128) + (kept if opening else []),
            [base] + got + [schur] + ([] if opening else [sol] + kept),
            scratch=[pltpu.VMEM((ROWS, width), F32), pltpu.VMEM((plan.wide, 128), F32)],
            flops=flops,
        )
        sol, base, *payloads = results[: 2 + len(plain[0])]
        if plan.ride and opening:
            h_high, h_low = results[-2:]
        got = assemble(False, base, payloads)
        third = residual
    out = jax.ShapeDtypeStruct((IFACE, 1, loads), F32)
    sol_out, residual_out = call(
        functools.partial(output_kernel, plan),
        [out, out],
        [canon, base] + got + [residual, sol],
        specs=[smem] + [vm()] * (3 + len(got)),
        scratch=[acc],
    )
    return tuple(o.reshape(1, 1, 1, IFACE, loads) for o in (sol_out, residual_out))


def solution(mesh):
    plan = Plan(tuple(mesh.shape[a] for a in AXES))
    in_specs = (
        P("gx", "gy", "gz", None, None),
        P("gx", "gy", "gz", None, None),
        P("gx", "gy", "gz", None, None),
        P("gx", "gy", "gz", None, None),
        P(("gx", "gy", "gz"), None),
        P("gx", "gy", "gz", None),
    )
    out_specs = (P("gx", "gy", "gz", None, None), P("gx", "gy", "gz", None, None))
    return jax.shard_map(
        functools.partial(local, plan), mesh=mesh, in_specs=in_specs, out_specs=out_specs, check_vma=False
    )
```

profile of v0, /device:TPU:1, one launch (start us, length us, event | category | flops | bytes accessed | tf_op | source)
XLA Modules:
  0.0 220.0 jit_solution(16528898022658882992)
XLA Ops:
  1.4 1.1 copy-done.4
  2.4 2.7 %shard_map.77 = (f32[1280,128]{1,0:T(8,128)S(1)}, f32[280,128]{1,0:T(8,128)S(1)}, f32[280,128]{1,0:T(8,128)S(1)}) custom-call(s32[1158]{0:T(1024)S(1)} %reduce.canon, f32[1158,1,128]{2,1,0:T(1,128)S(1)} %bitcast.11), custom_call_target="tpu_custom_call" | custom-call | bytes 1539608 | tf_op jit(solution)/shard_map/pallas_call | solution.py:178
  5.2 2.7 %collective-permute-start.1 = (f32[280,128]{1,0:T(8,128)S(1)}, f32[280,128]{1,0:T(8,128)S(1)}, u32[]{:S(2)}, u32[]{:S(2)}) collective-permute-start(f32[280,128]{1,0:T(8,128)S(1)} %get-tuple-element.82), channel_id=1, source_target_pairs={{0,3},{1,2},{2,1},{3,0},{4,7},{5,6},{6,5},{7,4},{8,11},{9,10},{10,... | collective-permute-start | bytes 430088 | tf_op jit(solution)/shard_map/ppermute | solution.py:169
  7.9 1.8 copy.10.canon
  9.7 1.3 pad.9.cinv
  11.0 1.4 pad.8.basis
  12.4 2.3 %collective-permute-start.5 = (f32[40,128]{1,0:T(8,128)S(1)}, f32[40,128]{1,0:T(8,128)S(1)}, u32[]{:S(2)}, u32[]{:S(2)}) collective-permute-start(f32[40,128]{1,0:T(8,128)S(1)} %get-tuple-element.86), channel_id=1, source_target_pairs={{0,20},{1,21},{2,22},{3,23},{4,16},{5,17},{6,18},{7,19},{8,28},{9,... | collective-permute-start | bytes 61448 | tf_op jit(solution)/shard_map/ppermute | solution.py:169
  14.7 2.2 collective-permute-start.6
  19.1 30.8 %shard_map.79 = (bf16[1280,1280]{1,0:T(8,128)(2,1)}, bf16[1280,1280]{1,0:T(8,128)(2,1)}, f32[1280,256]{1,0:T(8,128)}) custom-call(s32[1158,1]{1,0:T(8,128)} %copy.10.canon, bf16[1158,1158]{1,0:T(8,128)(2,1)} %bitcast.14, bf16[1158,1158]{1,0:T(8,128)(2,1)} %bitcast.15, bf16[16,1158]{1,0:T(8,128)(2,1)} %pad.8.basis, f32[16,192]{1,0:T(8,128)} %pad.9.cinv), custom_call_target="tpu_custom_call" | custom-call | flops 13731471360 | bytes 13282152 | tf_op jit(solution)/shard_map/pallas_call | solution.py:178
  50.0 1.9 copy-done.1
  51.9 1.3 copy-done.3
  53.2 1.1 shard_map.80
  54.4 1.6 collective-permute-start.7
  57.4 10.2 %collective-permute-done.9.refs_3_ = f32[8,384]{1,0:T(8,128)S(1)} collective-permute-done((f32[8,384]{1,0:T(8,128)S(1)}, f32[8,384]{1,0:T(8,128)S(1)}, u32[]{:S(2)}, u32[]{:S(2)}) %collective-permute-start.9) | collective-permute-done | bytes 12320 | tf_op jit(solution)/shard_map/ppermute | solution.py:169
  69.0 2.2 collective-permute-start.11
  71.6 3.2 %collective-permute-start.16 = (f32[32,384]{1,0:T(8,128)S(1)}, f32[32,384]{1,0:T(8,128)S(1)}, u32[]{:S(2)}, u32[]{:S(2)}) collective-permute-start(f32[32,384]{1,0:T(8,128)S(1)} %get-tuple-element.100), channel_id=1, source_target_pairs={{0,24},{1,25},{2,26},{3,27},{4,28},{5,29},{6,30},{7,31},{8,16},{9,... | collective-permute-start | bytes 147464 | tf_op jit(solution)/shard_map/ppermute | solution.py:169
  74.7 15.1 %collective-permute-done.12.refs_6_ = f32[32,384]{1,0:T(8,128)S(1)} collective-permute-done((f32[32,384]{1,0:T(8,128)S(1)}, f32[32,384]{1,0:T(8,128)S(1)}, u32[]{:S(2)}, u32[]{:S(2)}) %collective-permute-start.12) | collective-permute-done | bytes 49184 | tf_op jit(solution)/shard_map/ppermute | solution.py:169
  89.8 4.2 %collective-permute-start.14 = (f32[72,384]{1,0:T(8,128)S(1)}, f32[72,384]{1,0:T(8,128)S(1)}, u32[]{:S(2)}, u32[]{:S(2)}) collective-permute-start(f32[72,384]{1,0:T(8,128)S(1)} %get-tuple-element.98), channel_id=1, source_target_pairs={{0,20},{1,21},{2,22},{3,23},{4,16},{5,17},{6,18},{7,19},{8,28},{9,... | collective-permute-start | bytes 331784 | tf_op jit(solution)/shard_map/ppermute | solution.py:169
  94.0 1.6 collective-permute-done.16.refs_10_
  95.6 3.0 %collective-permute-start.15 = (f32[72,384]{1,0:T(8,128)S(1)}, f32[72,384]{1,0:T(8,128)S(1)}, u32[]{:S(2)}, u32[]{:S(2)}) collective-permute-start(f32[72,384]{1,0:T(8,128)S(1)} %get-tuple-element.99), channel_id=1, source_target_pairs={{0,28},{1,29},{2,30},{3,31},{4,24},{5,25},{6,26},{7,27},{8,20},{9,... | collective-permute-start | bytes 331784 | tf_op jit(solution)/shard_map/ppermute | solution.py:169
  98.6 4.5 %collective-permute-done.15.refs_9_ = f32[72,384]{1,0:T(8,128)S(1)} collective-permute-done((f32[72,384]{1,0:T(8,128)S(1)}, f32[72,384]{1,0:T(8,128)S(1)}, u32[]{:S(2)}, u32[]{:S(2)}) %collective-permute-start.15) | collective-permute-done | bytes 110624 | tf_op jit(solution)/shard_map/ppermute | solution.py:169
  103.1 2.5 %shard_map.82 = (f32[1280,128]{1,0:T(8,128)S(1)}, f32[1280,128]{1,0:T(8,128)S(1)}, f32[280,128]{1,0:T(8,128)S(1)}, f32[280,128]{1,0:T(8,128)S(1)}, bf16[1280,256...) custom-call(f32[1280,384]{1,0:T(8,128)S(1)} %get-tuple-element.90.refs_0_, ...), custom_call_target="tpu_custom_call" | custom-call | flops 419430400 | bytes 10805248 | tf_op jit(solution)/shard_map/pallas_call | solution.py:178
  105.7 2.2 collective-permute-start.17
  108.8 4.4 %collective-permute-done.18.refs_2_ = f32[280,128]{1,0:T(8,128)S(1)} collective-permute-done((f32[280,128]{1,0:T(8,128)S(1)}, f32[280,128]{1,0:T(8,128)S(1)}, u32[]{:S(2)}, u32[]{:S(2)}) %collective-permute-start.18) | collective-permute-done | bytes 143392 | tf_op jit(solution)/shard_map/ppermute | solution.py:169
  114.3 2.0 collective-permute-start.20
  116.3 1.2 collective-permute-start.21
  117.5 1.9 collective-permute-start.23
  119.4 2.2 collective-permute-done.22.refs_6_
  121.5 3.1 %collective-permute-done.23.refs_7_ = f32[40,128]{1,0:T(8,128)S(1)} collective-permute-done((f32[40,128]{1,0:T(8,128)S(1)}, f32[40,128]{1,0:T(8,128)S(1)}, u32[]{:S(2)}, u32[]{:S(2)}) %collective-permute-start.23) | collective-permute-done | bytes 20512 | tf_op jit(solution)/shard_map/ppermute | solution.py:169
  124.7 1.1 shard_map.84
  125.8 1.3 collective-permute-start.24
  128.5 3.8 %collective-permute-done.26.refs_3_ = f32[8,128]{1,0:T(8,128)S(1)} collective-permute-done((f32[8,128]{1,0:T(8,128)S(1)}, f32[8,128]{1,0:T(8,128)S(1)}, u32[]{:S(2)}, u32[]{:S(2)}) %collective-permute-start.26) | collective-permute-done | bytes 4128 | tf_op jit(solution)/shard_map/ppermute | solution.py:169
  132.8 2.4 %collective-permute-start.28 = (f32[312,128]{1,0:T(8,128)S(1)}, f32[312,128]{1,0:T(8,128)S(1)}, u32[]{:S(2)}, u32[]{:S(2)}) collective-permute-start(f32[312,128]{1,0:T(8,128)S(1)} %get-tuple-element.116), channel_id=1, source_target_pairs={{0,12},{1,13},{2,14},{3,15},{4,8},{5,9},{6,10},{7,11},{8,4},{9,5},... | collective-permute-start | bytes 479240 | tf_op jit(solution)/shard_map/ppermute | solution.py:169
  136.0 2.7 %collective-permute-start.33 = (f32[32,128]{1,0:T(8,128)S(1)}, f32[32,128]{1,0:T(8,128)S(1)}, u32[]{:S(2)}, u32[]{:S(2)}) collective-permute-start(f32[32,128]{1,0:T(8,128)S(1)} %get-tuple-element.121), channel_id=1, source_target_pairs={{0,24},{1,25},{2,26},{3,27},{4,28},{5,29},{6,30},{7,31},{8,16},{9,... | collective-permute-start | bytes 49160 | tf_op jit(solution)/shard_map/ppermute | solution.py:169
  139.5 2.9 %collective-permute-start.31 = (f32[72,128]{1,0:T(8,128)S(1)}, f32[72,128]{1,0:T(8,128)S(1)}, u32[]{:S(2)}, u32[]{:S(2)}) collective-permute-start(f32[72,128]{1,0:T(8,128)S(1)} %get-tuple-element.119), channel_id=1, source_target_pairs={{0,20},{1,21},{2,22},{3,23},{4,16},{5,17},{6,18},{7,19},{8,28},{9,... | collective-permute-start | bytes 110600 | tf_op jit(solution)/shard_map/ppermute | solution.py:169
  142.4 1.4 collective-permute-done.33.refs_10_
  143.8 1.7 collective-permute-start.32
  145.6 3.9 %collective-permute-done.32.refs_9_ = f32[72,128]{1,0:T(8,128)S(1)} collective-permute-done((f32[72,128]{1,0:T(8,128)S(1)}, f32[72,128]{1,0:T(8,128)S(1)}, u32[]{:S(2)}, u32[]{:S(2)}) %collective-permute-start.32) | collective-permute-done | bytes 36896 | tf_op jit(solution)/shard_map/ppermute | solution.py:169
  149.5 2.5 %shard_map.86 = (f32[1280,128]{1,0:T(8,128)S(1)}, f32[1280,128]{1,0:T(8,128)S(1)}, f32[280,128]{1,0:T(8,128)S(1)}, f32[280,128]{1,0:T(8,128)S(1)}) custom-call(f32[1280,128]{1,0:T(8,128)S(1)} %get-tuple-element.111.refs_0_, f32[288,128]{1,0:T(8,128)S(1)} %collective-permute-done.24.refs_1_, f32[288,128]{1,0:T(8,128)S(1)} %collective-permute-done.25.refs_2_, ...), custom_call_target="tpu_custom_call" | custom-call | flops 419430400 | bytes 8380416 | tf_op jit(solution)/shard_map/pallas_call | solution.py:178
  152.0 2.9 %collective-permute-start.34 = (f32[280,128]{1,0:T(8,128)S(1)}, f32[280,128]{1,0:T(8,128)S(1)}, u32[]{:S(2)}, u32[]{:S(2)}) collective-permute-start(f32[280,128]{1,0:T(8,128)S(1)} %get-tuple-element.126), channel_id=1, source_target_pairs={{0,1},{1,0},{2,3},{3,2},{4,5},{5,4},{6,7},{7,6},{8,9},{9,8},{10,11... | collective-permute-start | bytes 430088 | tf_op jit(solution)/shard_map/ppermute | solution.py:169
  155.8 4.4 %collective-permute-done.35.refs_2_ = f32[280,128]{1,0:T(8,128)S(1)} collective-permute-done((f32[280,128]{1,0:T(8,128)S(1)}, f32[280,128]{1,0:T(8,128)S(1)}, u32[]{:S(2)}, u32[]{:S(2)}) %collective-permute-start.35) | collective-permute-done | bytes 143392 | tf_op jit(solution)/shard_map/ppermute | solution.py:169
  160.4 1.0 collective-permute-start.37
  161.4 1.2 collective-permute-start.38
  163.1 2.9 %collective-permute-start.40 = (f32[40,128]{1,0:T(8,128)S(1)}, f32[40,128]{1,0:T(8,128)S(1)}, u32[]{:S(2)}, u32[]{:S(2)}) collective-permute-start(f32[40,128]{1,0:T(8,128)S(1)} %get-tuple-element.132), channel_id=1, source_target_pairs={{0,28},{1,29},{2,30},{3,31},{4,24},{5,25},{6,26},{7,27},{8,20},{9,... | collective-permute-start | bytes 61448 | tf_op jit(solution)/shard_map/ppermute | solution.py:169
  166.0 3.4 %collective-permute-done.39.refs_6_ = f32[40,128]{1,0:T(8,128)S(1)} collective-permute-done((f32[40,128]{1,0:T(8,128)S(1)}, f32[40,128]{1,0:T(8,128)S(1)}, u32[]{:S(2)}, u32[]{:S(2)}) %collective-permute-start.39) | collective-permute-done | bytes 20512 | tf_op jit(solution)/shard_map/ppermute | solution.py:169
  170.0 1.1 shard_map.88
  171.1 1.1 collective-permute-start.41
  173.7 3.8 %collective-permute-done.43.refs_3_ = f32[8,128]{1,0:T(8,128)S(1)} collective-permute-done((f32[8,128]{1,0:T(8,128)S(1)}, f32[8,128]{1,0:T(8,128)S(1)}, u32[]{:S(2)}, u32[]{:S(2)}) %collective-permute-start.43) | collective-permute-done | bytes 4128 | tf_op jit(solution)/shard_map/ppermute | solution.py:169
  177.9 1.5 collective-permute-start.44
  179.4 1.3 collective-permute-start.45
  181.7 2.6 %collective-permute-start.50 = (f32[32,128]{1,0:T(8,128)S(1)}, f32[32,128]{1,0:T(8,128)S(1)}, u32[]{:S(2)}, u32[]{:S(2)}) collective-permute-start(f32[32,128]{1,0:T(8,128)S(1)} %get-tuple-element.144), channel_id=1, source_target_pairs={{0,24},{1,25},{2,26},{3,27},{4,28},{5,29},{6,30},{7,31},{8,16},{9,... | collective-permute-start | bytes 49160 | tf_op jit(solution)/shard_map/ppermute | solution.py:169
  184.3 1.6 collective-permute-done.46.refs_6_
  185.9 2.2 %collective-permute-start.48 = (f32[72,128]{1,0:T(8,128)S(1)}, f32[72,128]{1,0:T(8,128)S(1)}, u32[]{:S(2)}, u32[]{:S(2)}) collective-permute-start(f32[72,128]{1,0:T(8,128)S(1)} %get-tuple-element.142), channel_id=1, source_target_pairs={{0,20},{1,21},{2,22},{3,23},{4,16},{5,17},{6,18},{7,19},{8,28},{9,... | collective-permute-start | bytes 110600 | tf_op jit(solution)/shard_map/ppermute | solution.py:169
  188.1 1.2 collective-permute-done.50.refs_10_
  189.3 1.6 collective-permute-start.49
  190.9 4.3 %collective-permute-done.49.refs_9_ = f32[72,128]{1,0:T(8,128)S(1)} collective-permute-done((f32[72,128]{1,0:T(8,128)S(1)}, f32[72,128]{1,0:T(8,128)S(1)}, u32[]{:S(2)}, u32[]{:S(2)}) %collective-permute-start.49) | collective-permute-done | bytes 36896 | tf_op jit(solution)/shard_map/ppermute | solution.py:169
  195.2 2.5 %shard_map.90 = (f32[1280,128]{1,0:T(8,128)S(1)}, f32[1280,128]{1,0:T(8,128)S(1)}, f32[280,128]{1,0:T(8,128)S(1)}, f32[280,128]{1,0:T(8,128)S(1)}) custom-call(f32[1280,128]{1,0:T(8,128)S(1)} %get-tuple-element.134.refs_0_, f32[288,128]{1,0:T(8,128)S(1)} %collective-permute-done.41.refs_1_, f32[288,128]{1,0:T(8,128)S(1)} %collective-permute-done.42.refs_2_, ...), custom_call_target="tpu_custom_call" | custom-call | flops 419430400 | bytes 8380416 | tf_op jit(solution)/shard_map/pallas_call | solution.py:178
  197.7 2.9 %collective-permute-start.51 = (f32[280,128]{1,0:T(8,128)S(1)}, f32[280,128]{1,0:T(8,128)S(1)}, u32[]{:S(2)}, u32[]{:S(2)}) collective-permute-start(f32[280,128]{1,0:T(8,128)S(1)} %get-tuple-element.147), channel_id=1, source_target_pairs={{0,1},{1,0},{2,3},{3,2},{4,5},{5,4},{6,7},{7,6},{8,9},{9,8},{10,11... | collective-permute-start | bytes 430088 | tf_op jit(solution)/shard_map/ppermute | solution.py:169
  201.5 4.4 %collective-permute-done.52.refs_2_.refs_1_ = f32[280,128]{1,0:T(8,128)S(1)} collective-permute-done((f32[280,128]{1,0:T(8,128)S(1)}, f32[280,128]{1,0:T(8,128)S(1)}, u32[]{:S(2)}, u32[]{:S(2)}) %collective-permute-start.52) | collective-permute-done | bytes 143392 | tf_op jit(solution)/shard_map/ppermute | solution.py:169
  206.1 1.9 collective-permute-start.54
  209.6 1.6 collective-permute-start.57
  211.3 1.7 collective-permute-done.56.refs_5_
  212.9 3.0 %collective-permute-done.57.refs_6_ = f32[40,128]{1,0:T(8,128)S(1)} collective-permute-done((f32[40,128]{1,0:T(8,128)S(1)}, f32[40,128]{1,0:T(8,128)S(1)}, u32[]{:S(2)}, u32[]{:S(2)}) %collective-permute-start.57) | collective-permute-done | bytes 20512 | tf_op jit(solution)/shard_map/ppermute | solution.py:169
  216.0 4.0 %shard_map.92 = (f32[1158,1,128]{2,1,0:T(1,128)}, f32[1158,1,128]{2,1,0:T(1,128)}) custom-call(s32[1158]{0:T(1024)S(1)} %reduce.canon, f32[1280,128]{1,0:T(8,128)S(1)} %get-tuple-element.146.refs_0_.base, f32[280,128]{1,0:T(8,128)S(1)} %collective-permute-done.51.refs_1_.refs_0_, f32[280,128]{1,0:T(8,128)S(1)} %collective-permute-done.52.refs_2_.refs_1_, ...), custom_call_target="tpu_custom_call" | custom-call | bytes 3914264 | tf_op jit(solution)/shard_map/pallas_call | solution.py:178
  (82 shorter events, 19.8 us)
Async XLA Ops:
  1.3 1.1 copy-start.4
  5.1 7.2 %collective-permute-start = (f32[280,128]{1,0:T(8,128)S(1)}, f32[280,128]{1,0:T(8,128)S(1)}, u32[]{:S(2)}, u32[]{:S(2)}) collective-permute-start(f32[280,128]{1,0:T(8,128)S(1)} %get-tuple-element.81), channel_id=1, source_target_pairs={{0,1},{1,0},{2,3},{3,2},{4,5},{5,4},{6,7},{7,6},{8,9},{9,8},{10,11... | collective-permute-start | bytes 430088 | tf_op jit(solution)/shard_map/ppermute | solution.py:169
  5.2 7.1 %collective-permute-start.1 = (f32[280,128]{1,0:T(8,128)S(1)}, f32[280,128]{1,0:T(8,128)S(1)}, u32[]{:S(2)}, u32[]{:S(2)}) collective-permute-start(f32[280,128]{1,0:T(8,128)S(1)} %get-tuple-element.82), channel_id=1, source_target_pairs={{0,3},{1,2},{2,1},{3,0},{4,7},{5,6},{6,5},{7,4},{8,11},{9,10},{10,... | collective-permute-start | bytes 430088 | tf_op jit(solution)/shard_map/ppermute | solution.py:169
  12.4 37.6 %collective-permute-start.5 = (f32[40,128]{1,0:T(8,128)S(1)}, f32[40,128]{1,0:T(8,128)S(1)}, u32[]{:S(2)}, u32[]{:S(2)}) collective-permute-start(f32[40,128]{1,0:T(8,128)S(1)} %get-tuple-element.86), channel_id=1, source_target_pairs={{0,20},{1,21},{2,22},{3,23},{4,16},{5,17},{6,18},{7,19},{8,28},{9,... | collective-permute-start | bytes 61448 | tf_op jit(solution)/shard_map/ppermute | solution.py:169
  14.7 35.3 %collective-permute-start.6 = (f32[40,128]{1,0:T(8,128)S(1)}, f32[40,128]{1,0:T(8,128)S(1)}, u32[]{:S(2)}, u32[]{:S(2)}) collective-permute-start(f32[40,128]{1,0:T(8,128)S(1)} %get-tuple-element.87), channel_id=1, source_target_pairs={{0,28},{1,29},{2,30},{3,31},{4,24},{5,25},{6,26},{7,27},{8,20},{9,... | collective-permute-start | bytes 61448 | tf_op jit(solution)/shard_map/ppermute | solution.py:169
  16.8 33.1 %collective-permute-start.2 = (f32[280,128]{1,0:T(8,128)S(1)}, f32[280,128]{1,0:T(8,128)S(1)}, u32[]{:S(2)}, u32[]{:S(2)}) collective-permute-start(f32[280,128]{1,0:T(8,128)S(1)} %get-tuple-element.83), channel_id=1, source_target_pairs={{0,4},{1,5},{2,6},{3,7},{4,0},{5,1},{6,2},{7,3},{8,12},{9,13},{10,... | collective-permute-start | bytes 430088 | tf_op jit(solution)/shard_map/ppermute | solution.py:169
  17.2 32.7 %collective-permute-start.3 = (f32[280,128]{1,0:T(8,128)S(1)}, f32[280,128]{1,0:T(8,128)S(1)}, u32[]{:S(2)}, u32[]{:S(2)}) collective-permute-start(f32[280,128]{1,0:T(8,128)S(1)} %get-tuple-element.84), channel_id=1, source_target_pairs={{0,12},{1,13},{2,14},{3,15},{4,8},{5,9},{6,10},{7,11},{8,4},{9,5},... | collective-permute-start | bytes 430088 | tf_op jit(solution)/shard_map/ppermute | solution.py:169
  18.2 31.8 %collective-permute-start.4 = (f32[280,128]{1,0:T(8,128)S(1)}, f32[280,128]{1,0:T(8,128)S(1)}, u32[]{:S(2)}, u32[]{:S(2)}) collective-permute-start(f32[280,128]{1,0:T(8,128)S(1)} %get-tuple-element.85), channel_id=1, source_target_pairs={{0,16},{1,17},{2,18},{3,19},{4,20},{5,21},{6,22},{7,23},{8,24},{9,... | collective-permute-start | bytes 430088 | tf_op jit(solution)/shard_map/ppermute | solution.py:169
  50.0 1.9 copy-start.1
  51.9 1.3 copy-start.3
  53.2 49.9 %copy-start = (bf16[1280,1280]{1,0:T(8,128)(2,1)S(1)}, bf16[1280,1280]{1,0:T(8,128)(2,1)}, u32[]{:S(2)}) copy-start(bf16[1280,1280]{1,0:T(8,128)(2,1)} %get-tuple-element.101.refs_11_) | copy-start | bytes 9830404
  54.4 13.2 %collective-permute-start.7 = (f32[288,384]{1,0:T(8,128)S(1)}, f32[288,384]{1,0:T(8,128)S(1)}, u32[]{:S(2)}, u32[]{:S(2)}) collective-permute-start(f32[288,384]{1,0:T(8,128)S(1)} %get-tuple-element.91), channel_id=1, source_target_pairs={{0,1},{1,0},{2,3},{3,2},{4,5},{5,4},{6,7},{7,6},{8,9},{9,8},{10,11... | collective-permute-start | bytes 1327112 | tf_op jit(solution)/shard_map/ppermute | solution.py:169
  56.0 12.0 %collective-permute-start.8 = (f32[288,384]{1,0:T(8,128)S(1)}, f32[288,384]{1,0:T(8,128)S(1)}, u32[]{:S(2)}, u32[]{:S(2)}) collective-permute-start(f32[288,384]{1,0:T(8,128)S(1)} %get-tuple-element.92), channel_id=1, source_target_pairs={{0,3},{1,2},{2,1},{3,0},{4,7},{5,6},{6,5},{7,4},{8,11},{9,10},{10,... | collective-permute-start | bytes 1327112 | tf_op jit(solution)/shard_map/ppermute | solution.py:169
  56.7 10.9 %collective-permute-start.9 = (f32[8,384]{1,0:T(8,128)S(1)}, f32[8,384]{1,0:T(8,128)S(1)}, u32[]{:S(2)}, u32[]{:S(2)}) collective-permute-start(f32[8,384]{1,0:T(8,128)S(1)} %get-tuple-element.93), channel_id=1, source_target_pairs={{0,2},{1,3},{2,0},{3,1},{4,6},{5,7},{6,4},{7,5},{8,10},{9,11},{10,... | collective-permute-start | bytes 36872 | tf_op jit(solution)/shard_map/ppermute | solution.py:169
  68.1 35.0 %collective-permute-start.10 = (f32[312,384]{1,0:T(8,128)S(1)}, f32[312,384]{1,0:T(8,128)S(1)}, u32[]{:S(2)}, u32[]{:S(2)}) collective-permute-start(f32[312,384]{1,0:T(8,128)S(1)} %get-tuple-element.94), channel_id=1, source_target_pairs={{0,4},{1,5},{2,6},{3,7},{4,0},{5,1},{6,2},{7,3},{8,12},{9,13},{10,... | collective-permute-start | bytes 1437704 | tf_op jit(solution)/shard_map/ppermute | solution.py:169
  69.0 34.1 %collective-permute-start.11 = (f32[312,384]{1,0:T(8,128)S(1)}, f32[312,384]{1,0:T(8,128)S(1)}, u32[]{:S(2)}, u32[]{:S(2)}) collective-permute-start(f32[312,384]{1,0:T(8,128)S(1)} %get-tuple-element.95), channel_id=1, source_target_pairs={{0,12},{1,13},{2,14},{3,15},{4,8},{5,9},{6,10},{7,11},{8,4},{9,5},... | collective-permute-start | bytes 1437704 | tf_op jit(solution)/shard_map/ppermute | solution.py:169
  71.2 31.9 %collective-permute-start.13 = (f32[312,384]{1,0:T(8,128)S(1)}, f32[312,384]{1,0:T(8,128)S(1)}, u32[]{:S(2)}, u32[]{:S(2)}) collective-permute-start(f32[312,384]{1,0:T(8,128)S(1)} %get-tuple-element.97), channel_id=1, source_target_pairs={{0,16},{1,17},{2,18},{3,19},{4,20},{5,21},{6,22},{7,23},{8,24},{9,... | collective-permute-start | bytes 1437704 | tf_op jit(solution)/shard_map/ppermute | solution.py:169
  71.5 18.4 %collective-permute-start.12 = (f32[32,384]{1,0:T(8,128)S(1)}, f32[32,384]{1,0:T(8,128)S(1)}, u32[]{:S(2)}, u32[]{:S(2)}) collective-permute-start(f32[32,384]{1,0:T(8,128)S(1)} %get-tuple-element.96), channel_id=1, source_target_pairs={{0,8},{1,9},{2,10},{3,11},{4,12},{5,13},{6,14},{7,15},{8,0},{9,1},... | collective-permute-start | bytes 147464 | tf_op jit(solution)/shard_map/ppermute | solution.py:169
  71.6 24.1 %collective-permute-start.16 = (f32[32,384]{1,0:T(8,128)S(1)}, f32[32,384]{1,0:T(8,128)S(1)}, u32[]{:S(2)}, u32[]{:S(2)}) collective-permute-start(f32[32,384]{1,0:T(8,128)S(1)} %get-tuple-element.100), channel_id=1, source_target_pairs={{0,24},{1,25},{2,26},{3,27},{4,28},{5,29},{6,30},{7,31},{8,16},{9,... | collective-permute-start | bytes 147464 | tf_op jit(solution)/shard_map/ppermute | solution.py:169
  89.8 8.8 %collective-permute-start.14 = (f32[72,384]{1,0:T(8,128)S(1)}, f32[72,384]{1,0:T(8,128)S(1)}, u32[]{:S(2)}, u32[]{:S(2)}) collective-permute-start(f32[72,384]{1,0:T(8,128)S(1)} %get-tuple-element.98), channel_id=1, source_target_pairs={{0,20},{1,21},{2,22},{3,23},{4,16},{5,17},{6,18},{7,19},{8,28},{9,... | collective-permute-start | bytes 331784 | tf_op jit(solution)/shard_map/ppermute | solution.py:169
  95.6 7.5 %collective-permute-start.15 = (f32[72,384]{1,0:T(8,128)S(1)}, f32[72,384]{1,0:T(8,128)S(1)}, u32[]{:S(2)}, u32[]{:S(2)}) collective-permute-start(f32[72,384]{1,0:T(8,128)S(1)} %get-tuple-element.99), channel_id=1, source_target_pairs={{0,28},{1,29},{2,30},{3,31},{4,24},{5,25},{6,26},{7,27},{8,20},{9,... | collective-permute-start | bytes 331784 | tf_op jit(solution)/shard_map/ppermute | solution.py:169
  103.1 21.5 %copy-start.2 = (bf16[1280,1280]{1,0:T(8,128)(2,1)S(1)}, bf16[1280,1280]{1,0:T(8,128)(2,1)}, u32[]{:S(2)}) copy-start(bf16[1280,1280]{1,0:T(8,128)(2,1)} %get-tuple-element.88.refs_8_) | copy-start | bytes 9830404
  105.7 3.2 %collective-permute-start.17 = (f32[280,128]{1,0:T(8,128)S(1)}, f32[280,128]{1,0:T(8,128)S(1)}, u32[]{:S(2)}, u32[]{:S(2)}) collective-permute-start(f32[280,128]{1,0:T(8,128)S(1)} %get-tuple-element.103), channel_id=1, source_target_pairs={{0,1},{1,0},{2,3},{3,2},{4,5},{5,4},{6,7},{7,6},{8,9},{9,8},{10,11... | collective-permute-start | bytes 430088 | tf_op jit(solution)/shard_map/ppermute | solution.py:169
  107.8 5.5 %collective-permute-start.18 = (f32[280,128]{1,0:T(8,128)S(1)}, f32[280,128]{1,0:T(8,128)S(1)}, u32[]{:S(2)}, u32[]{:S(2)}) collective-permute-start(f32[280,128]{1,0:T(8,128)S(1)} %get-tuple-element.104), channel_id=1, source_target_pairs={{0,3},{1,2},{2,1},{3,0},{4,7},{5,6},{6,5},{7,4},{8,11},{9,10},{10,... | collective-permute-start | bytes 430088 | tf_op jit(solution)/shard_map/ppermute | solution.py:169
  113.3 11.3 %collective-permute-start.19 = (f32[280,128]{1,0:T(8,128)S(1)}, f32[280,128]{1,0:T(8,128)S(1)}, u32[]{:S(2)}, u32[]{:S(2)}) collective-permute-start(f32[280,128]{1,0:T(8,128)S(1)} %get-tuple-element.105), channel_id=1, source_target_pairs={{0,4},{1,5},{2,6},{3,7},{4,0},{5,1},{6,2},{7,3},{8,12},{9,13},{10,... | collective-permute-start | bytes 430088 | tf_op jit(solution)/shard_map/ppermute | solution.py:169
  114.3 10.3 %collective-permute-start.20 = (f32[280,128]{1,0:T(8,128)S(1)}, f32[280,128]{1,0:T(8,128)S(1)}, u32[]{:S(2)}, u32[]{:S(2)}) collective-permute-start(f32[280,128]{1,0:T(8,128)S(1)} %get-tuple-element.106), channel_id=1, source_target_pairs={{0,12},{1,13},{2,14},{3,15},{4,8},{5,9},{6,10},{7,11},{8,4},{9,5},... | collective-permute-start | bytes 430088 | tf_op jit(solution)/shard_map/ppermute | solution.py:169
  116.3 8.4 %collective-permute-start.21 = (f32[280,128]{1,0:T(8,128)S(1)}, f32[280,128]{1,0:T(8,128)S(1)}, u32[]{:S(2)}, u32[]{:S(2)}) collective-permute-start(f32[280,128]{1,0:T(8,128)S(1)} %get-tuple-element.107), channel_id=1, source_target_pairs={{0,16},{1,17},{2,18},{3,19},{4,20},{5,21},{6,22},{7,23},{8,24},{9,... | collective-permute-start | bytes 430088 | tf_op jit(solution)/shard_map/ppermute | solution.py:169
  117.5 4.0 %collective-permute-start.22 = (f32[40,128]{1,0:T(8,128)S(1)}, f32[40,128]{1,0:T(8,128)S(1)}, u32[]{:S(2)}, u32[]{:S(2)}) collective-permute-start(f32[40,128]{1,0:T(8,128)S(1)} %get-tuple-element.108), channel_id=1, source_target_pairs={{0,20},{1,21},{2,22},{3,23},{4,16},{5,17},{6,18},{7,19},{8,28},{9,... | collective-permute-start | bytes 61448 | tf_op jit(solution)/shard_map/ppermute | solution.py:169
  117.5 7.1 %collective-permute-start.23 = (f32[40,128]{1,0:T(8,128)S(1)}, f32[40,128]{1,0:T(8,128)S(1)}, u32[]{:S(2)}, u32[]{:S(2)}) collective-permute-start(f32[40,128]{1,0:T(8,128)S(1)} %get-tuple-element.109), channel_id=1, source_target_pairs={{0,28},{1,29},{2,30},{3,31},{4,24},{5,25},{6,26},{7,27},{8,20},{9,... | collective-permute-start | bytes 61448 | tf_op jit(solution)/shard_map/ppermute | solution.py:169
  125.8 6.6 %collective-permute-start.24 = (f32[288,128]{1,0:T(8,128)S(1)}, f32[288,128]{1,0:T(8,128)S(1)}, u32[]{:S(2)}, u32[]{:S(2)}) collective-permute-start(f32[288,128]{1,0:T(8,128)S(1)} %get-tuple-element.112), channel_id=1, source_target_pairs={{0,1},{1,0},{2,3},{3,2},{4,5},{5,4},{6,7},{7,6},{8,9},{9,8},{10,11... | collective-permute-start | bytes 442376 | tf_op jit(solution)/shard_map/ppermute | solution.py:169
  127.1 5.6 %collective-permute-start.25 = (f32[288,128]{1,0:T(8,128)S(1)}, f32[288,128]{1,0:T(8,128)S(1)}, u32[]{:S(2)}, u32[]{:S(2)}) collective-permute-start(f32[288,128]{1,0:T(8,128)S(1)} %get-tuple-element.113), channel_id=1, source_target_pairs={{0,3},{1,2},{2,1},{3,0},{4,7},{5,6},{6,5},{7,4},{8,11},{9,10},{10,... | collective-permute-start | bytes 442376 | tf_op jit(solution)/shard_map/ppermute | solution.py:169
  127.8 4.5 %collective-permute-start.26 = (f32[8,128]{1,0:T(8,128)S(1)}, f32[8,128]{1,0:T(8,128)S(1)}, u32[]{:S(2)}, u32[]{:S(2)}) collective-permute-start(f32[8,128]{1,0:T(8,128)S(1)} %get-tuple-element.114), channel_id=1, source_target_pairs={{0,2},{1,3},{2,0},{3,1},{4,6},{5,7},{6,4},{7,5},{8,10},{9,11},{10,... | collective-permute-start | bytes 12296 | tf_op jit(solution)/shard_map/ppermute | solution.py:169
  132.7 16.8 %collective-permute-start.27 = (f32[312,128]{1,0:T(8,128)S(1)}, f32[312,128]{1,0:T(8,128)S(1)}, u32[]{:S(2)}, u32[]{:S(2)}) collective-permute-start(f32[312,128]{1,0:T(8,128)S(1)} %get-tuple-element.115), channel_id=1, source_target_pairs={{0,4},{1,5},{2,6},{3,7},{4,0},{5,1},{6,2},{7,3},{8,12},{9,13},{10,... | collective-permute-start | bytes 479240 | tf_op jit(solution)/shard_map/ppermute | solution.py:169
  132.8 16.7 %collective-permute-start.28 = (f32[312,128]{1,0:T(8,128)S(1)}, f32[312,128]{1,0:T(8,128)S(1)}, u32[]{:S(2)}, u32[]{:S(2)}) collective-permute-start(f32[312,128]{1,0:T(8,128)S(1)} %get-tuple-element.116), channel_id=1, source_target_pairs={{0,12},{1,13},{2,14},{3,15},{4,8},{5,9},{6,10},{7,11},{8,4},{9,5},... | collective-permute-start | bytes 479240 | tf_op jit(solution)/shard_map/ppermute | solution.py:169
  135.2 14.3 %collective-permute-start.30 = (f32[312,128]{1,0:T(8,128)S(1)}, f32[312,128]{1,0:T(8,128)S(1)}, u32[]{:S(2)}, u32[]{:S(2)}) collective-permute-start(f32[312,128]{1,0:T(8,128)S(1)} %get-tuple-element.118), channel_id=1, source_target_pairs={{0,16},{1,17},{2,18},{3,19},{4,20},{5,21},{6,22},{7,23},{8,24},{9,... | collective-permute-start | bytes 479240 | tf_op jit(solution)/shard_map/ppermute | solution.py:169
  135.4 4.1 %collective-permute-start.29 = (f32[32,128]{1,0:T(8,128)S(1)}, f32[32,128]{1,0:T(8,128)S(1)}, u32[]{:S(2)}, u32[]{:S(2)}) collective-permute-start(f32[32,128]{1,0:T(8,128)S(1)} %get-tuple-element.117), channel_id=1, source_target_pairs={{0,8},{1,9},{2,10},{3,11},{4,12},{5,13},{6,14},{7,15},{8,0},{9,1},... | collective-permute-start | bytes 49160 | tf_op jit(solution)/shard_map/ppermute | solution.py:169
  136.0 7.8 %collective-permute-start.33 = (f32[32,128]{1,0:T(8,128)S(1)}, f32[32,128]{1,0:T(8,128)S(1)}, u32[]{:S(2)}, u32[]{:S(2)}) collective-permute-start(f32[32,128]{1,0:T(8,128)S(1)} %get-tuple-element.121), channel_id=1, source_target_pairs={{0,24},{1,25},{2,26},{3,27},{4,28},{5,29},{6,30},{7,31},{8,16},{9,... | collective-permute-start | bytes 49160 | tf_op jit(solution)/shard_map/ppermute | solution.py:169
  139.5 6.1 %collective-permute-start.31 = (f32[72,128]{1,0:T(8,128)S(1)}, f32[72,128]{1,0:T(8,128)S(1)}, u32[]{:S(2)}, u32[]{:S(2)}) collective-permute-start(f32[72,128]{1,0:T(8,128)S(1)} %get-tuple-element.119), channel_id=1, source_target_pairs={{0,20},{1,21},{2,22},{3,23},{4,16},{5,17},{6,18},{7,19},{8,28},{9,... | collective-permute-start | bytes 110600 | tf_op jit(solution)/shard_map/ppermute | solution.py:169
  143.8 5.6 %collective-permute-start.32 = (f32[72,128]{1,0:T(8,128)S(1)}, f32[72,128]{1,0:T(8,128)S(1)}, u32[]{:S(2)}, u32[]{:S(2)}) collective-permute-start(f32[72,128]{1,0:T(8,128)S(1)} %get-tuple-element.120), channel_id=1, source_target_pairs={{0,28},{1,29},{2,30},{3,31},{4,24},{5,25},{6,26},{7,27},{8,20},{9,... | collective-permute-start | bytes 110600 | tf_op jit(solution)/shard_map/ppermute | solution.py:169
  152.0 3.9 %collective-permute-start.34 = (f32[280,128]{1,0:T(8,128)S(1)}, f32[280,128]{1,0:T(8,128)S(1)}, u32[]{:S(2)}, u32[]{:S(2)}) collective-permute-start(f32[280,128]{1,0:T(8,128)S(1)} %get-tuple-element.126), channel_id=1, source_target_pairs={{0,1},{1,0},{2,3},{3,2},{4,5},{5,4},{6,7},{7,6},{8,9},{9,8},{10,11... | collective-permute-start | bytes 430088 | tf_op jit(solution)/shard_map/ppermute | solution.py:169
  154.8 5.5 %collective-permute-start.35 = (f32[280,128]{1,0:T(8,128)S(1)}, f32[280,128]{1,0:T(8,128)S(1)}, u32[]{:S(2)}, u32[]{:S(2)}) collective-permute-start(f32[280,128]{1,0:T(8,128)S(1)} %get-tuple-element.127), channel_id=1, source_target_pairs={{0,3},{1,2},{2,1},{3,0},{4,7},{5,6},{6,5},{7,4},{8,11},{9,10},{10,... | collective-permute-start | bytes 430088 | tf_op jit(solution)/shard_map/ppermute | solution.py:169
  160.3 9.7 %collective-permute-start.36 = (f32[280,128]{1,0:T(8,128)S(1)}, f32[280,128]{1,0:T(8,128)S(1)}, u32[]{:S(2)}, u32[]{:S(2)}) collective-permute-start(f32[280,128]{1,0:T(8,128)S(1)} %get-tuple-element.128), channel_id=1, source_target_pairs={{0,4},{1,5},{2,6},{3,7},{4,0},{5,1},{6,2},{7,3},{8,12},{9,13},{10,... | collective-permute-start | bytes 430088 | tf_op jit(solution)/shard_map/ppermute | solution.py:169
  160.4 9.6 %collective-permute-start.37 = (f32[280,128]{1,0:T(8,128)S(1)}, f32[280,128]{1,0:T(8,128)S(1)}, u32[]{:S(2)}, u32[]{:S(2)}) collective-permute-start(f32[280,128]{1,0:T(8,128)S(1)} %get-tuple-element.129), channel_id=1, source_target_pairs={{0,12},{1,13},{2,14},{3,15},{4,8},{5,9},{6,10},{7,11},{8,4},{9,5},... | collective-permute-start | bytes 430088 | tf_op jit(solution)/shard_map/ppermute | solution.py:169
  161.4 8.6 %collective-permute-start.38 = (f32[280,128]{1,0:T(8,128)S(1)}, f32[280,128]{1,0:T(8,128)S(1)}, u32[]{:S(2)}, u32[]{:S(2)}) collective-permute-start(f32[280,128]{1,0:T(8,128)S(1)} %get-tuple-element.130), channel_id=1, source_target_pairs={{0,16},{1,17},{2,18},{3,19},{4,20},{5,21},{6,22},{7,23},{8,24},{9,... | collective-permute-start | bytes 430088 | tf_op jit(solution)/shard_map/ppermute | solution.py:169
  162.7 6.7 %collective-permute-start.39 = (f32[40,128]{1,0:T(8,128)S(1)}, f32[40,128]{1,0:T(8,128)S(1)}, u32[]{:S(2)}, u32[]{:S(2)}) collective-permute-start(f32[40,128]{1,0:T(8,128)S(1)} %get-tuple-element.131), channel_id=1, source_target_pairs={{0,20},{1,21},{2,22},{3,23},{4,16},{5,17},{6,18},{7,19},{8,28},{9,... | collective-permute-start | bytes 61448 | tf_op jit(solution)/shard_map/ppermute | solution.py:169
  163.1 6.9 %collective-permute-start.40 = (f32[40,128]{1,0:T(8,128)S(1)}, f32[40,128]{1,0:T(8,128)S(1)}, u32[]{:S(2)}, u32[]{:S(2)}) collective-permute-start(f32[40,128]{1,0:T(8,128)S(1)} %get-tuple-element.132), channel_id=1, source_target_pairs={{0,28},{1,29},{2,30},{3,31},{4,24},{5,25},{6,26},{7,27},{8,20},{9,... | collective-permute-start | bytes 61448 | tf_op jit(solution)/shard_map/ppermute | solution.py:169
  171.1 6.4 %collective-permute-start.41 = (f32[288,128]{1,0:T(8,128)S(1)}, f32[288,128]{1,0:T(8,128)S(1)}, u32[]{:S(2)}, u32[]{:S(2)}) collective-permute-start(f32[288,128]{1,0:T(8,128)S(1)} %get-tuple-element.135), channel_id=1, source_target_pairs={{0,1},{1,0},{2,3},{3,2},{4,5},{5,4},{6,7},{7,6},{8,9},{9,8},{10,11... | collective-permute-start | bytes 442376 | tf_op jit(solution)/shard_map/ppermute | solution.py:169
  172.3 5.6 %collective-permute-start.42 = (f32[288,128]{1,0:T(8,128)S(1)}, f32[288,128]{1,0:T(8,128)S(1)}, u32[]{:S(2)}, u32[]{:S(2)}) collective-permute-start(f32[288,128]{1,0:T(8,128)S(1)} %get-tuple-element.136), channel_id=1, source_target_pairs={{0,3},{1,2},{2,1},{3,0},{4,7},{5,6},{6,5},{7,4},{8,11},{9,10},{10,... | collective-permute-start | bytes 442376 | tf_op jit(solution)/shard_map/ppermute | solution.py:169
  173.0 4.5 %collective-permute-start.43 = (f32[8,128]{1,0:T(8,128)S(1)}, f32[8,128]{1,0:T(8,128)S(1)}, u32[]{:S(2)}, u32[]{:S(2)}) collective-permute-start(f32[8,128]{1,0:T(8,128)S(1)} %get-tuple-element.137), channel_id=1, source_target_pairs={{0,2},{1,3},{2,0},{3,1},{4,6},{5,7},{6,4},{7,5},{8,10},{9,11},{10,... | collective-permute-start | bytes 12296 | tf_op jit(solution)/shard_map/ppermute | solution.py:169
  177.9 17.3 %collective-permute-start.44 = (f32[312,128]{1,0:T(8,128)S(1)}, f32[312,128]{1,0:T(8,128)S(1)}, u32[]{:S(2)}, u32[]{:S(2)}) collective-permute-start(f32[312,128]{1,0:T(8,128)S(1)} %get-tuple-element.138), channel_id=1, source_target_pairs={{0,4},{1,5},{2,6},{3,7},{4,0},{5,1},{6,2},{7,3},{8,12},{9,13},{10,... | collective-permute-start | bytes 479240 | tf_op jit(solution)/shard_map/ppermute | solution.py:169
  179.4 15.8 %collective-permute-start.45 = (f32[312,128]{1,0:T(8,128)S(1)}, f32[312,128]{1,0:T(8,128)S(1)}, u32[]{:S(2)}, u32[]{:S(2)}) collective-permute-start(f32[312,128]{1,0:T(8,128)S(1)} %get-tuple-element.139), channel_id=1, source_target_pairs={{0,12},{1,13},{2,14},{3,15},{4,8},{5,9},{6,10},{7,11},{8,4},{9,5},... | collective-permute-start | bytes 479240 | tf_op jit(solution)/shard_map/ppermute | solution.py:169
  180.8 14.4 %collective-permute-start.47 = (f32[312,128]{1,0:T(8,128)S(1)}, f32[312,128]{1,0:T(8,128)S(1)}, u32[]{:S(2)}, u32[]{:S(2)}) collective-permute-start(f32[312,128]{1,0:T(8,128)S(1)} %get-tuple-element.141), channel_id=1, source_target_pairs={{0,16},{1,17},{2,18},{3,19},{4,20},{5,21},{6,22},{7,23},{8,24},{9,... | collective-permute-start | bytes 479240 | tf_op jit(solution)/shard_map/ppermute | solution.py:169
  180.9 5.0 %collective-permute-start.46 = (f32[32,128]{1,0:T(8,128)S(1)}, f32[32,128]{1,0:T(8,128)S(1)}, u32[]{:S(2)}, u32[]{:S(2)}) collective-permute-start(f32[32,128]{1,0:T(8,128)S(1)} %get-tuple-element.140), channel_id=1, source_target_pairs={{0,8},{1,9},{2,10},{3,11},{4,12},{5,13},{6,14},{7,15},{8,0},{9,1},... | collective-permute-start | bytes 49160 | tf_op jit(solution)/shard_map/ppermute | solution.py:169
  181.7 7.6 %collective-permute-start.50 = (f32[32,128]{1,0:T(8,128)S(1)}, f32[32,128]{1,0:T(8,128)S(1)}, u32[]{:S(2)}, u32[]{:S(2)}) collective-permute-start(f32[32,128]{1,0:T(8,128)S(1)} %get-tuple-element.144), channel_id=1, source_target_pairs={{0,24},{1,25},{2,26},{3,27},{4,28},{5,29},{6,30},{7,31},{8,16},{9,... | collective-permute-start | bytes 49160 | tf_op jit(solution)/shard_map/ppermute | solution.py:169
  185.9 4.9 %collective-permute-start.48 = (f32[72,128]{1,0:T(8,128)S(1)}, f32[72,128]{1,0:T(8,128)S(1)}, u32[]{:S(2)}, u32[]{:S(2)}) collective-permute-start(f32[72,128]{1,0:T(8,128)S(1)} %get-tuple-element.142), channel_id=1, source_target_pairs={{0,20},{1,21},{2,22},{3,23},{4,16},{5,17},{6,18},{7,19},{8,28},{9,... | collective-permute-start | bytes 110600 | tf_op jit(solution)/shard_map/ppermute | solution.py:169
  189.3 5.8 %collective-permute-start.49 = (f32[72,128]{1,0:T(8,128)S(1)}, f32[72,128]{1,0:T(8,128)S(1)}, u32[]{:S(2)}, u32[]{:S(2)}) collective-permute-start(f32[72,128]{1,0:T(8,128)S(1)} %get-tuple-element.143), channel_id=1, source_target_pairs={{0,28},{1,29},{2,30},{3,31},{4,24},{5,25},{6,26},{7,27},{8,20},{9,... | collective-permute-start | bytes 110600 | tf_op jit(solution)/shard_map/ppermute | solution.py:169
  197.7 3.9 %collective-permute-start.51 = (f32[280,128]{1,0:T(8,128)S(1)}, f32[280,128]{1,0:T(8,128)S(1)}, u32[]{:S(2)}, u32[]{:S(2)}) collective-permute-start(f32[280,128]{1,0:T(8,128)S(1)} %get-tuple-element.147), channel_id=1, source_target_pairs={{0,1},{1,0},{2,3},{3,2},{4,5},{5,4},{6,7},{7,6},{8,9},{9,8},{10,11... | collective-permute-start | bytes 430088 | tf_op jit(solution)/shard_map/ppermute | solution.py:169
  200.5 5.5 %collective-permute-start.52 = (f32[280,128]{1,0:T(8,128)S(1)}, f32[280,128]{1,0:T(8,128)S(1)}, u32[]{:S(2)}, u32[]{:S(2)}) collective-permute-start(f32[280,128]{1,0:T(8,128)S(1)} %get-tuple-element.148), channel_id=1, source_target_pairs={{0,3},{1,2},{2,1},{3,0},{4,7},{5,6},{6,5},{7,4},{8,11},{9,10},{10,... | collective-permute-start | bytes 430088 | tf_op jit(solution)/shard_map/ppermute | solution.py:169
  206.0 10.0 %collective-permute-start.53 = (f32[280,128]{1,0:T(8,128)S(1)}, f32[280,128]{1,0:T(8,128)S(1)}, u32[]{:S(2)}, u32[]{:S(2)}) collective-permute-start(f32[280,128]{1,0:T(8,128)S(1)} %get-tuple-element.149), channel_id=1, source_target_pairs={{0,4},{1,5},{2,6},{3,7},{4,0},{5,1},{6,2},{7,3},{8,12},{9,13},{10,... | collective-permute-start | bytes 430088 | tf_op jit(solution)/shard_map/ppermute | solution.py:169
  206.1 9.9 %collective-permute-start.54 = (f32[280,128]{1,0:T(8,128)S(1)}, f32[280,128]{1,0:T(8,128)S(1)}, u32[]{:S(2)}, u32[]{:S(2)}) collective-permute-start(f32[280,128]{1,0:T(8,128)S(1)} %get-tuple-element.150), channel_id=1, source_target_pairs={{0,12},{1,13},{2,14},{3,15},{4,8},{5,9},{6,10},{7,11},{8,4},{9,5},... | collective-permute-start | bytes 430088 | tf_op jit(solution)/shard_map/ppermute | solution.py:169
  208.0 8.0 %collective-permute-start.55 = (f32[280,128]{1,0:T(8,128)S(1)}, f32[280,128]{1,0:T(8,128)S(1)}, u32[]{:S(2)}, u32[]{:S(2)}) collective-permute-start(f32[280,128]{1,0:T(8,128)S(1)} %get-tuple-element.151), channel_id=1, source_target_pairs={{0,16},{1,17},{2,18},{3,19},{4,20},{5,21},{6,22},{7,23},{8,24},{9,... | collective-permute-start | bytes 430088 | tf_op jit(solution)/shard_map/ppermute | solution.py:169
  208.6 4.3 %collective-permute-start.56 = (f32[40,128]{1,0:T(8,128)S(1)}, f32[40,128]{1,0:T(8,128)S(1)}, u32[]{:S(2)}, u32[]{:S(2)}) collective-permute-start(f32[40,128]{1,0:T(8,128)S(1)} %get-tuple-element.152), channel_id=1, source_target_pairs={{0,20},{1,21},{2,22},{3,23},{4,16},{5,17},{6,18},{7,19},{8,28},{9,... | collective-permute-start | bytes 61448 | tf_op jit(solution)/shard_map/ppermute | solution.py:169
  209.6 6.3 %collective-permute-start.57 = (f32[40,128]{1,0:T(8,128)S(1)}, f32[40,128]{1,0:T(8,128)S(1)}, u32[]{:S(2)}, u32[]{:S(2)}) collective-permute-start(f32[40,128]{1,0:T(8,128)S(1)} %get-tuple-element.153), channel_id=1, source_target_pairs={{0,28},{1,29},{2,30},{3,31},{4,24},{5,25},{6,26},{7,27},{8,20},{9,... | collective-permute-start | bytes 61448 | tf_op jit(solution)/shard_map/ppermute | solution.py:169
where the time goes:
time: 222 us; the launch traced here: 220 us
  waiting for transfers between devices  81.5 us (37%)
  starting transfers between devices  79.5 us (36%)
  Pallas kernels  48.6 us (22%)
  local copies, waits for them, and re-layouts  8.74 us (4%)
    ppermute x58, waiting for transfers between devices, transfer(): lax.ppermute(p, AXES, m.pairs())  81.5 us
    ppermute x58, starting transfers between devices, transfer(): lax.ppermute(p, AXES, m.pairs())  79.5 us
    pallas_call x16, Pallas kernels, call(): pl.pallas_call(kernel, out_shape=tuple(outs), in_specs=specs or [vm()] *...  48.6 us
  transfers between devices with their start and end apart: 58, of which 27 were waited for; matrix products, arithmetic and copies ran while one was open for 2% of the time, Pallas kernels for 14%

commit v1 on v0

v1 whole, which is shorter than its diff:
```python
import functools
import itertools

import jax
import jax.numpy as jnp
from jax import lax
from jax.experimental import pallas as pl
from jax.experimental.pallas import tpu as pltpu
from jax.sharding import PartitionSpec as P

NODES = 7
DOF = 3
ITERS = 3
AXES = ("gx", "gy", "gz")
STAGES = ((2,), (0, 1))
PAD = 8
CHUNK = 24
TILE = 256
F32 = jnp.float32
BF16 = jnp.bfloat16


def piece_length(placed):
    return DOF * NODES ** sum(1 for c in placed if c == 1)


PLACES = [p for p in itertools.product(range(3), repeat=3) if p != (1, 1, 1)]
CANON_OFFSET = {}
_at = 0
for _p in PLACES:
    CANON_OFFSET[_p] = _at
    _at += piece_length(_p)
IFACE = _at
SLOT_OFFSET = {}
SLOT_ROWS = {}
_at = 0
for _p in PLACES:
    SLOT_OFFSET[_p] = _at
    SLOT_ROWS[_p] = -(-piece_length(_p) // PAD) * PAD
    _at += SLOT_ROWS[_p]
COARSE_AT = _at
ROWS = -(-(COARSE_AT + 16) // TILE) * TILE


class Message:
    def __init__(self, moves, sizes):
        self.moves = moves
        self.sizes = sizes
        self.faces = "C" not in moves
        self.slots = []
        if self.faces:
            for place in PLACES:
                if all(m is None or c == (0 if m == "A" else 2) for m, c in zip(moves, place)):
                    self.slots.append(place)
        self.rows = sum(SLOT_ROWS[s] for s in self.slots)
        self.basis = []

    def xor(self):
        code = 0
        for move, size in zip(self.moves, self.sizes):
            code = code * size + {None: 0, "A": 1, "B": 3, "C": 2}[move]
        return code

    def pairs(self):
        out = []
        for place in itertools.product(*(range(s) for s in self.sizes)):
            to = []
            for at, move, size in zip(place, self.moves, self.sizes):
                if move == "A":
                    at = at ^ 1
                elif move == "B":
                    at = (at - 1) % size if at % 2 == 0 else (at + 1) % size
                elif move == "C":
                    at = at ^ 2
                to.append(at)
            flat = [0, 0]
            for a, b, size in zip(place, to, self.sizes):
                flat = [flat[0] * size + a, flat[1] * size + b]
            out.append(tuple(flat))
        return out


def ports(size):
    return ("A",) if size == 2 else ("A", "B")


def stage_messages(dims, sizes, coarse):
    choices = []
    for d in range(3):
        if d not in dims:
            choices.append((None,))
        else:
            extra = ("C",) if coarse and sizes[d] == 4 else ()
            choices.append((None,) + ports(sizes[d]) + extra)
    return [Message(m, sizes) for m in itertools.product(*choices) if any(c is not None for c in m)]


class Plan:
    def __init__(self, sizes):
        self.sizes = sizes
        self.subs = sizes[0] * sizes[1] * sizes[2]
        self.ride = all(s in (2, 4) for s in sizes)
        self.plain = [stage_messages(d, sizes, False) for d in STAGES]
        self.coarse = [stage_messages(d, sizes, True) for d in STAGES]
        self.wide = self.subs * 8
        first, second = self.coarse
        for message in first:
            message.basis = [((), slot) for slot in message.slots]
        for message in second:
            message.basis = [((), slot) for slot in message.slots]
            for other in first:
                message.basis += [((other,), slot) for slot in message.slots if slot in other.slots]

    def messages(self, coarse):
        return self.coarse if coarse and self.ride else self.plain


def position():
    return [lax.axis_index(a) for a in AXES]


def has_b(index, size):
    if size == 2:
        return None
    return jnp.logical_and(index > 0, index < size - 1)


def pick(slot, index, of):
    def choose(d, place):
        if d == 3:
            return of(tuple(place))
        if slot[d] == 1:
            return choose(d + 1, place + [1])
        even, odd = (2, 0) if slot[d] == 0 else (0, 2)
        return jnp.where(index[d] % 2 == 0, choose(d + 1, place + [even]), choose(d + 1, place + [odd]))

    return choose(0, [])


def add_received(plan, index, messages, received, acc):
    for message, ref in zip(messages, received):
        if not message.faces:
            continue
        ok = None
        for d, move in enumerate(message.moves):
            if move == "B":
                here = has_b(index[d], plan.sizes[d])
                ok = here if ok is None else jnp.logical_and(ok, here)
        at = 0
        for slot in message.slots:
            rows, to = SLOT_ROWS[slot], SLOT_OFFSET[slot]
            value = ref[at : at + rows, :]
            if ok is not None:
                value = jnp.where(ok, value, 0.0)
            acc[to : to + rows, :] += value
            at += rows


def write_payloads(messages, outs, acc, blocks, pack=None):
    for message, out in zip(messages, outs):
        at = 0
        for slot in message.slots:
            rows, frm = SLOT_ROWS[slot], SLOT_OFFSET[slot]
            out[at : at + rows, :] = acc[frm : frm + rows, :]
            at += rows
        for block in blocks:
            out[at : at + 8, :] = block
            at += 8
        if pack is not None and message.faces:
            out[at : at + CHUNK, :] = pack(message)


def payload_shapes(messages, blocks, packed=False):
    return [
        jax.ShapeDtypeStruct((m.rows + 8 * blocks + (CHUNK if packed and m.faces else 0), 128), F32)
        for m in messages
    ]


def packer(own, stage, unpacked):
    def pack(message):
        at = 0
        for source, slot in message.basis:
            rows = SLOT_ROWS[slot]
            if source:
                ref = unpacked[source[0]]
                frm = sum(SLOT_ROWS[s] for s in source[0].slots[: source[0].slots.index(slot)])
            else:
                ref, frm = own, SLOT_OFFSET[slot]
            stage[at : at + rows, :] = ref[frm : frm + rows, :]
            at += rows
        count = -(-at // CHUNK)
        if at < count * CHUNK:
            stage[at : count * CHUNK, :] = jnp.zeros((count * CHUNK - at, 128), F32)
        total = stage[0:CHUNK, :]
        for k in range(1, count):
            total += pltpu.roll(stage[k * CHUNK : (k + 1) * CHUNK, :], 8 * k, 1)
        return total

    return pack


def unpack(message, block, out):
    count = -(-sum(SLOT_ROWS[slot] for _, slot in message.basis) // CHUNK)
    lane = lax.broadcasted_iota(jnp.int32, (CHUNK, 128), 1)
    for k in range(count):
        turned = pltpu.roll(block, 128 - 8 * k, 1) if k else block
        out[k * CHUNK : (k + 1) * CHUNK, :] = jnp.where(lane < 8, turned, 0.0)


def transfer(messages, payloads):
    return [lax.ppermute(p, AXES, m.pairs()) for m, p in zip(messages, payloads)]


def vm():
    return pl.BlockSpec(memory_space=pltpu.VMEM)


def call(kernel, outs, operands, specs=None, scratch=(), limit=20, flops=0):
    nbytes = sum(o.size * o.dtype.itemsize for o in list(outs) + list(operands))
    return pl.pallas_call(
        kernel,
        out_shape=tuple(outs),
        in_specs=specs or [vm()] * len(operands),
        out_specs=tuple(vm() for _ in outs),
        scratch_shapes=list(scratch),
        compiler_params=pltpu.CompilerParams(vmem_limit_bytes=limit << 20),
        cost_estimate=pl.CostEstimate(flops=flops, bytes_accessed=nbytes, transcendentals=0),
    )(*operands)


def gather_rows(index, canon, load, acc):
    for slot in PLACES:
        rows, at = SLOT_ROWS[slot], SLOT_OFFSET[slot]
        acc[at + rows - 8 : at + rows, :] = jnp.zeros((8, acc.shape[1]), F32)
    acc[COARSE_AT:, :] = jnp.zeros((ROWS - COARSE_AT, acc.shape[1]), F32)
    for slot in PLACES:
        length, at = piece_length(slot), SLOT_OFFSET[slot]
        off = pick(slot, index, lambda place: jnp.int32(CANON_OFFSET[place]))
        step = 7 if length % 7 == 0 else 3

        def body(i, _, off=off, at=at, step=step):
            for j in range(step):
                row = i * step + j
                acc[pl.ds(at + row, 1), :] = load[canon[off + row], :, :]
            return 0

        lax.fori_loop(0, length // step, body, 0)


def input_kernel(plan, canon, load, acc, *outs):
    gather_rows(position(), canon, load, acc)
    write_payloads(plan.plain[0], outs, acc, [])


def scatter_rows(index, canon, pairs):
    for slot in PLACES:
        length, at = piece_length(slot), SLOT_OFFSET[slot]
        off = pick(slot, index, lambda place: jnp.int32(CANON_OFFSET[place]))
        step = 7 if length % 7 == 0 else 3

        def body(i, _, off=off, at=at, step=step):
            for j in range(step):
                row = i * step + j
                to = canon[off + row]
                for acc, out in pairs:
                    out[to, :, :] = acc[pl.ds(at + row, 1), :]
            return 0

        lax.fori_loop(0, length // step, body, 0)


def split(value, parts):
    out = []
    for _ in range(parts):
        piece = value.astype(BF16)
        out.append(piece)
        value = value - piece.astype(F32)
    return out


def dot(a, b):
    return jnp.dot(a, b, preferred_element_type=F32)


def dot_last(a, b):
    return lax.dot_general(a, b, (((1,), (1,)), ((), ())), preferred_element_type=F32)


def tile(t):
    return pl.ds(pl.multiple_of(t * TILE, TILE), TILE)


def each_tile(body):
    def step(t, _):
        body(tile(t))
        return 0

    lax.fori_loop(0, ROWS // TILE, step, 0)


def select_kernel(plan, canon, basis, cinv, one, one_w, turned, *rest):
    src, wgt = rest[-2:]
    index = position()
    src[...] = jnp.full(src.shape, -1, jnp.int32)
    wgt[...] = jnp.zeros(wgt.shape, F32)
    for slot in PLACES:
        at, length = SLOT_OFFSET[slot], piece_length(slot)
        src[at : at + length, :] = pick(
            slot, index, lambda place, length=length: canon[CANON_OFFSET[place] : CANON_OFFSET[place] + length, :]
        )
        weight = jnp.float32(1.0)
        for d in range(3):
            if slot[d] == 0:
                weight = weight * 0.5
            elif slot[d] == 2 and plan.sizes[d] > 2:
                weight = weight * jnp.where(has_b(index[d], plan.sizes[d]), 0.5, 1.0)
        wgt[at : at + length, :] = jnp.full((length, 1), 1.0, F32) * weight
    if plan.ride:
        nc = cinv.shape[1]
        row = lax.broadcasted_iota(jnp.int32, (nc, plan.wide), 0)
        col = lax.broadcasted_iota(jnp.int32, (nc, plan.wide), 1)
        spread = jnp.where(jnp.logical_and((col >> 3) * 6 + (col & 7) == row, (col & 7) < 6), 1.0, 0.0).astype(BF16)
        rest[0][...] = sum(dot(part, spread) for part in split(cinv[...], 3))[:8]

    def build(rows):
        hit = src[rows, :] == lax.broadcasted_iota(jnp.int32, (TILE, IFACE), 1)
        one[rows, :] = jnp.where(hit, 1.0, 0.0).astype(BF16)
        weighted = jnp.where(hit, wgt[rows, :], 0.0).astype(BF16)
        one_w[rows, :] = weighted
        turned[rows, :] = dot_last(weighted, basis[...])

    each_tile(build)


def left_kernel(one, matrix, mid):
    def body(rows):
        mid[rows, :] = dot(one[rows, :], matrix[...]).astype(BF16)

    each_tile(body)


def right_kernel(one, mid, basis, out):
    def body(rows):
        out[rows, :] = dot_last(mid[rows, :], one[...]).astype(BF16)

    each_tile(body)
    if basis is not None:
        out[COARSE_AT : COARSE_AT + 16, :] = dot_last(basis[:16, :], one[...]).astype(BF16)


def middle_kernel(plan, coarse, opening, *refs):
    first, second = plan.messages(coarse)
    ride = coarse and plan.ride
    setup = ride and opening
    refs = list(refs)
    base = refs.pop(0)
    received = [refs.pop(0) for _ in first]
    own_blocks, pack = [], None
    if setup:
        spread, turned = refs.pop(0), refs.pop(0)
        own_blocks = [spread[:, 128 * i : 128 * (i + 1)] for i in range(plan.wide // 128)]
        stage = refs.pop(-1)
        kept = {m: refs.pop(-1) for m in reversed(first) if m.faces}
        for message, ref in zip(first, received):
            if message.faces:
                at = message.rows + 8 * (1 + len(own_blocks))
                unpack(message, ref[at : at + CHUNK, :], kept[message])
        pack = packer(turned, stage, kept)
    acc = refs.pop(-1)
    outs = refs
    acc[...] = base[...]
    add_received(plan, position(), first, received, acc)
    blocks = []
    if ride:
        per = 1 + len(own_blocks)
        blocks = [base[COARSE_AT : COARSE_AT + 8, :]] + own_blocks
        for message, ref in zip(first, received):
            blocks += [ref[message.rows + 8 * i : message.rows + 8 * (i + 1), :] for i in range(per)]
    write_payloads(second, outs, acc, blocks, pack)


def multiply(matrix, vector, out):
    for t in range(ROWS // TILE):
        out[t * TILE : (t + 1) * TILE, :] = dot(matrix[t * TILE : (t + 1) * TILE, :], vector)


def inverse_kernel(plan, opening, *refs):
    first, second = plan.plain
    refs = list(refs)
    base = refs.pop(0)
    got = [refs.pop(0) for _ in range(len(first) + len(second))]
    matrix = refs.pop(0)
    before = None if opening else refs.pop(0)
    own_blocks, pack = [], None
    if opening and plan.ride:
        spread, turned = refs.pop(0), refs.pop(0)
        own_blocks = [spread[:, 128 * i : 128 * (i + 1)] for i in range(plan.wide // 128)]
        pack = packer(turned, refs.pop(-1), {})
    acc = refs.pop(-1)
    residual, out, *outs = refs
    index = position()
    acc[...] = base[...]
    add_received(plan, index, first, got[: len(first)], acc)
    add_received(plan, index, second, got[len(first) :], acc)
    value = acc[...] if opening else before[...] - acc[...]
    residual[...] = value
    multiply(matrix, value.astype(BF16), out)
    if plan.ride:
        write_payloads(plan.coarse[0], outs, out, [out[COARSE_AT : COARSE_AT + 8, :]] + own_blocks, pack)


def lift_kernel(plan, base, turned, correction, out, *outs):
    lifted = turned[...].astype(BF16)
    out[...] = base[...] + sum(dot(lifted, part) for part in split(correction[...], 3))
    write_payloads(plan.plain[0], outs, out, [])


def collect(plan, index, own, got, per, which, stack, at_column):
    first, second = plan.coarse
    me = (index[0] * plan.sizes[1] + index[1]) * plan.sizes[2] + index[2]
    near = [0] + [m.xor() for m in first]

    def put(code, value):
        stack[pl.ds(pl.multiple_of((me ^ code) * 8, 8), 8), at_column : at_column + 128] = value

    put(0, own)
    for m, ref in zip(first, got):
        at = m.rows + 8 * which
        put(m.xor(), ref[at : at + 8, :])
    for m, ref in zip(second, got[len(first) :]):
        for i, code in enumerate(near):
            at = m.rows + 8 * (per * i + which)
            put(code ^ m.xor(), ref[at : at + 8, :])


def lifting(plan, index, got, per, turned, spread, stack, many, unpacked, out):
    first, second = plan.coarse
    halves = plan.wide // 128
    me = (index[0] * plan.sizes[1] + index[1]) * plan.sizes[2] + index[2]

    def place(code, value, to, ok):
        there = me ^ code
        value = pltpu.roll(value, (there & 15) * 8, 1)
        rows = value.shape[0]
        for half in range(halves):
            here = (there >> 4) == half
            if ok is not None:
                here = jnp.logical_and(here, ok)
            many[to : to + rows, 128 * half : 128 * (half + 1)] += jnp.where(here, value, 0.0)

    def exists(message):
        ok = None
        for d, move in enumerate(message.moves):
            if move == "B":
                here = has_b(index[d], plan.sizes[d])
                ok = here if ok is None else jnp.logical_and(ok, here)
        return ok

    many[...] = jnp.zeros(many.shape, F32)
    for t in range(ROWS // TILE):
        place(0, turned[t * TILE : (t + 1) * TILE, :], t * TILE, None)
    for m, ref in zip(first + second, got):
        if not m.faces:
            continue
        blocks = per * (1 if m in first else 1 + len(first))
        at = m.rows + 8 * blocks
        unpack(m, ref[at : at + CHUNK, :], unpacked)
        at, ok = 0, exists(m)
        for source, slot in m.basis:
            code, fine = m.xor(), ok
            if source:
                code ^= source[0].xor()
                also = exists(source[0])
                if also is not None:
                    fine = also if fine is None else jnp.logical_and(fine, also)
            place(code, unpacked[at : at + SLOT_ROWS[slot], :], SLOT_OFFSET[slot], fine)
            at += SLOT_ROWS[slot]
    for half in range(halves):
        own = spread[:, 128 * half : 128 * (half + 1)]
        collect(plan, index, own, got, per, 1 + half, stack, 128 * half)
    parts = jnp.concatenate(split(stack[...], 3), axis=0)

    def body(rows):
        basis = many[rows, :].astype(BF16)
        whole = dot(jnp.concatenate([basis] * 3, axis=1), parts)
        high, low = split(whole, 2)
        out[rows, :] = jnp.concatenate([high, high, low], axis=1)

    each_tile(body)


def schur_kernel(plan, opening, *refs):
    first, second = plan.messages(True)
    refs = list(refs)
    base = refs.pop(0)
    got = [refs.pop(0) for _ in range(len(first) + len(second))]
    matrix = refs.pop(0)
    setup = plan.ride and opening
    sol_in = None if opening else refs.pop(0)
    if setup:
        spread, turned = refs.pop(0), refs.pop(0)
        unpacked, many, wide_stack = refs.pop(-1), refs.pop(-1), refs.pop(-1)
    elif plan.ride:
        lift = refs.pop(0)
    acc, stack = refs.pop(-2), refs.pop(-1)
    sol, out = refs.pop(0), refs.pop(0)
    outs = refs[: len(plan.plain[0])]
    index = position()
    per = 1
    if setup:
        lift = refs[-1]
        per = 1 + plan.wide // 128
        lifting(plan, index, got, per, turned, spread, wide_stack, many, unpacked, lift)
    acc[...] = base[...]
    add_received(plan, index, first, got[: len(first)], acc)
    add_received(plan, index, second, got[len(first) :], acc)
    if plan.ride:
        collect(plan, index, base[COARSE_AT : COARSE_AT + 8, :], got, per, 0, stack, 0)
        high, low = split(stack[...], 2)
        multiply(lift, jnp.concatenate([high, low, high], axis=0), out)
        update = acc[...] + out[...]
    else:
        update = acc[...]
    sol[...] = update if opening else sol_in[...] + update
    multiply(matrix, update.astype(BF16), out)
    write_payloads(plan.plain[0], outs, out, [])


def output_kernel(plan, canon, base, *refs):
    first, second = plan.plain
    count = len(first) + len(second)
    got = refs[:count]
    residual, sol, sol_out, residual_out, acc = refs[count:]
    index = position()
    acc[...] = base[...]
    add_received(plan, index, first, got[: len(first)], acc)
    add_received(plan, index, second, got[len(first) :], acc)
    acc[...] = residual[...] - acc[...]
    scatter_rows(index, canon, [(sol, sol_out), (acc, residual_out)])


def shape(rows, cols, dtype=F32):
    return jax.ShapeDtypeStruct((rows, cols), dtype)


def local(plan, load_cases, schur_matrix, local_inverse, coarse_basis, coarse_inverse, canon_rows):
    smem = pl.BlockSpec(memory_space=pltpu.SMEM)
    loads = load_cases.shape[-1]
    canon = canon_rows.reshape(IFACE)
    load = load_cases.reshape(IFACE, 1, loads)
    basis = jnp.pad(coarse_basis[0, 0, 0], ((0, 122), (0, 0)))
    cinv = jnp.pad(coarse_inverse, ((0, 10), (0, 0)))
    plain, coarse = plan.plain, plan.messages(True)
    acc = pltpu.VMEM((ROWS, 128), F32)
    pieces = pltpu.VMEM((16 * CHUNK, 128), F32)
    setup_blocks = plan.wide // 128 if plan.ride else 0

    def middle(is_coarse, opening, base, got, extra):
        first, second = plan.messages(is_coarse)
        setup = is_coarse and opening and plan.ride
        blocks = 0
        if is_coarse and plan.ride:
            blocks = (len(first) + 1) * (1 + (setup_blocks if opening else 0))
        return call(
            functools.partial(middle_kernel, plan, is_coarse, opening),
            payload_shapes(second, blocks, setup),
            [base] + got + (extra if setup else []),
            scratch=[acc] + ([pieces] * (1 + sum(m.faces for m in first)) if setup else []),
        )

    def assemble(is_coarse, opening, base, payloads, extra):
        first, second = plan.messages(is_coarse)
        got = transfer(first, payloads)
        return got + transfer(second, middle(is_coarse, opening, base, got, extra))

    base, *payloads = call(
        functools.partial(input_kernel, plan),
        [shape(ROWS, 128)] + payload_shapes(plain[0], 0),
        [canon, load],
        specs=[smem, vm()],
    )
    one, one_w, turned, *spread = call(
        functools.partial(select_kernel, plan),
        [shape(ROWS, IFACE, BF16), shape(ROWS, IFACE, BF16), shape(ROWS, 128)]
        + ([shape(8, plan.wide)] if plan.ride else []),
        [canon_rows.reshape(IFACE, 1), basis, cinv],
        scratch=[pltpu.VMEM((ROWS, 1), jnp.int32), pltpu.VMEM((ROWS, 1), F32)],
        flops=2 * ROWS * IFACE * 1158,
    )
    flops = 2 * ROWS * IFACE * IFACE
    middle_shape, square = shape(ROWS, IFACE, BF16), shape(ROWS, ROWS, BF16)

    def right_plain(a, b, out):
        right_kernel(a, b, None, out)

    (half,) = call(left_kernel, [middle_shape], [one_w, local_inverse[0, 0, 0]], flops=flops)
    (inverse,) = call(right_kernel, [square], [one_w, half, basis], flops=flops)
    (half,) = call(left_kernel, [middle_shape], [one, schur_matrix[0, 0, 0]], flops=flops)
    (schur,) = call(right_plain, [square], [one, half], flops=flops)
    got = assemble(False, False, base, payloads, [])
    sol = None
    extra = spread + [turned]
    flops = 2 * ROWS * ROWS * 128
    for iteration in range(ITERS):
        opening = iteration == 0
        setup = opening and plan.ride
        residual, base, *payloads = call(
            functools.partial(inverse_kernel, plan, opening),
            [shape(ROWS, 128), shape(ROWS, 128)]
            + (payload_shapes(coarse[0], 1 + (setup_blocks if opening else 0), setup) if plan.ride else []),
            [base] + got + [inverse] + ([] if opening else [residual]) + (extra if setup else []),
            scratch=[acc] + ([pieces] if setup else []),
            flops=flops,
        )
        if not plan.ride:
            rows = lax.all_gather(base[COARSE_AT : COARSE_AT + 6], AXES, axis=0, tiled=True)
            correction = jnp.dot(cinv, rows, precision=lax.Precision.HIGHEST, preferred_element_type=F32)
            base, *payloads = call(
                functools.partial(lift_kernel, plan),
                [shape(ROWS, 128)] + payload_shapes(plain[0], 0),
                [base, turned, jnp.pad(correction, ((0, 112), (0, 0)))],
            )
        got = assemble(True, opening, base, payloads, extra)
        given = [] if opening else [sol]
        if plan.ride:
            given += extra if opening else [lift]
        stack = [pltpu.VMEM((plan.wide, plan.wide), F32), pltpu.VMEM((ROWS, plan.wide), F32), pieces]
        results = call(
            functools.partial(schur_kernel, plan, opening),
            [shape(ROWS, 128), shape(ROWS, 128)]
            + payload_shapes(plain[0], 0)
            + ([shape(ROWS, 3 * plan.wide, BF16)] if setup else []),
            [base] + got + [schur] + given,
            scratch=[acc, pltpu.VMEM((plan.wide, 128), F32)] + (stack if setup else []),
            flops=flops,
        )
        sol, base, *payloads = results[: 2 + len(plain[0])]
        if setup:
            lift = results[-1]
        got = assemble(False, opening, base, payloads, [])
    out = jax.ShapeDtypeStruct((IFACE, 1, loads), F32)
    sol_out, residual_out = call(
        functools.partial(output_kernel, plan),
        [out, out],
        [canon, base] + got + [residual, sol],
        specs=[smem] + [vm()] * (3 + len(got)),
        scratch=[acc],
    )
    return tuple(o.reshape(1, 1, 1, IFACE, loads) for o in (sol_out, residual_out))


def solution(mesh):
    plan = Plan(tuple(mesh.shape[a] for a in AXES))
    in_specs = (
        P("gx", "gy", "gz", None, None),
        P("gx", "gy", "gz", None, None),
        P("gx", "gy", "gz", None, None),
        P("gx", "gy", "gz", None, None),
        P(("gx", "gy", "gz"), None),
        P("gx", "gy", "gz", None),
    )
    out_specs = (P("gx", "gy", "gz", None, None), P("gx", "gy", "gz", None, None))
    return jax.shard_map(
        functools.partial(local, plan), mesh=mesh, in_specs=in_specs, out_specs=out_specs, check_vma=False
    )
```

time: 222 us -> 182 us (0.82)
  waiting for transfers between devices: 81.5 us -> 61.2 us
  starting transfers between devices: 79.5 us -> 71.9 us
  Pallas kernels: 48.6 us -> 42.2 us
  local copies, waits for them, and re-layouts: 8.74 us -> 3.46 us
    ppermute x58, waiting for transfers between devices: 81.5 us -> 61.2 us  [transfer(): lax.ppermute(p, AXES, m.pairs())]
    ppermute x58, starting transfers between devices: 79.5 us -> 71.9 us  [transfer(): lax.ppermute(p, AXES, m.pairs())]
    pallas_call x16 -> x20, Pallas kernels: 48.6 us -> 42.2 us  [call(): pl.pallas_call(kernel, out_shape=tuple(outs), in_specs=specs or [vm()] *...]
    unnamed x10 -> x6, local copies, waits for them, and re-layouts: 4.3 us -> 1.07 us
  transfers between devices with their start and end apart: 58 -> 58, of which waited for: 27 -> 25; matrix products, arithmetic and copies ran while one was open for 2% -> 1% of each run, Pallas kernels for 14% -> 13%
where the time goes in v1:
time: 182 us; the launch traced here: 180 us
  starting transfers between devices  71.9 us (40%)
  waiting for transfers between devices  61.2 us (34%)
  Pallas kernels  42.2 us (23%)
  local copies, waits for them, and re-layouts  3.46 us (2%)
    ppermute x58, starting transfers between devices, transfer(): lax.ppermute(p, AXES, m.pairs())  71.9 us
    ppermute x58, waiting for transfers between devices, transfer(): lax.ppermute(p, AXES, m.pairs())  61.2 us
    pallas_call x20, Pallas kernels, call(): pl.pallas_call(kernel, out_shape=tuple(outs), in_specs=specs or [vm()] *...  42.2 us
  transfers between devices with their start and end apart: 58, of which 25 were waited for; matrix products, arithmetic and copies ran while one was open for 1% of the time, Pallas kernels for 13%

profile of v1, /device:TPU:1, one launch (start us, length us, event | category | flops | bytes accessed | tf_op | source)
XLA Modules:
  0.0 180.5 jit_solution(14836279540202370585)
XLA Ops:
  1.4 1.1 copy-done
  2.4 2.7 %shard_map.77 = (f32[1280,128]{1,0:T(8,128)S(1)}, f32[280,128]{1,0:T(8,128)S(1)}, f32[280,128]{1,0:T(8,128)S(1)}) custom-call(s32[1158]{0:T(1024)S(1)} %reduce.canon, f32[1158,1,128]{2,1,0:T(1,128)S(1)} %bitcast.11), custom_call_target="tpu_custom_call" | custom-call | bytes 1539608 | tf_op jit(solution)/shard_map/pallas_call | solution.py:221
  5.2 2.7 %collective-permute-start.1 = (f32[280,128]{1,0:T(8,128)S(1)}, f32[280,128]{1,0:T(8,128)S(1)}, u32[]{:S(2)}, u32[]{:S(2)}) collective-permute-start(f32[280,128]{1,0:T(8,128)S(1)} %get-tuple-element.82), channel_id=1, source_target_pairs={{0,3},{1,2},{2,1},{3,0},{4,7},{5,6},{6,5},{7,4},{8,11},{9,10},{10,... | collective-permute-start | bytes 430088 | tf_op jit(solution)/shard_map/ppermute | solution.py:212
  10.3 2.6 %shard_map.79 = (bf16[1280,1158]{1,0:T(8,128)(2,1)S(1)}, bf16[1280,1158]{1,0:T(8,128)(2,1)S(1)}, f32[1280,128]{1,0:T(8,128)S(1)}, f32[8,256]{1,0:T(8,128)S(1)}) custom-call(s32[1158,1]{1,0:T(8,128)S(1)} %copy.10.canon, bf16[128,1158]{1,0:T(8,128)(2,1)S(1)} %pad.8.basis, f32[16,192]{1,0:T(8,128)S(1)} %pad.9.cinv), custom_call_target="tpu_custom_call" | custom-call | flops 3432867840 | bytes 6905880 | tf_op jit(solution)/shard_map/pallas_call | solution.py:221
  12.9 5.1 %shard_map.80.mid = bf16[1280,1158]{1,0:T(8,128)(2,1)S(1)} custom-call(bf16[1280,1158]{1,0:T(8,128)(2,1)S(1)} %get-tuple-element.88.one, bf16[1158,1158]{1,0:T(8,128)(2,1)S(1)} %bitcast.12), custom_call_target="tpu_custom_call" | custom-call | flops 3432867840 | bytes 8610888 | tf_op jit(solution)/shard_map/pallas_call | solution.py:221
  18.1 2.3 %collective-permute-start.5 = (f32[40,128]{1,0:T(8,128)S(1)}, f32[40,128]{1,0:T(8,128)S(1)}, u32[]{:S(2)}, u32[]{:S(2)}) collective-permute-start(f32[40,128]{1,0:T(8,128)S(1)} %get-tuple-element.86), channel_id=1, source_target_pairs={{0,20},{1,21},{2,22},{3,23},{4,16},{5,17},{6,18},{7,19},{8,28},{9,... | collective-permute-start | bytes 61448 | tf_op jit(solution)/shard_map/ppermute | solution.py:212
  20.4 2.2 %collective-permute-start.6 = (f32[40,128]{1,0:T(8,128)S(1)}, f32[40,128]{1,0:T(8,128)S(1)}, u32[]{:S(2)}, u32[]{:S(2)}) collective-permute-start(f32[40,128]{1,0:T(8,128)S(1)} %get-tuple-element.87), channel_id=1, source_target_pairs={{0,28},{1,29},{2,30},{3,31},{4,24},{5,25},{6,26},{7,27},{8,20},{9,... | collective-permute-start | bytes 61448 | tf_op jit(solution)/shard_map/ppermute | solution.py:212
  24.8 6.2 %shard_map.81.refs_8_ = bf16[1280,1280]{1,0:T(8,128)(2,1)S(1)} custom-call(bf16[1280,1158]{1,0:T(8,128)(2,1)S(1)} %get-tuple-element.88.one, bf16[1280,1158]{1,0:T(8,128)(2,1)S(1)} %shard_map.80.mid, bf16[128,1158]{1,0:T(8,128)(2,1)S(1)} %pad.8.basis), custom_call_target="tpu_custom_call" | custom-call | flops 3432867840 | bytes 9502208 | tf_op jit(solution)/shard_map/pallas_call | solution.py:221
  31.1 1.1 shard_map.82
  32.2 1.6 collective-permute-start.7
  34.0 1.2 collective-permute-start.9
  35.3 4.3 %collective-permute-done.9.refs_3_ = f32[24,128]{1,0:T(8,128)S(1)} collective-permute-done((f32[24,128]{1,0:T(8,128)S(1)}, f32[24,128]{1,0:T(8,128)S(1)}, u32[]{:S(2)}, u32[]{:S(2)}) %collective-permute-start.9) | collective-permute-done | bytes 12320 | tf_op jit(solution)/shard_map/ppermute | solution.py:212
  40.2 2.0 %collective-permute-start.12 = (f32[96,128]{1,0:T(8,128)S(1)}, f32[96,128]{1,0:T(8,128)S(1)}, u32[]{:S(2)}, u32[]{:S(2)}) collective-permute-start(f32[96,128]{1,0:T(8,128)S(1)} %get-tuple-element.97), channel_id=1, source_target_pairs={{0,8},{1,9},{2,10},{3,11},{4,12},{5,13},{6,14},{7,15},{8,0},{9,1},... | collective-permute-start | bytes 147464 | tf_op jit(solution)/shard_map/ppermute | solution.py:212
  42.9 5.1 %shard_map.84.b = bf16[1280,1158]{1,0:T(8,128)(2,1)S(1)} custom-call(bf16[1280,1158]{1,0:T(8,128)(2,1)S(1)} %get-tuple-element.102.one.a, bf16[1158,1158]{1,0:T(8,128)(2,1)S(1)} %bitcast.13), custom_call_target="tpu_custom_call" | custom-call | flops 3432867840 | bytes 8610888 | tf_op jit(solution)/shard_map/pallas_call | solution.py:221
  48.0 1.6 collective-permute-start.14
  49.6 2.2 %collective-permute-start.15 = (f32[160,128]{1,0:T(8,128)S(1)}, f32[160,128]{1,0:T(8,128)S(1)}, u32[]{:S(2)}, u32[]{:S(2)}) collective-permute-start(f32[160,128]{1,0:T(8,128)S(1)} %get-tuple-element.100), channel_id=1, source_target_pairs={{0,28},{1,29},{2,30},{3,31},{4,24},{5,25},{6,26},{7,27},{8,20},{9,... | collective-permute-start | bytes 245768 | tf_op jit(solution)/shard_map/ppermute | solution.py:212
  52.2 1.4 collective-permute-start.11
  54.1 5.3 %shard_map.85.refs_11_ = bf16[1280,1280]{1,0:T(8,128)(2,1)S(1)} custom-call(bf16[1280,1158]{1,0:T(8,128)(2,1)S(1)} %get-tuple-element.102.one.a, bf16[1280,1158]{1,0:T(8,128)(2,1)S(1)} %shard_map.84.b), custom_call_target="tpu_custom_call" | custom-call | flops 3432867840 | bytes 9205760 | tf_op jit(solution)/shard_map/pallas_call | solution.py:221
  59.4 5.5 %collective-permute-done.11.refs_5_ = f32[400,128]{1,0:T(8,128)S(1)} collective-permute-done((f32[400,128]{1,0:T(8,128)S(1)}, f32[400,128]{1,0:T(8,128)S(1)}, u32[]{:S(2)}, u32[]{:S(2)}) %collective-permute-start.11) | collective-permute-done | bytes 204832 | tf_op jit(solution)/shard_map/ppermute | solution.py:212
  64.9 4.1 %shard_map.86 = (f32[1280,128]{1,0:T(8,128)S(1)}, f32[1280,128]{1,0:T(8,128)S(1)}, f32[280,128]{1,0:T(8,128)S(1)}, f32[280,128]{1,0:T(8,128)S(1)}, bf16[1280,768]{1,0:T(8,128)(2,1)S(1)}) custom-call(f32[1280,128]{1,0:T(8,128)S(1)} %get-tuple-element.91.refs_0_, f32[328,128]{1,0:T(8,128)S(1)} %collective-permute-done.7.refs_1_, ...), custom_call_target="tpu_custom_call" | custom-call | flops 419430400 | bytes 9383936 | tf_op jit(solution)/shard_map/pallas_call | solution.py:221
  68.9 1.8 %collective-permute-start.17 = (f32[280,128]{1,0:T(8,128)S(1)}, f32[280,128]{1,0:T(8,128)S(1)}, u32[]{:S(2)}, u32[]{:S(2)}) collective-permute-start(f32[280,128]{1,0:T(8,128)S(1)} %get-tuple-element.104), channel_id=1, source_target_pairs={{0,1},{1,0},{2,3},{3,2},{4,5},{5,4},{6,7},{7,6},{8,9},{9,8},{10,11... | collective-permute-start | bytes 430088 | tf_op jit(solution)/shard_map/ppermute | solution.py:212
  71.7 4.4 %collective-permute-done.18.refs_2_ = f32[280,128]{1,0:T(8,128)S(1)} collective-permute-done((f32[280,128]{1,0:T(8,128)S(1)}, f32[280,128]{1,0:T(8,128)S(1)}, u32[]{:S(2)}, u32[]{:S(2)}) %collective-permute-start.18) | collective-permute-done | bytes 143392 | tf_op jit(solution)/shard_map/ppermute | solution.py:212
  76.3 2.3 %collective-permute-start.20 = (f32[280,128]{1,0:T(8,128)S(1)}, f32[280,128]{1,0:T(8,128)S(1)}, u32[]{:S(2)}, u32[]{:S(2)}) collective-permute-start(f32[280,128]{1,0:T(8,128)S(1)} %get-tuple-element.107), channel_id=1, source_target_pairs={{0,12},{1,13},{2,14},{3,15},{4,8},{5,9},{6,10},{7,11},{8,4},{9,5},... | collective-permute-start | bytes 430088 | tf_op jit(solution)/shard_map/ppermute | solution.py:212
  79.5 2.0 %collective-permute-start.23 = (f32[40,128]{1,0:T(8,128)S(1)}, f32[40,128]{1,0:T(8,128)S(1)}, u32[]{:S(2)}, u32[]{:S(2)}) collective-permute-start(f32[40,128]{1,0:T(8,128)S(1)} %get-tuple-element.110), channel_id=1, source_target_pairs={{0,28},{1,29},{2,30},{3,31},{4,24},{5,25},{6,26},{7,27},{8,20},{9,... | collective-permute-start | bytes 61448 | tf_op jit(solution)/shard_map/ppermute | solution.py:212
  81.5 2.1 %collective-permute-done.22.refs_6_ = f32[40,128]{1,0:T(8,128)S(1)} collective-permute-done((f32[40,128]{1,0:T(8,128)S(1)}, f32[40,128]{1,0:T(8,128)S(1)}, u32[]{:S(2)}, u32[]{:S(2)}) %collective-permute-start.22) | collective-permute-done | bytes 20512 | tf_op jit(solution)/shard_map/ppermute | solution.py:212
  83.5 3.1 %collective-permute-done.23.refs_7_ = f32[40,128]{1,0:T(8,128)S(1)} collective-permute-done((f32[40,128]{1,0:T(8,128)S(1)}, f32[40,128]{1,0:T(8,128)S(1)}, u32[]{:S(2)}, u32[]{:S(2)}) %collective-permute-start.23) | collective-permute-done | bytes 20512 | tf_op jit(solution)/shard_map/ppermute | solution.py:212
  86.7 1.1 shard_map.88
  87.8 1.3 collective-permute-start.24
  89.3 1.2 collective-permute-start.26
  90.5 3.8 %collective-permute-done.26.refs_3_ = f32[8,128]{1,0:T(8,128)S(1)} collective-permute-done((f32[8,128]{1,0:T(8,128)S(1)}, f32[8,128]{1,0:T(8,128)S(1)}, u32[]{:S(2)}, u32[]{:S(2)}) %collective-permute-start.26) | collective-permute-done | bytes 4128 | tf_op jit(solution)/shard_map/ppermute | solution.py:212
  94.8 1.9 %collective-permute-start.28 = (f32[312,128]{1,0:T(8,128)S(1)}, f32[312,128]{1,0:T(8,128)S(1)}, u32[]{:S(2)}, u32[]{:S(2)}) collective-permute-start(f32[312,128]{1,0:T(8,128)S(1)} %get-tuple-element.117), channel_id=1, source_target_pairs={{0,12},{1,13},{2,14},{3,15},{4,8},{5,9},{6,10},{7,11},{8,4},{9,5},... | collective-permute-start | bytes 479240 | tf_op jit(solution)/shard_map/ppermute | solution.py:212
  98.0 2.2 %collective-permute-start.33 = (f32[32,128]{1,0:T(8,128)S(1)}, f32[32,128]{1,0:T(8,128)S(1)}, u32[]{:S(2)}, u32[]{:S(2)}) collective-permute-start(f32[32,128]{1,0:T(8,128)S(1)} %get-tuple-element.122), channel_id=1, source_target_pairs={{0,24},{1,25},{2,26},{3,27},{4,28},{5,29},{6,30},{7,31},{8,16},{9,... | collective-permute-start | bytes 49160 | tf_op jit(solution)/shard_map/ppermute | solution.py:212
  100.2 1.1 collective-permute-done.29.refs_6_
  101.3 3.0 %collective-permute-start.31 = (f32[72,128]{1,0:T(8,128)S(1)}, f32[72,128]{1,0:T(8,128)S(1)}, u32[]{:S(2)}, u32[]{:S(2)}) collective-permute-start(f32[72,128]{1,0:T(8,128)S(1)} %get-tuple-element.120), channel_id=1, source_target_pairs={{0,20},{1,21},{2,22},{3,23},{4,16},{5,17},{6,18},{7,19},{8,28},{9,... | collective-permute-start | bytes 110600 | tf_op jit(solution)/shard_map/ppermute | solution.py:212
  104.3 1.2 collective-permute-done.33.refs_10_
  105.6 1.9 %collective-permute-start.32 = (f32[72,128]{1,0:T(8,128)S(1)}, f32[72,128]{1,0:T(8,128)S(1)}, u32[]{:S(2)}, u32[]{:S(2)}) collective-permute-start(f32[72,128]{1,0:T(8,128)S(1)} %get-tuple-element.121), channel_id=1, source_target_pairs={{0,28},{1,29},{2,30},{3,31},{4,24},{5,25},{6,26},{7,27},{8,20},{9,... | collective-permute-start | bytes 110600 | tf_op jit(solution)/shard_map/ppermute | solution.py:212
  107.5 3.6 %collective-permute-done.32.refs_9_ = f32[72,128]{1,0:T(8,128)S(1)} collective-permute-done((f32[72,128]{1,0:T(8,128)S(1)}, f32[72,128]{1,0:T(8,128)S(1)}, u32[]{:S(2)}, u32[]{:S(2)}) %collective-permute-start.32) | collective-permute-done | bytes 36896 | tf_op jit(solution)/shard_map/ppermute | solution.py:212
  111.1 1.7 shard_map.90
  112.8 3.2 %collective-permute-start.34 = (f32[280,128]{1,0:T(8,128)S(1)}, f32[280,128]{1,0:T(8,128)S(1)}, u32[]{:S(2)}, u32[]{:S(2)}) collective-permute-start(f32[280,128]{1,0:T(8,128)S(1)} %get-tuple-element.126), channel_id=1, source_target_pairs={{0,1},{1,0},{2,3},{3,2},{4,5},{5,4},{6,7},{7,6},{8,9},{9,8},{10,11... | collective-permute-start | bytes 430088 | tf_op jit(solution)/shard_map/ppermute | solution.py:212
  117.1 4.4 %collective-permute-done.35.refs_2_ = f32[280,128]{1,0:T(8,128)S(1)} collective-permute-done((f32[280,128]{1,0:T(8,128)S(1)}, f32[280,128]{1,0:T(8,128)S(1)}, u32[]{:S(2)}, u32[]{:S(2)}) %collective-permute-start.35) | collective-permute-done | bytes 143392 | tf_op jit(solution)/shard_map/ppermute | solution.py:212
  121.7 1.1 collective-permute-start.37
  122.7 1.0 collective-permute-start.38
  124.4 2.8 %collective-permute-start.40 = (f32[40,128]{1,0:T(8,128)S(1)}, f32[40,128]{1,0:T(8,128)S(1)}, u32[]{:S(2)}, u32[]{:S(2)}) collective-permute-start(f32[40,128]{1,0:T(8,128)S(1)} %get-tuple-element.132), channel_id=1, source_target_pairs={{0,28},{1,29},{2,30},{3,31},{4,24},{5,25},{6,26},{7,27},{8,20},{9,... | collective-permute-start | bytes 61448 | tf_op jit(solution)/shard_map/ppermute | solution.py:212
  127.2 3.2 %collective-permute-done.39.refs_6_ = f32[40,128]{1,0:T(8,128)S(1)} collective-permute-done((f32[40,128]{1,0:T(8,128)S(1)}, f32[40,128]{1,0:T(8,128)S(1)}, u32[]{:S(2)}, u32[]{:S(2)}) %collective-permute-start.39) | collective-permute-done | bytes 20512 | tf_op jit(solution)/shard_map/ppermute | solution.py:212
  131.2 1.1 shard_map.92
  132.2 1.3 collective-permute-start.41
  133.7 1.2 collective-permute-start.43
  134.9 3.8 %collective-permute-done.43.refs_3_ = f32[8,128]{1,0:T(8,128)S(1)} collective-permute-done((f32[8,128]{1,0:T(8,128)S(1)}, f32[8,128]{1,0:T(8,128)S(1)}, u32[]{:S(2)}, u32[]{:S(2)}) %collective-permute-start.43) | collective-permute-done | bytes 4128 | tf_op jit(solution)/shard_map/ppermute | solution.py:212
  139.1 1.5 collective-permute-start.44
  140.7 1.2 collective-permute-start.45
  142.8 2.6 %collective-permute-start.50 = (f32[32,128]{1,0:T(8,128)S(1)}, f32[32,128]{1,0:T(8,128)S(1)}, u32[]{:S(2)}, u32[]{:S(2)}) collective-permute-start(f32[32,128]{1,0:T(8,128)S(1)} %get-tuple-element.144), channel_id=1, source_target_pairs={{0,24},{1,25},{2,26},{3,27},{4,28},{5,29},{6,30},{7,31},{8,16},{9,... | collective-permute-start | bytes 49160 | tf_op jit(solution)/shard_map/ppermute | solution.py:212
  145.4 1.8 collective-permute-done.46.refs_6_
  147.2 2.2 %collective-permute-start.48 = (f32[72,128]{1,0:T(8,128)S(1)}, f32[72,128]{1,0:T(8,128)S(1)}, u32[]{:S(2)}, u32[]{:S(2)}) collective-permute-start(f32[72,128]{1,0:T(8,128)S(1)} %get-tuple-element.142), channel_id=1, source_target_pairs={{0,20},{1,21},{2,22},{3,23},{4,16},{5,17},{6,18},{7,19},{8,28},{9,... | collective-permute-start | bytes 110600 | tf_op jit(solution)/shard_map/ppermute | solution.py:212
  149.4 1.1 collective-permute-done.50.refs_10_
  150.5 1.6 collective-permute-start.49
  152.1 4.3 %collective-permute-done.49.refs_9_ = f32[72,128]{1,0:T(8,128)S(1)} collective-permute-done((f32[72,128]{1,0:T(8,128)S(1)}, f32[72,128]{1,0:T(8,128)S(1)}, u32[]{:S(2)}, u32[]{:S(2)}) %collective-permute-start.49) | collective-permute-done | bytes 36896 | tf_op jit(solution)/shard_map/ppermute | solution.py:212
  156.4 1.7 shard_map.94
  158.1 2.7 %collective-permute-start.51 = (f32[280,128]{1,0:T(8,128)S(1)}, f32[280,128]{1,0:T(8,128)S(1)}, u32[]{:S(2)}, u32[]{:S(2)}) collective-permute-start(f32[280,128]{1,0:T(8,128)S(1)} %get-tuple-element.147), channel_id=1, source_target_pairs={{0,1},{1,0},{2,3},{3,2},{4,5},{5,4},{6,7},{7,6},{8,9},{9,8},{10,11... | collective-permute-start | bytes 430088 | tf_op jit(solution)/shard_map/ppermute | solution.py:212
  161.9 4.4 %collective-permute-done.52.refs_2_.refs_1_ = f32[280,128]{1,0:T(8,128)S(1)} collective-permute-done((f32[280,128]{1,0:T(8,128)S(1)}, f32[280,128]{1,0:T(8,128)S(1)}, u32[]{:S(2)}, u32[]{:S(2)}) %collective-permute-start.52) | collective-permute-done | bytes 143392 | tf_op jit(solution)/shard_map/ppermute | solution.py:212
  166.5 2.0 %collective-permute-start.54 = (f32[280,128]{1,0:T(8,128)S(1)}, f32[280,128]{1,0:T(8,128)S(1)}, u32[]{:S(2)}, u32[]{:S(2)}) collective-permute-start(f32[280,128]{1,0:T(8,128)S(1)} %get-tuple-element.150), channel_id=1, source_target_pairs={{0,12},{1,13},{2,14},{3,15},{4,8},{5,9},{6,10},{7,11},{8,4},{9,5},... | collective-permute-start | bytes 430088 | tf_op jit(solution)/shard_map/ppermute | solution.py:212
  170.1 1.6 collective-permute-start.57
  171.7 1.5 collective-permute-done.56.refs_5_
  173.3 3.2 %collective-permute-done.57.refs_6_ = f32[40,128]{1,0:T(8,128)S(1)} collective-permute-done((f32[40,128]{1,0:T(8,128)S(1)}, f32[40,128]{1,0:T(8,128)S(1)}, u32[]{:S(2)}, u32[]{:S(2)}) %collective-permute-start.57) | collective-permute-done | bytes 20512 | tf_op jit(solution)/shard_map/ppermute | solution.py:212
  176.5 4.0 %shard_map.96 = (f32[1158,1,128]{2,1,0:T(1,128)}, f32[1158,1,128]{2,1,0:T(1,128)}) custom-call(s32[1158]{0:T(1024)S(1)} %reduce.canon, f32[1280,128]{1,0:T(8,128)S(1)} %get-tuple-element.146.refs_0_.base, f32[280,128]{1,0:T(8,128)S(1)} %collective-permute-done.51.refs_1_.refs_0_, f32[280,128]{1,0:T(8,128)S(1)} %collective-permute-done.52.refs_2_.refs_1_, ...), custom_call_target="tpu_custom_call" | custom-call | bytes 3914264 | tf_op jit(solution)/shard_map/pallas_call | solution.py:221
  (82 shorter events, 18.9 us)
Async XLA Ops:
  1.3 1.1 copy-start
  5.1 12.9 %collective-permute-start = (f32[280,128]{1,0:T(8,128)S(1)}, f32[280,128]{1,0:T(8,128)S(1)}, u32[]{:S(2)}, u32[]{:S(2)}) collective-permute-start(f32[280,128]{1,0:T(8,128)S(1)} %get-tuple-element.81), channel_id=1, source_target_pairs={{0,1},{1,0},{2,3},{3,2},{4,5},{5,4},{6,7},{7,6},{8,9},{9,8},{10,11... | collective-permute-start | bytes 430088 | tf_op jit(solution)/shard_map/ppermute | solution.py:212
  5.2 12.8 %collective-permute-start.1 = (f32[280,128]{1,0:T(8,128)S(1)}, f32[280,128]{1,0:T(8,128)S(1)}, u32[]{:S(2)}, u32[]{:S(2)}) collective-permute-start(f32[280,128]{1,0:T(8,128)S(1)} %get-tuple-element.82), channel_id=1, source_target_pairs={{0,3},{1,2},{2,1},{3,0},{4,7},{5,6},{6,5},{7,4},{8,11},{9,10},{10,... | collective-permute-start | bytes 430088 | tf_op jit(solution)/shard_map/ppermute | solution.py:212
  10.3 2.6 %copy-start.1 = (bf16[1,1,1,1158,1158]{4,3,2,1,0:T(8,128)(2,1)S(1)}, bf16[1,1,1,1158,1158]{4,3,2,1,0:T(8,128)(2,1)}, u32[]{:S(2)}) copy-start(bf16[1,1,1,1158,1158]{4,3,2,1,0:T(8,128)(2,1)} %param.8) | copy-start | bytes 8045788
  18.1 13.0 %collective-permute-start.5 = (f32[40,128]{1,0:T(8,128)S(1)}, f32[40,128]{1,0:T(8,128)S(1)}, u32[]{:S(2)}, u32[]{:S(2)}) collective-permute-start(f32[40,128]{1,0:T(8,128)S(1)} %get-tuple-element.86), channel_id=1, source_target_pairs={{0,20},{1,21},{2,22},{3,23},{4,16},{5,17},{6,18},{7,19},{8,28},{9,... | collective-permute-start | bytes 61448 | tf_op jit(solution)/shard_map/ppermute | solution.py:212
  20.4 10.7 %collective-permute-start.6 = (f32[40,128]{1,0:T(8,128)S(1)}, f32[40,128]{1,0:T(8,128)S(1)}, u32[]{:S(2)}, u32[]{:S(2)}) collective-permute-start(f32[40,128]{1,0:T(8,128)S(1)} %get-tuple-element.87), channel_id=1, source_target_pairs={{0,28},{1,29},{2,30},{3,31},{4,24},{5,25},{6,26},{7,27},{8,20},{9,... | collective-permute-start | bytes 61448 | tf_op jit(solution)/shard_map/ppermute | solution.py:212
  22.5 8.6 %collective-permute-start.2 = (f32[280,128]{1,0:T(8,128)S(1)}, f32[280,128]{1,0:T(8,128)S(1)}, u32[]{:S(2)}, u32[]{:S(2)}) collective-permute-start(f32[280,128]{1,0:T(8,128)S(1)} %get-tuple-element.83), channel_id=1, source_target_pairs={{0,4},{1,5},{2,6},{3,7},{4,0},{5,1},{6,2},{7,3},{8,12},{9,13},{10,... | collective-permute-start | bytes 430088 | tf_op jit(solution)/shard_map/ppermute | solution.py:212
  22.9 8.2 %collective-permute-start.3 = (f32[280,128]{1,0:T(8,128)S(1)}, f32[280,128]{1,0:T(8,128)S(1)}, u32[]{:S(2)}, u32[]{:S(2)}) collective-permute-start(f32[280,128]{1,0:T(8,128)S(1)} %get-tuple-element.84), channel_id=1, source_target_pairs={{0,12},{1,13},{2,14},{3,15},{4,8},{5,9},{6,10},{7,11},{8,4},{9,5},... | collective-permute-start | bytes 430088 | tf_op jit(solution)/shard_map/ppermute | solution.py:212
  23.9 7.2 %collective-permute-start.4 = (f32[280,128]{1,0:T(8,128)S(1)}, f32[280,128]{1,0:T(8,128)S(1)}, u32[]{:S(2)}, u32[]{:S(2)}) collective-permute-start(f32[280,128]{1,0:T(8,128)S(1)} %get-tuple-element.85), channel_id=1, source_target_pairs={{0,16},{1,17},{2,18},{3,19},{4,20},{5,21},{6,22},{7,23},{8,24},{9,... | collective-permute-start | bytes 430088 | tf_op jit(solution)/shard_map/ppermute | solution.py:212
  31.1 11.8 %copy-start.2 = (bf16[1,1,1,1158,1158]{4,3,2,1,0:T(8,128)(2,1)S(1)}, bf16[1,1,1,1158,1158]{4,3,2,1,0:T(8,128)(2,1)}, u32[]{:S(2)}) copy-start(bf16[1,1,1,1158,1158]{4,3,2,1,0:T(8,128)(2,1)} %param.7) | copy-start | bytes 8045788
  32.2 7.3 %collective-permute-start.7 = (f32[328,128]{1,0:T(8,128)S(1)}, f32[328,128]{1,0:T(8,128)S(1)}, u32[]{:S(2)}, u32[]{:S(2)}) collective-permute-start(f32[328,128]{1,0:T(8,128)S(1)} %get-tuple-element.92), channel_id=1, source_target_pairs={{0,1},{1,0},{2,3},{3,2},{4,5},{5,4},{6,7},{7,6},{8,9},{9,8},{10,11... | collective-permute-start | bytes 503816 | tf_op jit(solution)/shard_map/ppermute | solution.py:212
  33.8 6.1 %collective-permute-start.8 = (f32[328,128]{1,0:T(8,128)S(1)}, f32[328,128]{1,0:T(8,128)S(1)}, u32[]{:S(2)}, u32[]{:S(2)}) collective-permute-start(f32[328,128]{1,0:T(8,128)S(1)} %get-tuple-element.93), channel_id=1, source_target_pairs={{0,3},{1,2},{2,1},{3,0},{4,7},{5,6},{6,5},{7,4},{8,11},{9,10},{10,... | collective-permute-start | bytes 503816 | tf_op jit(solution)/shard_map/ppermute | solution.py:212
  34.0 5.5 %collective-permute-start.9 = (f32[24,128]{1,0:T(8,128)S(1)}, f32[24,128]{1,0:T(8,128)S(1)}, u32[]{:S(2)}, u32[]{:S(2)}) collective-permute-start(f32[24,128]{1,0:T(8,128)S(1)} %get-tuple-element.94), channel_id=1, source_target_pairs={{0,2},{1,3},{2,0},{3,1},{4,6},{5,7},{6,4},{7,5},{8,10},{9,11},{10,... | collective-permute-start | bytes 36872 | tf_op jit(solution)/shard_map/ppermute | solution.py:212
  40.2 12.0 %collective-permute-start.12 = (f32[96,128]{1,0:T(8,128)S(1)}, f32[96,128]{1,0:T(8,128)S(1)}, u32[]{:S(2)}, u32[]{:S(2)}) collective-permute-start(f32[96,128]{1,0:T(8,128)S(1)} %get-tuple-element.97), channel_id=1, source_target_pairs={{0,8},{1,9},{2,10},{3,11},{4,12},{5,13},{6,14},{7,15},{8,0},{9,1},... | collective-permute-start | bytes 147464 | tf_op jit(solution)/shard_map/ppermute | solution.py:212
  42.2 11.3 %collective-permute-start.16 = (f32[96,128]{1,0:T(8,128)S(1)}, f32[96,128]{1,0:T(8,128)S(1)}, u32[]{:S(2)}, u32[]{:S(2)}) collective-permute-start(f32[96,128]{1,0:T(8,128)S(1)} %get-tuple-element.101), channel_id=1, source_target_pairs={{0,24},{1,25},{2,26},{3,27},{4,28},{5,29},{6,30},{7,31},{8,16},{9,... | collective-permute-start | bytes 147464 | tf_op jit(solution)/shard_map/ppermute | solution.py:212
  48.0 11.3 %collective-permute-start.14 = (f32[160,128]{1,0:T(8,128)S(1)}, f32[160,128]{1,0:T(8,128)S(1)}, u32[]{:S(2)}, u32[]{:S(2)}) collective-permute-start(f32[160,128]{1,0:T(8,128)S(1)} %get-tuple-element.99), channel_id=1, source_target_pairs={{0,20},{1,21},{2,22},{3,23},{4,16},{5,17},{6,18},{7,19},{8,28},{9,... | collective-permute-start | bytes 245768 | tf_op jit(solution)/shard_map/ppermute | solution.py:212
  49.6 9.8 %collective-permute-start.15 = (f32[160,128]{1,0:T(8,128)S(1)}, f32[160,128]{1,0:T(8,128)S(1)}, u32[]{:S(2)}, u32[]{:S(2)}) collective-permute-start(f32[160,128]{1,0:T(8,128)S(1)} %get-tuple-element.100), channel_id=1, source_target_pairs={{0,28},{1,29},{2,30},{3,31},{4,24},{5,25},{6,26},{7,27},{8,20},{9,... | collective-permute-start | bytes 245768 | tf_op jit(solution)/shard_map/ppermute | solution.py:212
  51.8 7.6 %collective-permute-start.10 = (f32[400,128]{1,0:T(8,128)S(1)}, f32[400,128]{1,0:T(8,128)S(1)}, u32[]{:S(2)}, u32[]{:S(2)}) collective-permute-start(f32[400,128]{1,0:T(8,128)S(1)} %get-tuple-element.95), channel_id=1, source_target_pairs={{0,4},{1,5},{2,6},{3,7},{4,0},{5,1},{6,2},{7,3},{8,12},{9,13},{10,... | collective-permute-start | bytes 614408 | tf_op jit(solution)/shard_map/ppermute | solution.py:212
  52.2 12.7 %collective-permute-start.11 = (f32[400,128]{1,0:T(8,128)S(1)}, f32[400,128]{1,0:T(8,128)S(1)}, u32[]{:S(2)}, u32[]{:S(2)}) collective-permute-start(f32[400,128]{1,0:T(8,128)S(1)} %get-tuple-element.96), channel_id=1, source_target_pairs={{0,12},{1,13},{2,14},{3,15},{4,8},{5,9},{6,10},{7,11},{8,4},{9,5},... | collective-permute-start | bytes 614408 | tf_op jit(solution)/shard_map/ppermute | solution.py:212
  53.5 11.3 %collective-permute-start.13 = (f32[400,128]{1,0:T(8,128)S(1)}, f32[400,128]{1,0:T(8,128)S(1)}, u32[]{:S(2)}, u32[]{:S(2)}) collective-permute-start(f32[400,128]{1,0:T(8,128)S(1)} %get-tuple-element.98), channel_id=1, source_target_pairs={{0,16},{1,17},{2,18},{3,19},{4,20},{5,21},{6,22},{7,23},{8,24},{9,... | collective-permute-start | bytes 614408 | tf_op jit(solution)/shard_map/ppermute | solution.py:212
  68.9 2.8 %collective-permute-start.17 = (f32[280,128]{1,0:T(8,128)S(1)}, f32[280,128]{1,0:T(8,128)S(1)}, u32[]{:S(2)}, u32[]{:S(2)}) collective-permute-start(f32[280,128]{1,0:T(8,128)S(1)} %get-tuple-element.104), channel_id=1, source_target_pairs={{0,1},{1,0},{2,3},{3,2},{4,5},{5,4},{6,7},{7,6},{8,9},{9,8},{10,11... | collective-permute-start | bytes 430088 | tf_op jit(solution)/shard_map/ppermute | solution.py:212
  70.7 5.5 %collective-permute-start.18 = (f32[280,128]{1,0:T(8,128)S(1)}, f32[280,128]{1,0:T(8,128)S(1)}, u32[]{:S(2)}, u32[]{:S(2)}) collective-permute-start(f32[280,128]{1,0:T(8,128)S(1)} %get-tuple-element.105), channel_id=1, source_target_pairs={{0,3},{1,2},{2,1},{3,0},{4,7},{5,6},{6,5},{7,4},{8,11},{9,10},{10,... | collective-permute-start | bytes 430088 | tf_op jit(solution)/shard_map/ppermute | solution.py:212
  76.2 10.4 %collective-permute-start.19 = (f32[280,128]{1,0:T(8,128)S(1)}, f32[280,128]{1,0:T(8,128)S(1)}, u32[]{:S(2)}, u32[]{:S(2)}) collective-permute-start(f32[280,128]{1,0:T(8,128)S(1)} %get-tuple-element.106), channel_id=1, source_target_pairs={{0,4},{1,5},{2,6},{3,7},{4,0},{5,1},{6,2},{7,3},{8,12},{9,13},{10,... | collective-permute-start | bytes 430088 | tf_op jit(solution)/shard_map/ppermute | solution.py:212
  76.3 10.3 %collective-permute-start.20 = (f32[280,128]{1,0:T(8,128)S(1)}, f32[280,128]{1,0:T(8,128)S(1)}, u32[]{:S(2)}, u32[]{:S(2)}) collective-permute-start(f32[280,128]{1,0:T(8,128)S(1)} %get-tuple-element.107), channel_id=1, source_target_pairs={{0,12},{1,13},{2,14},{3,15},{4,8},{5,9},{6,10},{7,11},{8,4},{9,5},... | collective-permute-start | bytes 430088 | tf_op jit(solution)/shard_map/ppermute | solution.py:212
  78.6 8.0 %collective-permute-start.21 = (f32[280,128]{1,0:T(8,128)S(1)}, f32[280,128]{1,0:T(8,128)S(1)}, u32[]{:S(2)}, u32[]{:S(2)}) collective-permute-start(f32[280,128]{1,0:T(8,128)S(1)} %get-tuple-element.108), channel_id=1, source_target_pairs={{0,16},{1,17},{2,18},{3,19},{4,20},{5,21},{6,22},{7,23},{8,24},{9,... | collective-permute-start | bytes 430088 | tf_op jit(solution)/shard_map/ppermute | solution.py:212
  79.5 4.0 %collective-permute-start.22 = (f32[40,128]{1,0:T(8,128)S(1)}, f32[40,128]{1,0:T(8,128)S(1)}, u32[]{:S(2)}, u32[]{:S(2)}) collective-permute-start(f32[40,128]{1,0:T(8,128)S(1)} %get-tuple-element.109), channel_id=1, source_target_pairs={{0,20},{1,21},{2,22},{3,23},{4,16},{5,17},{6,18},{7,19},{8,28},{9,... | collective-permute-start | bytes 61448 | tf_op jit(solution)/shard_map/ppermute | solution.py:212
  79.5 7.1 %collective-permute-start.23 = (f32[40,128]{1,0:T(8,128)S(1)}, f32[40,128]{1,0:T(8,128)S(1)}, u32[]{:S(2)}, u32[]{:S(2)}) collective-permute-start(f32[40,128]{1,0:T(8,128)S(1)} %get-tuple-element.110), channel_id=1, source_target_pairs={{0,28},{1,29},{2,30},{3,31},{4,24},{5,25},{6,26},{7,27},{8,20},{9,... | collective-permute-start | bytes 61448 | tf_op jit(solution)/shard_map/ppermute | solution.py:212
  87.8 6.6 %collective-permute-start.24 = (f32[288,128]{1,0:T(8,128)S(1)}, f32[288,128]{1,0:T(8,128)S(1)}, u32[]{:S(2)}, u32[]{:S(2)}) collective-permute-start(f32[288,128]{1,0:T(8,128)S(1)} %get-tuple-element.113), channel_id=1, source_target_pairs={{0,1},{1,0},{2,3},{3,2},{4,5},{5,4},{6,7},{7,6},{8,9},{9,8},{10,11... | collective-permute-start | bytes 442376 | tf_op jit(solution)/shard_map/ppermute | solution.py:212
  89.1 5.6 %collective-permute-start.25 = (f32[288,128]{1,0:T(8,128)S(1)}, f32[288,128]{1,0:T(8,128)S(1)}, u32[]{:S(2)}, u32[]{:S(2)}) collective-permute-start(f32[288,128]{1,0:T(8,128)S(1)} %get-tuple-element.114), channel_id=1, source_target_pairs={{0,3},{1,2},{2,1},{3,0},{4,7},{5,6},{6,5},{7,4},{8,11},{9,10},{10,... | collective-permute-start | bytes 442376 | tf_op jit(solution)/shard_map/ppermute | solution.py:212
  89.3 5.1 %collective-permute-start.26 = (f32[8,128]{1,0:T(8,128)S(1)}, f32[8,128]{1,0:T(8,128)S(1)}, u32[]{:S(2)}, u32[]{:S(2)}) collective-permute-start(f32[8,128]{1,0:T(8,128)S(1)} %get-tuple-element.115), channel_id=1, source_target_pairs={{0,2},{1,3},{2,0},{3,1},{4,6},{5,7},{6,4},{7,5},{8,10},{9,11},{10,... | collective-permute-start | bytes 12296 | tf_op jit(solution)/shard_map/ppermute | solution.py:212
  94.7 16.4 %collective-permute-start.27 = (f32[312,128]{1,0:T(8,128)S(1)}, f32[312,128]{1,0:T(8,128)S(1)}, u32[]{:S(2)}, u32[]{:S(2)}) collective-permute-start(f32[312,128]{1,0:T(8,128)S(1)} %get-tuple-element.116), channel_id=1, source_target_pairs={{0,4},{1,5},{2,6},{3,7},{4,0},{5,1},{6,2},{7,3},{8,12},{9,13},{10,... | collective-permute-start | bytes 479240 | tf_op jit(solution)/shard_map/ppermute | solution.py:212
  94.8 16.3 %collective-permute-start.28 = (f32[312,128]{1,0:T(8,128)S(1)}, f32[312,128]{1,0:T(8,128)S(1)}, u32[]{:S(2)}, u32[]{:S(2)}) collective-permute-start(f32[312,128]{1,0:T(8,128)S(1)} %get-tuple-element.117), channel_id=1, source_target_pairs={{0,12},{1,13},{2,14},{3,15},{4,8},{5,9},{6,10},{7,11},{8,4},{9,5},... | collective-permute-start | bytes 479240 | tf_op jit(solution)/shard_map/ppermute | solution.py:212
  96.7 14.4 %collective-permute-start.30 = (f32[312,128]{1,0:T(8,128)S(1)}, f32[312,128]{1,0:T(8,128)S(1)}, u32[]{:S(2)}, u32[]{:S(2)}) collective-permute-start(f32[312,128]{1,0:T(8,128)S(1)} %get-tuple-element.119), channel_id=1, source_target_pairs={{0,16},{1,17},{2,18},{3,19},{4,20},{5,21},{6,22},{7,23},{8,24},{9,... | collective-permute-start | bytes 479240 | tf_op jit(solution)/shard_map/ppermute | solution.py:212
  97.3 4.0 %collective-permute-start.29 = (f32[32,128]{1,0:T(8,128)S(1)}, f32[32,128]{1,0:T(8,128)S(1)}, u32[]{:S(2)}, u32[]{:S(2)}) collective-permute-start(f32[32,128]{1,0:T(8,128)S(1)} %get-tuple-element.118), channel_id=1, source_target_pairs={{0,8},{1,9},{2,10},{3,11},{4,12},{5,13},{6,14},{7,15},{8,0},{9,1},... | collective-permute-start | bytes 49160 | tf_op jit(solution)/shard_map/ppermute | solution.py:212
  98.0 7.5 %collective-permute-start.33 = (f32[32,128]{1,0:T(8,128)S(1)}, f32[32,128]{1,0:T(8,128)S(1)}, u32[]{:S(2)}, u32[]{:S(2)}) collective-permute-start(f32[32,128]{1,0:T(8,128)S(1)} %get-tuple-element.122), channel_id=1, source_target_pairs={{0,24},{1,25},{2,26},{3,27},{4,28},{5,29},{6,30},{7,31},{8,16},{9,... | collective-permute-start | bytes 49160 | tf_op jit(solution)/shard_map/ppermute | solution.py:212
  101.3 6.1 %collective-permute-start.31 = (f32[72,128]{1,0:T(8,128)S(1)}, f32[72,128]{1,0:T(8,128)S(1)}, u32[]{:S(2)}, u32[]{:S(2)}) collective-permute-start(f32[72,128]{1,0:T(8,128)S(1)} %get-tuple-element.120), channel_id=1, source_target_pairs={{0,20},{1,21},{2,22},{3,23},{4,16},{5,17},{6,18},{7,19},{8,28},{9,... | collective-permute-start | bytes 110600 | tf_op jit(solution)/shard_map/ppermute | solution.py:212
  105.6 5.5 %collective-permute-start.32 = (f32[72,128]{1,0:T(8,128)S(1)}, f32[72,128]{1,0:T(8,128)S(1)}, u32[]{:S(2)}, u32[]{:S(2)}) collective-permute-start(f32[72,128]{1,0:T(8,128)S(1)} %get-tuple-element.121), channel_id=1, source_target_pairs={{0,28},{1,29},{2,30},{3,31},{4,24},{5,25},{6,26},{7,27},{8,20},{9,... | collective-permute-start | bytes 110600 | tf_op jit(solution)/shard_map/ppermute | solution.py:212
  112.8 4.3 %collective-permute-start.34 = (f32[280,128]{1,0:T(8,128)S(1)}, f32[280,128]{1,0:T(8,128)S(1)}, u32[]{:S(2)}, u32[]{:S(2)}) collective-permute-start(f32[280,128]{1,0:T(8,128)S(1)} %get-tuple-element.126), channel_id=1, source_target_pairs={{0,1},{1,0},{2,3},{3,2},{4,5},{5,4},{6,7},{7,6},{8,9},{9,8},{10,11... | collective-permute-start | bytes 430088 | tf_op jit(solution)/shard_map/ppermute | solution.py:212
  116.1 5.5 %collective-permute-start.35 = (f32[280,128]{1,0:T(8,128)S(1)}, f32[280,128]{1,0:T(8,128)S(1)}, u32[]{:S(2)}, u32[]{:S(2)}) collective-permute-start(f32[280,128]{1,0:T(8,128)S(1)} %get-tuple-element.127), channel_id=1, source_target_pairs={{0,3},{1,2},{2,1},{3,0},{4,7},{5,6},{6,5},{7,4},{8,11},{9,10},{10,... | collective-permute-start | bytes 430088 | tf_op jit(solution)/shard_map/ppermute | solution.py:212
  121.6 9.6 %collective-permute-start.36 = (f32[280,128]{1,0:T(8,128)S(1)}, f32[280,128]{1,0:T(8,128)S(1)}, u32[]{:S(2)}, u32[]{:S(2)}) collective-permute-start(f32[280,128]{1,0:T(8,128)S(1)} %get-tuple-element.128), channel_id=1, source_target_pairs={{0,4},{1,5},{2,6},{3,7},{4,0},{5,1},{6,2},{7,3},{8,12},{9,13},{10,... | collective-permute-start | bytes 430088 | tf_op jit(solution)/shard_map/ppermute | solution.py:212
  121.7 9.5 %collective-permute-start.37 = (f32[280,128]{1,0:T(8,128)S(1)}, f32[280,128]{1,0:T(8,128)S(1)}, u32[]{:S(2)}, u32[]{:S(2)}) collective-permute-start(f32[280,128]{1,0:T(8,128)S(1)} %get-tuple-element.129), channel_id=1, source_target_pairs={{0,12},{1,13},{2,14},{3,15},{4,8},{5,9},{6,10},{7,11},{8,4},{9,5},... | collective-permute-start | bytes 430088 | tf_op jit(solution)/shard_map/ppermute | solution.py:212
  122.7 8.4 %collective-permute-start.38 = (f32[280,128]{1,0:T(8,128)S(1)}, f32[280,128]{1,0:T(8,128)S(1)}, u32[]{:S(2)}, u32[]{:S(2)}) collective-permute-start(f32[280,128]{1,0:T(8,128)S(1)} %get-tuple-element.130), channel_id=1, source_target_pairs={{0,16},{1,17},{2,18},{3,19},{4,20},{5,21},{6,22},{7,23},{8,24},{9,... | collective-permute-start | bytes 430088 | tf_op jit(solution)/shard_map/ppermute | solution.py:212
  123.8 6.6 %collective-permute-start.39 = (f32[40,128]{1,0:T(8,128)S(1)}, f32[40,128]{1,0:T(8,128)S(1)}, u32[]{:S(2)}, u32[]{:S(2)}) collective-permute-start(f32[40,128]{1,0:T(8,128)S(1)} %get-tuple-element.131), channel_id=1, source_target_pairs={{0,20},{1,21},{2,22},{3,23},{4,16},{5,17},{6,18},{7,19},{8,28},{9,... | collective-permute-start | bytes 61448 | tf_op jit(solution)/shard_map/ppermute | solution.py:212
  124.4 6.7 %collective-permute-start.40 = (f32[40,128]{1,0:T(8,128)S(1)}, f32[40,128]{1,0:T(8,128)S(1)}, u32[]{:S(2)}, u32[]{:S(2)}) collective-permute-start(f32[40,128]{1,0:T(8,128)S(1)} %get-tuple-element.132), channel_id=1, source_target_pairs={{0,28},{1,29},{2,30},{3,31},{4,24},{5,25},{6,26},{7,27},{8,20},{9,... | collective-permute-start | bytes 61448 | tf_op jit(solution)/shard_map/ppermute | solution.py:212
  132.2 6.5 %collective-permute-start.41 = (f32[288,128]{1,0:T(8,128)S(1)}, f32[288,128]{1,0:T(8,128)S(1)}, u32[]{:S(2)}, u32[]{:S(2)}) collective-permute-start(f32[288,128]{1,0:T(8,128)S(1)} %get-tuple-element.135), channel_id=1, source_target_pairs={{0,1},{1,0},{2,3},{3,2},{4,5},{5,4},{6,7},{7,6},{8,9},{9,8},{10,11... | collective-permute-start | bytes 442376 | tf_op jit(solution)/shard_map/ppermute | solution.py:212
  133.5 5.6 %collective-permute-start.42 = (f32[288,128]{1,0:T(8,128)S(1)}, f32[288,128]{1,0:T(8,128)S(1)}, u32[]{:S(2)}, u32[]{:S(2)}) collective-permute-start(f32[288,128]{1,0:T(8,128)S(1)} %get-tuple-element.136), channel_id=1, source_target_pairs={{0,3},{1,2},{2,1},{3,0},{4,7},{5,6},{6,5},{7,4},{8,11},{9,10},{10,... | collective-permute-start | bytes 442376 | tf_op jit(solution)/shard_map/ppermute | solution.py:212
  133.7 5.1 %collective-permute-start.43 = (f32[8,128]{1,0:T(8,128)S(1)}, f32[8,128]{1,0:T(8,128)S(1)}, u32[]{:S(2)}, u32[]{:S(2)}) collective-permute-start(f32[8,128]{1,0:T(8,128)S(1)} %get-tuple-element.137), channel_id=1, source_target_pairs={{0,2},{1,3},{2,0},{3,1},{4,6},{5,7},{6,4},{7,5},{8,10},{9,11},{10,... | collective-permute-start | bytes 12296 | tf_op jit(solution)/shard_map/ppermute | solution.py:212
  139.1 17.3 %collective-permute-start.44 = (f32[312,128]{1,0:T(8,128)S(1)}, f32[312,128]{1,0:T(8,128)S(1)}, u32[]{:S(2)}, u32[]{:S(2)}) collective-permute-start(f32[312,128]{1,0:T(8,128)S(1)} %get-tuple-element.138), channel_id=1, source_target_pairs={{0,4},{1,5},{2,6},{3,7},{4,0},{5,1},{6,2},{7,3},{8,12},{9,13},{10,... | collective-permute-start | bytes 479240 | tf_op jit(solution)/shard_map/ppermute | solution.py:212
  140.7 15.8 %collective-permute-start.45 = (f32[312,128]{1,0:T(8,128)S(1)}, f32[312,128]{1,0:T(8,128)S(1)}, u32[]{:S(2)}, u32[]{:S(2)}) collective-permute-start(f32[312,128]{1,0:T(8,128)S(1)} %get-tuple-element.139), channel_id=1, source_target_pairs={{0,12},{1,13},{2,14},{3,15},{4,8},{5,9},{6,10},{7,11},{8,4},{9,5},... | collective-permute-start | bytes 479240 | tf_op jit(solution)/shard_map/ppermute | solution.py:212
  141.9 14.5 %collective-permute-start.47 = (f32[312,128]{1,0:T(8,128)S(1)}, f32[312,128]{1,0:T(8,128)S(1)}, u32[]{:S(2)}, u32[]{:S(2)}) collective-permute-start(f32[312,128]{1,0:T(8,128)S(1)} %get-tuple-element.141), channel_id=1, source_target_pairs={{0,16},{1,17},{2,18},{3,19},{4,20},{5,21},{6,22},{7,23},{8,24},{9,... | collective-permute-start | bytes 479240 | tf_op jit(solution)/shard_map/ppermute | solution.py:212
  142.2 5.0 %collective-permute-start.46 = (f32[32,128]{1,0:T(8,128)S(1)}, f32[32,128]{1,0:T(8,128)S(1)}, u32[]{:S(2)}, u32[]{:S(2)}) collective-permute-start(f32[32,128]{1,0:T(8,128)S(1)} %get-tuple-element.140), channel_id=1, source_target_pairs={{0,8},{1,9},{2,10},{3,11},{4,12},{5,13},{6,14},{7,15},{8,0},{9,1},... | collective-permute-start | bytes 49160 | tf_op jit(solution)/shard_map/ppermute | solution.py:212
  142.8 7.7 %collective-permute-start.50 = (f32[32,128]{1,0:T(8,128)S(1)}, f32[32,128]{1,0:T(8,128)S(1)}, u32[]{:S(2)}, u32[]{:S(2)}) collective-permute-start(f32[32,128]{1,0:T(8,128)S(1)} %get-tuple-element.144), channel_id=1, source_target_pairs={{0,24},{1,25},{2,26},{3,27},{4,28},{5,29},{6,30},{7,31},{8,16},{9,... | collective-permute-start | bytes 49160 | tf_op jit(solution)/shard_map/ppermute | solution.py:212
  147.2 4.9 %collective-permute-start.48 = (f32[72,128]{1,0:T(8,128)S(1)}, f32[72,128]{1,0:T(8,128)S(1)}, u32[]{:S(2)}, u32[]{:S(2)}) collective-permute-start(f32[72,128]{1,0:T(8,128)S(1)} %get-tuple-element.142), channel_id=1, source_target_pairs={{0,20},{1,21},{2,22},{3,23},{4,16},{5,17},{6,18},{7,19},{8,28},{9,... | collective-permute-start | bytes 110600 | tf_op jit(solution)/shard_map/ppermute | solution.py:212
  150.5 5.9 %collective-permute-start.49 = (f32[72,128]{1,0:T(8,128)S(1)}, f32[72,128]{1,0:T(8,128)S(1)}, u32[]{:S(2)}, u32[]{:S(2)}) collective-permute-start(f32[72,128]{1,0:T(8,128)S(1)} %get-tuple-element.143), channel_id=1, source_target_pairs={{0,28},{1,29},{2,30},{3,31},{4,24},{5,25},{6,26},{7,27},{8,20},{9,... | collective-permute-start | bytes 110600 | tf_op jit(solution)/shard_map/ppermute | solution.py:212
  158.1 3.7 %collective-permute-start.51 = (f32[280,128]{1,0:T(8,128)S(1)}, f32[280,128]{1,0:T(8,128)S(1)}, u32[]{:S(2)}, u32[]{:S(2)}) collective-permute-start(f32[280,128]{1,0:T(8,128)S(1)} %get-tuple-element.147), channel_id=1, source_target_pairs={{0,1},{1,0},{2,3},{3,2},{4,5},{5,4},{6,7},{7,6},{8,9},{9,8},{10,11... | collective-permute-start | bytes 430088 | tf_op jit(solution)/shard_map/ppermute | solution.py:212
  160.9 5.5 %collective-permute-start.52 = (f32[280,128]{1,0:T(8,128)S(1)}, f32[280,128]{1,0:T(8,128)S(1)}, u32[]{:S(2)}, u32[]{:S(2)}) collective-permute-start(f32[280,128]{1,0:T(8,128)S(1)} %get-tuple-element.148), channel_id=1, source_target_pairs={{0,3},{1,2},{2,1},{3,0},{4,7},{5,6},{6,5},{7,4},{8,11},{9,10},{10,... | collective-permute-start | bytes 430088 | tf_op jit(solution)/shard_map/ppermute | solution.py:212
  166.4 10.1 %collective-permute-start.53 = (f32[280,128]{1,0:T(8,128)S(1)}, f32[280,128]{1,0:T(8,128)S(1)}, u32[]{:S(2)}, u32[]{:S(2)}) collective-permute-start(f32[280,128]{1,0:T(8,128)S(1)} %get-tuple-element.149), channel_id=1, source_target_pairs={{0,4},{1,5},{2,6},{3,7},{4,0},{5,1},{6,2},{7,3},{8,12},{9,13},{10,... | collective-permute-start | bytes 430088 | tf_op jit(solution)/shard_map/ppermute | solution.py:212
  166.5 10.0 %collective-permute-start.54 = (f32[280,128]{1,0:T(8,128)S(1)}, f32[280,128]{1,0:T(8,128)S(1)}, u32[]{:S(2)}, u32[]{:S(2)}) collective-permute-start(f32[280,128]{1,0:T(8,128)S(1)} %get-tuple-element.150), channel_id=1, source_target_pairs={{0,12},{1,13},{2,14},{3,15},{4,8},{5,9},{6,10},{7,11},{8,4},{9,5},... | collective-permute-start | bytes 430088 | tf_op jit(solution)/shard_map/ppermute | solution.py:212
  168.5 8.0 %collective-permute-start.55 = (f32[280,128]{1,0:T(8,128)S(1)}, f32[280,128]{1,0:T(8,128)S(1)}, u32[]{:S(2)}, u32[]{:S(2)}) collective-permute-start(f32[280,128]{1,0:T(8,128)S(1)} %get-tuple-element.151), channel_id=1, source_target_pairs={{0,16},{1,17},{2,18},{3,19},{4,20},{5,21},{6,22},{7,23},{8,24},{9,... | collective-permute-start | bytes 430088 | tf_op jit(solution)/shard_map/ppermute | solution.py:212
  169.1 4.2 %collective-permute-start.56 = (f32[40,128]{1,0:T(8,128)S(1)}, f32[40,128]{1,0:T(8,128)S(1)}, u32[]{:S(2)}, u32[]{:S(2)}) collective-permute-start(f32[40,128]{1,0:T(8,128)S(1)} %get-tuple-element.152), channel_id=1, source_target_pairs={{0,20},{1,21},{2,22},{3,23},{4,16},{5,17},{6,18},{7,19},{8,28},{9,... | collective-permute-start | bytes 61448 | tf_op jit(solution)/shard_map/ppermute | solution.py:212
  170.1 6.3 %collective-permute-start.57 = (f32[40,128]{1,0:T(8,128)S(1)}, f32[40,128]{1,0:T(8,128)S(1)}, u32[]{:S(2)}, u32[]{:S(2)}) collective-permute-start(f32[40,128]{1,0:T(8,128)S(1)} %get-tuple-element.153), channel_id=1, source_target_pairs={{0,28},{1,29},{2,30},{3,31},{4,24},{5,25},{6,26},{7,27},{8,20},{9,... | collective-permute-start | bytes 61448 | tf_op jit(solution)/shard_map/ppermute | solution.py:212

commit v2 on v1

v2 whole, which is shorter than its diff:
```python
import functools
import itertools

import jax
import jax.numpy as jnp
from jax import lax
from jax.experimental import pallas as pl
from jax.experimental.pallas import tpu as pltpu
from jax.sharding import PartitionSpec as P

NODES = 7
DOF = 3
ITERS = 3
AXES = ("gx", "gy", "gz")
STAGES = ((1,), (0, 2))
SPARE = (2, 1)
PAD = 8
CHUNK = 24
TILE = 256
F32 = jnp.float32
BF16 = jnp.bfloat16


def piece_length(placed):
    return DOF * NODES ** sum(1 for c in placed if c == 1)


PLACES = [p for p in itertools.product(range(3), repeat=3) if p != (1, 1, 1)]
CANON_OFFSET = {}
_at = 0
for _p in PLACES:
    CANON_OFFSET[_p] = _at
    _at += piece_length(_p)
IFACE = _at
LENGTH = {p: piece_length(p) for p in PLACES}
EARLY = [p for p in PLACES if p[1] != 1]
LATE = [p for p in PLACES if p[1] == 1]
SLOT_OFFSET = {}


def _lay(slots, at):
    for slot in slots:
        SLOT_OFFSET[slot] = at
        at += -(-LENGTH[slot] // PAD) * PAD
    return at


COARSE_AT = _lay(EARLY, 0)
SPLIT = -(-(COARSE_AT + 16) // 16) * 16
ROWS = -(-_lay(LATE, SPLIT) // TILE) * TILE
PARTS = {"all": (0, ROWS), "early": (0, SPLIT), "late": (SPLIT, ROWS)}


class Message:
    def __init__(self, moves, sizes, wrap, ride, spare):
        self.moves = moves
        self.sizes = sizes
        self.wrap = wrap
        self.ride = ride
        self.spare = spare
        self.faces = not any(m in ("C", "W") for m in moves)
        self.slots = []
        if self.faces:
            for place in EARLY + LATE:
                if all(m is None or c == (0 if m == "A" else 2) for m, c in zip(moves, place)):
                    self.slots.append(place)
        self.rows = -(-sum(LENGTH[s] for s in self.slots) // PAD) * PAD
        self.basis = []

    def xor(self):
        code = 0
        for move, size in zip(self.moves, self.sizes):
            code = code * size + {None: 0, "A": 1, "B": 3, "C": 2, "W": 3}[move]
        return code

    def pairs(self):
        out = []
        for place in itertools.product(*(range(s) for s in self.sizes)):
            to, whole = [], True
            for at, move, size in zip(place, self.moves, self.sizes):
                if move == "A":
                    at = at ^ 1
                elif move == "B":
                    whole = whole and (self.wrap or 0 < at < size - 1)
                    at = (at - 1) % size if at % 2 == 0 else (at + 1) % size
                elif move == "C":
                    at = at ^ 2
                elif move == "W":
                    at = at ^ 3
                to.append(at)
            if not whole:
                to = [at ^ 1 if d == self.spare else at for d, at in enumerate(place)]
            flat = [0, 0]
            for a, b, size in zip(place, to, self.sizes):
                flat = [flat[0] * size + a, flat[1] * size + b]
            out.append(tuple(flat))
        return out


def stage_messages(stage, sizes, coarse):
    choices = []
    for d in range(3):
        if d not in STAGES[stage]:
            choices.append((None,))
        else:
            extra = ("C", "W") if coarse and stage == 0 and sizes[d] == 4 else ()
            choices.append((None, "A") + (("B",) if sizes[d] > 2 else ()) + extra)
    out = []
    for moves in itertools.product(*choices):
        if all(m is None for m in moves):
            continue
        ride = coarse and (moves[1] != "B" if stage == 0 else moves[2] != "A")
        out.append(Message(moves, sizes, ride and stage == 1, ride, SPARE[stage]))
    return out


class Plan:
    def __init__(self, sizes):
        self.sizes = sizes
        self.subs = sizes[0] * sizes[1] * sizes[2]
        self.ride = all(s in (2, 4) for s in sizes)
        self.wide = self.subs * 8
        self.plain = [stage_messages(i, sizes, False) for i in range(2)]
        self.coarse = self.plain
        self.setup = 0
        if self.ride:
            self.local = Message((None, None, "A"), sizes, False, True, 0)
            self.coarse = [stage_messages(i, sizes, True) for i in range(2)]
            self.setup = self.wide // 128
            first, second = self.coarse
            for message in first:
                message.basis = [(None, slot) for slot in message.slots]
            for message in second:
                message.basis = [(None, slot) for slot in message.slots]
                for other in first:
                    message.basis += [(other, slot) for slot in message.slots if slot in other.slots]

    def per(self, kind):
        return {"plain": 0, "update": 1, "initial": self.setup}[kind] if self.ride else 0

    def messages(self, kind):
        return self.plain if self.per(kind) == 0 else self.coarse

    def codes(self, stage):
        known = [0, self.local.xor()]
        if stage == 1:
            known = [k ^ m for m in [0] + [m.xor() for m in self.coarse[0] if m.ride] for k in known]
        return known

    def payload_shapes(self, kind, stage):
        per = self.per(kind)
        out = []
        for m in self.messages(kind)[stage]:
            rows = m.rows
            if m.ride:
                rows += 8 * per * len(self.codes(stage))
            if kind == "initial" and self.ride and m.faces:
                rows += CHUNK
            out.append(shape(rows, 128))
        return out


def position():
    return [lax.axis_index(a) for a in AXES]


def has_b(index, size):
    return jnp.logical_and(index > 0, index < size - 1)


def exists(plan, index, message):
    ok = None
    for d, move in enumerate(message.moves):
        if move == "B":
            here = has_b(index[d], plan.sizes[d])
            ok = here if ok is None else jnp.logical_and(ok, here)
    return ok


def both(a, b):
    return b if a is None else a if b is None else jnp.logical_and(a, b)


def pick(slot, index, of):
    def choose(d, place):
        if d == 3:
            return of(tuple(place))
        if slot[d] == 1:
            return choose(d + 1, place + [1])
        even, odd = (2, 0) if slot[d] == 0 else (0, 2)
        return jnp.where(index[d] % 2 == 0, choose(d + 1, place + [even]), choose(d + 1, place + [odd]))

    return choose(0, [])


def add_received(plan, index, messages, received, acc):
    for message, ref in zip(messages, received):
        if not message.faces:
            continue
        ok = exists(plan, index, message)
        at = 0
        for slot in message.slots:
            rows, to = LENGTH[slot], SLOT_OFFSET[slot]
            value = ref[at : at + rows, :]
            if ok is not None:
                value = jnp.where(ok, value, 0.0)
            acc[to : to + rows, :] += value
            at += rows


def write_payloads(messages, outs, acc, blocks, pack=None):
    for message, out in zip(messages, outs):
        at = 0
        for slot in message.slots:
            rows, frm = LENGTH[slot], SLOT_OFFSET[slot]
            out[at : at + rows, :] = acc[frm : frm + rows, :]
            at += rows
        at = message.rows
        if message.ride:
            for block in blocks:
                out[at : at + 8, :] = block
                at += 8
        if pack is not None and message.faces:
            out[at : at + CHUNK, :] = pack(message)


def packer(own, stage, unpacked):
    def pack(message):
        at = 0
        for source, slot in message.basis:
            rows = LENGTH[slot]
            if source is not None:
                ref = unpacked[source]
                frm = sum(LENGTH[s] for s in source.slots[: source.slots.index(slot)])
            else:
                ref, frm = own, SLOT_OFFSET[slot]
            stage[at : at + rows, :] = ref[frm : frm + rows, :]
            at += rows
        count = -(-at // CHUNK)
        if at < count * CHUNK:
            stage[at : count * CHUNK, :] = jnp.zeros((count * CHUNK - at, 128), F32)
        total = stage[0:CHUNK, :]
        for k in range(1, count):
            total += pltpu.roll(stage[k * CHUNK : (k + 1) * CHUNK, :], 8 * k, 1)
        return total

    return pack


def unpack(message, block, out):
    count = -(-sum(LENGTH[slot] for _, slot in message.basis) // CHUNK)
    lane = lax.broadcasted_iota(jnp.int32, (CHUNK, 128), 1)
    for k in range(count):
        turned = pltpu.roll(block, 128 - 8 * k, 1) if k else block
        out[k * CHUNK : (k + 1) * CHUNK, :] = jnp.where(lane < 8, turned, 0.0)


def transfer(messages, payloads):
    return [lax.ppermute(p, AXES, m.pairs()) for m, p in zip(messages, payloads)]


def vm():
    return pl.BlockSpec(memory_space=pltpu.VMEM)


def shape(rows, cols, dtype=F32):
    return jax.ShapeDtypeStruct((rows, cols), dtype)


def call(kernel, outs, operands, specs=None, scratch=(), limit=20, flops=0):
    nbytes = sum(o.size * o.dtype.itemsize for o in list(outs) + list(operands))
    return pl.pallas_call(
        kernel,
        out_shape=tuple(outs),
        in_specs=specs or [vm()] * len(operands),
        out_specs=tuple(vm() for _ in outs),
        scratch_shapes=list(scratch),
        compiler_params=pltpu.CompilerParams(vmem_limit_bytes=limit << 20),
        cost_estimate=pl.CostEstimate(flops=flops, bytes_accessed=nbytes, transcendentals=0),
    )(*operands)


def gather_kernel(slots, start, canon, load, acc):
    index = position()
    acc[...] = jnp.zeros(acc.shape, F32)
    for slot in slots:
        length, at = LENGTH[slot], SLOT_OFFSET[slot] - start
        off = pick(slot, index, lambda place: jnp.int32(CANON_OFFSET[place]))
        step = 21 if length % 21 == 0 else 3

        def body(i, _, off=off, at=at, step=step):
            for j in range(step):
                row = i * step + j
                acc[pl.ds(at + row, 1), :] = load[canon[0, off + row], :, :]
            return 0

        lax.fori_loop(0, length // step, body, 0)


def scatter_rows(index, canon, acc, out):
    for slot in PLACES:
        length, at = LENGTH[slot], SLOT_OFFSET[slot]
        off = pick(slot, index, lambda place: jnp.int32(CANON_OFFSET[place]))
        step = 21 if length % 21 == 0 else 3

        def body(i, _, off=off, at=at, step=step):
            for j in range(step):
                row = i * step + j
                out[canon[0, off + row], :, :] = acc[pl.ds(at + row, 1), :]
            return 0

        lax.fori_loop(0, length // step, body, 0)


def scatter_kernel(canon, acc, out):
    scatter_rows(position(), canon, acc, out)


def split(value, parts):
    out = []
    for _ in range(parts):
        piece = value.astype(BF16)
        out.append(piece)
        value = value - piece.astype(F32)
    return out


def dot(a, b):
    return jnp.dot(a, b, preferred_element_type=F32)


def dot_last(a, b):
    return lax.dot_general(a, b, (((1,), (1,)), ((), ())), preferred_element_type=F32)


def tile(t):
    return pl.ds(pl.multiple_of(t * TILE, TILE), TILE)


def each_tile(body):
    def step(t, _):
        body(tile(t))
        return 0

    lax.fori_loop(0, ROWS // TILE, step, 0)


def select_kernel(plan, canon, basis, cinv, one, one_w, turned, *rest):
    src, wgt = rest[-2:]
    index = position()
    src[...] = jnp.full(src.shape, -1, jnp.int32)
    wgt[...] = jnp.zeros(wgt.shape, F32)
    for slot in PLACES:
        at, length = SLOT_OFFSET[slot], LENGTH[slot]
        src[at : at + length, :] = pick(
            slot, index, lambda place, length=length: canon[CANON_OFFSET[place] : CANON_OFFSET[place] + length, :]
        )
        weight = jnp.float32(1.0)
        for d in range(3):
            if slot[d] == 0:
                weight = weight * 0.5
            elif slot[d] == 2 and plan.sizes[d] > 2:
                weight = weight * jnp.where(has_b(index[d], plan.sizes[d]), 0.5, 1.0)
        wgt[at : at + length, :] = jnp.full((length, 1), 1.0, F32) * weight
    if plan.ride:
        spread_out = rest[0]
        nc = cinv.shape[1]
        row = lax.broadcasted_iota(jnp.int32, (nc, plan.wide), 0)
        col = lax.broadcasted_iota(jnp.int32, (nc, plan.wide), 1)
        spread = jnp.where(jnp.logical_and((col >> 3) * 6 + (col & 7) == row, (col & 7) < 6), 1.0, 0.0).astype(BF16)
        value = sum(dot(part, spread) for part in split(cinv[...], 3))
        spread_out[...] = jnp.zeros(spread_out.shape, F32)
        for i in range(plan.setup):
            spread_out[8 * i : 8 * i + 6, :] = value[:, 128 * i : 128 * (i + 1)]
    turned[...] = jnp.zeros(turned.shape, F32)

    def build(rows):
        hit = src[rows, :] == lax.broadcasted_iota(jnp.int32, (TILE, IFACE), 1)
        one[rows, :] = jnp.where(hit, 1.0, 0.0).astype(BF16)
        weighted = jnp.where(hit, wgt[rows, :], 0.0).astype(BF16)
        one_w[rows, :] = weighted
        turned[rows, :6] = dot_last(weighted, basis[...])

    each_tile(build)


def left_kernel(one, matrix, mid):
    def body(rows):
        mid[rows, :] = dot(one[rows, :], matrix[...]).astype(BF16)

    each_tile(body)


def right_kernel(one, mid, basis, out, few):
    def body(rows):
        out[rows, :] = dot_last(mid[rows, :], one[...]).astype(BF16)

    each_tile(body)
    if basis is not None:
        few[...] = jnp.zeros(few.shape, F32)
        few[:6, :] = dot_last(basis[...], one[...])
        out[COARSE_AT : COARSE_AT + 16, :] = few[...].astype(BF16)


def fill(acc, parts):
    at = 0
    for part in parts:
        acc[at : at + part.shape[0], :] = part[...]
        at += part.shape[0]


def known_blocks(plan, own, received, messages, per):
    blocks = own + [received[0][8 * i : 8 * (i + 1), :] for i in range(per)]
    for message, ref in zip(messages, received[1:]):
        if message.ride:
            blocks += [ref[message.rows + 8 * i : message.rows + 8 * (i + 1), :] for i in range(2 * per)]
    return blocks


def first_kernel(plan, kind, *refs):
    refs = list(refs)
    base, own, local = refs[:3]
    refs = refs[3:]
    per = plan.per(kind)
    pack = None
    if kind == "initial":
        turned = refs.pop(0)
        pack = packer(turned, refs.pop(-1), {})
        mine = [own[8 * i : 8 * (i + 1), :] for i in range(per)]
    else:
        mine = [own[...]]
    write_payloads(plan.coarse[0], refs, base, known_blocks(plan, mine, [local], [], per), pack)


def middle_kernel(plan, kind, count, *refs):
    first, second = plan.messages(kind)
    per = plan.per(kind)
    refs = list(refs)
    parts = [refs.pop(0) for _ in range(count)]
    received = [refs.pop(0) for _ in first]
    blocks, pack = [], None
    if per:
        own, local = refs.pop(0), refs.pop(0)
        mine = [own[8 * i : 8 * (i + 1), :] for i in range(per)]
        blocks = known_blocks(plan, mine, [local] + received, first, per)
    if per and kind == "initial":
        turned = refs.pop(0)
        stage = refs.pop(-1)
        kept = {m: refs.pop(-1) for m in reversed(first) if m.faces}
        for message, ref in zip(first, received):
            if message.faces:
                unpack(message, ref[ref.shape[0] - CHUNK :, :], kept[message])
        pack = packer(turned, stage, kept)
    acc = refs.pop(-1)
    fill(acc, parts)
    add_received(plan, position(), first, received, acc)
    write_payloads(second, refs, acc, blocks, pack)


def product_kernel(part, matrix, vector, out):
    start, stop = PARTS[part]
    size = (stop - start) // (4 if part == "all" else 2)
    for t in range(start, stop, size):
        out[t - start : t - start + size, :] = dot(matrix[t : t + size, :], vector[...])


def finish(plan, kind, parts, got, acc):
    first, second = plan.messages(kind)
    index = position()
    fill(acc, parts)
    add_received(plan, index, first, got[: len(first)], acc)
    add_received(plan, index, second, got[len(first) :], acc)


def residual_kernel(plan, opening, count, *refs):
    kind = "initial" if opening else "plain"
    refs = list(refs)
    parts = [refs.pop(0) for _ in range(count)]
    got = [refs.pop(0) for _ in range(sum(len(m) for m in plan.messages(kind)))]
    matrix = refs.pop(0)
    before = None if opening else refs.pop(0)
    residual, rounded, restricted, acc = refs
    finish(plan, kind, parts, got, acc)
    value = acc[...] if opening else before[...] - acc[...]
    residual[...] = value
    rounded[...] = value.astype(BF16)
    restricted[...] = dot(matrix[COARSE_AT : COARSE_AT + 16, :], rounded[...])[:8]


def lift_kernel(plan, base, turned, correction, out, *outs):
    lifted = turned[...].astype(BF16)
    out[...] = base[...] + sum(dot(lifted, part) for part in split(correction[...], 3))
    write_payloads(plan.plain[0], outs, out, [])


def collect(plan, own, got, per, which, stack, at_column):
    first, second = plan.coarse
    index = position()
    me = (index[0] * plan.sizes[1] + index[1]) * plan.sizes[2] + index[2]

    def put(code, value):
        stack[pl.ds(pl.multiple_of((me ^ code) * 8, 8), 8), at_column : at_column + 128] = value

    local, got = got[0], got[1:]
    put(0, own[8 * which : 8 * (which + 1), :])
    put(plan.local.xor(), local[8 * which : 8 * (which + 1), :])
    for stage, messages in enumerate((first, second)):
        for m, ref in zip(messages, got):
            if m.ride:
                for i, code in enumerate(plan.codes(stage)):
                    at = m.rows + 8 * (per * i + which)
                    put(code ^ m.xor(), ref[at : at + 8, :])
        got = got[len(messages) :]


def lifting_kernel(plan, *refs):
    first, second = plan.coarse
    turned, spread, local, *got, out, stack, many, unpacked = refs
    per = plan.setup
    index = position()
    me = (index[0] * plan.sizes[1] + index[1]) * plan.sizes[2] + index[2]

    def place(code, value, to, ok):
        there = me ^ code
        value = pltpu.roll(value, (there & 15) * 8, 1)
        rows = value.shape[0]
        for half in range(per):
            here = both((there >> 4) == half, ok)
            many[to : to + rows, 128 * half : 128 * (half + 1)] += jnp.where(here, value, 0.0)

    many[...] = jnp.zeros(many.shape, F32)
    for t in range(ROWS // TILE):
        place(0, turned[t * TILE : (t + 1) * TILE, :], t * TILE, None)
    for m, ref in zip(first + second, got):
        if not m.faces:
            continue
        unpack(m, ref[ref.shape[0] - CHUNK :, :], unpacked)
        at, ok = 0, exists(plan, index, m)
        for source, slot in m.basis:
            code, fine = m.xor(), ok
            if source is not None:
                code ^= source.xor()
                fine = both(exists(plan, index, source), ok)
            place(code, unpacked[at : at + LENGTH[slot], :], SLOT_OFFSET[slot], fine)
            at += LENGTH[slot]
    for half in range(per):
        collect(plan, spread, [local] + got, per, half, stack, 128 * half)
    parts = jnp.concatenate(split(stack[...], 3), axis=0)

    def body(rows):
        basis = many[rows, :].astype(BF16)
        whole = dot(jnp.concatenate([basis] * 3, axis=1), parts)
        high, low = split(whole, 2)
        out[rows, :] = jnp.concatenate([high, high, low], axis=1)

    each_tile(body)


def update_kernel(plan, *refs):
    refs = list(refs)
    base = refs.pop(0)
    got = [refs.pop(0) for _ in range(sum(len(m) for m in plan.messages("update")))]
    matrix = refs.pop(0)
    if plan.ride:
        lift, own, local = refs.pop(0), refs.pop(0), refs.pop(0)
        stack = refs.pop(-1)
    acc = refs.pop(-1)
    update, rounded, early, *outs = refs
    finish(plan, "update", [base], got, acc)
    if plan.ride:
        collect(plan, own, [local] + got, 1, 0, stack, 0)
        high, low = split(stack[...], 2)
        right = jnp.concatenate([high, low, high], axis=0)
        for t in range(0, ROWS, 320):
            value = acc[t : t + 320, :] + dot(lift[t : t + 320, :], right)
            update[t : t + 320, :] = value
            rounded[t : t + 320, :] = value.astype(BF16)
    else:
        update[...] = acc[...]
        rounded[...] = acc[...].astype(BF16)
    product_kernel("early", matrix, rounded, early)
    write_payloads(plan.plain[0], outs, early, [])


def later_kernel(opening, matrix, rounded, update, *refs):
    late, total = refs[-2:]
    product_kernel("late", matrix, rounded, late)
    total[...] = update[...] if opening else refs[0][...] + update[...]


def output_kernel(plan, canon, early, late, *refs):
    *got, residual, out, acc = refs
    finish(plan, "plain", [early, late], got, acc)
    acc[...] = residual[...] - acc[...]
    scatter_rows(position(), canon, acc, out)


def local(plan, load_cases, schur_matrix, local_inverse, coarse_basis, coarse_inverse, canon_rows):
    smem = pl.BlockSpec(memory_space=pltpu.SMEM)
    loads = load_cases.shape[-1]
    canon = canon_rows.reshape(1, IFACE)
    load = load_cases.reshape(IFACE, 1, loads)
    basis = coarse_basis[0, 0, 0]
    acc = pltpu.VMEM((ROWS, 128), F32)
    pieces = pltpu.VMEM((16 * CHUNK, 128), F32)
    early_rows, late_rows = SPLIT, ROWS - SPLIT

    def first(kind, base, own, swapped, more):
        return call(
            functools.partial(first_kernel, plan, kind),
            plan.payload_shapes(kind, 0),
            [base, own, swapped] + more,
            scratch=[pieces] if kind == "initial" else [],
        )

    def assemble(kind, parts, payloads, blocks, more, late=None):
        messages = plan.messages(kind)
        got = transfer(messages[0], payloads)
        setup = kind == "initial" and plan.ride
        payloads = call(
            functools.partial(middle_kernel, plan, kind, len(parts)),
            plan.payload_shapes(kind, 1),
            parts + got + blocks + (more if setup else []),
            scratch=[acc] + ([pieces] * (1 + sum(m.faces for m in messages[0])) if setup else []),
        )
        return got + transfer(messages[1], payloads)

    one, one_w, turned, *spread = call(
        functools.partial(select_kernel, plan),
        [shape(ROWS, IFACE, BF16), shape(ROWS, IFACE, BF16), shape(ROWS, 128)]
        + ([shape(8 * plan.setup, 128)] if plan.ride else []),
        [canon_rows.reshape(IFACE, 1), basis, coarse_inverse],
        scratch=[pltpu.VMEM((ROWS, 1), jnp.int32), pltpu.VMEM((ROWS, 1), F32)],
        flops=ROWS * IFACE * 1158,
    )
    (early,) = call(
        functools.partial(gather_kernel, EARLY, 0), [shape(early_rows, 128)], [canon, load], specs=[smem, vm()]
    )
    (late,) = call(
        functools.partial(gather_kernel, LATE, SPLIT), [shape(late_rows, 128)], [canon, load], specs=[smem, vm()]
    )
    flops = 2 * ROWS * IFACE * IFACE
    middle_shape, square = shape(ROWS, IFACE, BF16), shape(ROWS, ROWS, BF16)

    def right_plain(a, b, out):
        right_kernel(a, b, None, out, None)

    (half,) = call(left_kernel, [middle_shape], [one_w, local_inverse[0, 0, 0]], flops=flops)
    (inverse,) = call(
        right_kernel, [square], [one_w, half, basis], scratch=[pltpu.VMEM((16, ROWS), F32)], flops=flops
    )
    blocks = []
    if plan.ride:
        blocks = spread + transfer([plan.local], spread)
        payloads = first("initial", early, *blocks, [turned])
    else:
        payloads = call(
            lambda base, *outs: write_payloads(plan.plain[0], outs, base, []),
            plan.payload_shapes("plain", 0),
            [early],
        )
    parts = [early, late]
    got = assemble("initial", parts, payloads, blocks, [turned])
    if plan.ride:
        (lift,) = call(
            functools.partial(lifting_kernel, plan),
            [shape(ROWS, 3 * plan.wide, BF16)],
            [turned] + blocks + got,
            scratch=[pltpu.VMEM((plan.wide, plan.wide), F32), pltpu.VMEM((ROWS, plan.wide), F32), pieces],
            flops=2 * ROWS * 3 * plan.wide * plan.wide,
        )
    (half,) = call(left_kernel, [middle_shape], [one, schur_matrix[0, 0, 0]], flops=flops)
    (schur,) = call(right_plain, [square], [one, half], flops=flops)
    sol = residual = None
    flops = 2 * ROWS * ROWS * 128
    for iteration in range(ITERS):
        opening = iteration == 0
        residual, rounded, restricted = call(
            functools.partial(residual_kernel, plan, opening, len(parts)),
            [shape(ROWS, 128), shape(ROWS, 128, BF16), shape(8, 128)],
            parts + got + [inverse] + ([] if opening else [residual]),
            scratch=[acc],
        )
        (base,) = call(
            functools.partial(product_kernel, "all"), [shape(ROWS, 128)], [inverse, rounded], flops=flops
        )
        if plan.ride:
            blocks = [restricted] + transfer([plan.local], [restricted])
            payloads = first("update", base, *blocks, [])
        else:
            blocks = []
            rows = lax.all_gather(restricted[:6], AXES, axis=0, tiled=True)
            correction = jnp.dot(coarse_inverse, rows, precision=lax.Precision.HIGHEST, preferred_element_type=F32)
            base, *payloads = call(
                functools.partial(lift_kernel, plan),
                [shape(ROWS, 128)] + plan.payload_shapes("plain", 0),
                [base, turned, jnp.pad(correction, ((0, 122), (0, 0)))],
            )
        got = assemble("update", [base], payloads, blocks, [])
        update, rounded, early, *payloads = call(
            functools.partial(update_kernel, plan),
            [shape(ROWS, 128), shape(ROWS, 128, BF16), shape(early_rows, 128)] + plan.payload_shapes("plain", 0),
            [base] + got + [schur] + ([lift] + blocks if plan.ride else []),
            scratch=[acc] + ([pltpu.VMEM((plan.wide, 128), F32)] if plan.ride else []),
            flops=flops,
        )
        late, sol = call(
            functools.partial(later_kernel, opening),
            [shape(late_rows, 128), shape(ROWS, 128)],
            [schur, rounded, update] + ([] if opening else [sol]),
            flops=flops // 2,
        )
        parts = [early, late]
        got = assemble("plain", parts, payloads, [], [])
    out = jax.ShapeDtypeStruct((IFACE, 1, loads), F32)
    (sol_out,) = call(scatter_kernel, [out], [canon, sol], specs=[smem, vm()])
    (residual_out,) = call(
        functools.partial(output_kernel, plan),
        [out],
        [canon] + parts + got + [residual],
        specs=[smem] + [vm()] * (3 + len(got)),
        scratch=[acc],
    )
    return tuple(o.reshape(1, 1, 1, IFACE, loads) for o in (sol_out, residual_out))


def solution(mesh):
    plan = Plan(tuple(mesh.shape[a] for a in AXES))
    in_specs = (
        P("gx", "gy", "gz", None, None),
        P("gx", "gy", "gz", None, None),
        P("gx", "gy", "gz", None, None),
        P("gx", "gy", "gz", None, None),
        P(("gx", "gy", "gz"), None),
        P("gx", "gy", "gz", None),
    )
    out_specs = (P("gx", "gy", "gz", None, None), P("gx", "gy", "gz", None, None))
    return jax.shard_map(
        functools.partial(local, plan), mesh=mesh, in_specs=in_specs, out_specs=out_specs, check_vma=False
    )
```

time: 182 us -> 143 us (0.79)
  waiting for transfers between devices: 61.2 us -> 27.5 us
  starting transfers between devices: 71.9 us -> 66.3 us
  Pallas kernels: 42.2 us -> 45.7 us
    ppermute x58 -> x61, waiting for transfers between devices: 61.2 us -> 27.5 us  [transfer(): lax.ppermute(p, AXES, m.pairs())]
    ppermute x58 -> x61, starting transfers between devices: 71.9 us -> 66.3 us  [transfer(): lax.ppermute(p, AXES, m.pairs())]
    pallas_call x20 -> x33, Pallas kernels: 42.2 us -> 45.7 us  [call(): pl.pallas_call(kernel, out_shape=tuple(outs), in_specs=specs or [vm()] *...]
  transfers between devices with their start and end apart: 58 -> 61, of which waited for: 25 -> 19; matrix products, arithmetic and copies ran while one was open for 1% -> 0% of each run, Pallas kernels for 13% -> 24%
where the time goes in v2:
time: 143 us
  starting transfers between devices  66.3 us (46%)
  Pallas kernels  45.7 us (32%)
  waiting for transfers between devices  27.5 us (19%)
  local copies, waits for them, and re-layouts  2.43 us (2%)
    ppermute x61, starting transfers between devices, transfer(): lax.ppermute(p, AXES, m.pairs())  66.3 us
    pallas_call x33, Pallas kernels, call(): pl.pallas_call(kernel, out_shape=tuple(outs), in_specs=specs or [vm()] *...  45.7 us
    ppermute x61, waiting for transfers between devices, transfer(): lax.ppermute(p, AXES, m.pairs())  27.5 us
  transfers between devices with their start and end apart: 61, of which 19 were waited for; matrix products, arithmetic and copies ran while one was open for 0% of the time, Pallas kernels for 24%

profile of v2, /device:TPU:1, one launch (start us, length us, event | category | flops | bytes accessed | tf_op | source)
XLA Modules:
  0.0 143.0 jit_solution(717688614558920214)
XLA Ops:
  0.6 0.9 copy.10.canon
  3.1 2.6 %shard_map.77 = (bf16[1280,1158]{1,0:T(8,128)(2,1)S(1)}, bf16[1280,1158]{1,0:T(8,128)(2,1)S(1)}, f32[1280,128]{1,0:T(8,128)S(1)}, f32[16,128]{1,0:T(8,128)S(1)}) custom-call(s32[1158,1]{1,0:T(8,128)S(1)} %copy.10.canon, bf16[6,1158]{1,0:T(8,128)(2,1)S(1)} %bitcast.21, f32[6,192]{1,0:T(8,128)S(1)} %copy-done.6), custom_call_target="tpu_custom_call" | custom-call | flops 1716433920 | bytes 6615648 | tf_op jit(solution)/shard_map/pallas_call | solution.py:272
  5.8 1.2 shard_map.82.refs_0_
  7.1 2.8 %collective-permute-start.1 = (f32[304,128]{1,0:T(8,128)S(1)}, f32[304,128]{1,0:T(8,128)S(1)}, u32[]{:S(2)}, u32[]{:S(2)}) collective-permute-start(f32[304,128]{1,0:T(8,128)S(1)} %get-tuple-element.91), channel_id=1, source_target_pairs={{0,4},{1,5},{2,6},{3,7},{4,0},{5,1},{6,2},{7,3},{8,12},{9,13},{10,... | collective-permute-start | bytes 466952 | tf_op jit(solution)/shard_map/ppermute | solution.py:259
  10.3 2.0 %collective-permute-start.3 = (f32[32,128]{1,0:T(8,128)S(1)}, f32[32,128]{1,0:T(8,128)S(1)}, u32[]{:S(2)}, u32[]{:S(2)}) collective-permute-start(f32[32,128]{1,0:T(8,128)S(1)} %get-tuple-element.93), channel_id=1, source_target_pairs={{0,8},{1,9},{2,10},{3,11},{4,12},{5,13},{6,14},{7,15},{8,0},{9,1},... | collective-permute-start | bytes 49160 | tf_op jit(solution)/shard_map/ppermute | solution.py:259
  12.3 2.4 %collective-permute-start.4 = (f32[32,128]{1,0:T(8,128)S(1)}, f32[32,128]{1,0:T(8,128)S(1)}, u32[]{:S(2)}, u32[]{:S(2)}) collective-permute-start(f32[32,128]{1,0:T(8,128)S(1)} %get-tuple-element.94), channel_id=1, source_target_pairs={{0,12},{1,13},{2,14},{3,15},{4,8},{5,9},{6,10},{7,11},{8,4},{9,5},... | collective-permute-start | bytes 49160 | tf_op jit(solution)/shard_map/ppermute | solution.py:259
  14.6 5.1 %shard_map.80.mid = bf16[1280,1158]{1,0:T(8,128)(2,1)S(1)} custom-call(bf16[1280,1158]{1,0:T(8,128)(2,1)S(1)} %get-tuple-element.88.one, bf16[1158,1158]{1,0:T(8,128)(2,1)S(1)} %bitcast.19), custom_call_target="tpu_custom_call" | custom-call | flops 3432867840 | bytes 8610888 | tf_op jit(solution)/shard_map/pallas_call | solution.py:272
  19.8 1.5 %shard_map.83.refs_1_ = f32[704,128]{1,0:T(8,128)S(1)} custom-call(s32[1,1158]{1,0:T(1,128)S(1)} %bitcast.16, f32[1158,1,128]{2,1,0:T(1,128)S(1)} %bitcast.13), custom_call_target="tpu_custom_call" | custom-call | bytes 957976 | tf_op jit(solution)/shard_map/pallas_call | solution.py:272
  21.7 1.2 collective-permute-start.5
  22.9 1.2 collective-permute-start.6
  24.1 1.2 collective-permute-start.7
  27.0 6.2 %shard_map.81.refs_11_.matrix.refs_9_ = bf16[1280,1280]{1,0:T(8,128)(2,1)S(1)} custom-call(bf16[1280,1158]{1,0:T(8,128)(2,1)S(1)} %get-tuple-element.88.one, bf16[1280,1158]{1,0:T(8,128)(2,1)S(1)} %shard_map.80.mid, bf16[6,1158]{1,0:T(8,128)(2,1)S(1)} %bitcast.22), custom_call_target="tpu_custom_call" | custom-call | flops 3432867840 | bytes 9219656 | tf_op jit(solution)/shard_map/pallas_call | solution.py:272
  34.4 1.0 shard_map.87.refs_0_
  35.7 2.4 %collective-permute-start.13 = (f32[16,128]{1,0:T(8,128)S(1)}, f32[16,128]{1,0:T(8,128)S(1)}, u32[]{:S(2)}, u32[]{:S(2)}) collective-permute-start(f32[16,128]{1,0:T(8,128)S(1)} %get-tuple-element.104), channel_id=1, source_target_pairs={{0,8},{1,9},{2,10},{3,11},{4,12},{5,13},{6,14},{7,15},{8,0},{9,1},... | collective-permute-start | bytes 24584 | tf_op jit(solution)/shard_map/ppermute | solution.py:259
  38.1 0.9 collective-permute-start.14
  39.0 5.1 %shard_map.78.b = bf16[1280,1158]{1,0:T(8,128)(2,1)S(1)} custom-call(bf16[1280,1158]{1,0:T(8,128)(2,1)S(1)} %get-tuple-element.87.one.a, bf16[1158,1158]{1,0:T(8,128)(2,1)S(1)} %bitcast.20), custom_call_target="tpu_custom_call" | custom-call | flops 3432867840 | bytes 8610888 | tf_op jit(solution)/shard_map/pallas_call | solution.py:272
  44.3 1.1 collective-permute-start.15
  45.3 1.2 collective-permute-start.16
  46.6 1.0 collective-permute-start.17
  47.6 1.0 collective-permute-start.19
  48.6 5.3 %shard_map.79.refs_10_.matrix = bf16[1280,1280]{1,0:T(8,128)(2,1)S(1)} custom-call(bf16[1280,1158]{1,0:T(8,128)(2,1)S(1)} %get-tuple-element.87.one.a, bf16[1280,1158]{1,0:T(8,128)(2,1)S(1)} %shard_map.78.b), custom_call_target="tpu_custom_call" | custom-call | flops 3432867840 | bytes 9205760 | tf_op jit(solution)/shard_map/pallas_call | solution.py:272
  54.6 2.4 %shard_map.90.refs_11_ = bf16[1280,768]{1,0:T(8,128)(2,1)S(1)} custom-call(f32[1280,128]{1,0:T(8,128)S(1)} %get-tuple-element.90.refs_3_.refs_8_.refs_0_, f32[16,128]{1,0:T(8,128)S(1)} %get-tuple-element.89.refs_1_.refs_6_, f32[16,128]{1,0:T(8,128)S(1)} %collective-permute-done.refs_2_.refs_7_, f32[304,128]{1,0:T(8,128)S(1)} %collective-permute-done.1.refs_2_.refs_3_, ...), custom_call_target="tpu_custom_call" | custom-call | flops 503316480 | bytes 3637248 | tf_op jit(solution)/shard_map/pallas_call | solution.py:272
  57.2 1.2 shard_map.91
  59.8 2.9 %collective-permute-done.20.refs_2_ = f32[248,128]{1,0:T(8,128)S(1)} collective-permute-done((f32[248,128]{1,0:T(8,128)S(1)}, f32[248,128]{1,0:T(8,128)S(1)}, u32[]{:S(2)}, u32[]{:S(2)}) %collective-permute-start.20) | collective-permute-done | bytes 127008 | tf_op jit(solution)/shard_map/ppermute | solution.py:259
  62.8 1.6 %collective-permute-start.22 = (f32[248,128]{1,0:T(8,128)S(1)}, f32[248,128]{1,0:T(8,128)S(1)}, u32[]{:S(2)}, u32[]{:S(2)}) collective-permute-start(f32[248,128]{1,0:T(8,128)S(1)} %get-tuple-element.117), channel_id=1, source_target_pairs={{0,1},{1,0},{2,3},{3,2},{4,5},{5,4},{6,7},{7,6},{8,9},{9,8},{10,11... | collective-permute-start | bytes 380936 | tf_op jit(solution)/shard_map/ppermute | solution.py:259
  64.4 1.2 collective-permute-start.23
  65.5 1.0 collective-permute-start.24
  66.5 1.5 %collective-permute-start.25 = (f32[32,128]{1,0:T(8,128)S(1)}, f32[32,128]{1,0:T(8,128)S(1)}, u32[]{:S(2)}, u32[]{:S(2)}) collective-permute-start(f32[32,128]{1,0:T(8,128)S(1)} %get-tuple-element.120), channel_id=1, source_target_pairs={{0,17},{1,16},{2,19},{3,18},{4,21},{5,20},{6,23},{7,22},{8,25},{9,... | collective-permute-start | bytes 49160 | tf_op jit(solution)/shard_map/ppermute | solution.py:259
  68.0 1.8 %collective-permute-start.26 = (f32[32,128]{1,0:T(8,128)S(1)}, f32[32,128]{1,0:T(8,128)S(1)}, u32[]{:S(2)}, u32[]{:S(2)}) collective-permute-start(f32[32,128]{1,0:T(8,128)S(1)} %get-tuple-element.121), channel_id=1, source_target_pairs={{0,4},{1,18},{2,17},{3,7},{4,0},{5,22},{6,21},{7,3},{8,12},{9,26},... | collective-permute-start | bytes 49160 | tf_op jit(solution)/shard_map/ppermute | solution.py:259
  69.8 1.3 collective-permute-done.25.refs_7_
  71.1 1.0 collective-permute-done.26.refs_8_
  72.5 1.0 shard_map.95.refs_0_
  75.0 1.6 %collective-permute-start.30 = (f32[16,128]{1,0:T(8,128)S(1)}, f32[16,128]{1,0:T(8,128)S(1)}, u32[]{:S(2)}, u32[]{:S(2)}) collective-permute-start(f32[16,128]{1,0:T(8,128)S(1)} %get-tuple-element.127), channel_id=1, source_target_pairs={{0,8},{1,9},{2,10},{3,11},{4,12},{5,13},{6,14},{7,15},{8,0},{9,1},... | collective-permute-start | bytes 24584 | tf_op jit(solution)/shard_map/ppermute | solution.py:259
  76.6 2.4 %collective-permute-start.31 = (f32[16,128]{1,0:T(8,128)S(1)}, f32[16,128]{1,0:T(8,128)S(1)}, u32[]{:S(2)}, u32[]{:S(2)}) collective-permute-start(f32[16,128]{1,0:T(8,128)S(1)} %get-tuple-element.128), channel_id=1, source_target_pairs={{0,12},{1,13},{2,14},{3,15},{4,8},{5,9},{6,10},{7,11},{8,4},{9,5},... | collective-permute-start | bytes 24584 | tf_op jit(solution)/shard_map/ppermute | solution.py:259
  79.5 1.4 %collective-permute-done.31.refs_4_ = f32[16,128]{1,0:T(8,128)S(1)} collective-permute-done((f32[16,128]{1,0:T(8,128)S(1)}, f32[16,128]{1,0:T(8,128)S(1)}, u32[]{:S(2)}, u32[]{:S(2)}) %collective-permute-start.31) | collective-permute-done | bytes 8224 | tf_op jit(solution)/shard_map/ppermute | solution.py:259
  81.0 2.8 %collective-permute-start.33 = (f32[312,128]{1,0:T(8,128)S(1)}, f32[312,128]{1,0:T(8,128)S(1)}, u32[]{:S(2)}, u32[]{:S(2)}) collective-permute-start(f32[312,128]{1,0:T(8,128)S(1)} %get-tuple-element.130), channel_id=1, source_target_pairs={{0,3},{1,2},{2,1},{3,0},{4,7},{5,6},{6,5},{7,4},{8,11},{9,10},{10,... | collective-permute-start | bytes 479240 | tf_op jit(solution)/shard_map/ppermute | solution.py:259
  83.8 1.1 collective-permute-start.34
  84.9 1.2 collective-permute-start.36
  87.0 4.1 %collective-permute-done.35.refs_8_ = f32[32,128]{1,0:T(8,128)S(1)} collective-permute-done((f32[32,128]{1,0:T(8,128)S(1)}, f32[32,128]{1,0:T(8,128)S(1)}, u32[]{:S(2)}, u32[]{:S(2)}) %collective-permute-start.35) | collective-permute-done | bytes 16416 | tf_op jit(solution)/shard_map/ppermute | solution.py:259
  91.3 1.2 shard_map.98
  93.8 3.2 %collective-permute-done.37.refs_2_ = f32[248,128]{1,0:T(8,128)S(1)} collective-permute-done((f32[248,128]{1,0:T(8,128)S(1)}, f32[248,128]{1,0:T(8,128)S(1)}, u32[]{:S(2)}, u32[]{:S(2)}) %collective-permute-start.37) | collective-permute-done | bytes 127008 | tf_op jit(solution)/shard_map/ppermute | solution.py:259
  97.1 1.4 collective-permute-start.39
  99.2 1.1 collective-permute-start.41
  100.3 1.9 %collective-permute-start.42 = (f32[32,128]{1,0:T(8,128)S(1)}, f32[32,128]{1,0:T(8,128)S(1)}, u32[]{:S(2)}, u32[]{:S(2)}) collective-permute-start(f32[32,128]{1,0:T(8,128)S(1)} %get-tuple-element.144), channel_id=1, source_target_pairs={{0,17},{1,16},{2,19},{3,18},{4,21},{5,20},{6,23},{7,22},{8,25},{9,... | collective-permute-start | bytes 49160 | tf_op jit(solution)/shard_map/ppermute | solution.py:259
  102.1 1.2 collective-permute-start.43
  103.4 2.0 %collective-permute-done.42.refs_7_ = f32[32,128]{1,0:T(8,128)S(1)} collective-permute-done((f32[32,128]{1,0:T(8,128)S(1)}, f32[32,128]{1,0:T(8,128)S(1)}, u32[]{:S(2)}, u32[]{:S(2)}) %collective-permute-start.42) | collective-permute-done | bytes 16416 | tf_op jit(solution)/shard_map/ppermute | solution.py:259
  105.3 0.9 collective-permute-done.43.refs_8_
  106.6 1.0 shard_map.102.refs_0_
  109.0 1.6 %collective-permute-start.47 = (f32[16,128]{1,0:T(8,128)S(1)}, f32[16,128]{1,0:T(8,128)S(1)}, u32[]{:S(2)}, u32[]{:S(2)}) collective-permute-start(f32[16,128]{1,0:T(8,128)S(1)} %get-tuple-element.151), channel_id=1, source_target_pairs={{0,8},{1,9},{2,10},{3,11},{4,12},{5,13},{6,14},{7,15},{8,0},{9,1},... | collective-permute-start | bytes 24584 | tf_op jit(solution)/shard_map/ppermute | solution.py:259
  110.5 2.4 %collective-permute-start.48 = (f32[16,128]{1,0:T(8,128)S(1)}, f32[16,128]{1,0:T(8,128)S(1)}, u32[]{:S(2)}, u32[]{:S(2)}) collective-permute-start(f32[16,128]{1,0:T(8,128)S(1)} %get-tuple-element.152), channel_id=1, source_target_pairs={{0,12},{1,13},{2,14},{3,15},{4,8},{5,9},{6,10},{7,11},{8,4},{9,5},... | collective-permute-start | bytes 24584 | tf_op jit(solution)/shard_map/ppermute | solution.py:259
  113.3 1.6 %collective-permute-done.48.refs_4_ = f32[16,128]{1,0:T(8,128)S(1)} collective-permute-done((f32[16,128]{1,0:T(8,128)S(1)}, f32[16,128]{1,0:T(8,128)S(1)}, u32[]{:S(2)}, u32[]{:S(2)}) %collective-permute-start.48) | collective-permute-done | bytes 8224 | tf_op jit(solution)/shard_map/ppermute | solution.py:259
  114.9 2.8 %collective-permute-start.50 = (f32[312,128]{1,0:T(8,128)S(1)}, f32[312,128]{1,0:T(8,128)S(1)}, u32[]{:S(2)}, u32[]{:S(2)}) collective-permute-start(f32[312,128]{1,0:T(8,128)S(1)} %get-tuple-element.154), channel_id=1, source_target_pairs={{0,3},{1,2},{2,1},{3,0},{4,7},{5,6},{6,5},{7,4},{8,11},{9,10},{10,... | collective-permute-start | bytes 479240 | tf_op jit(solution)/shard_map/ppermute | solution.py:259
  117.7 1.0 collective-permute-start.51
  118.7 1.6 %collective-permute-start.53 = (f32[96,128]{1,0:T(8,128)S(1)}, f32[96,128]{1,0:T(8,128)S(1)}, u32[]{:S(2)}, u32[]{:S(2)}) collective-permute-start(f32[96,128]{1,0:T(8,128)S(1)} %get-tuple-element.157), channel_id=1, source_target_pairs={{0,19},{1,18},{2,17},{3,16},{4,23},{5,22},{6,21},{7,20},{8,27},{9,... | collective-permute-start | bytes 147464 | tf_op jit(solution)/shard_map/ppermute | solution.py:259
  120.3 0.9 collective-permute-start.52
  121.2 4.0 %collective-permute-done.52.refs_8_ = f32[32,128]{1,0:T(8,128)S(1)} collective-permute-done((f32[32,128]{1,0:T(8,128)S(1)}, f32[32,128]{1,0:T(8,128)S(1)}, u32[]{:S(2)}, u32[]{:S(2)}) %collective-permute-start.52) | collective-permute-done | bytes 16416 | tf_op jit(solution)/shard_map/ppermute | solution.py:259
  125.2 1.2 shard_map.105
  127.8 3.1 %collective-permute-done.54.refs_2_.refs_0_ = f32[248,128]{1,0:T(8,128)S(1)} collective-permute-done((f32[248,128]{1,0:T(8,128)S(1)}, f32[248,128]{1,0:T(8,128)S(1)}, u32[]{:S(2)}, u32[]{:S(2)}) %collective-permute-start.54) | collective-permute-done | bytes 127008 | tf_op jit(solution)/shard_map/ppermute | solution.py:259
  130.9 1.5 %collective-permute-start.56 = (f32[248,128]{1,0:T(8,128)S(1)}, f32[248,128]{1,0:T(8,128)S(1)}, u32[]{:S(2)}, u32[]{:S(2)}) collective-permute-start(f32[248,128]{1,0:T(8,128)S(1)} %get-tuple-element.166), channel_id=1, source_target_pairs={{0,1},{1,0},{2,3},{3,2},{4,5},{5,4},{6,7},{7,6},{8,9},{9,8},{10,11... | collective-permute-start | bytes 380936 | tf_op jit(solution)/shard_map/ppermute | solution.py:259
  133.1 1.0 collective-permute-start.58
  134.1 1.8 %collective-permute-start.59 = (f32[32,128]{1,0:T(8,128)S(1)}, f32[32,128]{1,0:T(8,128)S(1)}, u32[]{:S(2)}, u32[]{:S(2)}) collective-permute-start(f32[32,128]{1,0:T(8,128)S(1)} %get-tuple-element.169), channel_id=1, source_target_pairs={{0,17},{1,16},{2,19},{3,18},{4,21},{5,20},{6,23},{7,22},{8,25},{9,... | collective-permute-start | bytes 49160 | tf_op jit(solution)/shard_map/ppermute | solution.py:259
  135.9 1.1 collective-permute-start.60
  137.0 2.8 %shard_map.107 = f32[1158,1,128]{2,1,0:T(1,128)} custom-call(s32[1,1158]{1,0:T(1,128)S(1)} %bitcast.17, f32[1280,128]{1,0:T(8,128)S(1)} %get-tuple-element.161.acc), custom_call_target="tpu_custom_call" | custom-call | bytes 1252888 | tf_op jit(solution)/shard_map/pallas_call | solution.py:272
  140.0 3.0 %shard_map.109 = f32[1158,1,128]{2,1,0:T(1,128)} custom-call(s32[1,1158]{1,0:T(1,128)S(1)} %bitcast.18, f32[576,128]{1,0:T(8,128)S(1)} %get-tuple-element.162.refs_0_.early, f32[704,128]{1,0:T(8,128)S(1)} %get-tuple-element.163.refs_1_.late, f32[248,128]{1,0:T(8,128)S(1)} %collective-permute-done.54.refs_2_.refs_0_, ...), custom_call_target="tpu_custom_call" | custom-call | bytes 2575896 | tf_op jit(solution)/shard_map/pallas_call | solution.py:272
  (106 shorter events, 17.8 us)
Async XLA Ops:
  3.1 11.6 %copy-start.2 = (bf16[1,1,1,1158,1158]{4,3,2,1,0:T(8,128)(2,1)S(1)}, bf16[1,1,1,1158,1158]{4,3,2,1,0:T(8,128)(2,1)}, u32[]{:S(2)}) copy-start(bf16[1,1,1,1158,1158]{4,3,2,1,0:T(8,128)(2,1)} %param.8) | copy-start | bytes 8045788
  5.7 1.3 collective-permute-start
  7.1 14.1 %collective-permute-start.1 = (f32[304,128]{1,0:T(8,128)S(1)}, f32[304,128]{1,0:T(8,128)S(1)}, u32[]{:S(2)}, u32[]{:S(2)}) collective-permute-start(f32[304,128]{1,0:T(8,128)S(1)} %get-tuple-element.91), channel_id=1, source_target_pairs={{0,4},{1,5},{2,6},{3,7},{4,0},{5,1},{6,2},{7,3},{8,12},{9,13},{10,... | collective-permute-start | bytes 466952 | tf_op jit(solution)/shard_map/ppermute | solution.py:259
  10.0 11.3 %collective-permute-start.2 = (f32[272,128]{1,0:T(8,128)S(1)}, f32[272,128]{1,0:T(8,128)S(1)}, u32[]{:S(2)}, u32[]{:S(2)}) collective-permute-start(f32[272,128]{1,0:T(8,128)S(1)} %get-tuple-element.92), channel_id=1, source_target_pairs={{0,1},{1,0},{2,3},{3,2},{4,8},{5,9},{6,10},{7,11},{8,4},{9,5},{10,... | collective-permute-start | bytes 417800 | tf_op jit(solution)/shard_map/ppermute | solution.py:259
  10.3 11.0 %collective-permute-start.3 = (f32[32,128]{1,0:T(8,128)S(1)}, f32[32,128]{1,0:T(8,128)S(1)}, u32[]{:S(2)}, u32[]{:S(2)}) collective-permute-start(f32[32,128]{1,0:T(8,128)S(1)} %get-tuple-element.93), channel_id=1, source_target_pairs={{0,8},{1,9},{2,10},{3,11},{4,12},{5,13},{6,14},{7,15},{8,0},{9,1},... | collective-permute-start | bytes 49160 | tf_op jit(solution)/shard_map/ppermute | solution.py:259
  12.3 9.0 %collective-permute-start.4 = (f32[32,128]{1,0:T(8,128)S(1)}, f32[32,128]{1,0:T(8,128)S(1)}, u32[]{:S(2)}, u32[]{:S(2)}) collective-permute-start(f32[32,128]{1,0:T(8,128)S(1)} %get-tuple-element.94), channel_id=1, source_target_pairs={{0,12},{1,13},{2,14},{3,15},{4,8},{5,9},{6,10},{7,11},{8,4},{9,5},... | collective-permute-start | bytes 49160 | tf_op jit(solution)/shard_map/ppermute | solution.py:259
  14.6 12.3 %copy-start.5 = (bf16[1,1,1,6,1158]{4,3,2,1,0:T(8,128)(2,1)S(1)}, bf16[1,1,1,6,1158]{4,3,2,1,0:T(8,128)(2,1)}, u32[]{:S(2)}) copy-start(bf16[1,1,1,6,1158]{4,3,2,1,0:T(8,128)(2,1)} %param.9) | copy-start | bytes 41692
  21.7 11.8 %collective-permute-start.5 = (f32[272,128]{1,0:T(8,128)S(1)}, f32[272,128]{1,0:T(8,128)S(1)}, u32[]{:S(2)}, u32[]{:S(2)}) collective-permute-start(f32[272,128]{1,0:T(8,128)S(1)} %get-tuple-element.95), channel_id=1, source_target_pairs={{0,1},{1,0},{2,3},{3,2},{4,5},{5,4},{6,7},{7,6},{8,9},{9,8},{10,11... | collective-permute-start | bytes 417800 | tf_op jit(solution)/shard_map/ppermute | solution.py:259
  22.9 10.6 %collective-permute-start.6 = (f32[400,128]{1,0:T(8,128)S(1)}, f32[400,128]{1,0:T(8,128)S(1)}, u32[]{:S(2)}, u32[]{:S(2)}) collective-permute-start(f32[400,128]{1,0:T(8,128)S(1)} %get-tuple-element.96), channel_id=1, source_target_pairs={{0,3},{1,2},{2,1},{3,0},{4,7},{5,6},{6,5},{7,4},{8,11},{9,10},{10,... | collective-permute-start | bytes 614408 | tf_op jit(solution)/shard_map/ppermute | solution.py:259
  24.1 9.4 %collective-permute-start.7 = (f32[400,128]{1,0:T(8,128)S(1)}, f32[400,128]{1,0:T(8,128)S(1)}, u32[]{:S(2)}, u32[]{:S(2)}) collective-permute-start(f32[400,128]{1,0:T(8,128)S(1)} %get-tuple-element.97), channel_id=1, source_target_pairs={{0,16},{1,17},{2,18},{3,19},{4,20},{5,21},{6,22},{7,23},{8,24},{9,... | collective-permute-start | bytes 614408 | tf_op jit(solution)/shard_map/ppermute | solution.py:259
  25.3 7.9 %collective-permute-start.8 = (f32[56,128]{1,0:T(8,128)S(1)}, f32[56,128]{1,0:T(8,128)S(1)}, u32[]{:S(2)}, u32[]{:S(2)}) collective-permute-start(f32[56,128]{1,0:T(8,128)S(1)} %get-tuple-element.98), channel_id=1, source_target_pairs={{0,17},{1,16},{2,19},{3,18},{4,21},{5,20},{6,23},{7,22},{8,25},{9,... | collective-permute-start | bytes 86024 | tf_op jit(solution)/shard_map/ppermute | solution.py:259
  26.2 7.3 %collective-permute-start.9 = (f32[184,128]{1,0:T(8,128)S(1)}, f32[184,128]{1,0:T(8,128)S(1)}, u32[]{:S(2)}, u32[]{:S(2)}) collective-permute-start(f32[184,128]{1,0:T(8,128)S(1)} %get-tuple-element.99), channel_id=1, source_target_pairs={{0,19},{1,18},{2,17},{3,16},{4,23},{5,22},{6,21},{7,20},{8,27},{9,... | collective-permute-start | bytes 282632 | tf_op jit(solution)/shard_map/ppermute | solution.py:259
  33.8 5.3 %copy-start.3 = (bf16[1,1,1,1158,1158]{4,3,2,1,0:T(8,128)(2,1)S(1)}, bf16[1,1,1,1158,1158]{4,3,2,1,0:T(8,128)(2,1)}, u32[]{:S(2)}) copy-start(bf16[1,1,1,1158,1158]{4,3,2,1,0:T(8,128)(2,1)} %param.7) | copy-start | bytes 8045788
  33.8 1.6 %collective-permute-start.10 = (f32[8,128]{1,0:T(8,128)S(1)}, f32[8,128]{1,0:T(8,128)S(1)}, u32[]{:S(2)}, u32[]{:S(2)}) collective-permute-start(f32[8,128]{1,0:T(8,128)S(1)} %get-tuple-element.101.refs_1_.refs_5_.refs_12_), channel_id=1, source_target_pairs={{0,1},{1,0},{2,3},{3,2},{4,5},{5,4},{6,7},{7,6},{8,9},{9,8},{10,11... | collective-permute-start | bytes 12296 | tf_op jit(solution)/shard_map/ppermute | solution.py:259
  35.4 8.8 %collective-permute-start.11 = (f32[264,128]{1,0:T(8,128)S(1)}, f32[264,128]{1,0:T(8,128)S(1)}, u32[]{:S(2)}, u32[]{:S(2)}) collective-permute-start(f32[264,128]{1,0:T(8,128)S(1)} %get-tuple-element.102), channel_id=1, source_target_pairs={{0,4},{1,5},{2,6},{3,7},{4,0},{5,1},{6,2},{7,3},{8,12},{9,13},{10,... | collective-permute-start | bytes 405512 | tf_op jit(solution)/shard_map/ppermute | solution.py:259
  35.5 8.7 %collective-permute-start.12 = (f32[248,128]{1,0:T(8,128)S(1)}, f32[248,128]{1,0:T(8,128)S(1)}, u32[]{:S(2)}, u32[]{:S(2)}) collective-permute-start(f32[248,128]{1,0:T(8,128)S(1)} %get-tuple-element.103), channel_id=1, source_target_pairs={{0,1},{1,0},{2,3},{3,2},{4,8},{5,9},{6,10},{7,11},{8,4},{9,5},{10,... | collective-permute-start | bytes 380936 | tf_op jit(solution)/shard_map/ppermute | solution.py:259
  35.7 8.5 %collective-permute-start.13 = (f32[16,128]{1,0:T(8,128)S(1)}, f32[16,128]{1,0:T(8,128)S(1)}, u32[]{:S(2)}, u32[]{:S(2)}) collective-permute-start(f32[16,128]{1,0:T(8,128)S(1)} %get-tuple-element.104), channel_id=1, source_target_pairs={{0,8},{1,9},{2,10},{3,11},{4,12},{5,13},{6,14},{7,15},{8,0},{9,1},... | collective-permute-start | bytes 24584 | tf_op jit(solution)/shard_map/ppermute | solution.py:259
  38.1 6.1 %collective-permute-start.14 = (f32[16,128]{1,0:T(8,128)S(1)}, f32[16,128]{1,0:T(8,128)S(1)}, u32[]{:S(2)}, u32[]{:S(2)}) collective-permute-start(f32[16,128]{1,0:T(8,128)S(1)} %get-tuple-element.105), channel_id=1, source_target_pairs={{0,12},{1,13},{2,14},{3,15},{4,8},{5,9},{6,10},{7,11},{8,4},{9,5},... | collective-permute-start | bytes 24584 | tf_op jit(solution)/shard_map/ppermute | solution.py:259
  44.3 12.9 %collective-permute-start.15 = (f32[248,128]{1,0:T(8,128)S(1)}, f32[248,128]{1,0:T(8,128)S(1)}, u32[]{:S(2)}, u32[]{:S(2)}) collective-permute-start(f32[248,128]{1,0:T(8,128)S(1)} %get-tuple-element.106), channel_id=1, source_target_pairs={{0,1},{1,0},{2,3},{3,2},{4,5},{5,4},{6,7},{7,6},{8,9},{9,8},{10,11... | collective-permute-start | bytes 380936 | tf_op jit(solution)/shard_map/ppermute | solution.py:259
  45.3 11.8 %collective-permute-start.16 = (f32[312,128]{1,0:T(8,128)S(1)}, f32[312,128]{1,0:T(8,128)S(1)}, u32[]{:S(2)}, u32[]{:S(2)}) collective-permute-start(f32[312,128]{1,0:T(8,128)S(1)} %get-tuple-element.107), channel_id=1, source_target_pairs={{0,3},{1,2},{2,1},{3,0},{4,7},{5,6},{6,5},{7,4},{8,11},{9,10},{10,... | collective-permute-start | bytes 479240 | tf_op jit(solution)/shard_map/ppermute | solution.py:259
  46.6 10.6 %collective-permute-start.17 = (f32[312,128]{1,0:T(8,128)S(1)}, f32[312,128]{1,0:T(8,128)S(1)}, u32[]{:S(2)}, u32[]{:S(2)}) collective-permute-start(f32[312,128]{1,0:T(8,128)S(1)} %get-tuple-element.108), channel_id=1, source_target_pairs={{0,16},{1,17},{2,18},{3,19},{4,20},{5,21},{6,22},{7,23},{8,24},{9,... | collective-permute-start | bytes 479240 | tf_op jit(solution)/shard_map/ppermute | solution.py:259
  47.6 9.6 %collective-permute-start.19 = (f32[96,128]{1,0:T(8,128)S(1)}, f32[96,128]{1,0:T(8,128)S(1)}, u32[]{:S(2)}, u32[]{:S(2)}) collective-permute-start(f32[96,128]{1,0:T(8,128)S(1)} %get-tuple-element.110), channel_id=1, source_target_pairs={{0,19},{1,18},{2,17},{3,16},{4,23},{5,22},{6,21},{7,20},{8,27},{9,... | collective-permute-start | bytes 147464 | tf_op jit(solution)/shard_map/ppermute | solution.py:259
  53.9 3.2 %collective-permute-start.18 = (f32[32,128]{1,0:T(8,128)S(1)}, f32[32,128]{1,0:T(8,128)S(1)}, u32[]{:S(2)}, u32[]{:S(2)}) collective-permute-start(f32[32,128]{1,0:T(8,128)S(1)} %get-tuple-element.109), channel_id=1, source_target_pairs={{0,17},{1,16},{2,19},{3,18},{4,21},{5,20},{6,23},{7,22},{8,25},{9,... | collective-permute-start | bytes 49160 | tf_op jit(solution)/shard_map/ppermute | solution.py:259
  58.4 4.4 %collective-permute-start.20 = (f32[248,128]{1,0:T(8,128)S(1)}, f32[248,128]{1,0:T(8,128)S(1)}, u32[]{:S(2)}, u32[]{:S(2)}) collective-permute-start(f32[248,128]{1,0:T(8,128)S(1)} %get-tuple-element.115), channel_id=1, source_target_pairs={{0,4},{1,5},{2,6},{3,7},{4,0},{5,1},{6,2},{7,3},{8,12},{9,13},{10,... | collective-permute-start | bytes 380936 | tf_op jit(solution)/shard_map/ppermute | solution.py:259
  58.4 4.3 %collective-permute-start.21 = (f32[248,128]{1,0:T(8,128)S(1)}, f32[248,128]{1,0:T(8,128)S(1)}, u32[]{:S(2)}, u32[]{:S(2)}) collective-permute-start(f32[248,128]{1,0:T(8,128)S(1)} %get-tuple-element.116), channel_id=1, source_target_pairs={{0,1},{1,0},{2,3},{3,2},{4,8},{5,9},{6,10},{7,11},{8,4},{9,5},{10,... | collective-permute-start | bytes 380936 | tf_op jit(solution)/shard_map/ppermute | solution.py:259
  62.8 9.3 %collective-permute-start.22 = (f32[248,128]{1,0:T(8,128)S(1)}, f32[248,128]{1,0:T(8,128)S(1)}, u32[]{:S(2)}, u32[]{:S(2)}) collective-permute-start(f32[248,128]{1,0:T(8,128)S(1)} %get-tuple-element.117), channel_id=1, source_target_pairs={{0,1},{1,0},{2,3},{3,2},{4,5},{5,4},{6,7},{7,6},{8,9},{9,8},{10,11... | collective-permute-start | bytes 380936 | tf_op jit(solution)/shard_map/ppermute | solution.py:259
  64.4 7.7 %collective-permute-start.23 = (f32[248,128]{1,0:T(8,128)S(1)}, f32[248,128]{1,0:T(8,128)S(1)}, u32[]{:S(2)}, u32[]{:S(2)}) collective-permute-start(f32[248,128]{1,0:T(8,128)S(1)} %get-tuple-element.118), channel_id=1, source_target_pairs={{0,4},{1,2},{2,1},{3,7},{4,0},{5,6},{6,5},{7,3},{8,12},{9,10},{10,... | collective-permute-start | bytes 380936 | tf_op jit(solution)/shard_map/ppermute | solution.py:259
  65.5 6.6 %collective-permute-start.24 = (f32[248,128]{1,0:T(8,128)S(1)}, f32[248,128]{1,0:T(8,128)S(1)}, u32[]{:S(2)}, u32[]{:S(2)}) collective-permute-start(f32[248,128]{1,0:T(8,128)S(1)} %get-tuple-element.119), channel_id=1, source_target_pairs={{0,16},{1,17},{2,18},{3,19},{4,20},{5,21},{6,22},{7,23},{8,24},{9,... | collective-permute-start | bytes 380936 | tf_op jit(solution)/shard_map/ppermute | solution.py:259
  66.5 4.6 %collective-permute-start.25 = (f32[32,128]{1,0:T(8,128)S(1)}, f32[32,128]{1,0:T(8,128)S(1)}, u32[]{:S(2)}, u32[]{:S(2)}) collective-permute-start(f32[32,128]{1,0:T(8,128)S(1)} %get-tuple-element.120), channel_id=1, source_target_pairs={{0,17},{1,16},{2,19},{3,18},{4,21},{5,20},{6,23},{7,22},{8,25},{9,... | collective-permute-start | bytes 49160 | tf_op jit(solution)/shard_map/ppermute | solution.py:259
  68.0 4.1 %collective-permute-start.26 = (f32[32,128]{1,0:T(8,128)S(1)}, f32[32,128]{1,0:T(8,128)S(1)}, u32[]{:S(2)}, u32[]{:S(2)}) collective-permute-start(f32[32,128]{1,0:T(8,128)S(1)} %get-tuple-element.121), channel_id=1, source_target_pairs={{0,4},{1,18},{2,17},{3,7},{4,0},{5,22},{6,21},{7,3},{8,12},{9,26},... | collective-permute-start | bytes 49160 | tf_op jit(solution)/shard_map/ppermute | solution.py:259
  72.5 1.2 collective-permute-start.27
  73.7 7.3 %collective-permute-start.28 = (f32[264,128]{1,0:T(8,128)S(1)}, f32[264,128]{1,0:T(8,128)S(1)}, u32[]{:S(2)}, u32[]{:S(2)}) collective-permute-start(f32[264,128]{1,0:T(8,128)S(1)} %get-tuple-element.125), channel_id=1, source_target_pairs={{0,4},{1,5},{2,6},{3,7},{4,0},{5,1},{6,2},{7,3},{8,12},{9,13},{10,... | collective-permute-start | bytes 405512 | tf_op jit(solution)/shard_map/ppermute | solution.py:259
  74.4 6.6 %collective-permute-start.29 = (f32[248,128]{1,0:T(8,128)S(1)}, f32[248,128]{1,0:T(8,128)S(1)}, u32[]{:S(2)}, u32[]{:S(2)}) collective-permute-start(f32[248,128]{1,0:T(8,128)S(1)} %get-tuple-element.126), channel_id=1, source_target_pairs={{0,1},{1,0},{2,3},{3,2},{4,8},{5,9},{6,10},{7,11},{8,4},{9,5},{10,... | collective-permute-start | bytes 380936 | tf_op jit(solution)/shard_map/ppermute | solution.py:259
  75.0 4.5 %collective-permute-start.30 = (f32[16,128]{1,0:T(8,128)S(1)}, f32[16,128]{1,0:T(8,128)S(1)}, u32[]{:S(2)}, u32[]{:S(2)}) collective-permute-start(f32[16,128]{1,0:T(8,128)S(1)} %get-tuple-element.127), channel_id=1, source_target_pairs={{0,8},{1,9},{2,10},{3,11},{4,12},{5,13},{6,14},{7,15},{8,0},{9,1},... | collective-permute-start | bytes 24584 | tf_op jit(solution)/shard_map/ppermute | solution.py:259
  76.6 4.4 %collective-permute-start.31 = (f32[16,128]{1,0:T(8,128)S(1)}, f32[16,128]{1,0:T(8,128)S(1)}, u32[]{:S(2)}, u32[]{:S(2)}) collective-permute-start(f32[16,128]{1,0:T(8,128)S(1)} %get-tuple-element.128), channel_id=1, source_target_pairs={{0,12},{1,13},{2,14},{3,15},{4,8},{5,9},{6,10},{7,11},{8,4},{9,5},... | collective-permute-start | bytes 24584 | tf_op jit(solution)/shard_map/ppermute | solution.py:259
  81.0 10.3 %collective-permute-start.33 = (f32[312,128]{1,0:T(8,128)S(1)}, f32[312,128]{1,0:T(8,128)S(1)}, u32[]{:S(2)}, u32[]{:S(2)}) collective-permute-start(f32[312,128]{1,0:T(8,128)S(1)} %get-tuple-element.130), channel_id=1, source_target_pairs={{0,3},{1,2},{2,1},{3,0},{4,7},{5,6},{6,5},{7,4},{8,11},{9,10},{10,... | collective-permute-start | bytes 479240 | tf_op jit(solution)/shard_map/ppermute | solution.py:259
  83.8 7.5 %collective-permute-start.34 = (f32[312,128]{1,0:T(8,128)S(1)}, f32[312,128]{1,0:T(8,128)S(1)}, u32[]{:S(2)}, u32[]{:S(2)}) collective-permute-start(f32[312,128]{1,0:T(8,128)S(1)} %get-tuple-element.131), channel_id=1, source_target_pairs={{0,16},{1,17},{2,18},{3,19},{4,20},{5,21},{6,22},{7,23},{8,24},{9,... | collective-permute-start | bytes 479240 | tf_op jit(solution)/shard_map/ppermute | solution.py:259
  84.9 6.4 %collective-permute-start.32 = (f32[248,128]{1,0:T(8,128)S(1)}, f32[248,128]{1,0:T(8,128)S(1)}, u32[]{:S(2)}, u32[]{:S(2)}) collective-permute-start(f32[248,128]{1,0:T(8,128)S(1)} %get-tuple-element.129), channel_id=1, source_target_pairs={{0,1},{1,0},{2,3},{3,2},{4,5},{5,4},{6,7},{7,6},{8,9},{9,8},{10,11... | collective-permute-start | bytes 380936 | tf_op jit(solution)/shard_map/ppermute | solution.py:259
  84.9 6.4 %collective-permute-start.36 = (f32[96,128]{1,0:T(8,128)S(1)}, f32[96,128]{1,0:T(8,128)S(1)}, u32[]{:S(2)}, u32[]{:S(2)}) collective-permute-start(f32[96,128]{1,0:T(8,128)S(1)} %get-tuple-element.133), channel_id=1, source_target_pairs={{0,19},{1,18},{2,17},{3,16},{4,23},{5,22},{6,21},{7,20},{8,27},{9,... | collective-permute-start | bytes 147464 | tf_op jit(solution)/shard_map/ppermute | solution.py:259
  86.1 5.0 %collective-permute-start.35 = (f32[32,128]{1,0:T(8,128)S(1)}, f32[32,128]{1,0:T(8,128)S(1)}, u32[]{:S(2)}, u32[]{:S(2)}) collective-permute-start(f32[32,128]{1,0:T(8,128)S(1)} %get-tuple-element.132), channel_id=1, source_target_pairs={{0,17},{1,16},{2,19},{3,18},{4,21},{5,20},{6,23},{7,22},{8,25},{9,... | collective-permute-start | bytes 49160 | tf_op jit(solution)/shard_map/ppermute | solution.py:259
  92.5 4.5 %collective-permute-start.37 = (f32[248,128]{1,0:T(8,128)S(1)}, f32[248,128]{1,0:T(8,128)S(1)}, u32[]{:S(2)}, u32[]{:S(2)}) collective-permute-start(f32[248,128]{1,0:T(8,128)S(1)} %get-tuple-element.139), channel_id=1, source_target_pairs={{0,4},{1,5},{2,6},{3,7},{4,0},{5,1},{6,2},{7,3},{8,12},{9,13},{10,... | collective-permute-start | bytes 380936 | tf_op jit(solution)/shard_map/ppermute | solution.py:259
  92.6 4.5 %collective-permute-start.38 = (f32[248,128]{1,0:T(8,128)S(1)}, f32[248,128]{1,0:T(8,128)S(1)}, u32[]{:S(2)}, u32[]{:S(2)}) collective-permute-start(f32[248,128]{1,0:T(8,128)S(1)} %get-tuple-element.140), channel_id=1, source_target_pairs={{0,1},{1,0},{2,3},{3,2},{4,8},{5,9},{6,10},{7,11},{8,4},{9,5},{10,... | collective-permute-start | bytes 380936 | tf_op jit(solution)/shard_map/ppermute | solution.py:259
  97.1 9.1 %collective-permute-start.39 = (f32[248,128]{1,0:T(8,128)S(1)}, f32[248,128]{1,0:T(8,128)S(1)}, u32[]{:S(2)}, u32[]{:S(2)}) collective-permute-start(f32[248,128]{1,0:T(8,128)S(1)} %get-tuple-element.141), channel_id=1, source_target_pairs={{0,1},{1,0},{2,3},{3,2},{4,5},{5,4},{6,7},{7,6},{8,9},{9,8},{10,11... | collective-permute-start | bytes 380936 | tf_op jit(solution)/shard_map/ppermute | solution.py:259
  98.6 7.7 %collective-permute-start.40 = (f32[248,128]{1,0:T(8,128)S(1)}, f32[248,128]{1,0:T(8,128)S(1)}, u32[]{:S(2)}, u32[]{:S(2)}) collective-permute-start(f32[248,128]{1,0:T(8,128)S(1)} %get-tuple-element.142), channel_id=1, source_target_pairs={{0,4},{1,2},{2,1},{3,7},{4,0},{5,6},{6,5},{7,3},{8,12},{9,10},{10,... | collective-permute-start | bytes 380936 | tf_op jit(solution)/shard_map/ppermute | solution.py:259
  99.2 7.1 %collective-permute-start.41 = (f32[248,128]{1,0:T(8,128)S(1)}, f32[248,128]{1,0:T(8,128)S(1)}, u32[]{:S(2)}, u32[]{:S(2)}) collective-permute-start(f32[248,128]{1,0:T(8,128)S(1)} %get-tuple-element.143), channel_id=1, source_target_pairs={{0,16},{1,17},{2,18},{3,19},{4,20},{5,21},{6,22},{7,23},{8,24},{9,... | collective-permute-start | bytes 380936 | tf_op jit(solution)/shard_map/ppermute | solution.py:259
  100.3 5.0 %collective-permute-start.42 = (f32[32,128]{1,0:T(8,128)S(1)}, f32[32,128]{1,0:T(8,128)S(1)}, u32[]{:S(2)}, u32[]{:S(2)}) collective-permute-start(f32[32,128]{1,0:T(8,128)S(1)} %get-tuple-element.144), channel_id=1, source_target_pairs={{0,17},{1,16},{2,19},{3,18},{4,21},{5,20},{6,23},{7,22},{8,25},{9,... | collective-permute-start | bytes 49160 | tf_op jit(solution)/shard_map/ppermute | solution.py:259
  102.1 4.1 %collective-permute-start.43 = (f32[32,128]{1,0:T(8,128)S(1)}, f32[32,128]{1,0:T(8,128)S(1)}, u32[]{:S(2)}, u32[]{:S(2)}) collective-permute-start(f32[32,128]{1,0:T(8,128)S(1)} %get-tuple-element.145), channel_id=1, source_target_pairs={{0,4},{1,18},{2,17},{3,7},{4,0},{5,22},{6,21},{7,3},{8,12},{9,26},... | collective-permute-start | bytes 49160 | tf_op jit(solution)/shard_map/ppermute | solution.py:259
  106.6 1.2 collective-permute-start.44
  107.8 7.0 %collective-permute-start.45 = (f32[264,128]{1,0:T(8,128)S(1)}, f32[264,128]{1,0:T(8,128)S(1)}, u32[]{:S(2)}, u32[]{:S(2)}) collective-permute-start(f32[264,128]{1,0:T(8,128)S(1)} %get-tuple-element.149), channel_id=1, source_target_pairs={{0,4},{1,5},{2,6},{3,7},{4,0},{5,1},{6,2},{7,3},{8,12},{9,13},{10,... | collective-permute-start | bytes 405512 | tf_op jit(solution)/shard_map/ppermute | solution.py:259
  108.5 6.3 %collective-permute-start.46 = (f32[248,128]{1,0:T(8,128)S(1)}, f32[248,128]{1,0:T(8,128)S(1)}, u32[]{:S(2)}, u32[]{:S(2)}) collective-permute-start(f32[248,128]{1,0:T(8,128)S(1)} %get-tuple-element.150), channel_id=1, source_target_pairs={{0,1},{1,0},{2,3},{3,2},{4,8},{5,9},{6,10},{7,11},{8,4},{9,5},{10,... | collective-permute-start | bytes 380936 | tf_op jit(solution)/shard_map/ppermute | solution.py:259
  109.0 4.3 %collective-permute-start.47 = (f32[16,128]{1,0:T(8,128)S(1)}, f32[16,128]{1,0:T(8,128)S(1)}, u32[]{:S(2)}, u32[]{:S(2)}) collective-permute-start(f32[16,128]{1,0:T(8,128)S(1)} %get-tuple-element.151), channel_id=1, source_target_pairs={{0,8},{1,9},{2,10},{3,11},{4,12},{5,13},{6,14},{7,15},{8,0},{9,1},... | collective-permute-start | bytes 24584 | tf_op jit(solution)/shard_map/ppermute | solution.py:259
  110.5 4.3 %collective-permute-start.48 = (f32[16,128]{1,0:T(8,128)S(1)}, f32[16,128]{1,0:T(8,128)S(1)}, u32[]{:S(2)}, u32[]{:S(2)}) collective-permute-start(f32[16,128]{1,0:T(8,128)S(1)} %get-tuple-element.152), channel_id=1, source_target_pairs={{0,12},{1,13},{2,14},{3,15},{4,8},{5,9},{6,10},{7,11},{8,4},{9,5},... | collective-permute-start | bytes 24584 | tf_op jit(solution)/shard_map/ppermute | solution.py:259
  114.9 10.3 %collective-permute-start.50 = (f32[312,128]{1,0:T(8,128)S(1)}, f32[312,128]{1,0:T(8,128)S(1)}, u32[]{:S(2)}, u32[]{:S(2)}) collective-permute-start(f32[312,128]{1,0:T(8,128)S(1)} %get-tuple-element.154), channel_id=1, source_target_pairs={{0,3},{1,2},{2,1},{3,0},{4,7},{5,6},{6,5},{7,4},{8,11},{9,10},{10,... | collective-permute-start | bytes 479240 | tf_op jit(solution)/shard_map/ppermute | solution.py:259
  117.7 7.6 %collective-permute-start.51 = (f32[312,128]{1,0:T(8,128)S(1)}, f32[312,128]{1,0:T(8,128)S(1)}, u32[]{:S(2)}, u32[]{:S(2)}) collective-permute-start(f32[312,128]{1,0:T(8,128)S(1)} %get-tuple-element.155), channel_id=1, source_target_pairs={{0,16},{1,17},{2,18},{3,19},{4,20},{5,21},{6,22},{7,23},{8,24},{9,... | collective-permute-start | bytes 479240 | tf_op jit(solution)/shard_map/ppermute | solution.py:259
  118.7 6.6 %collective-permute-start.49 = (f32[248,128]{1,0:T(8,128)S(1)}, f32[248,128]{1,0:T(8,128)S(1)}, u32[]{:S(2)}, u32[]{:S(2)}) collective-permute-start(f32[248,128]{1,0:T(8,128)S(1)} %get-tuple-element.153), channel_id=1, source_target_pairs={{0,1},{1,0},{2,3},{3,2},{4,5},{5,4},{6,7},{7,6},{8,9},{9,8},{10,11... | collective-permute-start | bytes 380936 | tf_op jit(solution)/shard_map/ppermute | solution.py:259
  118.7 6.5 %collective-permute-start.53 = (f32[96,128]{1,0:T(8,128)S(1)}, f32[96,128]{1,0:T(8,128)S(1)}, u32[]{:S(2)}, u32[]{:S(2)}) collective-permute-start(f32[96,128]{1,0:T(8,128)S(1)} %get-tuple-element.157), channel_id=1, source_target_pairs={{0,19},{1,18},{2,17},{3,16},{4,23},{5,22},{6,21},{7,20},{8,27},{9,... | collective-permute-start | bytes 147464 | tf_op jit(solution)/shard_map/ppermute | solution.py:259
  120.3 4.9 %collective-permute-start.52 = (f32[32,128]{1,0:T(8,128)S(1)}, f32[32,128]{1,0:T(8,128)S(1)}, u32[]{:S(2)}, u32[]{:S(2)}) collective-permute-start(f32[32,128]{1,0:T(8,128)S(1)} %get-tuple-element.156), channel_id=1, source_target_pairs={{0,17},{1,16},{2,19},{3,18},{4,21},{5,20},{6,23},{7,22},{8,25},{9,... | collective-permute-start | bytes 49160 | tf_op jit(solution)/shard_map/ppermute | solution.py:259
  126.4 4.4 %collective-permute-start.54 = (f32[248,128]{1,0:T(8,128)S(1)}, f32[248,128]{1,0:T(8,128)S(1)}, u32[]{:S(2)}, u32[]{:S(2)}) collective-permute-start(f32[248,128]{1,0:T(8,128)S(1)} %get-tuple-element.164), channel_id=1, source_target_pairs={{0,4},{1,5},{2,6},{3,7},{4,0},{5,1},{6,2},{7,3},{8,12},{9,13},{10,... | collective-permute-start | bytes 380936 | tf_op jit(solution)/shard_map/ppermute | solution.py:259
  126.5 4.4 %collective-permute-start.55 = (f32[248,128]{1,0:T(8,128)S(1)}, f32[248,128]{1,0:T(8,128)S(1)}, u32[]{:S(2)}, u32[]{:S(2)}) collective-permute-start(f32[248,128]{1,0:T(8,128)S(1)} %get-tuple-element.165), channel_id=1, source_target_pairs={{0,1},{1,0},{2,3},{3,2},{4,8},{5,9},{6,10},{7,11},{8,4},{9,5},{10,... | collective-permute-start | bytes 380936 | tf_op jit(solution)/shard_map/ppermute | solution.py:259
  130.9 9.1 %collective-permute-start.56 = (f32[248,128]{1,0:T(8,128)S(1)}, f32[248,128]{1,0:T(8,128)S(1)}, u32[]{:S(2)}, u32[]{:S(2)}) collective-permute-start(f32[248,128]{1,0:T(8,128)S(1)} %get-tuple-element.166), channel_id=1, source_target_pairs={{0,1},{1,0},{2,3},{3,2},{4,5},{5,4},{6,7},{7,6},{8,9},{9,8},{10,11... | collective-permute-start | bytes 380936 | tf_op jit(solution)/shard_map/ppermute | solution.py:259
  132.4 7.5 %collective-permute-start.57 = (f32[248,128]{1,0:T(8,128)S(1)}, f32[248,128]{1,0:T(8,128)S(1)}, u32[]{:S(2)}, u32[]{:S(2)}) collective-permute-start(f32[248,128]{1,0:T(8,128)S(1)} %get-tuple-element.167), channel_id=1, source_target_pairs={{0,4},{1,2},{2,1},{3,7},{4,0},{5,6},{6,5},{7,3},{8,12},{9,10},{10,... | collective-permute-start | bytes 380936 | tf_op jit(solution)/shard_map/ppermute | solution.py:259
  133.1 6.9 %collective-permute-start.58 = (f32[248,128]{1,0:T(8,128)S(1)}, f32[248,128]{1,0:T(8,128)S(1)}, u32[]{:S(2)}, u32[]{:S(2)}) collective-permute-start(f32[248,128]{1,0:T(8,128)S(1)} %get-tuple-element.168), channel_id=1, source_target_pairs={{0,16},{1,17},{2,18},{3,19},{4,20},{5,21},{6,22},{7,23},{8,24},{9,... | collective-permute-start | bytes 380936 | tf_op jit(solution)/shard_map/ppermute | solution.py:259
  134.1 5.8 %collective-permute-start.59 = (f32[32,128]{1,0:T(8,128)S(1)}, f32[32,128]{1,0:T(8,128)S(1)}, u32[]{:S(2)}, u32[]{:S(2)}) collective-permute-start(f32[32,128]{1,0:T(8,128)S(1)} %get-tuple-element.169), channel_id=1, source_target_pairs={{0,17},{1,16},{2,19},{3,18},{4,21},{5,20},{6,23},{7,22},{8,25},{9,... | collective-permute-start | bytes 49160 | tf_op jit(solution)/shard_map/ppermute | solution.py:259
  135.9 4.1 %collective-permute-start.60 = (f32[32,128]{1,0:T(8,128)S(1)}, f32[32,128]{1,0:T(8,128)S(1)}, u32[]{:S(2)}, u32[]{:S(2)}) collective-permute-start(f32[32,128]{1,0:T(8,128)S(1)} %get-tuple-element.170), channel_id=1, source_target_pairs={{0,4},{1,18},{2,17},{3,7},{4,0},{5,22},{6,21},{7,3},{8,12},{9,26},... | collective-permute-start | bytes 49160 | tf_op jit(solution)/shard_map/ppermute | solution.py:259
  (4 other events, 9.9 us)

commit v3 on v2

--- a/solution.py
+++ b/solution.py
@@ -97,13 +97,13 @@
         return out
 
 
-def stage_messages(stage, sizes, coarse):
+def stage_messages(stage, sizes, coarse=None):
     choices = []
     for d in range(3):
         if d not in STAGES[stage]:
             choices.append((None,))
         else:
-            extra = ("C", "W") if coarse and stage == 0 and sizes[d] == 4 else ()
+            extra = ("C", "W") if coarse == "update" and stage == 0 and sizes[d] == 4 else ()
             choices.append((None, "A") + (("B",) if sizes[d] > 2 else ()) + extra)
     out = []
     for moves in itertools.product(*choices):
@@ -120,14 +120,17 @@
         self.subs = sizes[0] * sizes[1] * sizes[2]
         self.ride = all(s in (2, 4) for s in sizes)
         self.wide = self.subs * 8
-        self.plain = [stage_messages(i, sizes, False) for i in range(2)]
-        self.coarse = self.plain
+        self.plain = [stage_messages(i, sizes) for i in range(2)]
         self.setup = 0
         if self.ride:
-            self.local = Message((None, None, "A"), sizes, False, True, 0)
-            self.coarse = [stage_messages(i, sizes, True) for i in range(2)]
             self.setup = self.wide // 128
-            first, second = self.coarse
+            self.coarse = {k: [stage_messages(i, sizes, k) for i in range(2)] for k in ("initial", "update")}
+            self.before = {"update": [Message((None, None, "A"), sizes, False, True, 0)]}
+            self.before["initial"] = list(self.before["update"])
+            if sizes[1] == 4:
+                more = [(None, "C", None), (None, "C", "A")]
+                self.before["initial"] += [Message(m, sizes, False, True, 0) for m in more]
+            first, second = self.coarse["initial"]
             for message in first:
                 message.basis = [(None, slot) for slot in message.slots]
             for message in second:
@@ -139,12 +142,12 @@
         return {"plain": 0, "update": 1, "initial": self.setup}[kind] if self.ride else 0
 
     def messages(self, kind):
-        return self.plain if self.per(kind) == 0 else self.coarse
-
-    def codes(self, stage):
-        known = [0, self.local.xor()]
+        return self.plain if self.per(kind) == 0 else self.coarse[kind]
+
+    def codes(self, kind, stage):
+        known = [0] + [m.xor() for m in self.before[kind]]
         if stage == 1:
-            known = [k ^ m for m in [0] + [m.xor() for m in self.coarse[0] if m.ride] for k in known]
+            known = [k ^ m for m in [0] + [m.xor() for m in self.coarse[kind][0] if m.ride] for k in known]
         return known
 
     def payload_shapes(self, kind, stage):
@@ -153,7 +156,7 @@
         for m in self.messages(kind)[stage]:
             rows = m.rows
             if m.ride:
-                rows += 8 * per * len(self.codes(stage))
+                rows += 8 * per * len(self.codes(kind, stage))
             if kind == "initial" and self.ride and m.faces:
                 rows += CHUNK
             out.append(shape(rows, 128))
@@ -345,11 +348,10 @@
     lax.fori_loop(0, ROWS // TILE, step, 0)
 
 
-def select_kernel(plan, canon, basis, cinv, one, one_w, turned, *rest):
-    src, wgt = rest[-2:]
+def select_kernel(plan, canon, one, weight_out, src):
     index = position()
     src[...] = jnp.full(src.shape, -1, jnp.int32)
-    wgt[...] = jnp.zeros(wgt.shape, F32)
+    weight_out[...] = jnp.zeros(weight_out.shape, F32)
     for slot in PLACES:
         at, length = SLOT_OFFSET[slot], LENGTH[slot]
         src[at : at + length, :] = pick(
@@ -361,45 +363,46 @@
                 weight = weight * 0.5
             elif slot[d] == 2 and plan.sizes[d] > 2:
                 weight = weight * jnp.where(has_b(index[d], plan.sizes[d]), 0.5, 1.0)
-        wgt[at : at + length, :] = jnp.full((length, 1), 1.0, F32) * weight
-    if plan.ride:
-        spread_out = rest[0]
-        nc = cinv.shape[1]
-        row = lax.broadcasted_iota(jnp.int32, (nc, plan.wide), 0)
-        col = lax.broadcasted_iota(jnp.int32, (nc, plan.wide), 1)
-        spread = jnp.where(jnp.logical_and((col >> 3) * 6 + (col & 7) == row, (col & 7) < 6), 1.0, 0.0).astype(BF16)
-        value = sum(dot(part, spread) for part in split(cinv[...], 3))
-        spread_out[...] = jnp.zeros(spread_out.shape, F32)
-        for i in range(plan.setup):
-            spread_out[8 * i : 8 * i + 6, :] = value[:, 128 * i : 128 * (i + 1)]
-    turned[...] = jnp.zeros(turned.shape, F32)
+        weight_out[at : at + length, :] = jnp.full((length, 128), 1.0, F32) * weight
 
     def build(rows):
         hit = src[rows, :] == lax.broadcasted_iota(jnp.int32, (TILE, IFACE), 1)
         one[rows, :] = jnp.where(hit, 1.0, 0.0).astype(BF16)
-        weighted = jnp.where(hit, wgt[rows, :], 0.0).astype(BF16)
-        one_w[rows, :] = weighted
-        turned[rows, :6] = dot_last(weighted, basis[...])
 
     each_tile(build)
 
 
-def left_kernel(one, matrix, mid):
-    def body(rows):
-        mid[rows, :] = dot(one[rows, :], matrix[...]).astype(BF16)
-
-    each_tile(body)
-
-
-def right_kernel(one, mid, basis, out, few):
-    def body(rows):
-        out[rows, :] = dot_last(mid[rows, :], one[...]).astype(BF16)
-
-    each_tile(body)
+def spread_kernel(plan, cinv, out):
+    nc = cinv.shape[1]
+    row = lax.broadcasted_iota(jnp.int32, (nc, plan.wide), 0)
+    col = lax.broadcasted_iota(jnp.int32, (nc, plan.wide), 1)
+    spread = jnp.where(jnp.logical_and((col >> 3) * 6 + (col & 7) == row, (col & 7) < 6), 1.0, 0.0).astype(BF16)
+    value = sum(dot(part, spread) for part in split(cinv[...], 3))
+    out[...] = jnp.zeros(out.shape, F32)
+    for i in range(plan.setup):
+        out[8 * i : 8 * i + 6, :] = value[:, 128 * i : 128 * (i + 1)]
+
+
+def turn_kernel(one, weight, basis, turned):
+    turned[...] = jnp.zeros(turned.shape, F32)
+    turned[:, :6] = dot_last(one[...], basis[...]) * weight[:, :6]
+
+
+def left_kernel(one, matrix, weight, basis, mid, few):
+    for t in range(0, ROWS, TILE):
+        value = dot(one[t : t + TILE, :], matrix[...])
+        if weight is not None:
+            value = value * weight[t : t + TILE, :1]
+        mid[t : t + TILE, :] = value.astype(BF16)
     if basis is not None:
         few[...] = jnp.zeros(few.shape, F32)
-        few[:6, :] = dot_last(basis[...], one[...])
-        out[COARSE_AT : COARSE_AT + 16, :] = few[...].astype(BF16)
+        few[:6, :] = basis[...].astype(F32)
+        mid[COARSE_AT : COARSE_AT + 16, :] = few[...].astype(BF16)
+
+
+def right_kernel(one, mid, out):
+    for t in range(0, ROWS, TILE):
+        out[t : t + TILE, :] = dot_last(mid[t : t + TILE, :], one[...]).astype(BF16)
 
 
 def fill(acc, parts):
@@ -409,27 +412,26 @@
         at += part.shape[0]
 
 
-def known_blocks(plan, own, received, messages, per):
-    blocks = own + [received[0][8 * i : 8 * (i + 1), :] for i in range(per)]
-    for message, ref in zip(messages, received[1:]):
+def known_blocks(plan, kind, own, swapped, arrived, per):
+    blocks = own + [ref[8 * i : 8 * (i + 1), :] for ref in swapped for i in range(per)]
+    count = len(blocks)
+    for message, ref in zip(plan.coarse[kind][0], arrived):
         if message.ride:
-            blocks += [ref[message.rows + 8 * i : message.rows + 8 * (i + 1), :] for i in range(2 * per)]
+            blocks += [ref[message.rows + 8 * i : message.rows + 8 * (i + 1), :] for i in range(count)]
     return blocks
 
 
 def first_kernel(plan, kind, *refs):
     refs = list(refs)
-    base, own, local = refs[:3]
-    refs = refs[3:]
+    base, own = refs.pop(0), refs.pop(0)
+    swapped = [refs.pop(0) for _ in plan.before[kind]]
     per = plan.per(kind)
     pack = None
     if kind == "initial":
         turned = refs.pop(0)
         pack = packer(turned, refs.pop(-1), {})
-        mine = [own[8 * i : 8 * (i + 1), :] for i in range(per)]
-    else:
-        mine = [own[...]]
-    write_payloads(plan.coarse[0], refs, base, known_blocks(plan, mine, [local], [], per), pack)
+    mine = [own[8 * i : 8 * (i + 1), :] for i in range(per)]
+    write_payloads(plan.coarse[kind][0], refs, base, known_blocks(plan, kind, mine, swapped, [], per), pack)
 
 
 def middle_kernel(plan, kind, count, *refs):
@@ -440,9 +442,10 @@
     received = [refs.pop(0) for _ in first]
     blocks, pack = [], None
     if per:
-        own, local = refs.pop(0), refs.pop(0)
+        own = refs.pop(0)
+        swapped = [refs.pop(0) for _ in plan.before[kind]]
         mine = [own[8 * i : 8 * (i + 1), :] for i in range(per)]
-        blocks = known_blocks(plan, mine, [local] + received, first, per)
+        blocks = known_blocks(plan, kind, mine, swapped, received, per)
     if per and kind == "initial":
         turned = refs.pop(0)
         stage = refs.pop(-1)
@@ -477,13 +480,13 @@
     refs = list(refs)
     parts = [refs.pop(0) for _ in range(count)]
     got = [refs.pop(0) for _ in range(sum(len(m) for m in plan.messages(kind)))]
-    matrix = refs.pop(0)
+    matrix, weight = refs.pop(0), refs.pop(0)
     before = None if opening else refs.pop(0)
     residual, rounded, restricted, acc = refs
     finish(plan, kind, parts, got, acc)
     value = acc[...] if opening else before[...] - acc[...]
     residual[...] = value
-    rounded[...] = value.astype(BF16)
+    rounded[...] = (weight[...] * value).astype(BF16)
     restricted[...] = dot(matrix[COARSE_AT : COARSE_AT + 16, :], rounded[...])[:8]
 
 
@@ -493,29 +496,31 @@
     write_payloads(plan.plain[0], outs, out, [])
 
 
-def collect(plan, own, got, per, which, stack, at_column):
-    first, second = plan.coarse
+def collect(plan, kind, own, got, per, which, stack, at_column):
+    first, second = plan.coarse[kind]
     index = position()
     me = (index[0] * plan.sizes[1] + index[1]) * plan.sizes[2] + index[2]
 
     def put(code, value):
         stack[pl.ds(pl.multiple_of((me ^ code) * 8, 8), 8), at_column : at_column + 128] = value
 
-    local, got = got[0], got[1:]
     put(0, own[8 * which : 8 * (which + 1), :])
-    put(plan.local.xor(), local[8 * which : 8 * (which + 1), :])
+    for m in plan.before[kind]:
+        put(m.xor(), got[0][8 * which : 8 * (which + 1), :])
+        got = got[1:]
     for stage, messages in enumerate((first, second)):
         for m, ref in zip(messages, got):
             if m.ride:
-                for i, code in enumerate(plan.codes(stage)):
+                for i, code in enumerate(plan.codes(kind, stage)):
                     at = m.rows + 8 * (per * i + which)
                     put(code ^ m.xor(), ref[at : at + 8, :])
         got = got[len(messages) :]
 
 
 def lifting_kernel(plan, *refs):
-    first, second = plan.coarse
-    turned, spread, local, *got, out, stack, many, unpacked = refs
+    first, second = plan.coarse["initial"]
+    turned, spread, *got, out, stack, many, unpacked = refs
+    swapped, got = got[: len(plan.before["initial"])], got[len(plan.before["initial"]) :]
     per = plan.setup
     index = position()
     me = (index[0] * plan.sizes[1] + index[1]) * plan.sizes[2] + index[2]
@@ -544,7 +549,7 @@
             place(code, unpacked[at : at + LENGTH[slot], :], SLOT_OFFSET[slot], fine)
             at += LENGTH[slot]
     for half in range(per):
-        collect(plan, spread, [local] + got, per, half, stack, 128 * half)
+        collect(plan, "initial", spread, swapped + got, per, half, stack, 128 * half)
     parts = jnp.concatenate(split(stack[...], 3), axis=0)
 
     def body(rows):
@@ -562,13 +567,14 @@
     got = [refs.pop(0) for _ in range(sum(len(m) for m in plan.messages("update")))]
     matrix = refs.pop(0)
     if plan.ride:
-        lift, own, local = refs.pop(0), refs.pop(0), refs.pop(0)
+        lift, own = refs.pop(0), refs.pop(0)
+        swapped = [refs.pop(0) for _ in plan.before["update"]]
         stack = refs.pop(-1)
     acc = refs.pop(-1)
     update, rounded, early, *outs = refs
     finish(plan, "update", [base], got, acc)
     if plan.ride:
-        collect(plan, own, [local] + got, 1, 0, stack, 0)
+        collect(plan, "update", own, swapped + got, 1, 0, stack, 0)
         high, low = split(stack[...], 2)
         right = jnp.concatenate([high, low, high], axis=0)
         for t in range(0, ROWS, 320):
@@ -605,15 +611,18 @@
     pieces = pltpu.VMEM((16 * CHUNK, 128), F32)
     early_rows, late_rows = SPLIT, ROWS - SPLIT
 
-    def first(kind, base, own, swapped, more):
+    def spread_out(kind, own):
+        return [own] + transfer(plan.before[kind], [own] * len(plan.before[kind]))
+
+    def first(kind, base, blocks, more):
         return call(
             functools.partial(first_kernel, plan, kind),
             plan.payload_shapes(kind, 0),
-            [base, own, swapped] + more,
+            [base] + blocks + more,
             scratch=[pieces] if kind == "initial" else [],
         )
 
-    def assemble(kind, parts, payloads, blocks, more, late=None):
+    def assemble(kind, parts, payloads, blocks, more):
         messages = plan.messages(kind)
         got = transfer(messages[0], payloads)
         setup = kind == "initial" and plan.ride
@@ -625,14 +634,18 @@
         )
         return got + transfer(messages[1], payloads)
 
-    one, one_w, turned, *spread = call(
+    one, weight = call(
         functools.partial(select_kernel, plan),
-        [shape(ROWS, IFACE, BF16), shape(ROWS, IFACE, BF16), shape(ROWS, 128)]
-        + ([shape(8 * plan.setup, 128)] if plan.ride else []),
-        [canon_rows.reshape(IFACE, 1), basis, coarse_inverse],
-        scratch=[pltpu.VMEM((ROWS, 1), jnp.int32), pltpu.VMEM((ROWS, 1), F32)],
+        [shape(ROWS, IFACE, BF16), shape(ROWS, 128)],
+        [canon_rows.reshape(IFACE, 1)],
+        scratch=[pltpu.VMEM((ROWS, 1), jnp.int32)],
         flops=ROWS * IFACE * 1158,
     )
+    if plan.ride:
+        (spread,) = call(
+            functools.partial(spread_kernel, plan), [shape(8 * plan.setup, 128)], [coarse_inverse]
+        )
+    (turned,) = call(turn_kernel, [shape(ROWS, 128)], [one, weight, basis])
     (early,) = call(
         functools.partial(gather_kernel, EARLY, 0), [shape(early_rows, 128)], [canon, load], specs=[smem, vm()]
     )
@@ -642,17 +655,21 @@
     flops = 2 * ROWS * IFACE * IFACE
     middle_shape, square = shape(ROWS, IFACE, BF16), shape(ROWS, ROWS, BF16)
 
-    def right_plain(a, b, out):
-        right_kernel(a, b, None, out, None)
-
-    (half,) = call(left_kernel, [middle_shape], [one_w, local_inverse[0, 0, 0]], flops=flops)
-    (inverse,) = call(
-        right_kernel, [square], [one_w, half, basis], scratch=[pltpu.VMEM((16, ROWS), F32)], flops=flops
+    def left_plain(one, matrix, mid):
+        left_kernel(one, matrix, None, None, mid, None)
+
+    (half,) = call(
+        left_kernel,
+        [middle_shape],
+        [one, local_inverse[0, 0, 0], weight, basis],
+        scratch=[pltpu.VMEM((16, IFACE), F32)],
+        flops=flops,
     )
+    (inverse,) = call(right_kernel, [square], [one, half], flops=flops)
     blocks = []
     if plan.ride:
-        blocks = spread + transfer([plan.local], spread)
-        payloads = first("initial", early, *blocks, [turned])
+        blocks = spread_out("initial", spread)
+        payloads = first("initial", early, blocks, [turned])
     else:
         payloads = call(
             lambda base, *outs: write_payloads(plan.plain[0], outs, base, []),
@@ -669,8 +686,8 @@
             scratch=[pltpu.VMEM((plan.wide, plan.wide), F32), pltpu.VMEM((ROWS, plan.wide), F32), pieces],
             flops=2 * ROWS * 3 * plan.wide * plan.wide,
         )
-    (half,) = call(left_kernel, [middle_shape], [one, schur_matrix[0, 0, 0]], flops=flops)
-    (schur,) = call(right_plain, [square], [one, half], flops=flops)
+    (half,) = call(left_plain, [middle_shape], [one, schur_matrix[0, 0, 0]], flops=flops)
+    (schur,) = call(right_kernel, [square], [one, half], flops=flops)
     sol = residual = None
     flops = 2 * ROWS * ROWS * 128
     for iteration in range(ITERS):
@@ -678,15 +695,16 @@
         residual, rounded, restricted = call(
             functools.partial(residual_kernel, plan, opening, len(parts)),
             [shape(ROWS, 128), shape(ROWS, 128, BF16), shape(8, 128)],
-            parts + got + [inverse] + ([] if opening else [residual]),
+            parts + got + [inverse, weight] + ([] if opening else [residual]),
             scratch=[acc],
         )
+        if plan.ride:
+            blocks = spread_out("update", restricted)
         (base,) = call(
             functools.partial(product_kernel, "all"), [shape(ROWS, 128)], [inverse, rounded], flops=flops
         )
         if plan.ride:
-            blocks = [restricted] + transfer([plan.local], [restricted])
-            payloads = first("update", base, *blocks, [])
+            payloads = first("update", base, blocks, [])
         else:
             blocks = []
             rows = lax.all_gather(restricted[:6], AXES, axis=0, tiled=True)

time: 143 us -> 139 us (0.972)
  Pallas kernels: 45.7 us -> 41.7 us
  waiting for transfers between devices: 27.5 us -> 29.2 us
    pallas_call x33 -> x35, Pallas kernels: 45.7 us -> 41.7 us  [call(): pl.pallas_call(kernel, out_shape=tuple(outs), in_specs=specs or [vm()] *...]
    ppermute x61, waiting for transfers between devices: 27.5 us -> 29.2 us  [transfer(): lax.ppermute(p, AXES, m.pairs())]
  transfers between devices with their start and end apart: 61 -> 61, of which waited for: 19 -> 17; matrix products, arithmetic and copies ran while one was open for 0% -> 1% of each run, Pallas kernels for 24% -> 24%
where the time goes in v3:
time: 139 us
  starting transfers between devices  65.4 us (47%)
  Pallas kernels  41.7 us (30%)
  waiting for transfers between devices  29.2 us (21%)
  local copies, waits for them, and re-layouts  1.65 us (1%)
    ppermute x61, starting transfers between devices, transfer(): lax.ppermute(p, AXES, m.pairs())  65.4 us
    pallas_call x35, Pallas kernels, call(): pl.pallas_call(kernel, out_shape=tuple(outs), in_specs=specs or [vm()] *...  41.7 us
    ppermute x61, waiting for transfers between devices, transfer(): lax.ppermute(p, AXES, m.pairs())  29.2 us
  transfers between devices with their start and end apart: 61, of which 17 were waited for; matrix products, arithmetic and copies ran while one was open for 1% of the time, Pallas kernels for 24%

profile of v3, /device:TPU:1, one launch (start us, length us, event | category | flops | bytes accessed | tf_op | source)
XLA Modules:
  0.0 139.1 jit_solution(14648296212108177317)
XLA Ops:
  1.6 3.8 %collective-permute-start.1 = (f32[16,128]{1,0:T(8,128)S(1)}, f32[16,128]{1,0:T(8,128)S(1)}, u32[]{:S(2)}, u32[]{:S(2)}) collective-permute-start(f32[16,128]{1,0:T(8,128)S(1)} %shard_map.84.refs_1_.refs_4_), channel_id=1, source_target_pairs={{0,8},{1,9},{2,10},{3,11},{4,12},{5,13},{6,14},{7,15},{8,0},{9,1},... | collective-permute-start | bytes 24584 | tf_op jit(solution)/shard_map/ppermute | solution.py:262
  6.3 1.0 shard_map.77
  7.4 1.2 shard_map.82.refs_0_
  8.6 1.0 shard_map.85.refs_5_.refs_8_.refs_0_
  9.8 1.6 %collective-permute-start.3 = (f32[336,128]{1,0:T(8,128)S(1)}, f32[336,128]{1,0:T(8,128)S(1)}, u32[]{:S(2)}, u32[]{:S(2)}) collective-permute-start(f32[336,128]{1,0:T(8,128)S(1)} %get-tuple-element.85), channel_id=1, source_target_pairs={{0,4},{1,5},{2,6},{3,7},{4,0},{5,1},{6,2},{7,3},{8,12},{9,13},{10,... | collective-permute-start | bytes 516104 | tf_op jit(solution)/shard_map/ppermute | solution.py:262
  11.9 4.4 %shard_map.80.mid = bf16[1280,1158]{1,0:T(8,128)(2,1)S(1)} custom-call(bf16[1280,1158]{1,0:T(8,128)(2,1)S(1)} %get-tuple-element.83.one, bf16[1158,1158]{1,0:T(8,128)(2,1)S(1)} %bitcast.21, f32[1280,128]{1,0:T(8,128)S(1)} %get-tuple-element.84.weight.refs_10_, bf16[6,1158]{1,0:T(8,128)(2,1)S(1)} %bitcast.20), custom_call_target="tpu_custom_call" | custom-call | flops 3432867840 | bytes 9280144 | tf_op jit(solution)/shard_map/pallas_call | solution.py:275
  16.4 1.6 %shard_map.83.refs_1_ = f32[704,128]{1,0:T(8,128)S(1)} custom-call(s32[1,1158]{1,0:T(1,128)S(1)} %bitcast.16, f32[1158,1,128]{2,1,0:T(1,128)S(1)} %bitcast.13), custom_call_target="tpu_custom_call" | custom-call | bytes 957976 | tf_op jit(solution)/shard_map/pallas_call | solution.py:275
  18.5 1.6 %collective-permute-start.6 = (f32[400,128]{1,0:T(8,128)S(1)}, f32[400,128]{1,0:T(8,128)S(1)}, u32[]{:S(2)}, u32[]{:S(2)}) collective-permute-start(f32[400,128]{1,0:T(8,128)S(1)} %get-tuple-element.88), channel_id=1, source_target_pairs={{0,3},{1,2},{2,1},{3,0},{4,7},{5,6},{6,5},{7,4},{8,11},{9,10},{10,... | collective-permute-start | bytes 614408 | tf_op jit(solution)/shard_map/ppermute | solution.py:262
  20.1 1.2 collective-permute-start.7
  21.8 1.2 collective-permute-start.9
  23.0 4.4 %shard_map.81.refs_9_.matrix = bf16[1280,1280]{1,0:T(8,128)(2,1)S(1)} custom-call(bf16[1280,1158]{1,0:T(8,128)(2,1)S(1)} %get-tuple-element.83.one, bf16[1280,1158]{1,0:T(8,128)(2,1)S(1)} %shard_map.80.mid), custom_call_target="tpu_custom_call" | custom-call | flops 3432867840 | bytes 9205760 | tf_op jit(solution)/shard_map/pallas_call | solution.py:275
  28.3 1.2 collective-permute-done.9.refs_8_.refs_11_
  30.1 1.0 shard_map.89.refs_0_
  31.2 2.4 %collective-permute-start.11 = (f32[264,128]{1,0:T(8,128)S(1)}, f32[264,128]{1,0:T(8,128)S(1)}, u32[]{:S(2)}, u32[]{:S(2)}) collective-permute-start(f32[264,128]{1,0:T(8,128)S(1)} %get-tuple-element.94), channel_id=1, source_target_pairs={{0,4},{1,5},{2,6},{3,7},{4,0},{5,1},{6,2},{7,3},{8,12},{9,13},{10,... | collective-permute-start | bytes 405512 | tf_op jit(solution)/shard_map/ppermute | solution.py:262
  34.8 1.3 collective-permute-start.14
  36.1 4.4 %shard_map.78.mid = bf16[1280,1158]{1,0:T(8,128)(2,1)S(1)} custom-call(bf16[1280,1158]{1,0:T(8,128)(2,1)S(1)} %get-tuple-element.83.one, bf16[1158,1158]{1,0:T(8,128)(2,1)S(1)} %bitcast.22), custom_call_target="tpu_custom_call" | custom-call | flops 3432867840 | bytes 8610888 | tf_op jit(solution)/shard_map/pallas_call | solution.py:275
  40.7 1.5 %collective-permute-start.15 = (f32[248,128]{1,0:T(8,128)S(1)}, f32[248,128]{1,0:T(8,128)S(1)}, u32[]{:S(2)}, u32[]{:S(2)}) collective-permute-start(f32[248,128]{1,0:T(8,128)S(1)} %get-tuple-element.98), channel_id=1, source_target_pairs={{0,1},{1,0},{2,3},{3,2},{4,5},{5,4},{6,7},{7,6},{8,9},{9,8},{10,11... | collective-permute-start | bytes 380936 | tf_op jit(solution)/shard_map/ppermute | solution.py:262
  42.1 1.2 collective-permute-start.16
  43.3 1.2 collective-permute-start.17
  45.4 4.7 %shard_map.79.refs_10_.matrix = bf16[1280,1280]{1,0:T(8,128)(2,1)S(1)} custom-call(bf16[1280,1158]{1,0:T(8,128)(2,1)S(1)} %get-tuple-element.83.one, bf16[1280,1158]{1,0:T(8,128)(2,1)S(1)} %shard_map.78.mid), custom_call_target="tpu_custom_call" | custom-call | flops 3432867840 | bytes 9205760 | tf_op jit(solution)/shard_map/pallas_call | solution.py:275
  51.0 2.3 %shard_map.92.refs_11_ = bf16[1280,768]{1,0:T(8,128)(2,1)S(1)} custom-call(f32[1280,128]{1,0:T(8,128)S(1)} %shard_map.85.refs_5_.refs_8_.refs_0_, f32[16,128]{1,0:T(8,128)S(1)} %shard_map.84.refs_1_.refs_4_, f32[16,128]{1,0:T(8,128)S(1)} %collective-permute-done.refs_2_.refs_5_, f32[16,128]{1,0:T(8,128)S(1)} %collective-permute-done.1.refs_3_.refs_6_, ...), custom_call_target="tpu_custom_call" | custom-call | flops 503316480 | bytes 3637248 | tf_op jit(solution)/shard_map/pallas_call | solution.py:275
  53.3 1.2 shard_map.93
  54.6 0.9 collective-permute-start.21
  56.2 2.7 %collective-permute-done.20.refs_2_ = f32[248,128]{1,0:T(8,128)S(1)} collective-permute-done((f32[248,128]{1,0:T(8,128)S(1)}, f32[248,128]{1,0:T(8,128)S(1)}, u32[]{:S(2)}, u32[]{:S(2)}) %collective-permute-start.20) | collective-permute-done | bytes 127008 | tf_op jit(solution)/shard_map/ppermute | solution.py:262
  58.9 1.7 %collective-permute-start.22 = (f32[248,128]{1,0:T(8,128)S(1)}, f32[248,128]{1,0:T(8,128)S(1)}, u32[]{:S(2)}, u32[]{:S(2)}) collective-permute-start(f32[248,128]{1,0:T(8,128)S(1)} %get-tuple-element.109), channel_id=1, source_target_pairs={{0,1},{1,0},{2,3},{3,2},{4,5},{5,4},{6,7},{7,6},{8,9},{9,8},{10,11... | collective-permute-start | bytes 380936 | tf_op jit(solution)/shard_map/ppermute | solution.py:262
  60.5 1.2 collective-permute-start.23
  61.7 1.2 collective-permute-start.24
  62.9 1.2 collective-permute-start.25
  64.1 1.8 %collective-permute-start.26 = (f32[32,128]{1,0:T(8,128)S(1)}, f32[32,128]{1,0:T(8,128)S(1)}, u32[]{:S(2)}, u32[]{:S(2)}) collective-permute-start(f32[32,128]{1,0:T(8,128)S(1)} %get-tuple-element.113), channel_id=1, source_target_pairs={{0,4},{1,18},{2,17},{3,7},{4,0},{5,22},{6,21},{7,3},{8,12},{9,26},... | collective-permute-start | bytes 49160 | tf_op jit(solution)/shard_map/ppermute | solution.py:262
  65.9 1.4 %collective-permute-done.25.refs_7_ = f32[32,128]{1,0:T(8,128)S(1)} collective-permute-done((f32[32,128]{1,0:T(8,128)S(1)}, f32[32,128]{1,0:T(8,128)S(1)}, u32[]{:S(2)}, u32[]{:S(2)}) %collective-permute-start.25) | collective-permute-done | bytes 16416 | tf_op jit(solution)/shard_map/ppermute | solution.py:262
  68.7 1.0 shard_map.97.refs_0_
  71.0 1.5 %collective-permute-start.30 = (f32[16,128]{1,0:T(8,128)S(1)}, f32[16,128]{1,0:T(8,128)S(1)}, u32[]{:S(2)}, u32[]{:S(2)}) collective-permute-start(f32[16,128]{1,0:T(8,128)S(1)} %get-tuple-element.119), channel_id=1, source_target_pairs={{0,8},{1,9},{2,10},{3,11},{4,12},{5,13},{6,14},{7,15},{8,0},{9,1},... | collective-permute-start | bytes 24584 | tf_op jit(solution)/shard_map/ppermute | solution.py:262
  72.6 1.8 %collective-permute-start.31 = (f32[16,128]{1,0:T(8,128)S(1)}, f32[16,128]{1,0:T(8,128)S(1)}, u32[]{:S(2)}, u32[]{:S(2)}) collective-permute-start(f32[16,128]{1,0:T(8,128)S(1)} %get-tuple-element.120), channel_id=1, source_target_pairs={{0,12},{1,13},{2,14},{3,15},{4,8},{5,9},{6,10},{7,11},{8,4},{9,5},... | collective-permute-start | bytes 24584 | tf_op jit(solution)/shard_map/ppermute | solution.py:262
  75.3 1.6 %collective-permute-done.31.refs_4_ = f32[16,128]{1,0:T(8,128)S(1)} collective-permute-done((f32[16,128]{1,0:T(8,128)S(1)}, f32[16,128]{1,0:T(8,128)S(1)}, u32[]{:S(2)}, u32[]{:S(2)}) %collective-permute-start.31) | collective-permute-done | bytes 8224 | tf_op jit(solution)/shard_map/ppermute | solution.py:262
  77.0 2.9 %collective-permute-start.33 = (f32[312,128]{1,0:T(8,128)S(1)}, f32[312,128]{1,0:T(8,128)S(1)}, u32[]{:S(2)}, u32[]{:S(2)}) collective-permute-start(f32[312,128]{1,0:T(8,128)S(1)} %get-tuple-element.122), channel_id=1, source_target_pairs={{0,3},{1,2},{2,1},{3,0},{4,7},{5,6},{6,5},{7,4},{8,11},{9,10},{10,... | collective-permute-start | bytes 479240 | tf_op jit(solution)/shard_map/ppermute | solution.py:262
  79.9 1.2 collective-permute-start.34
  81.1 1.2 collective-permute-start.36
  82.3 1.1 collective-permute-start.35
  83.4 4.0 %collective-permute-done.35.refs_8_ = f32[32,128]{1,0:T(8,128)S(1)} collective-permute-done((f32[32,128]{1,0:T(8,128)S(1)}, f32[32,128]{1,0:T(8,128)S(1)}, u32[]{:S(2)}, u32[]{:S(2)}) %collective-permute-start.35) | collective-permute-done | bytes 16416 | tf_op jit(solution)/shard_map/ppermute | solution.py:262
  87.4 1.2 shard_map.100
  90.0 3.1 %collective-permute-done.37.refs_2_ = f32[248,128]{1,0:T(8,128)S(1)} collective-permute-done((f32[248,128]{1,0:T(8,128)S(1)}, f32[248,128]{1,0:T(8,128)S(1)}, u32[]{:S(2)}, u32[]{:S(2)}) %collective-permute-start.37) | collective-permute-done | bytes 127008 | tf_op jit(solution)/shard_map/ppermute | solution.py:262
  93.1 1.5 %collective-permute-start.39 = (f32[248,128]{1,0:T(8,128)S(1)}, f32[248,128]{1,0:T(8,128)S(1)}, u32[]{:S(2)}, u32[]{:S(2)}) collective-permute-start(f32[248,128]{1,0:T(8,128)S(1)} %get-tuple-element.133), channel_id=1, source_target_pairs={{0,1},{1,0},{2,3},{3,2},{4,5},{5,4},{6,7},{7,6},{8,9},{9,8},{10,11... | collective-permute-start | bytes 380936 | tf_op jit(solution)/shard_map/ppermute | solution.py:262
  95.4 1.2 collective-permute-start.41
  96.6 1.5 %collective-permute-start.42 = (f32[32,128]{1,0:T(8,128)S(1)}, f32[32,128]{1,0:T(8,128)S(1)}, u32[]{:S(2)}, u32[]{:S(2)}) collective-permute-start(f32[32,128]{1,0:T(8,128)S(1)} %get-tuple-element.136), channel_id=1, source_target_pairs={{0,17},{1,16},{2,19},{3,18},{4,21},{5,20},{6,23},{7,22},{8,25},{9,... | collective-permute-start | bytes 49160 | tf_op jit(solution)/shard_map/ppermute | solution.py:262
  98.1 1.5 %collective-permute-start.43 = (f32[32,128]{1,0:T(8,128)S(1)}, f32[32,128]{1,0:T(8,128)S(1)}, u32[]{:S(2)}, u32[]{:S(2)}) collective-permute-start(f32[32,128]{1,0:T(8,128)S(1)} %get-tuple-element.137), channel_id=1, source_target_pairs={{0,4},{1,18},{2,17},{3,7},{4,0},{5,22},{6,21},{7,3},{8,12},{9,26},... | collective-permute-start | bytes 49160 | tf_op jit(solution)/shard_map/ppermute | solution.py:262
  99.6 1.7 %collective-permute-done.42.refs_7_ = f32[32,128]{1,0:T(8,128)S(1)} collective-permute-done((f32[32,128]{1,0:T(8,128)S(1)}, f32[32,128]{1,0:T(8,128)S(1)}, u32[]{:S(2)}, u32[]{:S(2)}) %collective-permute-start.42) | collective-permute-done | bytes 16416 | tf_op jit(solution)/shard_map/ppermute | solution.py:262
  101.3 1.0 collective-permute-done.43.refs_8_
  102.7 1.0 shard_map.104.refs_0_
  105.0 1.6 %collective-permute-start.47 = (f32[16,128]{1,0:T(8,128)S(1)}, f32[16,128]{1,0:T(8,128)S(1)}, u32[]{:S(2)}, u32[]{:S(2)}) collective-permute-start(f32[16,128]{1,0:T(8,128)S(1)} %get-tuple-element.143), channel_id=1, source_target_pairs={{0,8},{1,9},{2,10},{3,11},{4,12},{5,13},{6,14},{7,15},{8,0},{9,1},... | collective-permute-start | bytes 24584 | tf_op jit(solution)/shard_map/ppermute | solution.py:262
  106.6 1.8 %collective-permute-start.48 = (f32[16,128]{1,0:T(8,128)S(1)}, f32[16,128]{1,0:T(8,128)S(1)}, u32[]{:S(2)}, u32[]{:S(2)}) collective-permute-start(f32[16,128]{1,0:T(8,128)S(1)} %get-tuple-element.144), channel_id=1, source_target_pairs={{0,12},{1,13},{2,14},{3,15},{4,8},{5,9},{6,10},{7,11},{8,4},{9,5},... | collective-permute-start | bytes 24584 | tf_op jit(solution)/shard_map/ppermute | solution.py:262
  109.3 1.6 %collective-permute-done.48.refs_4_ = f32[16,128]{1,0:T(8,128)S(1)} collective-permute-done((f32[16,128]{1,0:T(8,128)S(1)}, f32[16,128]{1,0:T(8,128)S(1)}, u32[]{:S(2)}, u32[]{:S(2)}) %collective-permute-start.48) | collective-permute-done | bytes 8224 | tf_op jit(solution)/shard_map/ppermute | solution.py:262
  111.0 2.7 %collective-permute-start.50 = (f32[312,128]{1,0:T(8,128)S(1)}, f32[312,128]{1,0:T(8,128)S(1)}, u32[]{:S(2)}, u32[]{:S(2)}) collective-permute-start(f32[312,128]{1,0:T(8,128)S(1)} %get-tuple-element.146), channel_id=1, source_target_pairs={{0,3},{1,2},{2,1},{3,0},{4,7},{5,6},{6,5},{7,4},{8,11},{9,10},{10,... | collective-permute-start | bytes 479240 | tf_op jit(solution)/shard_map/ppermute | solution.py:262
  113.7 1.2 collective-permute-start.51
  115.0 1.4 %collective-permute-start.53 = (f32[96,128]{1,0:T(8,128)S(1)}, f32[96,128]{1,0:T(8,128)S(1)}, u32[]{:S(2)}, u32[]{:S(2)}) collective-permute-start(f32[96,128]{1,0:T(8,128)S(1)} %get-tuple-element.149), channel_id=1, source_target_pairs={{0,19},{1,18},{2,17},{3,16},{4,23},{5,22},{6,21},{7,20},{8,27},{9,... | collective-permute-start | bytes 147464 | tf_op jit(solution)/shard_map/ppermute | solution.py:262
  116.4 1.1 collective-permute-start.52
  117.4 3.9 %collective-permute-done.52.refs_8_ = f32[32,128]{1,0:T(8,128)S(1)} collective-permute-done((f32[32,128]{1,0:T(8,128)S(1)}, f32[32,128]{1,0:T(8,128)S(1)}, u32[]{:S(2)}, u32[]{:S(2)}) %collective-permute-start.52) | collective-permute-done | bytes 16416 | tf_op jit(solution)/shard_map/ppermute | solution.py:262
  121.3 1.2 shard_map.107
  123.9 3.1 %collective-permute-done.54.refs_2_.refs_0_ = f32[248,128]{1,0:T(8,128)S(1)} collective-permute-done((f32[248,128]{1,0:T(8,128)S(1)}, f32[248,128]{1,0:T(8,128)S(1)}, u32[]{:S(2)}, u32[]{:S(2)}) %collective-permute-start.54) | collective-permute-done | bytes 127008 | tf_op jit(solution)/shard_map/ppermute | solution.py:262
  127.0 1.5 %collective-permute-start.56 = (f32[248,128]{1,0:T(8,128)S(1)}, f32[248,128]{1,0:T(8,128)S(1)}, u32[]{:S(2)}, u32[]{:S(2)}) collective-permute-start(f32[248,128]{1,0:T(8,128)S(1)} %get-tuple-element.158), channel_id=1, source_target_pairs={{0,1},{1,0},{2,3},{3,2},{4,5},{5,4},{6,7},{7,6},{8,9},{9,8},{10,11... | collective-permute-start | bytes 380936 | tf_op jit(solution)/shard_map/ppermute | solution.py:262
  129.2 1.2 collective-permute-start.58
  130.3 1.6 %collective-permute-start.59 = (f32[32,128]{1,0:T(8,128)S(1)}, f32[32,128]{1,0:T(8,128)S(1)}, u32[]{:S(2)}, u32[]{:S(2)}) collective-permute-start(f32[32,128]{1,0:T(8,128)S(1)} %get-tuple-element.161), channel_id=1, source_target_pairs={{0,17},{1,16},{2,19},{3,18},{4,21},{5,20},{6,23},{7,22},{8,25},{9,... | collective-permute-start | bytes 49160 | tf_op jit(solution)/shard_map/ppermute | solution.py:262
  132.0 1.3 collective-permute-start.60
  133.3 2.8 %shard_map.109 = f32[1158,1,128]{2,1,0:T(1,128)} custom-call(s32[1,1158]{1,0:T(1,128)S(1)} %bitcast.17, f32[1280,128]{1,0:T(8,128)S(1)} %get-tuple-element.153.acc), custom_call_target="tpu_custom_call" | custom-call | bytes 1252888 | tf_op jit(solution)/shard_map/pallas_call | solution.py:275
  136.2 3.0 %shard_map.111 = f32[1158,1,128]{2,1,0:T(1,128)} custom-call(s32[1,1158]{1,0:T(1,128)S(1)} %bitcast.18, f32[576,128]{1,0:T(8,128)S(1)} %get-tuple-element.154.refs_0_.early, f32[704,128]{1,0:T(8,128)S(1)} %get-tuple-element.155.refs_1_.late, f32[248,128]{1,0:T(8,128)S(1)} %collective-permute-done.54.refs_2_.refs_0_, ...), custom_call_target="tpu_custom_call" | custom-call | bytes 2575896 | tf_op jit(solution)/shard_map/pallas_call | solution.py:275
  (106 shorter events, 19.5 us)
Async XLA Ops:
  1.5 8.2 %collective-permute-start = (f32[16,128]{1,0:T(8,128)S(1)}, f32[16,128]{1,0:T(8,128)S(1)}, u32[]{:S(2)}, u32[]{:S(2)}) collective-permute-start(f32[16,128]{1,0:T(8,128)S(1)} %shard_map.84.refs_1_.refs_4_), channel_id=1, source_target_pairs={{0,1},{1,0},{2,3},{3,2},{4,5},{5,4},{6,7},{7,6},{8,9},{9,8},{10,11... | collective-permute-start | bytes 24584 | tf_op jit(solution)/shard_map/ppermute | solution.py:262
  1.6 8.1 %collective-permute-start.1 = (f32[16,128]{1,0:T(8,128)S(1)}, f32[16,128]{1,0:T(8,128)S(1)}, u32[]{:S(2)}, u32[]{:S(2)}) collective-permute-start(f32[16,128]{1,0:T(8,128)S(1)} %shard_map.84.refs_1_.refs_4_), channel_id=1, source_target_pairs={{0,8},{1,9},{2,10},{3,11},{4,12},{5,13},{6,14},{7,15},{8,0},{9,1},... | collective-permute-start | bytes 24584 | tf_op jit(solution)/shard_map/ppermute | solution.py:262
  5.3 4.3 %collective-permute-start.2 = (f32[16,128]{1,0:T(8,128)S(1)}, f32[16,128]{1,0:T(8,128)S(1)}, u32[]{:S(2)}, u32[]{:S(2)}) collective-permute-start(f32[16,128]{1,0:T(8,128)S(1)} %shard_map.84.refs_1_.refs_4_), channel_id=1, source_target_pairs={{0,9},{1,8},{2,11},{3,10},{4,13},{5,12},{6,15},{7,14},{8,1},{9,0},... | collective-permute-start | bytes 24584 | tf_op jit(solution)/shard_map/ppermute | solution.py:262
  6.3 2.3 %copy-start.2 = (bf16[1,1,1,6,1158]{4,3,2,1,0:T(8,128)(2,1)S(1)}, bf16[1,1,1,6,1158]{4,3,2,1,0:T(8,128)(2,1)}, u32[]{:S(2)}) copy-start(bf16[1,1,1,6,1158]{4,3,2,1,0:T(8,128)(2,1)} %param.9) | copy-start | bytes 41692
  7.4 4.5 %copy-start.4 = (bf16[1,1,1,1158,1158]{4,3,2,1,0:T(8,128)(2,1)S(1)}, bf16[1,1,1,1158,1158]{4,3,2,1,0:T(8,128)(2,1)}, u32[]{:S(2)}) copy-start(bf16[1,1,1,1158,1158]{4,3,2,1,0:T(8,128)(2,1)} %param.8) | copy-start | bytes 8045788
  9.8 8.2 %collective-permute-start.3 = (f32[336,128]{1,0:T(8,128)S(1)}, f32[336,128]{1,0:T(8,128)S(1)}, u32[]{:S(2)}, u32[]{:S(2)}) collective-permute-start(f32[336,128]{1,0:T(8,128)S(1)} %get-tuple-element.85), channel_id=1, source_target_pairs={{0,4},{1,5},{2,6},{3,7},{4,0},{5,1},{6,2},{7,3},{8,12},{9,13},{10,... | collective-permute-start | bytes 516104 | tf_op jit(solution)/shard_map/ppermute | solution.py:262
  11.4 6.6 %collective-permute-start.4 = (f32[272,128]{1,0:T(8,128)S(1)}, f32[272,128]{1,0:T(8,128)S(1)}, u32[]{:S(2)}, u32[]{:S(2)}) collective-permute-start(f32[272,128]{1,0:T(8,128)S(1)} %get-tuple-element.86), channel_id=1, source_target_pairs={{0,1},{1,0},{2,3},{3,2},{4,8},{5,9},{6,10},{7,11},{8,4},{9,5},{10,... | collective-permute-start | bytes 417800 | tf_op jit(solution)/shard_map/ppermute | solution.py:262
  18.4 11.1 %collective-permute-start.5 = (f32[272,128]{1,0:T(8,128)S(1)}, f32[272,128]{1,0:T(8,128)S(1)}, u32[]{:S(2)}, u32[]{:S(2)}) collective-permute-start(f32[272,128]{1,0:T(8,128)S(1)} %get-tuple-element.87), channel_id=1, source_target_pairs={{0,1},{1,0},{2,3},{3,2},{4,5},{5,4},{6,7},{7,6},{8,9},{9,8},{10,11... | collective-permute-start | bytes 417800 | tf_op jit(solution)/shard_map/ppermute | solution.py:262
  18.5 11.0 %collective-permute-start.6 = (f32[400,128]{1,0:T(8,128)S(1)}, f32[400,128]{1,0:T(8,128)S(1)}, u32[]{:S(2)}, u32[]{:S(2)}) collective-permute-start(f32[400,128]{1,0:T(8,128)S(1)} %get-tuple-element.88), channel_id=1, source_target_pairs={{0,3},{1,2},{2,1},{3,0},{4,7},{5,6},{6,5},{7,4},{8,11},{9,10},{10,... | collective-permute-start | bytes 614408 | tf_op jit(solution)/shard_map/ppermute | solution.py:262
  20.1 9.4 %collective-permute-start.7 = (f32[400,128]{1,0:T(8,128)S(1)}, f32[400,128]{1,0:T(8,128)S(1)}, u32[]{:S(2)}, u32[]{:S(2)}) collective-permute-start(f32[400,128]{1,0:T(8,128)S(1)} %get-tuple-element.89), channel_id=1, source_target_pairs={{0,16},{1,17},{2,18},{3,19},{4,20},{5,21},{6,22},{7,23},{8,24},{9,... | collective-permute-start | bytes 614408 | tf_op jit(solution)/shard_map/ppermute | solution.py:262
  21.3 7.0 %collective-permute-start.8 = (f32[56,128]{1,0:T(8,128)S(1)}, f32[56,128]{1,0:T(8,128)S(1)}, u32[]{:S(2)}, u32[]{:S(2)}) collective-permute-start(f32[56,128]{1,0:T(8,128)S(1)} %get-tuple-element.90), channel_id=1, source_target_pairs={{0,17},{1,16},{2,19},{3,18},{4,21},{5,20},{6,23},{7,22},{8,25},{9,... | collective-permute-start | bytes 86024 | tf_op jit(solution)/shard_map/ppermute | solution.py:262
  21.8 7.7 %collective-permute-start.9 = (f32[184,128]{1,0:T(8,128)S(1)}, f32[184,128]{1,0:T(8,128)S(1)}, u32[]{:S(2)}, u32[]{:S(2)}) collective-permute-start(f32[184,128]{1,0:T(8,128)S(1)} %get-tuple-element.91), channel_id=1, source_target_pairs={{0,19},{1,18},{2,17},{3,16},{4,23},{5,22},{6,21},{7,20},{8,27},{9,... | collective-permute-start | bytes 282632 | tf_op jit(solution)/shard_map/ppermute | solution.py:262
  29.8 6.3 %copy-start.5 = (bf16[1,1,1,1158,1158]{4,3,2,1,0:T(8,128)(2,1)S(1)}, bf16[1,1,1,1158,1158]{4,3,2,1,0:T(8,128)(2,1)}, u32[]{:S(2)}) copy-start(bf16[1,1,1,1158,1158]{4,3,2,1,0:T(8,128)(2,1)} %param.7) | copy-start | bytes 8045788
  29.8 1.3 collective-permute-start.10
  31.2 9.4 %collective-permute-start.11 = (f32[264,128]{1,0:T(8,128)S(1)}, f32[264,128]{1,0:T(8,128)S(1)}, u32[]{:S(2)}, u32[]{:S(2)}) collective-permute-start(f32[264,128]{1,0:T(8,128)S(1)} %get-tuple-element.94), channel_id=1, source_target_pairs={{0,4},{1,5},{2,6},{3,7},{4,0},{5,1},{6,2},{7,3},{8,12},{9,13},{10,... | collective-permute-start | bytes 405512 | tf_op jit(solution)/shard_map/ppermute | solution.py:262
  33.6 7.0 %collective-permute-start.12 = (f32[248,128]{1,0:T(8,128)S(1)}, f32[248,128]{1,0:T(8,128)S(1)}, u32[]{:S(2)}, u32[]{:S(2)}) collective-permute-start(f32[248,128]{1,0:T(8,128)S(1)} %get-tuple-element.95), channel_id=1, source_target_pairs={{0,1},{1,0},{2,3},{3,2},{4,8},{5,9},{6,10},{7,11},{8,4},{9,5},{10,... | collective-permute-start | bytes 380936 | tf_op jit(solution)/shard_map/ppermute | solution.py:262
  34.2 6.3 %collective-permute-start.13 = (f32[16,128]{1,0:T(8,128)S(1)}, f32[16,128]{1,0:T(8,128)S(1)}, u32[]{:S(2)}, u32[]{:S(2)}) collective-permute-start(f32[16,128]{1,0:T(8,128)S(1)} %get-tuple-element.96), channel_id=1, source_target_pairs={{0,8},{1,9},{2,10},{3,11},{4,12},{5,13},{6,14},{7,15},{8,0},{9,1},... | collective-permute-start | bytes 24584 | tf_op jit(solution)/shard_map/ppermute | solution.py:262
  34.8 5.8 %collective-permute-start.14 = (f32[16,128]{1,0:T(8,128)S(1)}, f32[16,128]{1,0:T(8,128)S(1)}, u32[]{:S(2)}, u32[]{:S(2)}) collective-permute-start(f32[16,128]{1,0:T(8,128)S(1)} %get-tuple-element.97), channel_id=1, source_target_pairs={{0,12},{1,13},{2,14},{3,15},{4,8},{5,9},{6,10},{7,11},{8,4},{9,5},... | collective-permute-start | bytes 24584 | tf_op jit(solution)/shard_map/ppermute | solution.py:262
  40.7 12.6 %collective-permute-start.15 = (f32[248,128]{1,0:T(8,128)S(1)}, f32[248,128]{1,0:T(8,128)S(1)}, u32[]{:S(2)}, u32[]{:S(2)}) collective-permute-start(f32[248,128]{1,0:T(8,128)S(1)} %get-tuple-element.98), channel_id=1, source_target_pairs={{0,1},{1,0},{2,3},{3,2},{4,5},{5,4},{6,7},{7,6},{8,9},{9,8},{10,11... | collective-permute-start | bytes 380936 | tf_op jit(solution)/shard_map/ppermute | solution.py:262
  42.1 11.2 %collective-permute-start.16 = (f32[312,128]{1,0:T(8,128)S(1)}, f32[312,128]{1,0:T(8,128)S(1)}, u32[]{:S(2)}, u32[]{:S(2)}) collective-permute-start(f32[312,128]{1,0:T(8,128)S(1)} %get-tuple-element.99), channel_id=1, source_target_pairs={{0,3},{1,2},{2,1},{3,0},{4,7},{5,6},{6,5},{7,4},{8,11},{9,10},{10,... | collective-permute-start | bytes 479240 | tf_op jit(solution)/shard_map/ppermute | solution.py:262
  43.3 10.0 %collective-permute-start.17 = (f32[312,128]{1,0:T(8,128)S(1)}, f32[312,128]{1,0:T(8,128)S(1)}, u32[]{:S(2)}, u32[]{:S(2)}) collective-permute-start(f32[312,128]{1,0:T(8,128)S(1)} %get-tuple-element.100), channel_id=1, source_target_pairs={{0,16},{1,17},{2,18},{3,19},{4,20},{5,21},{6,22},{7,23},{8,24},{9,... | collective-permute-start | bytes 479240 | tf_op jit(solution)/shard_map/ppermute | solution.py:262
  44.5 8.8 %collective-permute-start.19 = (f32[96,128]{1,0:T(8,128)S(1)}, f32[96,128]{1,0:T(8,128)S(1)}, u32[]{:S(2)}, u32[]{:S(2)}) collective-permute-start(f32[96,128]{1,0:T(8,128)S(1)} %get-tuple-element.102), channel_id=1, source_target_pairs={{0,19},{1,18},{2,17},{3,16},{4,23},{5,22},{6,21},{7,20},{8,27},{9,... | collective-permute-start | bytes 147464 | tf_op jit(solution)/shard_map/ppermute | solution.py:262
  50.1 3.2 %collective-permute-start.18 = (f32[32,128]{1,0:T(8,128)S(1)}, f32[32,128]{1,0:T(8,128)S(1)}, u32[]{:S(2)}, u32[]{:S(2)}) collective-permute-start(f32[32,128]{1,0:T(8,128)S(1)} %get-tuple-element.101), channel_id=1, source_target_pairs={{0,17},{1,16},{2,19},{3,18},{4,21},{5,20},{6,23},{7,22},{8,25},{9,... | collective-permute-start | bytes 49160 | tf_op jit(solution)/shard_map/ppermute | solution.py:262
  54.5 4.3 %collective-permute-start.20 = (f32[248,128]{1,0:T(8,128)S(1)}, f32[248,128]{1,0:T(8,128)S(1)}, u32[]{:S(2)}, u32[]{:S(2)}) collective-permute-start(f32[248,128]{1,0:T(8,128)S(1)} %get-tuple-element.107), channel_id=1, source_target_pairs={{0,4},{1,5},{2,6},{3,7},{4,0},{5,1},{6,2},{7,3},{8,12},{9,13},{10,... | collective-permute-start | bytes 380936 | tf_op jit(solution)/shard_map/ppermute | solution.py:262
  54.6 4.2 %collective-permute-start.21 = (f32[248,128]{1,0:T(8,128)S(1)}, f32[248,128]{1,0:T(8,128)S(1)}, u32[]{:S(2)}, u32[]{:S(2)}) collective-permute-start(f32[248,128]{1,0:T(8,128)S(1)} %get-tuple-element.108), channel_id=1, source_target_pairs={{0,1},{1,0},{2,3},{3,2},{4,8},{5,9},{6,10},{7,11},{8,4},{9,5},{10,... | collective-permute-start | bytes 380936 | tf_op jit(solution)/shard_map/ppermute | solution.py:262
  58.9 9.4 %collective-permute-start.22 = (f32[248,128]{1,0:T(8,128)S(1)}, f32[248,128]{1,0:T(8,128)S(1)}, u32[]{:S(2)}, u32[]{:S(2)}) collective-permute-start(f32[248,128]{1,0:T(8,128)S(1)} %get-tuple-element.109), channel_id=1, source_target_pairs={{0,1},{1,0},{2,3},{3,2},{4,5},{5,4},{6,7},{7,6},{8,9},{9,8},{10,11... | collective-permute-start | bytes 380936 | tf_op jit(solution)/shard_map/ppermute | solution.py:262
  60.5 7.7 %collective-permute-start.23 = (f32[248,128]{1,0:T(8,128)S(1)}, f32[248,128]{1,0:T(8,128)S(1)}, u32[]{:S(2)}, u32[]{:S(2)}) collective-permute-start(f32[248,128]{1,0:T(8,128)S(1)} %get-tuple-element.110), channel_id=1, source_target_pairs={{0,4},{1,2},{2,1},{3,7},{4,0},{5,6},{6,5},{7,3},{8,12},{9,10},{10,... | collective-permute-start | bytes 380936 | tf_op jit(solution)/shard_map/ppermute | solution.py:262
  61.7 6.5 %collective-permute-start.24 = (f32[248,128]{1,0:T(8,128)S(1)}, f32[248,128]{1,0:T(8,128)S(1)}, u32[]{:S(2)}, u32[]{:S(2)}) collective-permute-start(f32[248,128]{1,0:T(8,128)S(1)} %get-tuple-element.111), channel_id=1, source_target_pairs={{0,16},{1,17},{2,18},{3,19},{4,20},{5,21},{6,22},{7,23},{8,24},{9,... | collective-permute-start | bytes 380936 | tf_op jit(solution)/shard_map/ppermute | solution.py:262
  62.9 4.4 %collective-permute-start.25 = (f32[32,128]{1,0:T(8,128)S(1)}, f32[32,128]{1,0:T(8,128)S(1)}, u32[]{:S(2)}, u32[]{:S(2)}) collective-permute-start(f32[32,128]{1,0:T(8,128)S(1)} %get-tuple-element.112), channel_id=1, source_target_pairs={{0,17},{1,16},{2,19},{3,18},{4,21},{5,20},{6,23},{7,22},{8,25},{9,... | collective-permute-start | bytes 49160 | tf_op jit(solution)/shard_map/ppermute | solution.py:262
  64.1 4.2 %collective-permute-start.26 = (f32[32,128]{1,0:T(8,128)S(1)}, f32[32,128]{1,0:T(8,128)S(1)}, u32[]{:S(2)}, u32[]{:S(2)}) collective-permute-start(f32[32,128]{1,0:T(8,128)S(1)} %get-tuple-element.113), channel_id=1, source_target_pairs={{0,4},{1,18},{2,17},{3,7},{4,0},{5,22},{6,21},{7,3},{8,12},{9,26},... | collective-permute-start | bytes 49160 | tf_op jit(solution)/shard_map/ppermute | solution.py:262
  68.6 1.2 collective-permute-start.27
  69.8 7.1 %collective-permute-start.28 = (f32[264,128]{1,0:T(8,128)S(1)}, f32[264,128]{1,0:T(8,128)S(1)}, u32[]{:S(2)}, u32[]{:S(2)}) collective-permute-start(f32[264,128]{1,0:T(8,128)S(1)} %get-tuple-element.117), channel_id=1, source_target_pairs={{0,4},{1,5},{2,6},{3,7},{4,0},{5,1},{6,2},{7,3},{8,12},{9,13},{10,... | collective-permute-start | bytes 405512 | tf_op jit(solution)/shard_map/ppermute | solution.py:262
  70.5 6.4 %collective-permute-start.29 = (f32[248,128]{1,0:T(8,128)S(1)}, f32[248,128]{1,0:T(8,128)S(1)}, u32[]{:S(2)}, u32[]{:S(2)}) collective-permute-start(f32[248,128]{1,0:T(8,128)S(1)} %get-tuple-element.118), channel_id=1, source_target_pairs={{0,1},{1,0},{2,3},{3,2},{4,8},{5,9},{6,10},{7,11},{8,4},{9,5},{10,... | collective-permute-start | bytes 380936 | tf_op jit(solution)/shard_map/ppermute | solution.py:262
  71.0 4.2 %collective-permute-start.30 = (f32[16,128]{1,0:T(8,128)S(1)}, f32[16,128]{1,0:T(8,128)S(1)}, u32[]{:S(2)}, u32[]{:S(2)}) collective-permute-start(f32[16,128]{1,0:T(8,128)S(1)} %get-tuple-element.119), channel_id=1, source_target_pairs={{0,8},{1,9},{2,10},{3,11},{4,12},{5,13},{6,14},{7,15},{8,0},{9,1},... | collective-permute-start | bytes 24584 | tf_op jit(solution)/shard_map/ppermute | solution.py:262
  72.6 4.3 %collective-permute-start.31 = (f32[16,128]{1,0:T(8,128)S(1)}, f32[16,128]{1,0:T(8,128)S(1)}, u32[]{:S(2)}, u32[]{:S(2)}) collective-permute-start(f32[16,128]{1,0:T(8,128)S(1)} %get-tuple-element.120), channel_id=1, source_target_pairs={{0,12},{1,13},{2,14},{3,15},{4,8},{5,9},{6,10},{7,11},{8,4},{9,5},... | collective-permute-start | bytes 24584 | tf_op jit(solution)/shard_map/ppermute | solution.py:262
  77.0 10.4 %collective-permute-start.33 = (f32[312,128]{1,0:T(8,128)S(1)}, f32[312,128]{1,0:T(8,128)S(1)}, u32[]{:S(2)}, u32[]{:S(2)}) collective-permute-start(f32[312,128]{1,0:T(8,128)S(1)} %get-tuple-element.122), channel_id=1, source_target_pairs={{0,3},{1,2},{2,1},{3,0},{4,7},{5,6},{6,5},{7,4},{8,11},{9,10},{10,... | collective-permute-start | bytes 479240 | tf_op jit(solution)/shard_map/ppermute | solution.py:262
  79.9 7.5 %collective-permute-start.34 = (f32[312,128]{1,0:T(8,128)S(1)}, f32[312,128]{1,0:T(8,128)S(1)}, u32[]{:S(2)}, u32[]{:S(2)}) collective-permute-start(f32[312,128]{1,0:T(8,128)S(1)} %get-tuple-element.123), channel_id=1, source_target_pairs={{0,16},{1,17},{2,18},{3,19},{4,20},{5,21},{6,22},{7,23},{8,24},{9,... | collective-permute-start | bytes 479240 | tf_op jit(solution)/shard_map/ppermute | solution.py:262
  81.1 6.3 %collective-permute-start.32 = (f32[248,128]{1,0:T(8,128)S(1)}, f32[248,128]{1,0:T(8,128)S(1)}, u32[]{:S(2)}, u32[]{:S(2)}) collective-permute-start(f32[248,128]{1,0:T(8,128)S(1)} %get-tuple-element.121), channel_id=1, source_target_pairs={{0,1},{1,0},{2,3},{3,2},{4,5},{5,4},{6,7},{7,6},{8,9},{9,8},{10,11... | collective-permute-start | bytes 380936 | tf_op jit(solution)/shard_map/ppermute | solution.py:262
  81.1 6.3 %collective-permute-start.36 = (f32[96,128]{1,0:T(8,128)S(1)}, f32[96,128]{1,0:T(8,128)S(1)}, u32[]{:S(2)}, u32[]{:S(2)}) collective-permute-start(f32[96,128]{1,0:T(8,128)S(1)} %get-tuple-element.125), channel_id=1, source_target_pairs={{0,19},{1,18},{2,17},{3,16},{4,23},{5,22},{6,21},{7,20},{8,27},{9,... | collective-permute-start | bytes 147464 | tf_op jit(solution)/shard_map/ppermute | solution.py:262
  82.3 5.1 %collective-permute-start.35 = (f32[32,128]{1,0:T(8,128)S(1)}, f32[32,128]{1,0:T(8,128)S(1)}, u32[]{:S(2)}, u32[]{:S(2)}) collective-permute-start(f32[32,128]{1,0:T(8,128)S(1)} %get-tuple-element.124), channel_id=1, source_target_pairs={{0,17},{1,16},{2,19},{3,18},{4,21},{5,20},{6,23},{7,22},{8,25},{9,... | collective-permute-start | bytes 49160 | tf_op jit(solution)/shard_map/ppermute | solution.py:262
  88.6 4.4 %collective-permute-start.37 = (f32[248,128]{1,0:T(8,128)S(1)}, f32[248,128]{1,0:T(8,128)S(1)}, u32[]{:S(2)}, u32[]{:S(2)}) collective-permute-start(f32[248,128]{1,0:T(8,128)S(1)} %get-tuple-element.131), channel_id=1, source_target_pairs={{0,4},{1,5},{2,6},{3,7},{4,0},{5,1},{6,2},{7,3},{8,12},{9,13},{10,... | collective-permute-start | bytes 380936 | tf_op jit(solution)/shard_map/ppermute | solution.py:262
  88.7 4.4 %collective-permute-start.38 = (f32[248,128]{1,0:T(8,128)S(1)}, f32[248,128]{1,0:T(8,128)S(1)}, u32[]{:S(2)}, u32[]{:S(2)}) collective-permute-start(f32[248,128]{1,0:T(8,128)S(1)} %get-tuple-element.132), channel_id=1, source_target_pairs={{0,1},{1,0},{2,3},{3,2},{4,8},{5,9},{6,10},{7,11},{8,4},{9,5},{10,... | collective-permute-start | bytes 380936 | tf_op jit(solution)/shard_map/ppermute | solution.py:262
  93.1 9.2 %collective-permute-start.39 = (f32[248,128]{1,0:T(8,128)S(1)}, f32[248,128]{1,0:T(8,128)S(1)}, u32[]{:S(2)}, u32[]{:S(2)}) collective-permute-start(f32[248,128]{1,0:T(8,128)S(1)} %get-tuple-element.133), channel_id=1, source_target_pairs={{0,1},{1,0},{2,3},{3,2},{4,5},{5,4},{6,7},{7,6},{8,9},{9,8},{10,11... | collective-permute-start | bytes 380936 | tf_op jit(solution)/shard_map/ppermute | solution.py:262
  94.6 7.7 %collective-permute-start.40 = (f32[248,128]{1,0:T(8,128)S(1)}, f32[248,128]{1,0:T(8,128)S(1)}, u32[]{:S(2)}, u32[]{:S(2)}) collective-permute-start(f32[248,128]{1,0:T(8,128)S(1)} %get-tuple-element.134), channel_id=1, source_target_pairs={{0,4},{1,2},{2,1},{3,7},{4,0},{5,6},{6,5},{7,3},{8,12},{9,10},{10,... | collective-permute-start | bytes 380936 | tf_op jit(solution)/shard_map/ppermute | solution.py:262
  95.4 6.9 %collective-permute-start.41 = (f32[248,128]{1,0:T(8,128)S(1)}, f32[248,128]{1,0:T(8,128)S(1)}, u32[]{:S(2)}, u32[]{:S(2)}) collective-permute-start(f32[248,128]{1,0:T(8,128)S(1)} %get-tuple-element.135), channel_id=1, source_target_pairs={{0,16},{1,17},{2,18},{3,19},{4,20},{5,21},{6,22},{7,23},{8,24},{9,... | collective-permute-start | bytes 380936 | tf_op jit(solution)/shard_map/ppermute | solution.py:262
  96.6 4.7 %collective-permute-start.42 = (f32[32,128]{1,0:T(8,128)S(1)}, f32[32,128]{1,0:T(8,128)S(1)}, u32[]{:S(2)}, u32[]{:S(2)}) collective-permute-start(f32[32,128]{1,0:T(8,128)S(1)} %get-tuple-element.136), channel_id=1, source_target_pairs={{0,17},{1,16},{2,19},{3,18},{4,21},{5,20},{6,23},{7,22},{8,25},{9,... | collective-permute-start | bytes 49160 | tf_op jit(solution)/shard_map/ppermute | solution.py:262
  98.1 4.2 %collective-permute-start.43 = (f32[32,128]{1,0:T(8,128)S(1)}, f32[32,128]{1,0:T(8,128)S(1)}, u32[]{:S(2)}, u32[]{:S(2)}) collective-permute-start(f32[32,128]{1,0:T(8,128)S(1)} %get-tuple-element.137), channel_id=1, source_target_pairs={{0,4},{1,18},{2,17},{3,7},{4,0},{5,22},{6,21},{7,3},{8,12},{9,26},... | collective-permute-start | bytes 49160 | tf_op jit(solution)/shard_map/ppermute | solution.py:262
  102.7 1.2 collective-permute-start.44
  103.9 7.1 %collective-permute-start.45 = (f32[264,128]{1,0:T(8,128)S(1)}, f32[264,128]{1,0:T(8,128)S(1)}, u32[]{:S(2)}, u32[]{:S(2)}) collective-permute-start(f32[264,128]{1,0:T(8,128)S(1)} %get-tuple-element.141), channel_id=1, source_target_pairs={{0,4},{1,5},{2,6},{3,7},{4,0},{5,1},{6,2},{7,3},{8,12},{9,13},{10,... | collective-permute-start | bytes 405512 | tf_op jit(solution)/shard_map/ppermute | solution.py:262
  104.6 6.4 %collective-permute-start.46 = (f32[248,128]{1,0:T(8,128)S(1)}, f32[248,128]{1,0:T(8,128)S(1)}, u32[]{:S(2)}, u32[]{:S(2)}) collective-permute-start(f32[248,128]{1,0:T(8,128)S(1)} %get-tuple-element.142), channel_id=1, source_target_pairs={{0,1},{1,0},{2,3},{3,2},{4,8},{5,9},{6,10},{7,11},{8,4},{9,5},{10,... | collective-permute-start | bytes 380936 | tf_op jit(solution)/shard_map/ppermute | solution.py:262
  105.0 4.3 %collective-permute-start.47 = (f32[16,128]{1,0:T(8,128)S(1)}, f32[16,128]{1,0:T(8,128)S(1)}, u32[]{:S(2)}, u32[]{:S(2)}) collective-permute-start(f32[16,128]{1,0:T(8,128)S(1)} %get-tuple-element.143), channel_id=1, source_target_pairs={{0,8},{1,9},{2,10},{3,11},{4,12},{5,13},{6,14},{7,15},{8,0},{9,1},... | collective-permute-start | bytes 24584 | tf_op jit(solution)/shard_map/ppermute | solution.py:262
  106.6 4.3 %collective-permute-start.48 = (f32[16,128]{1,0:T(8,128)S(1)}, f32[16,128]{1,0:T(8,128)S(1)}, u32[]{:S(2)}, u32[]{:S(2)}) collective-permute-start(f32[16,128]{1,0:T(8,128)S(1)} %get-tuple-element.144), channel_id=1, source_target_pairs={{0,12},{1,13},{2,14},{3,15},{4,8},{5,9},{6,10},{7,11},{8,4},{9,5},... | collective-permute-start | bytes 24584 | tf_op jit(solution)/shard_map/ppermute | solution.py:262
  111.0 10.2 %collective-permute-start.50 = (f32[312,128]{1,0:T(8,128)S(1)}, f32[312,128]{1,0:T(8,128)S(1)}, u32[]{:S(2)}, u32[]{:S(2)}) collective-permute-start(f32[312,128]{1,0:T(8,128)S(1)} %get-tuple-element.146), channel_id=1, source_target_pairs={{0,3},{1,2},{2,1},{3,0},{4,7},{5,6},{6,5},{7,4},{8,11},{9,10},{10,... | collective-permute-start | bytes 479240 | tf_op jit(solution)/shard_map/ppermute | solution.py:262
  113.7 7.6 %collective-permute-start.51 = (f32[312,128]{1,0:T(8,128)S(1)}, f32[312,128]{1,0:T(8,128)S(1)}, u32[]{:S(2)}, u32[]{:S(2)}) collective-permute-start(f32[312,128]{1,0:T(8,128)S(1)} %get-tuple-element.147), channel_id=1, source_target_pairs={{0,16},{1,17},{2,18},{3,19},{4,20},{5,21},{6,22},{7,23},{8,24},{9,... | collective-permute-start | bytes 479240 | tf_op jit(solution)/shard_map/ppermute | solution.py:262
  114.9 6.4 %collective-permute-start.49 = (f32[248,128]{1,0:T(8,128)S(1)}, f32[248,128]{1,0:T(8,128)S(1)}, u32[]{:S(2)}, u32[]{:S(2)}) collective-permute-start(f32[248,128]{1,0:T(8,128)S(1)} %get-tuple-element.145), channel_id=1, source_target_pairs={{0,1},{1,0},{2,3},{3,2},{4,5},{5,4},{6,7},{7,6},{8,9},{9,8},{10,11... | collective-permute-start | bytes 380936 | tf_op jit(solution)/shard_map/ppermute | solution.py:262
  115.0 6.3 %collective-permute-start.53 = (f32[96,128]{1,0:T(8,128)S(1)}, f32[96,128]{1,0:T(8,128)S(1)}, u32[]{:S(2)}, u32[]{:S(2)}) collective-permute-start(f32[96,128]{1,0:T(8,128)S(1)} %get-tuple-element.149), channel_id=1, source_target_pairs={{0,19},{1,18},{2,17},{3,16},{4,23},{5,22},{6,21},{7,20},{8,27},{9,... | collective-permute-start | bytes 147464 | tf_op jit(solution)/shard_map/ppermute | solution.py:262
  116.4 4.9 %collective-permute-start.52 = (f32[32,128]{1,0:T(8,128)S(1)}, f32[32,128]{1,0:T(8,128)S(1)}, u32[]{:S(2)}, u32[]{:S(2)}) collective-permute-start(f32[32,128]{1,0:T(8,128)S(1)} %get-tuple-element.148), channel_id=1, source_target_pairs={{0,17},{1,16},{2,19},{3,18},{4,21},{5,20},{6,23},{7,22},{8,25},{9,... | collective-permute-start | bytes 49160 | tf_op jit(solution)/shard_map/ppermute | solution.py:262
  122.5 4.4 %collective-permute-start.54 = (f32[248,128]{1,0:T(8,128)S(1)}, f32[248,128]{1,0:T(8,128)S(1)}, u32[]{:S(2)}, u32[]{:S(2)}) collective-permute-start(f32[248,128]{1,0:T(8,128)S(1)} %get-tuple-element.156), channel_id=1, source_target_pairs={{0,4},{1,5},{2,6},{3,7},{4,0},{5,1},{6,2},{7,3},{8,12},{9,13},{10,... | collective-permute-start | bytes 380936 | tf_op jit(solution)/shard_map/ppermute | solution.py:262
  122.6 4.4 %collective-permute-start.55 = (f32[248,128]{1,0:T(8,128)S(1)}, f32[248,128]{1,0:T(8,128)S(1)}, u32[]{:S(2)}, u32[]{:S(2)}) collective-permute-start(f32[248,128]{1,0:T(8,128)S(1)} %get-tuple-element.157), channel_id=1, source_target_pairs={{0,1},{1,0},{2,3},{3,2},{4,8},{5,9},{6,10},{7,11},{8,4},{9,5},{10,... | collective-permute-start | bytes 380936 | tf_op jit(solution)/shard_map/ppermute | solution.py:262
  127.0 9.1 %collective-permute-start.56 = (f32[248,128]{1,0:T(8,128)S(1)}, f32[248,128]{1,0:T(8,128)S(1)}, u32[]{:S(2)}, u32[]{:S(2)}) collective-permute-start(f32[248,128]{1,0:T(8,128)S(1)} %get-tuple-element.158), channel_id=1, source_target_pairs={{0,1},{1,0},{2,3},{3,2},{4,5},{5,4},{6,7},{7,6},{8,9},{9,8},{10,11... | collective-permute-start | bytes 380936 | tf_op jit(solution)/shard_map/ppermute | solution.py:262
  128.5 7.6 %collective-permute-start.57 = (f32[248,128]{1,0:T(8,128)S(1)}, f32[248,128]{1,0:T(8,128)S(1)}, u32[]{:S(2)}, u32[]{:S(2)}) collective-permute-start(f32[248,128]{1,0:T(8,128)S(1)} %get-tuple-element.159), channel_id=1, source_target_pairs={{0,4},{1,2},{2,1},{3,7},{4,0},{5,6},{6,5},{7,3},{8,12},{9,10},{10,... | collective-permute-start | bytes 380936 | tf_op jit(solution)/shard_map/ppermute | solution.py:262
  129.2 7.0 %collective-permute-start.58 = (f32[248,128]{1,0:T(8,128)S(1)}, f32[248,128]{1,0:T(8,128)S(1)}, u32[]{:S(2)}, u32[]{:S(2)}) collective-permute-start(f32[248,128]{1,0:T(8,128)S(1)} %get-tuple-element.160), channel_id=1, source_target_pairs={{0,16},{1,17},{2,18},{3,19},{4,20},{5,21},{6,22},{7,23},{8,24},{9,... | collective-permute-start | bytes 380936 | tf_op jit(solution)/shard_map/ppermute | solution.py:262
  130.3 5.8 %collective-permute-start.59 = (f32[32,128]{1,0:T(8,128)S(1)}, f32[32,128]{1,0:T(8,128)S(1)}, u32[]{:S(2)}, u32[]{:S(2)}) collective-permute-start(f32[32,128]{1,0:T(8,128)S(1)} %get-tuple-element.161), channel_id=1, source_target_pairs={{0,17},{1,16},{2,19},{3,18},{4,21},{5,20},{6,23},{7,22},{8,25},{9,... | collective-permute-start | bytes 49160 | tf_op jit(solution)/shard_map/ppermute | solution.py:262
  132.0 4.2 %collective-permute-start.60 = (f32[32,128]{1,0:T(8,128)S(1)}, f32[32,128]{1,0:T(8,128)S(1)}, u32[]{:S(2)}, u32[]{:S(2)}) collective-permute-start(f32[32,128]{1,0:T(8,128)S(1)} %get-tuple-element.162), channel_id=1, source_target_pairs={{0,4},{1,18},{2,17},{3,7},{4,0},{5,22},{6,21},{7,3},{8,12},{9,26},... | collective-permute-start | bytes 49160 | tf_op jit(solution)/shard_map/ppermute | solution.py:262
  (3 other events, 2.9 us)

commit v4 on v3

--- a/solution.py
+++ b/solution.py
@@ -17,6 +17,7 @@
 PAD = 8
 CHUNK = 24
 TILE = 256
+BATCH = 16
 F32 = jnp.float32
 BF16 = jnp.bfloat16
 
@@ -289,30 +290,23 @@
     for slot in slots:
         length, at = LENGTH[slot], SLOT_OFFSET[slot] - start
         off = pick(slot, index, lambda place: jnp.int32(CANON_OFFSET[place]))
-        step = 21 if length % 21 == 0 else 3
-
-        def body(i, _, off=off, at=at, step=step):
-            for j in range(step):
-                row = i * step + j
-                acc[pl.ds(at + row, 1), :] = load[canon[0, off + row], :, :]
-            return 0
-
-        lax.fori_loop(0, length // step, body, 0)
+        for first in range(0, length, BATCH):
+            batch = range(first, min(first + BATCH, length))
+            values = [load[canon[0, off + row], :, :] for row in batch]
+            for row, value in zip(batch, values):
+                acc[at + row : at + row + 1, :] = value
 
 
 def scatter_rows(index, canon, acc, out):
     for slot in PLACES:
         length, at = LENGTH[slot], SLOT_OFFSET[slot]
         off = pick(slot, index, lambda place: jnp.int32(CANON_OFFSET[place]))
-        step = 21 if length % 21 == 0 else 3
-
-        def body(i, _, off=off, at=at, step=step):
-            for j in range(step):
-                row = i * step + j
-                out[canon[0, off + row], :, :] = acc[pl.ds(at + row, 1), :]
-            return 0
-
-        lax.fori_loop(0, length // step, body, 0)
+        for first in range(0, length, BATCH):
+            batch = range(first, min(first + BATCH, length))
+            values = [acc[at + row : at + row + 1, :] for row in batch]
+            places = [canon[0, off + row] for row in batch]
+            for to, value in zip(places, values):
+                out[to, :, :] = value
 
 
 def scatter_kernel(canon, acc, out):
@@ -348,7 +342,7 @@
     lax.fori_loop(0, ROWS // TILE, step, 0)
 
 
-def select_kernel(plan, canon, one, weight_out, src):
+def select_kernel(plan, canon, basis, one, weight_out, turned, src):
     index = position()
     src[...] = jnp.full(src.shape, -1, jnp.int32)
     weight_out[...] = jnp.zeros(weight_out.shape, F32)
@@ -365,11 +359,13 @@
                 weight = weight * jnp.where(has_b(index[d], plan.sizes[d]), 0.5, 1.0)
         weight_out[at : at + length, :] = jnp.full((length, 128), 1.0, F32) * weight
 
-    def build(rows):
+    turned[...] = jnp.zeros(turned.shape, F32)
+    for t in range(0, ROWS, TILE):
+        rows = slice(t, t + TILE)
         hit = src[rows, :] == lax.broadcasted_iota(jnp.int32, (TILE, IFACE), 1)
-        one[rows, :] = jnp.where(hit, 1.0, 0.0).astype(BF16)
-
-    each_tile(build)
+        picked = jnp.where(hit, 1.0, 0.0).astype(BF16)
+        one[rows, :] = picked
+        turned[rows, :6] = dot_last(picked, basis[...]) * weight_out[rows, :6]
 
 
 def spread_kernel(plan, cinv, out):
@@ -381,11 +377,6 @@
     out[...] = jnp.zeros(out.shape, F32)
     for i in range(plan.setup):
         out[8 * i : 8 * i + 6, :] = value[:, 128 * i : 128 * (i + 1)]
-
-
-def turn_kernel(one, weight, basis, turned):
-    turned[...] = jnp.zeros(turned.shape, F32)
-    turned[:, :6] = dot_last(one[...], basis[...]) * weight[:, :6]
 
 
 def left_kernel(one, matrix, weight, basis, mid, few):
@@ -398,6 +389,11 @@
         few[...] = jnp.zeros(few.shape, F32)
         few[:6, :] = basis[...].astype(F32)
         mid[COARSE_AT : COARSE_AT + 16, :] = few[...].astype(BF16)
+
+
+def right_left_kernel(one, mid, other, out, mid_other):
+    right_kernel(one, mid, out)
+    left_kernel(one, other, None, None, mid_other, None)
 
 
 def right_kernel(one, mid, out):
@@ -434,11 +430,13 @@
     write_payloads(plan.coarse[kind][0], refs, base, known_blocks(plan, kind, mine, swapped, [], per), pack)
 
 
-def middle_kernel(plan, kind, count, *refs):
+def middle_kernel(plan, kind, count, after, *refs):
     first, second = plan.messages(kind)
     per = plan.per(kind)
     refs = list(refs)
     parts = [refs.pop(0) for _ in range(count)]
+    if after:
+        refs.pop(0)
     received = [refs.pop(0) for _ in first]
     blocks, pack = [], None
     if per:
@@ -622,22 +620,22 @@
             scratch=[pieces] if kind == "initial" else [],
         )
 
-    def assemble(kind, parts, payloads, blocks, more):
+    def assemble(kind, parts, payloads, blocks, more, after=()):
         messages = plan.messages(kind)
         got = transfer(messages[0], payloads)
         setup = kind == "initial" and plan.ride
         payloads = call(
-            functools.partial(middle_kernel, plan, kind, len(parts)),
+            functools.partial(middle_kernel, plan, kind, len(parts), bool(after)),
             plan.payload_shapes(kind, 1),
-            parts + got + blocks + (more if setup else []),
+            parts + list(after) + got + blocks + (more if setup else []),
             scratch=[acc] + ([pieces] * (1 + sum(m.faces for m in messages[0])) if setup else []),
         )
         return got + transfer(messages[1], payloads)
 
-    one, weight = call(
+    one, weight, turned = call(
         functools.partial(select_kernel, plan),
-        [shape(ROWS, IFACE, BF16), shape(ROWS, 128)],
-        [canon_rows.reshape(IFACE, 1)],
+        [shape(ROWS, IFACE, BF16), shape(ROWS, 128), shape(ROWS, 128)],
+        [canon_rows.reshape(IFACE, 1), basis],
         scratch=[pltpu.VMEM((ROWS, 1), jnp.int32)],
         flops=ROWS * IFACE * 1158,
     )
@@ -645,7 +643,6 @@
         (spread,) = call(
             functools.partial(spread_kernel, plan), [shape(8 * plan.setup, 128)], [coarse_inverse]
         )
-    (turned,) = call(turn_kernel, [shape(ROWS, 128)], [one, weight, basis])
     (early,) = call(
         functools.partial(gather_kernel, EARLY, 0), [shape(early_rows, 128)], [canon, load], specs=[smem, vm()]
     )
@@ -655,9 +652,6 @@
     flops = 2 * ROWS * IFACE * IFACE
     middle_shape, square = shape(ROWS, IFACE, BF16), shape(ROWS, ROWS, BF16)
 
-    def left_plain(one, matrix, mid):
-        left_kernel(one, matrix, None, None, mid, None)
-
     (half,) = call(
         left_kernel,
         [middle_shape],
@@ -665,7 +659,9 @@
         scratch=[pltpu.VMEM((16, IFACE), F32)],
         flops=flops,
     )
-    (inverse,) = call(right_kernel, [square], [one, half], flops=flops)
+    inverse, half = call(
+        right_left_kernel, [square, middle_shape], [one, half, schur_matrix[0, 0, 0]], flops=2 * flops
+    )
     blocks = []
     if plan.ride:
         blocks = spread_out("initial", spread)
@@ -686,7 +682,6 @@
             scratch=[pltpu.VMEM((plan.wide, plan.wide), F32), pltpu.VMEM((ROWS, plan.wide), F32), pieces],
             flops=2 * ROWS * 3 * plan.wide * plan.wide,
         )
-    (half,) = call(left_plain, [middle_shape], [one, schur_matrix[0, 0, 0]], flops=flops)
     (schur,) = call(right_kernel, [square], [one, half], flops=flops)
     sol = residual = None
     flops = 2 * ROWS * ROWS * 128
@@ -714,7 +709,7 @@
                 [shape(ROWS, 128)] + plan.payload_shapes("plain", 0),
                 [base, turned, jnp.pad(correction, ((0, 122), (0, 0)))],
             )
-        got = assemble("update", [base], payloads, blocks, [])
+        got = assemble("update", [base], payloads, blocks, [], [lift] if opening and plan.ride else [])
         update, rounded, early, *payloads = call(
             functools.partial(update_kernel, plan),
             [shape(ROWS, 128), shape(ROWS, 128, BF16), shape(early_rows, 128)] + plan.payload_shapes("plain", 0),

time: 139 us -> 138 us (level)
  starting transfers between devices: 65.4 us -> 59.7 us
  waiting for transfers between devices: 29.2 us -> 34.6 us
  Pallas kernels: 41.7 us -> 39.8 us
    ppermute x61, starting transfers between devices: 65.4 us -> 59.7 us  [transfer(): lax.ppermute(p, AXES, m.pairs())]
    ppermute x61, waiting for transfers between devices: 29.2 us -> 34.6 us  [transfer(): lax.ppermute(p, AXES, m.pairs())]
    pallas_call x35 -> x33, Pallas kernels: 41.7 us -> 39.8 us  [call(): pl.pallas_call(kernel, out_shape=tuple(outs), in_specs=specs or [vm()] *...]
  transfers between devices with their start and end apart: 61 -> 61, of which waited for: 17 -> 20; matrix products, arithmetic and copies ran while one was open for 1% -> 1% of each run, Pallas kernels for 24% -> 23%
where the time goes in v4:
time: 138 us
  starting transfers between devices  59.7 us (43%)
  Pallas kernels  39.8 us (29%)
  waiting for transfers between devices  34.6 us (25%)
  local copies, waits for them, and re-layouts  2.42 us (2%)
    ppermute x61, starting transfers between devices, transfer(): lax.ppermute(p, AXES, m.pairs())  59.7 us
    pallas_call x33, Pallas kernels, call(): pl.pallas_call(kernel, out_shape=tuple(outs), in_specs=specs or [vm()] *...  39.8 us
    ppermute x61, waiting for transfers between devices, transfer(): lax.ppermute(p, AXES, m.pairs())  34.6 us
  transfers between devices with their start and end apart: 61, of which 20 were waited for; matrix products, arithmetic and copies ran while one was open for 1% of the time, Pallas kernels for 23%

profile of v4, /device:TPU:1, one launch (start us, length us, event | category | flops | bytes accessed | tf_op | source)
XLA Modules:
  0.0 137.9 jit_solution(8018779037033683031)
XLA Ops:
  0.6 0.7 copy-done.2
  1.6 3.8 %collective-permute-start.1 = (f32[16,128]{1,0:T(8,128)S(1)}, f32[16,128]{1,0:T(8,128)S(1)}, u32[]{:S(2)}, u32[]{:S(2)}) collective-permute-start(f32[16,128]{1,0:T(8,128)S(1)} %shard_map.83.refs_1_.refs_4_), channel_id=1, source_target_pairs={{0,8},{1,9},{2,10},{3,11},{4,12},{5,13},{6,14},{7,15},{8,0},{9,1},... | collective-permute-start | bytes 24584 | tf_op jit(solution)/shard_map/ppermute | solution.py:263
  5.3 0.9 copy.10.canon
  6.3 0.8 copy-done.5
  7.1 1.8 %shard_map.77 = (bf16[1280,1158]{1,0:T(8,128)(2,1)S(1)}, f32[1280,128]{1,0:T(8,128)S(1)}, f32[1280,128]{1,0:T(8,128)S(1)}) custom-call(s32[1158,1]{1,0:T(8,128)S(1)} %copy.10.canon, bf16[6,1158]{1,0:T(8,128)(2,1)S(1)} %bitcast.21), custom_call_target="tpu_custom_call" | custom-call | flops 1716433920 | bytes 4293728 | tf_op jit(solution)/shard_map/pallas_call | solution.py:276
  8.9 1.0 shard_map.81.refs_0_
  10.1 1.6 %collective-permute-start.3 = (f32[336,128]{1,0:T(8,128)S(1)}, f32[336,128]{1,0:T(8,128)S(1)}, u32[]{:S(2)}, u32[]{:S(2)}) collective-permute-start(f32[336,128]{1,0:T(8,128)S(1)} %get-tuple-element.91), channel_id=1, source_target_pairs={{0,4},{1,5},{2,6},{3,7},{4,0},{5,1},{6,2},{7,3},{8,12},{9,13},{10,... | collective-permute-start | bytes 516104 | tf_op jit(solution)/shard_map/ppermute | solution.py:263
  12.2 4.4 %shard_map.78.mid = bf16[1280,1158]{1,0:T(8,128)(2,1)S(1)} custom-call(bf16[1280,1158]{1,0:T(8,128)(2,1)S(1)} %get-tuple-element.86.one, bf16[1158,1158]{1,0:T(8,128)(2,1)S(1)} %bitcast.19, f32[1280,128]{1,0:T(8,128)S(1)} %get-tuple-element.87.weight.refs_10_, bf16[6,1158]{1,0:T(8,128)(2,1)S(1)} %bitcast.22), custom_call_target="tpu_custom_call" | custom-call | flops 3432867840 | bytes 9280144 | tf_op jit(solution)/shard_map/pallas_call | solution.py:276
  16.7 1.2 shard_map.82.refs_1_
  18.3 1.6 %collective-permute-start.6 = (f32[400,128]{1,0:T(8,128)S(1)}, f32[400,128]{1,0:T(8,128)S(1)}, u32[]{:S(2)}, u32[]{:S(2)}) collective-permute-start(f32[400,128]{1,0:T(8,128)S(1)} %get-tuple-element.94), channel_id=1, source_target_pairs={{0,3},{1,2},{2,1},{3,0},{4,7},{5,6},{6,5},{7,4},{8,11},{9,10},{10,... | collective-permute-start | bytes 614408 | tf_op jit(solution)/shard_map/ppermute | solution.py:263
  19.9 1.2 collective-permute-start.7
  21.6 1.2 collective-permute-start.9
  22.8 8.9 %shard_map.79 = (bf16[1280,1280]{1,0:T(8,128)(2,1)S(1)}, bf16[1280,1158]{1,0:T(8,128)(2,1)S(1)}) custom-call(bf16[1280,1158]{1,0:T(8,128)(2,1)S(1)} %get-tuple-element.86.one, bf16[1280,1158]{1,0:T(8,128)(2,1)S(1)} %shard_map.78.mid, bf16[1158,1158]{1,0:T(8,128)(2,1)S(1)} %bitcast.20), custom_call_target="tpu_custom_call" | custom-call | flops 6865735680 | bytes 14852168 | tf_op jit(solution)/shard_map/pallas_call | solution.py:276
  32.5 1.0 shard_map.87.refs_0_
  33.5 2.9 %collective-permute-start.11 = (f32[264,128]{1,0:T(8,128)S(1)}, f32[264,128]{1,0:T(8,128)S(1)}, u32[]{:S(2)}, u32[]{:S(2)}) collective-permute-start(f32[264,128]{1,0:T(8,128)S(1)} %get-tuple-element.100), channel_id=1, source_target_pairs={{0,4},{1,5},{2,6},{3,7},{4,0},{5,1},{6,2},{7,3},{8,12},{9,13},{10,... | collective-permute-start | bytes 405512 | tf_op jit(solution)/shard_map/ppermute | solution.py:263
  36.9 0.8 collective-permute-start.13
  37.7 1.2 collective-permute-start.14
  38.9 2.3 %shard_map.89.refs_1_.refs_11_ = bf16[1280,768]{1,0:T(8,128)(2,1)S(1)} custom-call(f32[1280,128]{1,0:T(8,128)S(1)} %get-tuple-element.90.refs_5_.refs_8_.refs_0_, f32[16,128]{1,0:T(8,128)S(1)} %shard_map.83.refs_1_.refs_4_, f32[16,128]{1,0:T(8,128)S(1)} %collective-permute-done.refs_2_.refs_5_, f32[16,128]{1,0:T(8,128)S(1)} %collective-permute-done.1.refs_3_.refs_6_, ...), custom_call_target="tpu_custom_call" | custom-call | flops 503316480 | bytes 3637248 | tf_op jit(solution)/shard_map/pallas_call | solution.py:276
  41.2 0.8 collective-permute-done.14.refs_5_.refs_4_
  42.1 1.9 %collective-permute-start.15 = (f32[248,128]{1,0:T(8,128)S(1)}, f32[248,128]{1,0:T(8,128)S(1)}, u32[]{:S(2)}, u32[]{:S(2)}) collective-permute-start(f32[248,128]{1,0:T(8,128)S(1)} %get-tuple-element.104), channel_id=1, source_target_pairs={{0,1},{1,0},{2,3},{3,2},{4,5},{5,4},{6,7},{7,6},{8,9},{9,8},{10,11... | collective-permute-start | bytes 380936 | tf_op jit(solution)/shard_map/ppermute | solution.py:263
  44.0 1.2 collective-permute-start.16
  45.4 1.8 %collective-permute-start.18 = (f32[32,128]{1,0:T(8,128)S(1)}, f32[32,128]{1,0:T(8,128)S(1)}, u32[]{:S(2)}, u32[]{:S(2)}) collective-permute-start(f32[32,128]{1,0:T(8,128)S(1)} %get-tuple-element.107), channel_id=1, source_target_pairs={{0,17},{1,16},{2,19},{3,18},{4,21},{5,20},{6,23},{7,22},{8,25},{9,... | collective-permute-start | bytes 49160 | tf_op jit(solution)/shard_map/ppermute | solution.py:263
  47.3 4.4 %shard_map.80.refs_10_.matrix = bf16[1280,1280]{1,0:T(8,128)(2,1)S(1)} custom-call(bf16[1280,1158]{1,0:T(8,128)(2,1)S(1)} %get-tuple-element.86.one, bf16[1280,1158]{1,0:T(8,128)(2,1)S(1)} %get-tuple-element.88.mid), custom_call_target="tpu_custom_call" | custom-call | flops 3432867840 | bytes 9205760 | tf_op jit(solution)/shard_map/pallas_call | solution.py:276
  52.4 1.2 shard_map.91
  54.4 4.3 %collective-permute-done.20.refs_2_ = f32[248,128]{1,0:T(8,128)S(1)} collective-permute-done((f32[248,128]{1,0:T(8,128)S(1)}, f32[248,128]{1,0:T(8,128)S(1)}, u32[]{:S(2)}, u32[]{:S(2)}) %collective-permute-start.20) | collective-permute-done | bytes 127008 | tf_op jit(solution)/shard_map/ppermute | solution.py:263
  58.7 0.9 collective-permute-start.22
  59.6 1.2 collective-permute-start.23
  61.3 1.7 %collective-permute-start.25 = (f32[32,128]{1,0:T(8,128)S(1)}, f32[32,128]{1,0:T(8,128)S(1)}, u32[]{:S(2)}, u32[]{:S(2)}) collective-permute-start(f32[32,128]{1,0:T(8,128)S(1)} %get-tuple-element.118), channel_id=1, source_target_pairs={{0,17},{1,16},{2,19},{3,18},{4,21},{5,20},{6,23},{7,22},{8,25},{9,... | collective-permute-start | bytes 49160 | tf_op jit(solution)/shard_map/ppermute | solution.py:263
  63.0 1.3 collective-permute-start.26
  64.3 2.1 %collective-permute-done.25.refs_7_ = f32[32,128]{1,0:T(8,128)S(1)} collective-permute-done((f32[32,128]{1,0:T(8,128)S(1)}, f32[32,128]{1,0:T(8,128)S(1)}, u32[]{:S(2)}, u32[]{:S(2)}) %collective-permute-start.25) | collective-permute-done | bytes 16416 | tf_op jit(solution)/shard_map/ppermute | solution.py:263
  66.4 0.9 collective-permute-done.26.refs_8_
  67.7 1.0 shard_map.95.refs_0_
  68.9 0.7 collective-permute-start.28
  70.0 1.6 %collective-permute-start.30 = (f32[16,128]{1,0:T(8,128)S(1)}, f32[16,128]{1,0:T(8,128)S(1)}, u32[]{:S(2)}, u32[]{:S(2)}) collective-permute-start(f32[16,128]{1,0:T(8,128)S(1)} %get-tuple-element.125), channel_id=1, source_target_pairs={{0,8},{1,9},{2,10},{3,11},{4,12},{5,13},{6,14},{7,15},{8,0},{9,1},... | collective-permute-start | bytes 24584 | tf_op jit(solution)/shard_map/ppermute | solution.py:263
  71.6 1.5 %collective-permute-start.31 = (f32[16,128]{1,0:T(8,128)S(1)}, f32[16,128]{1,0:T(8,128)S(1)}, u32[]{:S(2)}, u32[]{:S(2)}) collective-permute-start(f32[16,128]{1,0:T(8,128)S(1)} %get-tuple-element.126), channel_id=1, source_target_pairs={{0,12},{1,13},{2,14},{3,15},{4,8},{5,9},{6,10},{7,11},{8,4},{9,5},... | collective-permute-start | bytes 24584 | tf_op jit(solution)/shard_map/ppermute | solution.py:263
  73.1 1.2 collective-permute-done.30.refs_3_
  74.3 1.6 %collective-permute-done.31.refs_4_ = f32[16,128]{1,0:T(8,128)S(1)} collective-permute-done((f32[16,128]{1,0:T(8,128)S(1)}, f32[16,128]{1,0:T(8,128)S(1)}, u32[]{:S(2)}, u32[]{:S(2)}) %collective-permute-start.31) | collective-permute-done | bytes 8224 | tf_op jit(solution)/shard_map/ppermute | solution.py:263
  76.0 3.0 %collective-permute-start.33 = (f32[312,128]{1,0:T(8,128)S(1)}, f32[312,128]{1,0:T(8,128)S(1)}, u32[]{:S(2)}, u32[]{:S(2)}) collective-permute-start(f32[312,128]{1,0:T(8,128)S(1)} %get-tuple-element.128), channel_id=1, source_target_pairs={{0,3},{1,2},{2,1},{3,0},{4,7},{5,6},{6,5},{7,4},{8,11},{9,10},{10,... | collective-permute-start | bytes 479240 | tf_op jit(solution)/shard_map/ppermute | solution.py:263
  79.5 1.9 %collective-permute-start.36 = (f32[96,128]{1,0:T(8,128)S(1)}, f32[96,128]{1,0:T(8,128)S(1)}, u32[]{:S(2)}, u32[]{:S(2)}) collective-permute-start(f32[96,128]{1,0:T(8,128)S(1)} %get-tuple-element.131), channel_id=1, source_target_pairs={{0,19},{1,18},{2,17},{3,16},{4,23},{5,22},{6,21},{7,20},{8,27},{9,... | collective-permute-start | bytes 147464 | tf_op jit(solution)/shard_map/ppermute | solution.py:263
  81.7 4.8 %collective-permute-done.35.refs_8_ = f32[32,128]{1,0:T(8,128)S(1)} collective-permute-done((f32[32,128]{1,0:T(8,128)S(1)}, f32[32,128]{1,0:T(8,128)S(1)}, u32[]{:S(2)}, u32[]{:S(2)}) %collective-permute-start.35) | collective-permute-done | bytes 16416 | tf_op jit(solution)/shard_map/ppermute | solution.py:263
  86.5 1.2 shard_map.98
  89.1 3.0 %collective-permute-done.37.refs_2_ = f32[248,128]{1,0:T(8,128)S(1)} collective-permute-done((f32[248,128]{1,0:T(8,128)S(1)}, f32[248,128]{1,0:T(8,128)S(1)}, u32[]{:S(2)}, u32[]{:S(2)}) %collective-permute-start.37) | collective-permute-done | bytes 127008 | tf_op jit(solution)/shard_map/ppermute | solution.py:263
  92.2 1.5 %collective-permute-start.39 = (f32[248,128]{1,0:T(8,128)S(1)}, f32[248,128]{1,0:T(8,128)S(1)}, u32[]{:S(2)}, u32[]{:S(2)}) collective-permute-start(f32[248,128]{1,0:T(8,128)S(1)} %get-tuple-element.139), channel_id=1, source_target_pairs={{0,1},{1,0},{2,3},{3,2},{4,5},{5,4},{6,7},{7,6},{8,9},{9,8},{10,11... | collective-permute-start | bytes 380936 | tf_op jit(solution)/shard_map/ppermute | solution.py:263
  93.7 0.8 collective-permute-start.40
  94.9 2.2 %collective-permute-start.42 = (f32[32,128]{1,0:T(8,128)S(1)}, f32[32,128]{1,0:T(8,128)S(1)}, u32[]{:S(2)}, u32[]{:S(2)}) collective-permute-start(f32[32,128]{1,0:T(8,128)S(1)} %get-tuple-element.142), channel_id=1, source_target_pairs={{0,17},{1,16},{2,19},{3,18},{4,21},{5,20},{6,23},{7,22},{8,25},{9,... | collective-permute-start | bytes 49160 | tf_op jit(solution)/shard_map/ppermute | solution.py:263
  97.1 0.7 collective-permute-start.43
  97.9 2.4 %collective-permute-done.42.refs_7_ = f32[32,128]{1,0:T(8,128)S(1)} collective-permute-done((f32[32,128]{1,0:T(8,128)S(1)}, f32[32,128]{1,0:T(8,128)S(1)}, u32[]{:S(2)}, u32[]{:S(2)}) %collective-permute-start.42) | collective-permute-done | bytes 16416 | tf_op jit(solution)/shard_map/ppermute | solution.py:263
  100.3 1.1 collective-permute-done.43.refs_8_
  101.8 1.0 shard_map.102.refs_0_
  104.0 1.6 %collective-permute-start.47 = (f32[16,128]{1,0:T(8,128)S(1)}, f32[16,128]{1,0:T(8,128)S(1)}, u32[]{:S(2)}, u32[]{:S(2)}) collective-permute-start(f32[16,128]{1,0:T(8,128)S(1)} %get-tuple-element.149), channel_id=1, source_target_pairs={{0,8},{1,9},{2,10},{3,11},{4,12},{5,13},{6,14},{7,15},{8,0},{9,1},... | collective-permute-start | bytes 24584 | tf_op jit(solution)/shard_map/ppermute | solution.py:263
  105.7 1.5 %collective-permute-start.48 = (f32[16,128]{1,0:T(8,128)S(1)}, f32[16,128]{1,0:T(8,128)S(1)}, u32[]{:S(2)}, u32[]{:S(2)}) collective-permute-start(f32[16,128]{1,0:T(8,128)S(1)} %get-tuple-element.150), channel_id=1, source_target_pairs={{0,12},{1,13},{2,14},{3,15},{4,8},{5,9},{6,10},{7,11},{8,4},{9,5},... | collective-permute-start | bytes 24584 | tf_op jit(solution)/shard_map/ppermute | solution.py:263
  107.2 1.2 collective-permute-done.47.refs_3_
  108.4 1.6 %collective-permute-done.48.refs_4_ = f32[16,128]{1,0:T(8,128)S(1)} collective-permute-done((f32[16,128]{1,0:T(8,128)S(1)}, f32[16,128]{1,0:T(8,128)S(1)}, u32[]{:S(2)}, u32[]{:S(2)}) %collective-permute-start.48) | collective-permute-done | bytes 8224 | tf_op jit(solution)/shard_map/ppermute | solution.py:263
  110.0 2.7 %collective-permute-start.50 = (f32[312,128]{1,0:T(8,128)S(1)}, f32[312,128]{1,0:T(8,128)S(1)}, u32[]{:S(2)}, u32[]{:S(2)}) collective-permute-start(f32[312,128]{1,0:T(8,128)S(1)} %get-tuple-element.152), channel_id=1, source_target_pairs={{0,3},{1,2},{2,1},{3,0},{4,7},{5,6},{6,5},{7,4},{8,11},{9,10},{10,... | collective-permute-start | bytes 479240 | tf_op jit(solution)/shard_map/ppermute | solution.py:263
  113.3 2.1 %collective-permute-start.53 = (f32[96,128]{1,0:T(8,128)S(1)}, f32[96,128]{1,0:T(8,128)S(1)}, u32[]{:S(2)}, u32[]{:S(2)}) collective-permute-start(f32[96,128]{1,0:T(8,128)S(1)} %get-tuple-element.155), channel_id=1, source_target_pairs={{0,19},{1,18},{2,17},{3,16},{4,23},{5,22},{6,21},{7,20},{8,27},{9,... | collective-permute-start | bytes 147464 | tf_op jit(solution)/shard_map/ppermute | solution.py:263
  115.7 4.6 %collective-permute-done.52.refs_8_ = f32[32,128]{1,0:T(8,128)S(1)} collective-permute-done((f32[32,128]{1,0:T(8,128)S(1)}, f32[32,128]{1,0:T(8,128)S(1)}, u32[]{:S(2)}, u32[]{:S(2)}) %collective-permute-start.52) | collective-permute-done | bytes 16416 | tf_op jit(solution)/shard_map/ppermute | solution.py:263
  120.3 1.2 shard_map.105
  123.1 3.1 %collective-permute-done.54.refs_2_.refs_0_ = f32[248,128]{1,0:T(8,128)S(1)} collective-permute-done((f32[248,128]{1,0:T(8,128)S(1)}, f32[248,128]{1,0:T(8,128)S(1)}, u32[]{:S(2)}, u32[]{:S(2)}) %collective-permute-start.54) | collective-permute-done | bytes 127008 | tf_op jit(solution)/shard_map/ppermute | solution.py:263
  126.3 1.5 %collective-permute-start.56 = (f32[248,128]{1,0:T(8,128)S(1)}, f32[248,128]{1,0:T(8,128)S(1)}, u32[]{:S(2)}, u32[]{:S(2)}) collective-permute-start(f32[248,128]{1,0:T(8,128)S(1)} %get-tuple-element.164), channel_id=1, source_target_pairs={{0,1},{1,0},{2,3},{3,2},{4,5},{5,4},{6,7},{7,6},{8,9},{9,8},{10,11... | collective-permute-start | bytes 380936 | tf_op jit(solution)/shard_map/ppermute | solution.py:263
  127.8 0.7 collective-permute-start.57
  128.8 2.4 %collective-permute-start.59 = (f32[32,128]{1,0:T(8,128)S(1)}, f32[32,128]{1,0:T(8,128)S(1)}, u32[]{:S(2)}, u32[]{:S(2)}) collective-permute-start(f32[32,128]{1,0:T(8,128)S(1)} %get-tuple-element.167), channel_id=1, source_target_pairs={{0,17},{1,16},{2,19},{3,18},{4,21},{5,20},{6,23},{7,22},{8,25},{9,... | collective-permute-start | bytes 49160 | tf_op jit(solution)/shard_map/ppermute | solution.py:263
  131.8 2.5 %shard_map.107 = f32[1158,1,128]{2,1,0:T(1,128)} custom-call(s32[1,1158]{1,0:T(1,128)S(1)} %bitcast.17, f32[1280,128]{1,0:T(8,128)S(1)} %get-tuple-element.159.acc), custom_call_target="tpu_custom_call" | custom-call | bytes 1252888 | tf_op jit(solution)/shard_map/pallas_call | solution.py:276
  134.4 0.9 collective-permute-done.60.refs_6_
  135.3 2.5 %shard_map.109 = f32[1158,1,128]{2,1,0:T(1,128)} custom-call(s32[1,1158]{1,0:T(1,128)S(1)} %bitcast.18, f32[576,128]{1,0:T(8,128)S(1)} %get-tuple-element.160.refs_0_.early, f32[704,128]{1,0:T(8,128)S(1)} %get-tuple-element.161.refs_1_.late, f32[248,128]{1,0:T(8,128)S(1)} %collective-permute-done.54.refs_2_.refs_0_, ...), custom_call_target="tpu_custom_call" | custom-call | bytes 2575896 | tf_op jit(solution)/shard_map/pallas_call | solution.py:276
  (106 shorter events, 14.2 us)
Async XLA Ops:
  1.5 8.5 %collective-permute-start = (f32[16,128]{1,0:T(8,128)S(1)}, f32[16,128]{1,0:T(8,128)S(1)}, u32[]{:S(2)}, u32[]{:S(2)}) collective-permute-start(f32[16,128]{1,0:T(8,128)S(1)} %shard_map.83.refs_1_.refs_4_), channel_id=1, source_target_pairs={{0,1},{1,0},{2,3},{3,2},{4,5},{5,4},{6,7},{7,6},{8,9},{9,8},{10,11... | collective-permute-start | bytes 24584 | tf_op jit(solution)/shard_map/ppermute | solution.py:263
  1.6 8.4 %collective-permute-start.1 = (f32[16,128]{1,0:T(8,128)S(1)}, f32[16,128]{1,0:T(8,128)S(1)}, u32[]{:S(2)}, u32[]{:S(2)}) collective-permute-start(f32[16,128]{1,0:T(8,128)S(1)} %shard_map.83.refs_1_.refs_4_), channel_id=1, source_target_pairs={{0,8},{1,9},{2,10},{3,11},{4,12},{5,13},{6,14},{7,15},{8,0},{9,1},... | collective-permute-start | bytes 24584 | tf_op jit(solution)/shard_map/ppermute | solution.py:263
  5.3 4.6 %collective-permute-start.2 = (f32[16,128]{1,0:T(8,128)S(1)}, f32[16,128]{1,0:T(8,128)S(1)}, u32[]{:S(2)}, u32[]{:S(2)}) collective-permute-start(f32[16,128]{1,0:T(8,128)S(1)} %shard_map.83.refs_1_.refs_4_), channel_id=1, source_target_pairs={{0,9},{1,8},{2,11},{3,10},{4,13},{5,12},{6,15},{7,14},{8,1},{9,0},... | collective-permute-start | bytes 24584 | tf_op jit(solution)/shard_map/ppermute | solution.py:263
  7.1 5.1 %copy-start.3 = (bf16[1,1,1,1158,1158]{4,3,2,1,0:T(8,128)(2,1)S(1)}, bf16[1,1,1,1158,1158]{4,3,2,1,0:T(8,128)(2,1)}, u32[]{:S(2)}) copy-start(bf16[1,1,1,1158,1158]{4,3,2,1,0:T(8,128)(2,1)} %param.8) | copy-start | bytes 8045788
  7.1 5.1 %copy-start.6 = (bf16[1,1,1,6,1158]{4,3,2,1,0:T(8,128)(2,1)S(1)}, bf16[1,1,1,6,1158]{4,3,2,1,0:T(8,128)(2,1)}, u32[]{:S(2)}) copy-start(bf16[1,1,1,6,1158]{4,3,2,1,0:T(8,128)(2,1)} %param.9) | copy-start | bytes 41692
  10.1 7.7 %collective-permute-start.3 = (f32[336,128]{1,0:T(8,128)S(1)}, f32[336,128]{1,0:T(8,128)S(1)}, u32[]{:S(2)}, u32[]{:S(2)}) collective-permute-start(f32[336,128]{1,0:T(8,128)S(1)} %get-tuple-element.91), channel_id=1, source_target_pairs={{0,4},{1,5},{2,6},{3,7},{4,0},{5,1},{6,2},{7,3},{8,12},{9,13},{10,... | collective-permute-start | bytes 516104 | tf_op jit(solution)/shard_map/ppermute | solution.py:263
  11.7 6.1 %collective-permute-start.4 = (f32[272,128]{1,0:T(8,128)S(1)}, f32[272,128]{1,0:T(8,128)S(1)}, u32[]{:S(2)}, u32[]{:S(2)}) collective-permute-start(f32[272,128]{1,0:T(8,128)S(1)} %get-tuple-element.92), channel_id=1, source_target_pairs={{0,1},{1,0},{2,3},{3,2},{4,8},{5,9},{6,10},{7,11},{8,4},{9,5},{10,... | collective-permute-start | bytes 417800 | tf_op jit(solution)/shard_map/ppermute | solution.py:263
  12.2 10.6 %copy-start.4 = (bf16[1,1,1,1158,1158]{4,3,2,1,0:T(8,128)(2,1)S(1)}, bf16[1,1,1,1158,1158]{4,3,2,1,0:T(8,128)(2,1)}, u32[]{:S(2)}) copy-start(bf16[1,1,1,1158,1158]{4,3,2,1,0:T(8,128)(2,1)} %param.7) | copy-start | bytes 8045788
  18.2 13.6 %collective-permute-start.5 = (f32[272,128]{1,0:T(8,128)S(1)}, f32[272,128]{1,0:T(8,128)S(1)}, u32[]{:S(2)}, u32[]{:S(2)}) collective-permute-start(f32[272,128]{1,0:T(8,128)S(1)} %get-tuple-element.93), channel_id=1, source_target_pairs={{0,1},{1,0},{2,3},{3,2},{4,5},{5,4},{6,7},{7,6},{8,9},{9,8},{10,11... | collective-permute-start | bytes 417800 | tf_op jit(solution)/shard_map/ppermute | solution.py:263
  18.3 13.5 %collective-permute-start.6 = (f32[400,128]{1,0:T(8,128)S(1)}, f32[400,128]{1,0:T(8,128)S(1)}, u32[]{:S(2)}, u32[]{:S(2)}) collective-permute-start(f32[400,128]{1,0:T(8,128)S(1)} %get-tuple-element.94), channel_id=1, source_target_pairs={{0,3},{1,2},{2,1},{3,0},{4,7},{5,6},{6,5},{7,4},{8,11},{9,10},{10,... | collective-permute-start | bytes 614408 | tf_op jit(solution)/shard_map/ppermute | solution.py:263
  19.9 11.9 %collective-permute-start.7 = (f32[400,128]{1,0:T(8,128)S(1)}, f32[400,128]{1,0:T(8,128)S(1)}, u32[]{:S(2)}, u32[]{:S(2)}) collective-permute-start(f32[400,128]{1,0:T(8,128)S(1)} %get-tuple-element.95), channel_id=1, source_target_pairs={{0,16},{1,17},{2,18},{3,19},{4,20},{5,21},{6,22},{7,23},{8,24},{9,... | collective-permute-start | bytes 614408 | tf_op jit(solution)/shard_map/ppermute | solution.py:263
  21.1 10.6 %collective-permute-start.8 = (f32[56,128]{1,0:T(8,128)S(1)}, f32[56,128]{1,0:T(8,128)S(1)}, u32[]{:S(2)}, u32[]{:S(2)}) collective-permute-start(f32[56,128]{1,0:T(8,128)S(1)} %get-tuple-element.96), channel_id=1, source_target_pairs={{0,17},{1,16},{2,19},{3,18},{4,21},{5,20},{6,23},{7,22},{8,25},{9,... | collective-permute-start | bytes 86024 | tf_op jit(solution)/shard_map/ppermute | solution.py:263
  21.6 10.1 %collective-permute-start.9 = (f32[184,128]{1,0:T(8,128)S(1)}, f32[184,128]{1,0:T(8,128)S(1)}, u32[]{:S(2)}, u32[]{:S(2)}) collective-permute-start(f32[184,128]{1,0:T(8,128)S(1)} %get-tuple-element.97), channel_id=1, source_target_pairs={{0,19},{1,18},{2,17},{3,16},{4,23},{5,22},{6,21},{7,20},{8,27},{9,... | collective-permute-start | bytes 282632 | tf_op jit(solution)/shard_map/ppermute | solution.py:263
  32.1 1.4 collective-permute-start.10
  33.5 8.4 %collective-permute-start.11 = (f32[264,128]{1,0:T(8,128)S(1)}, f32[264,128]{1,0:T(8,128)S(1)}, u32[]{:S(2)}, u32[]{:S(2)}) collective-permute-start(f32[264,128]{1,0:T(8,128)S(1)} %get-tuple-element.100), channel_id=1, source_target_pairs={{0,4},{1,5},{2,6},{3,7},{4,0},{5,1},{6,2},{7,3},{8,12},{9,13},{10,... | collective-permute-start | bytes 405512 | tf_op jit(solution)/shard_map/ppermute | solution.py:263
  36.4 5.6 %collective-permute-start.12 = (f32[248,128]{1,0:T(8,128)S(1)}, f32[248,128]{1,0:T(8,128)S(1)}, u32[]{:S(2)}, u32[]{:S(2)}) collective-permute-start(f32[248,128]{1,0:T(8,128)S(1)} %get-tuple-element.101), channel_id=1, source_target_pairs={{0,1},{1,0},{2,3},{3,2},{4,8},{5,9},{6,10},{7,11},{8,4},{9,5},{10,... | collective-permute-start | bytes 380936 | tf_op jit(solution)/shard_map/ppermute | solution.py:263
  36.9 4.3 %collective-permute-start.13 = (f32[16,128]{1,0:T(8,128)S(1)}, f32[16,128]{1,0:T(8,128)S(1)}, u32[]{:S(2)}, u32[]{:S(2)}) collective-permute-start(f32[16,128]{1,0:T(8,128)S(1)} %get-tuple-element.102), channel_id=1, source_target_pairs={{0,8},{1,9},{2,10},{3,11},{4,12},{5,13},{6,14},{7,15},{8,0},{9,1},... | collective-permute-start | bytes 24584 | tf_op jit(solution)/shard_map/ppermute | solution.py:263
  37.7 4.3 %collective-permute-start.14 = (f32[16,128]{1,0:T(8,128)S(1)}, f32[16,128]{1,0:T(8,128)S(1)}, u32[]{:S(2)}, u32[]{:S(2)}) collective-permute-start(f32[16,128]{1,0:T(8,128)S(1)} %get-tuple-element.103), channel_id=1, source_target_pairs={{0,12},{1,13},{2,14},{3,15},{4,8},{5,9},{6,10},{7,11},{8,4},{9,5},... | collective-permute-start | bytes 24584 | tf_op jit(solution)/shard_map/ppermute | solution.py:263
  42.1 10.3 %collective-permute-start.15 = (f32[248,128]{1,0:T(8,128)S(1)}, f32[248,128]{1,0:T(8,128)S(1)}, u32[]{:S(2)}, u32[]{:S(2)}) collective-permute-start(f32[248,128]{1,0:T(8,128)S(1)} %get-tuple-element.104), channel_id=1, source_target_pairs={{0,1},{1,0},{2,3},{3,2},{4,5},{5,4},{6,7},{7,6},{8,9},{9,8},{10,11... | collective-permute-start | bytes 380936 | tf_op jit(solution)/shard_map/ppermute | solution.py:263
  44.0 8.4 %collective-permute-start.16 = (f32[312,128]{1,0:T(8,128)S(1)}, f32[312,128]{1,0:T(8,128)S(1)}, u32[]{:S(2)}, u32[]{:S(2)}) collective-permute-start(f32[312,128]{1,0:T(8,128)S(1)} %get-tuple-element.105), channel_id=1, source_target_pairs={{0,3},{1,2},{2,1},{3,0},{4,7},{5,6},{6,5},{7,4},{8,11},{9,10},{10,... | collective-permute-start | bytes 479240 | tf_op jit(solution)/shard_map/ppermute | solution.py:263
  45.2 7.2 %collective-permute-start.17 = (f32[312,128]{1,0:T(8,128)S(1)}, f32[312,128]{1,0:T(8,128)S(1)}, u32[]{:S(2)}, u32[]{:S(2)}) collective-permute-start(f32[312,128]{1,0:T(8,128)S(1)} %get-tuple-element.106), channel_id=1, source_target_pairs={{0,16},{1,17},{2,18},{3,19},{4,20},{5,21},{6,22},{7,23},{8,24},{9,... | collective-permute-start | bytes 479240 | tf_op jit(solution)/shard_map/ppermute | solution.py:263
  45.4 6.6 %collective-permute-start.18 = (f32[32,128]{1,0:T(8,128)S(1)}, f32[32,128]{1,0:T(8,128)S(1)}, u32[]{:S(2)}, u32[]{:S(2)}) collective-permute-start(f32[32,128]{1,0:T(8,128)S(1)} %get-tuple-element.107), channel_id=1, source_target_pairs={{0,17},{1,16},{2,19},{3,18},{4,21},{5,20},{6,23},{7,22},{8,25},{9,... | collective-permute-start | bytes 49160 | tf_op jit(solution)/shard_map/ppermute | solution.py:263
  47.3 5.1 %collective-permute-start.19 = (f32[96,128]{1,0:T(8,128)S(1)}, f32[96,128]{1,0:T(8,128)S(1)}, u32[]{:S(2)}, u32[]{:S(2)}) collective-permute-start(f32[96,128]{1,0:T(8,128)S(1)} %get-tuple-element.108), channel_id=1, source_target_pairs={{0,19},{1,18},{2,17},{3,16},{4,23},{5,22},{6,21},{7,20},{8,27},{9,... | collective-permute-start | bytes 147464 | tf_op jit(solution)/shard_map/ppermute | solution.py:263
  53.6 5.1 %collective-permute-start.20 = (f32[248,128]{1,0:T(8,128)S(1)}, f32[248,128]{1,0:T(8,128)S(1)}, u32[]{:S(2)}, u32[]{:S(2)}) collective-permute-start(f32[248,128]{1,0:T(8,128)S(1)} %get-tuple-element.113), channel_id=1, source_target_pairs={{0,4},{1,5},{2,6},{3,7},{4,0},{5,1},{6,2},{7,3},{8,12},{9,13},{10,... | collective-permute-start | bytes 380936 | tf_op jit(solution)/shard_map/ppermute | solution.py:263
  53.6 5.0 %collective-permute-start.21 = (f32[248,128]{1,0:T(8,128)S(1)}, f32[248,128]{1,0:T(8,128)S(1)}, u32[]{:S(2)}, u32[]{:S(2)}) collective-permute-start(f32[248,128]{1,0:T(8,128)S(1)} %get-tuple-element.114), channel_id=1, source_target_pairs={{0,1},{1,0},{2,3},{3,2},{4,8},{5,9},{6,10},{7,11},{8,4},{9,5},{10,... | collective-permute-start | bytes 380936 | tf_op jit(solution)/shard_map/ppermute | solution.py:263
  58.7 8.6 %collective-permute-start.22 = (f32[248,128]{1,0:T(8,128)S(1)}, f32[248,128]{1,0:T(8,128)S(1)}, u32[]{:S(2)}, u32[]{:S(2)}) collective-permute-start(f32[248,128]{1,0:T(8,128)S(1)} %get-tuple-element.115), channel_id=1, source_target_pairs={{0,1},{1,0},{2,3},{3,2},{4,5},{5,4},{6,7},{7,6},{8,9},{9,8},{10,11... | collective-permute-start | bytes 380936 | tf_op jit(solution)/shard_map/ppermute | solution.py:263
  59.6 7.7 %collective-permute-start.23 = (f32[248,128]{1,0:T(8,128)S(1)}, f32[248,128]{1,0:T(8,128)S(1)}, u32[]{:S(2)}, u32[]{:S(2)}) collective-permute-start(f32[248,128]{1,0:T(8,128)S(1)} %get-tuple-element.116), channel_id=1, source_target_pairs={{0,4},{1,2},{2,1},{3,7},{4,0},{5,6},{6,5},{7,3},{8,12},{9,10},{10,... | collective-permute-start | bytes 380936 | tf_op jit(solution)/shard_map/ppermute | solution.py:263
  60.8 6.5 %collective-permute-start.24 = (f32[248,128]{1,0:T(8,128)S(1)}, f32[248,128]{1,0:T(8,128)S(1)}, u32[]{:S(2)}, u32[]{:S(2)}) collective-permute-start(f32[248,128]{1,0:T(8,128)S(1)} %get-tuple-element.117), channel_id=1, source_target_pairs={{0,16},{1,17},{2,18},{3,19},{4,20},{5,21},{6,22},{7,23},{8,24},{9,... | collective-permute-start | bytes 380936 | tf_op jit(solution)/shard_map/ppermute | solution.py:263
  61.3 5.1 %collective-permute-start.25 = (f32[32,128]{1,0:T(8,128)S(1)}, f32[32,128]{1,0:T(8,128)S(1)}, u32[]{:S(2)}, u32[]{:S(2)}) collective-permute-start(f32[32,128]{1,0:T(8,128)S(1)} %get-tuple-element.118), channel_id=1, source_target_pairs={{0,17},{1,16},{2,19},{3,18},{4,21},{5,20},{6,23},{7,22},{8,25},{9,... | collective-permute-start | bytes 49160 | tf_op jit(solution)/shard_map/ppermute | solution.py:263
  63.0 4.2 %collective-permute-start.26 = (f32[32,128]{1,0:T(8,128)S(1)}, f32[32,128]{1,0:T(8,128)S(1)}, u32[]{:S(2)}, u32[]{:S(2)}) collective-permute-start(f32[32,128]{1,0:T(8,128)S(1)} %get-tuple-element.119), channel_id=1, source_target_pairs={{0,4},{1,18},{2,17},{3,7},{4,0},{5,22},{6,21},{7,3},{8,12},{9,26},... | collective-permute-start | bytes 49160 | tf_op jit(solution)/shard_map/ppermute | solution.py:263
  67.7 1.2 collective-permute-start.27
  68.9 7.0 %collective-permute-start.28 = (f32[264,128]{1,0:T(8,128)S(1)}, f32[264,128]{1,0:T(8,128)S(1)}, u32[]{:S(2)}, u32[]{:S(2)}) collective-permute-start(f32[264,128]{1,0:T(8,128)S(1)} %get-tuple-element.123), channel_id=1, source_target_pairs={{0,4},{1,5},{2,6},{3,7},{4,0},{5,1},{6,2},{7,3},{8,12},{9,13},{10,... | collective-permute-start | bytes 405512 | tf_op jit(solution)/shard_map/ppermute | solution.py:263
  69.6 6.3 %collective-permute-start.29 = (f32[248,128]{1,0:T(8,128)S(1)}, f32[248,128]{1,0:T(8,128)S(1)}, u32[]{:S(2)}, u32[]{:S(2)}) collective-permute-start(f32[248,128]{1,0:T(8,128)S(1)} %get-tuple-element.124), channel_id=1, source_target_pairs={{0,1},{1,0},{2,3},{3,2},{4,8},{5,9},{6,10},{7,11},{8,4},{9,5},{10,... | collective-permute-start | bytes 380936 | tf_op jit(solution)/shard_map/ppermute | solution.py:263
  70.0 4.3 %collective-permute-start.30 = (f32[16,128]{1,0:T(8,128)S(1)}, f32[16,128]{1,0:T(8,128)S(1)}, u32[]{:S(2)}, u32[]{:S(2)}) collective-permute-start(f32[16,128]{1,0:T(8,128)S(1)} %get-tuple-element.125), channel_id=1, source_target_pairs={{0,8},{1,9},{2,10},{3,11},{4,12},{5,13},{6,14},{7,15},{8,0},{9,1},... | collective-permute-start | bytes 24584 | tf_op jit(solution)/shard_map/ppermute | solution.py:263
  71.6 4.3 %collective-permute-start.31 = (f32[16,128]{1,0:T(8,128)S(1)}, f32[16,128]{1,0:T(8,128)S(1)}, u32[]{:S(2)}, u32[]{:S(2)}) collective-permute-start(f32[16,128]{1,0:T(8,128)S(1)} %get-tuple-element.126), channel_id=1, source_target_pairs={{0,12},{1,13},{2,14},{3,15},{4,8},{5,9},{6,10},{7,11},{8,4},{9,5},... | collective-permute-start | bytes 24584 | tf_op jit(solution)/shard_map/ppermute | solution.py:263
  76.0 10.5 %collective-permute-start.33 = (f32[312,128]{1,0:T(8,128)S(1)}, f32[312,128]{1,0:T(8,128)S(1)}, u32[]{:S(2)}, u32[]{:S(2)}) collective-permute-start(f32[312,128]{1,0:T(8,128)S(1)} %get-tuple-element.128), channel_id=1, source_target_pairs={{0,3},{1,2},{2,1},{3,0},{4,7},{5,6},{6,5},{7,4},{8,11},{9,10},{10,... | collective-permute-start | bytes 479240 | tf_op jit(solution)/shard_map/ppermute | solution.py:263
  79.0 7.5 %collective-permute-start.34 = (f32[312,128]{1,0:T(8,128)S(1)}, f32[312,128]{1,0:T(8,128)S(1)}, u32[]{:S(2)}, u32[]{:S(2)}) collective-permute-start(f32[312,128]{1,0:T(8,128)S(1)} %get-tuple-element.129), channel_id=1, source_target_pairs={{0,16},{1,17},{2,18},{3,19},{4,20},{5,21},{6,22},{7,23},{8,24},{9,... | collective-permute-start | bytes 479240 | tf_op jit(solution)/shard_map/ppermute | solution.py:263
  79.5 7.0 %collective-permute-start.32 = (f32[248,128]{1,0:T(8,128)S(1)}, f32[248,128]{1,0:T(8,128)S(1)}, u32[]{:S(2)}, u32[]{:S(2)}) collective-permute-start(f32[248,128]{1,0:T(8,128)S(1)} %get-tuple-element.127), channel_id=1, source_target_pairs={{0,1},{1,0},{2,3},{3,2},{4,5},{5,4},{6,7},{7,6},{8,9},{9,8},{10,11... | collective-permute-start | bytes 380936 | tf_op jit(solution)/shard_map/ppermute | solution.py:263
  79.5 7.0 %collective-permute-start.36 = (f32[96,128]{1,0:T(8,128)S(1)}, f32[96,128]{1,0:T(8,128)S(1)}, u32[]{:S(2)}, u32[]{:S(2)}) collective-permute-start(f32[96,128]{1,0:T(8,128)S(1)} %get-tuple-element.131), channel_id=1, source_target_pairs={{0,19},{1,18},{2,17},{3,16},{4,23},{5,22},{6,21},{7,20},{8,27},{9,... | collective-permute-start | bytes 147464 | tf_op jit(solution)/shard_map/ppermute | solution.py:263
  81.4 5.1 %collective-permute-start.35 = (f32[32,128]{1,0:T(8,128)S(1)}, f32[32,128]{1,0:T(8,128)S(1)}, u32[]{:S(2)}, u32[]{:S(2)}) collective-permute-start(f32[32,128]{1,0:T(8,128)S(1)} %get-tuple-element.130), channel_id=1, source_target_pairs={{0,17},{1,16},{2,19},{3,18},{4,21},{5,20},{6,23},{7,22},{8,25},{9,... | collective-permute-start | bytes 49160 | tf_op jit(solution)/shard_map/ppermute | solution.py:263
  87.7 4.4 %collective-permute-start.37 = (f32[248,128]{1,0:T(8,128)S(1)}, f32[248,128]{1,0:T(8,128)S(1)}, u32[]{:S(2)}, u32[]{:S(2)}) collective-permute-start(f32[248,128]{1,0:T(8,128)S(1)} %get-tuple-element.137), channel_id=1, source_target_pairs={{0,4},{1,5},{2,6},{3,7},{4,0},{5,1},{6,2},{7,3},{8,12},{9,13},{10,... | collective-permute-start | bytes 380936 | tf_op jit(solution)/shard_map/ppermute | solution.py:263
  87.7 4.4 %collective-permute-start.38 = (f32[248,128]{1,0:T(8,128)S(1)}, f32[248,128]{1,0:T(8,128)S(1)}, u32[]{:S(2)}, u32[]{:S(2)}) collective-permute-start(f32[248,128]{1,0:T(8,128)S(1)} %get-tuple-element.138), channel_id=1, source_target_pairs={{0,1},{1,0},{2,3},{3,2},{4,8},{5,9},{6,10},{7,11},{8,4},{9,5},{10,... | collective-permute-start | bytes 380936 | tf_op jit(solution)/shard_map/ppermute | solution.py:263
  92.2 9.2 %collective-permute-start.39 = (f32[248,128]{1,0:T(8,128)S(1)}, f32[248,128]{1,0:T(8,128)S(1)}, u32[]{:S(2)}, u32[]{:S(2)}) collective-permute-start(f32[248,128]{1,0:T(8,128)S(1)} %get-tuple-element.139), channel_id=1, source_target_pairs={{0,1},{1,0},{2,3},{3,2},{4,5},{5,4},{6,7},{7,6},{8,9},{9,8},{10,11... | collective-permute-start | bytes 380936 | tf_op jit(solution)/shard_map/ppermute | solution.py:263
  93.7 7.7 %collective-permute-start.40 = (f32[248,128]{1,0:T(8,128)S(1)}, f32[248,128]{1,0:T(8,128)S(1)}, u32[]{:S(2)}, u32[]{:S(2)}) collective-permute-start(f32[248,128]{1,0:T(8,128)S(1)} %get-tuple-element.140), channel_id=1, source_target_pairs={{0,4},{1,2},{2,1},{3,7},{4,0},{5,6},{6,5},{7,3},{8,12},{9,10},{10,... | collective-permute-start | bytes 380936 | tf_op jit(solution)/shard_map/ppermute | solution.py:263
  94.5 6.9 %collective-permute-start.41 = (f32[248,128]{1,0:T(8,128)S(1)}, f32[248,128]{1,0:T(8,128)S(1)}, u32[]{:S(2)}, u32[]{:S(2)}) collective-permute-start(f32[248,128]{1,0:T(8,128)S(1)} %get-tuple-element.141), channel_id=1, source_target_pairs={{0,16},{1,17},{2,18},{3,19},{4,20},{5,21},{6,22},{7,23},{8,24},{9,... | collective-permute-start | bytes 380936 | tf_op jit(solution)/shard_map/ppermute | solution.py:263
  94.9 5.4 %collective-permute-start.42 = (f32[32,128]{1,0:T(8,128)S(1)}, f32[32,128]{1,0:T(8,128)S(1)}, u32[]{:S(2)}, u32[]{:S(2)}) collective-permute-start(f32[32,128]{1,0:T(8,128)S(1)} %get-tuple-element.142), channel_id=1, source_target_pairs={{0,17},{1,16},{2,19},{3,18},{4,21},{5,20},{6,23},{7,22},{8,25},{9,... | collective-permute-start | bytes 49160 | tf_op jit(solution)/shard_map/ppermute | solution.py:263
  97.1 4.2 %collective-permute-start.43 = (f32[32,128]{1,0:T(8,128)S(1)}, f32[32,128]{1,0:T(8,128)S(1)}, u32[]{:S(2)}, u32[]{:S(2)}) collective-permute-start(f32[32,128]{1,0:T(8,128)S(1)} %get-tuple-element.143), channel_id=1, source_target_pairs={{0,4},{1,18},{2,17},{3,7},{4,0},{5,22},{6,21},{7,3},{8,12},{9,26},... | collective-permute-start | bytes 49160 | tf_op jit(solution)/shard_map/ppermute | solution.py:263
  101.8 1.2 collective-permute-start.44
  103.0 7.0 %collective-permute-start.45 = (f32[264,128]{1,0:T(8,128)S(1)}, f32[264,128]{1,0:T(8,128)S(1)}, u32[]{:S(2)}, u32[]{:S(2)}) collective-permute-start(f32[264,128]{1,0:T(8,128)S(1)} %get-tuple-element.147), channel_id=1, source_target_pairs={{0,4},{1,5},{2,6},{3,7},{4,0},{5,1},{6,2},{7,3},{8,12},{9,13},{10,... | collective-permute-start | bytes 405512 | tf_op jit(solution)/shard_map/ppermute | solution.py:263
  103.6 6.4 %collective-permute-start.46 = (f32[248,128]{1,0:T(8,128)S(1)}, f32[248,128]{1,0:T(8,128)S(1)}, u32[]{:S(2)}, u32[]{:S(2)}) collective-permute-start(f32[248,128]{1,0:T(8,128)S(1)} %get-tuple-element.148), channel_id=1, source_target_pairs={{0,1},{1,0},{2,3},{3,2},{4,8},{5,9},{6,10},{7,11},{8,4},{9,5},{10,... | collective-permute-start | bytes 380936 | tf_op jit(solution)/shard_map/ppermute | solution.py:263
  104.0 4.3 %collective-permute-start.47 = (f32[16,128]{1,0:T(8,128)S(1)}, f32[16,128]{1,0:T(8,128)S(1)}, u32[]{:S(2)}, u32[]{:S(2)}) collective-permute-start(f32[16,128]{1,0:T(8,128)S(1)} %get-tuple-element.149), channel_id=1, source_target_pairs={{0,8},{1,9},{2,10},{3,11},{4,12},{5,13},{6,14},{7,15},{8,0},{9,1},... | collective-permute-start | bytes 24584 | tf_op jit(solution)/shard_map/ppermute | solution.py:263
  105.7 4.3 %collective-permute-start.48 = (f32[16,128]{1,0:T(8,128)S(1)}, f32[16,128]{1,0:T(8,128)S(1)}, u32[]{:S(2)}, u32[]{:S(2)}) collective-permute-start(f32[16,128]{1,0:T(8,128)S(1)} %get-tuple-element.150), channel_id=1, source_target_pairs={{0,12},{1,13},{2,14},{3,15},{4,8},{5,9},{6,10},{7,11},{8,4},{9,5},... | collective-permute-start | bytes 24584 | tf_op jit(solution)/shard_map/ppermute | solution.py:263
  110.0 10.3 %collective-permute-start.50 = (f32[312,128]{1,0:T(8,128)S(1)}, f32[312,128]{1,0:T(8,128)S(1)}, u32[]{:S(2)}, u32[]{:S(2)}) collective-permute-start(f32[312,128]{1,0:T(8,128)S(1)} %get-tuple-element.152), channel_id=1, source_target_pairs={{0,3},{1,2},{2,1},{3,0},{4,7},{5,6},{6,5},{7,4},{8,11},{9,10},{10,... | collective-permute-start | bytes 479240 | tf_op jit(solution)/shard_map/ppermute | solution.py:263
  112.8 7.6 %collective-permute-start.51 = (f32[312,128]{1,0:T(8,128)S(1)}, f32[312,128]{1,0:T(8,128)S(1)}, u32[]{:S(2)}, u32[]{:S(2)}) collective-permute-start(f32[312,128]{1,0:T(8,128)S(1)} %get-tuple-element.153), channel_id=1, source_target_pairs={{0,16},{1,17},{2,18},{3,19},{4,20},{5,21},{6,22},{7,23},{8,24},{9,... | collective-permute-start | bytes 479240 | tf_op jit(solution)/shard_map/ppermute | solution.py:263
  113.2 7.1 %collective-permute-start.49 = (f32[248,128]{1,0:T(8,128)S(1)}, f32[248,128]{1,0:T(8,128)S(1)}, u32[]{:S(2)}, u32[]{:S(2)}) collective-permute-start(f32[248,128]{1,0:T(8,128)S(1)} %get-tuple-element.151), channel_id=1, source_target_pairs={{0,1},{1,0},{2,3},{3,2},{4,5},{5,4},{6,7},{7,6},{8,9},{9,8},{10,11... | collective-permute-start | bytes 380936 | tf_op jit(solution)/shard_map/ppermute | solution.py:263
  113.3 7.1 %collective-permute-start.53 = (f32[96,128]{1,0:T(8,128)S(1)}, f32[96,128]{1,0:T(8,128)S(1)}, u32[]{:S(2)}, u32[]{:S(2)}) collective-permute-start(f32[96,128]{1,0:T(8,128)S(1)} %get-tuple-element.155), channel_id=1, source_target_pairs={{0,19},{1,18},{2,17},{3,16},{4,23},{5,22},{6,21},{7,20},{8,27},{9,... | collective-permute-start | bytes 147464 | tf_op jit(solution)/shard_map/ppermute | solution.py:263
  115.4 4.9 %collective-permute-start.52 = (f32[32,128]{1,0:T(8,128)S(1)}, f32[32,128]{1,0:T(8,128)S(1)}, u32[]{:S(2)}, u32[]{:S(2)}) collective-permute-start(f32[32,128]{1,0:T(8,128)S(1)} %get-tuple-element.154), channel_id=1, source_target_pairs={{0,17},{1,16},{2,19},{3,18},{4,21},{5,20},{6,23},{7,22},{8,25},{9,... | collective-permute-start | bytes 49160 | tf_op jit(solution)/shard_map/ppermute | solution.py:263
  121.7 4.4 %collective-permute-start.54 = (f32[248,128]{1,0:T(8,128)S(1)}, f32[248,128]{1,0:T(8,128)S(1)}, u32[]{:S(2)}, u32[]{:S(2)}) collective-permute-start(f32[248,128]{1,0:T(8,128)S(1)} %get-tuple-element.162), channel_id=1, source_target_pairs={{0,4},{1,5},{2,6},{3,7},{4,0},{5,1},{6,2},{7,3},{8,12},{9,13},{10,... | collective-permute-start | bytes 380936 | tf_op jit(solution)/shard_map/ppermute | solution.py:263
  121.8 4.4 %collective-permute-start.55 = (f32[248,128]{1,0:T(8,128)S(1)}, f32[248,128]{1,0:T(8,128)S(1)}, u32[]{:S(2)}, u32[]{:S(2)}) collective-permute-start(f32[248,128]{1,0:T(8,128)S(1)} %get-tuple-element.163), channel_id=1, source_target_pairs={{0,1},{1,0},{2,3},{3,2},{4,8},{5,9},{6,10},{7,11},{8,4},{9,5},{10,... | collective-permute-start | bytes 380936 | tf_op jit(solution)/shard_map/ppermute | solution.py:263
  126.3 9.1 %collective-permute-start.56 = (f32[248,128]{1,0:T(8,128)S(1)}, f32[248,128]{1,0:T(8,128)S(1)}, u32[]{:S(2)}, u32[]{:S(2)}) collective-permute-start(f32[248,128]{1,0:T(8,128)S(1)} %get-tuple-element.164), channel_id=1, source_target_pairs={{0,1},{1,0},{2,3},{3,2},{4,5},{5,4},{6,7},{7,6},{8,9},{9,8},{10,11... | collective-permute-start | bytes 380936 | tf_op jit(solution)/shard_map/ppermute | solution.py:263
  127.8 7.5 %collective-permute-start.57 = (f32[248,128]{1,0:T(8,128)S(1)}, f32[248,128]{1,0:T(8,128)S(1)}, u32[]{:S(2)}, u32[]{:S(2)}) collective-permute-start(f32[248,128]{1,0:T(8,128)S(1)} %get-tuple-element.165), channel_id=1, source_target_pairs={{0,4},{1,2},{2,1},{3,7},{4,0},{5,6},{6,5},{7,3},{8,12},{9,10},{10,... | collective-permute-start | bytes 380936 | tf_op jit(solution)/shard_map/ppermute | solution.py:263
  128.4 6.9 %collective-permute-start.58 = (f32[248,128]{1,0:T(8,128)S(1)}, f32[248,128]{1,0:T(8,128)S(1)}, u32[]{:S(2)}, u32[]{:S(2)}) collective-permute-start(f32[248,128]{1,0:T(8,128)S(1)} %get-tuple-element.166), channel_id=1, source_target_pairs={{0,16},{1,17},{2,18},{3,19},{4,20},{5,21},{6,22},{7,23},{8,24},{9,... | collective-permute-start | bytes 380936 | tf_op jit(solution)/shard_map/ppermute | solution.py:263
  128.8 5.6 %collective-permute-start.59 = (f32[32,128]{1,0:T(8,128)S(1)}, f32[32,128]{1,0:T(8,128)S(1)}, u32[]{:S(2)}, u32[]{:S(2)}) collective-permute-start(f32[32,128]{1,0:T(8,128)S(1)} %get-tuple-element.167), channel_id=1, source_target_pairs={{0,17},{1,16},{2,19},{3,18},{4,21},{5,20},{6,23},{7,22},{8,25},{9,... | collective-permute-start | bytes 49160 | tf_op jit(solution)/shard_map/ppermute | solution.py:263
  131.2 4.1 %collective-permute-start.60 = (f32[32,128]{1,0:T(8,128)S(1)}, f32[32,128]{1,0:T(8,128)S(1)}, u32[]{:S(2)}, u32[]{:S(2)}) collective-permute-start(f32[32,128]{1,0:T(8,128)S(1)} %get-tuple-element.168), channel_id=1, source_target_pairs={{0,4},{1,18},{2,17},{3,7},{4,0},{5,22},{6,21},{7,3},{8,12},{9,26},... | collective-permute-start | bytes 49160 | tf_op jit(solution)/shard_map/ppermute | solution.py:263
  (4 other events, 6.7 us)

commit v5 on v4

--- a/solution.py
+++ b/solution.py
@@ -342,7 +342,7 @@
     lax.fori_loop(0, ROWS // TILE, step, 0)
 
 
-def select_kernel(plan, canon, basis, one, weight_out, turned, src):
+def select_kernel(plan, canon, one, weight_out, src):
     index = position()
     src[...] = jnp.full(src.shape, -1, jnp.int32)
     weight_out[...] = jnp.zeros(weight_out.shape, F32)
@@ -359,13 +359,10 @@
                 weight = weight * jnp.where(has_b(index[d], plan.sizes[d]), 0.5, 1.0)
         weight_out[at : at + length, :] = jnp.full((length, 128), 1.0, F32) * weight
 
-    turned[...] = jnp.zeros(turned.shape, F32)
     for t in range(0, ROWS, TILE):
         rows = slice(t, t + TILE)
         hit = src[rows, :] == lax.broadcasted_iota(jnp.int32, (TILE, IFACE), 1)
-        picked = jnp.where(hit, 1.0, 0.0).astype(BF16)
-        one[rows, :] = picked
-        turned[rows, :6] = dot_last(picked, basis[...]) * weight_out[rows, :6]
+        one[rows, :] = jnp.where(hit, 1.0, 0.0).astype(BF16)
 
 
 def spread_kernel(plan, cinv, out):
@@ -379,26 +376,48 @@
         out[8 * i : 8 * i + 6, :] = value[:, 128 * i : 128 * (i + 1)]
 
 
-def left_kernel(one, matrix, weight, basis, mid, few):
+def turn_kernel(one, weight, basis, turned):
+    turned[...] = jnp.zeros(turned.shape, F32)
+    turned[:, :6] = dot_last(one[...], basis[...]) * weight[:, :6]
+
+
+def left_kernel(one, matrix, basis, mid, few):
     for t in range(0, ROWS, TILE):
-        value = dot(one[t : t + TILE, :], matrix[...])
-        if weight is not None:
-            value = value * weight[t : t + TILE, :1]
-        mid[t : t + TILE, :] = value.astype(BF16)
+        mid[t : t + TILE, :] = dot(one[t : t + TILE, :], matrix[...]).astype(BF16)
     if basis is not None:
         few[...] = jnp.zeros(few.shape, F32)
         few[:6, :] = basis[...].astype(F32)
         mid[COARSE_AT : COARSE_AT + 16, :] = few[...].astype(BF16)
 
 
-def right_left_kernel(one, mid, other, out, mid_other):
-    right_kernel(one, mid, out)
-    left_kernel(one, other, None, None, mid_other, None)
+def right_left_kernel(one, mid, weight, other, out, mid_other):
+    right(one, mid, weight, out)
+    left_kernel(one, other, None, mid_other, None)
 
 
 def right_kernel(one, mid, out):
-    for t in range(0, ROWS, TILE):
-        out[t : t + TILE, :] = dot_last(mid[t : t + TILE, :], one[...]).astype(BF16)
+    right(one, mid, None, out)
+
+
+def right(one, mid, weight, out):
+    order = sorted(range(ROWS // TILE), key=lambda t: (t != COARSE_AT // TILE, t))
+
+    def put(value, i, j):
+        if weight is not None:
+            scale = weight[i * TILE : (i + 1) * TILE, :1]
+            if i == order[0]:
+                row = lax.broadcasted_iota(jnp.int32, (TILE, 1), 0) + i * TILE
+                inside = jnp.logical_and(row >= COARSE_AT, row < COARSE_AT + 16)
+                scale = jnp.where(inside, 1.0, scale)
+            value = value * scale
+        out[i * TILE : (i + 1) * TILE, j * TILE : (j + 1) * TILE] = value.astype(BF16)
+
+    for a, i in enumerate(order):
+        for j in order[a:]:
+            value = dot_last(mid[i * TILE : (i + 1) * TILE, :], one[j * TILE : (j + 1) * TILE, :])
+            put(value, i, j)
+            if i != j:
+                put(value.T, j, i)
 
 
 def fill(acc, parts):
@@ -632,10 +651,10 @@
         )
         return got + transfer(messages[1], payloads)
 
-    one, weight, turned = call(
+    one, weight = call(
         functools.partial(select_kernel, plan),
-        [shape(ROWS, IFACE, BF16), shape(ROWS, 128), shape(ROWS, 128)],
-        [canon_rows.reshape(IFACE, 1), basis],
+        [shape(ROWS, IFACE, BF16), shape(ROWS, 128)],
+        [canon_rows.reshape(IFACE, 1)],
         scratch=[pltpu.VMEM((ROWS, 1), jnp.int32)],
         flops=ROWS * IFACE * 1158,
     )
@@ -643,6 +662,7 @@
         (spread,) = call(
             functools.partial(spread_kernel, plan), [shape(8 * plan.setup, 128)], [coarse_inverse]
         )
+    (turned,) = call(turn_kernel, [shape(ROWS, 128)], [one, weight, basis])
     (early,) = call(
         functools.partial(gather_kernel, EARLY, 0), [shape(early_rows, 128)], [canon, load], specs=[smem, vm()]
     )
@@ -655,12 +675,12 @@
     (half,) = call(
         left_kernel,
         [middle_shape],
-        [one, local_inverse[0, 0, 0], weight, basis],
+        [one, local_inverse[0, 0, 0], basis],
         scratch=[pltpu.VMEM((16, IFACE), F32)],
         flops=flops,
     )
     inverse, half = call(
-        right_left_kernel, [square, middle_shape], [one, half, schur_matrix[0, 0, 0]], flops=2 * flops
+        right_left_kernel, [square, middle_shape], [one, half, weight, schur_matrix[0, 0, 0]], flops=2 * flops
     )
     blocks = []
     if plan.ride:

time: 138 us -> 136 us (0.986)
  Pallas kernels: 39.8 us -> 36.7 us
  waiting for transfers between devices: 34.6 us -> 37.3 us
    pallas_call x33 -> x34, Pallas kernels: 39.8 us -> 36.7 us  [call(): pl.pallas_call(kernel, out_shape=tuple(outs), in_specs=specs or [vm()] *...]
    ppermute x61, waiting for transfers between devices: 34.6 us -> 37.3 us  [transfer(): lax.ppermute(p, AXES, m.pairs())]
  transfers between devices with their start and end apart: 61 -> 61, of which waited for: 20 -> 20; matrix products, arithmetic and copies ran while one was open for 1% -> 1% of each run, Pallas kernels for 23% -> 21%
where the time goes in v5:
time: 136 us; the launch traced here: 135 us
  starting transfers between devices  58.4 us (43%)
  waiting for transfers between devices  37.3 us (27%)
  Pallas kernels  36.7 us (27%)
  local copies, waits for them, and re-layouts  1.9 us (1%)
    ppermute x61, starting transfers between devices, transfer(): lax.ppermute(p, AXES, m.pairs())  58.4 us
    ppermute x61, waiting for transfers between devices, transfer(): lax.ppermute(p, AXES, m.pairs())  37.3 us
    pallas_call x34, Pallas kernels, call(): pl.pallas_call(kernel, out_shape=tuple(outs), in_specs=specs or [vm()] *...  36.7 us
  transfers between devices with their start and end apart: 61, of which 20 were waited for; matrix products, arithmetic and copies ran while one was open for 1% of the time, Pallas kernels for 21%

profile of v5, /device:TPU:1, one launch (start us, length us, event | category | flops | bytes accessed | tf_op | source)
XLA Modules:
  0.0 135.5 jit_solution(7284404212045027598)
XLA Ops:
  0.6 0.7 copy-done.3
  1.6 3.8 %collective-permute-start.1 = (f32[16,128]{1,0:T(8,128)S(1)}, f32[16,128]{1,0:T(8,128)S(1)}, u32[]{:S(2)}, u32[]{:S(2)}) collective-permute-start(f32[16,128]{1,0:T(8,128)S(1)} %shard_map.83.refs_1_.refs_4_), channel_id=1, source_target_pairs={{0,8},{1,9},{2,10},{3,11},{4,12},{5,13},{6,14},{7,15},{8,0},{9,1},... | collective-permute-start | bytes 24584 | tf_op jit(solution)/shard_map/ppermute | solution.py:263
  5.3 0.9 copy.10.canon
  6.3 0.8 shard_map.77
  7.4 1.0 shard_map.81.refs_0_
  8.4 1.0 shard_map.84.refs_5_.refs_8_.refs_0_
  9.7 1.6 %collective-permute-start.3 = (f32[336,128]{1,0:T(8,128)S(1)}, f32[336,128]{1,0:T(8,128)S(1)}, u32[]{:S(2)}, u32[]{:S(2)}) collective-permute-start(f32[336,128]{1,0:T(8,128)S(1)} %get-tuple-element.89), channel_id=1, source_target_pairs={{0,4},{1,5},{2,6},{3,7},{4,0},{5,1},{6,2},{7,3},{8,12},{9,13},{10,... | collective-permute-start | bytes 516104 | tf_op jit(solution)/shard_map/ppermute | solution.py:263
  11.7 4.4 %shard_map.78.mid = bf16[1280,1158]{1,0:T(8,128)(2,1)S(1)} custom-call(bf16[1280,1158]{1,0:T(8,128)(2,1)S(1)} %get-tuple-element.85.one, bf16[1158,1158]{1,0:T(8,128)(2,1)S(1)} %bitcast.21, bf16[6,1158]{1,0:T(8,128)(2,1)S(1)} %bitcast.20), custom_call_target="tpu_custom_call" | custom-call | flops 3432867840 | bytes 8624784 | tf_op jit(solution)/shard_map/pallas_call | solution.py:276
  16.2 1.2 shard_map.82.refs_1_
  17.8 1.6 %collective-permute-start.6 = (f32[400,128]{1,0:T(8,128)S(1)}, f32[400,128]{1,0:T(8,128)S(1)}, u32[]{:S(2)}, u32[]{:S(2)}) collective-permute-start(f32[400,128]{1,0:T(8,128)S(1)} %get-tuple-element.92), channel_id=1, source_target_pairs={{0,3},{1,2},{2,1},{3,0},{4,7},{5,6},{6,5},{7,4},{8,11},{9,10},{10,... | collective-permute-start | bytes 614408 | tf_op jit(solution)/shard_map/ppermute | solution.py:263
  19.4 1.2 collective-permute-start.7
  21.1 1.2 collective-permute-start.9
  22.3 7.1 %shard_map.79 = (bf16[1280,1280]{1,0:T(8,128)(2,1)S(1)}, bf16[1280,1158]{1,0:T(8,128)(2,1)S(1)}) custom-call(bf16[1280,1158]{1,0:T(8,128)(2,1)S(1)} %get-tuple-element.85.one, bf16[1280,1158]{1,0:T(8,128)(2,1)S(1)} %shard_map.78.mid, f32[1280,128]{1,0:T(8,128)S(1)} %get-tuple-element.86.weight.refs_10_, bf16[1158,1158]{1,0:T(8,128)(2,1)S(1)} %bitcast.22), custom_call_target="tpu_custom_call" | custom-call | flops 6865735680 | bytes 15507528 | tf_op jit(solution)/shard_map/pallas_call | solution.py:276
  30.2 1.0 shard_map.88.refs_0_
  31.3 2.9 %collective-permute-start.11 = (f32[264,128]{1,0:T(8,128)S(1)}, f32[264,128]{1,0:T(8,128)S(1)}, u32[]{:S(2)}, u32[]{:S(2)}) collective-permute-start(f32[264,128]{1,0:T(8,128)S(1)} %get-tuple-element.98), channel_id=1, source_target_pairs={{0,4},{1,5},{2,6},{3,7},{4,0},{5,1},{6,2},{7,3},{8,12},{9,13},{10,... | collective-permute-start | bytes 405512 | tf_op jit(solution)/shard_map/ppermute | solution.py:263
  34.6 0.8 collective-permute-start.13
  35.4 1.2 collective-permute-start.14
  36.6 2.4 %shard_map.90.refs_1_.refs_11_ = bf16[1280,768]{1,0:T(8,128)(2,1)S(1)} custom-call(f32[1280,128]{1,0:T(8,128)S(1)} %shard_map.84.refs_5_.refs_8_.refs_0_, f32[16,128]{1,0:T(8,128)S(1)} %shard_map.83.refs_1_.refs_4_, f32[16,128]{1,0:T(8,128)S(1)} %collective-permute-done.refs_2_.refs_5_, f32[16,128]{1,0:T(8,128)S(1)} %collective-permute-done.1.refs_3_.refs_6_, ...), custom_call_target="tpu_custom_call" | custom-call | flops 503316480 | bytes 3637248 | tf_op jit(solution)/shard_map/pallas_call | solution.py:276
  39.1 0.7 collective-permute-done.14.refs_5_.refs_4_
  39.8 1.9 %collective-permute-start.15 = (f32[248,128]{1,0:T(8,128)S(1)}, f32[248,128]{1,0:T(8,128)S(1)}, u32[]{:S(2)}, u32[]{:S(2)}) collective-permute-start(f32[248,128]{1,0:T(8,128)S(1)} %get-tuple-element.102), channel_id=1, source_target_pairs={{0,1},{1,0},{2,3},{3,2},{4,5},{5,4},{6,7},{7,6},{8,9},{9,8},{10,11... | collective-permute-start | bytes 380936 | tf_op jit(solution)/shard_map/ppermute | solution.py:263
  41.7 1.2 collective-permute-start.16
  43.2 1.8 %collective-permute-start.18 = (f32[32,128]{1,0:T(8,128)S(1)}, f32[32,128]{1,0:T(8,128)S(1)}, u32[]{:S(2)}, u32[]{:S(2)}) collective-permute-start(f32[32,128]{1,0:T(8,128)S(1)} %get-tuple-element.105), channel_id=1, source_target_pairs={{0,17},{1,16},{2,19},{3,18},{4,21},{5,20},{6,23},{7,22},{8,25},{9,... | collective-permute-start | bytes 49160 | tf_op jit(solution)/shard_map/ppermute | solution.py:263
  45.0 2.9 %shard_map.80.refs_10_.matrix = bf16[1280,1280]{1,0:T(8,128)(2,1)S(1)} custom-call(bf16[1280,1158]{1,0:T(8,128)(2,1)S(1)} %get-tuple-element.85.one, bf16[1280,1158]{1,0:T(8,128)(2,1)S(1)} %get-tuple-element.87.mid), custom_call_target="tpu_custom_call" | custom-call | flops 3432867840 | bytes 9205760 | tf_op jit(solution)/shard_map/pallas_call | solution.py:276
  47.9 1.8 %collective-permute-done.18.refs_8_ = f32[32,128]{1,0:T(8,128)S(1)} collective-permute-done((f32[32,128]{1,0:T(8,128)S(1)}, f32[32,128]{1,0:T(8,128)S(1)}, u32[]{:S(2)}, u32[]{:S(2)}) %collective-permute-start.18) | collective-permute-done | bytes 16416 | tf_op jit(solution)/shard_map/ppermute | solution.py:263
  50.1 1.2 shard_map.92
  52.1 4.3 %collective-permute-done.20.refs_2_ = f32[248,128]{1,0:T(8,128)S(1)} collective-permute-done((f32[248,128]{1,0:T(8,128)S(1)}, f32[248,128]{1,0:T(8,128)S(1)}, u32[]{:S(2)}, u32[]{:S(2)}) %collective-permute-start.20) | collective-permute-done | bytes 127008 | tf_op jit(solution)/shard_map/ppermute | solution.py:263
  56.5 0.9 collective-permute-start.22
  57.3 1.2 collective-permute-start.23
  58.8 2.0 %collective-permute-start.25 = (f32[32,128]{1,0:T(8,128)S(1)}, f32[32,128]{1,0:T(8,128)S(1)}, u32[]{:S(2)}, u32[]{:S(2)}) collective-permute-start(f32[32,128]{1,0:T(8,128)S(1)} %get-tuple-element.116), channel_id=1, source_target_pairs={{0,17},{1,16},{2,19},{3,18},{4,21},{5,20},{6,23},{7,22},{8,25},{9,... | collective-permute-start | bytes 49160 | tf_op jit(solution)/shard_map/ppermute | solution.py:263
  60.8 1.0 collective-permute-start.26
  61.8 2.4 %collective-permute-done.25.refs_7_ = f32[32,128]{1,0:T(8,128)S(1)} collective-permute-done((f32[32,128]{1,0:T(8,128)S(1)}, f32[32,128]{1,0:T(8,128)S(1)}, u32[]{:S(2)}, u32[]{:S(2)}) %collective-permute-start.25) | collective-permute-done | bytes 16416 | tf_op jit(solution)/shard_map/ppermute | solution.py:263
  64.1 0.9 collective-permute-done.26.refs_8_
  65.5 1.0 shard_map.96.refs_0_
  66.7 0.7 collective-permute-start.28
  67.8 1.6 %collective-permute-start.30 = (f32[16,128]{1,0:T(8,128)S(1)}, f32[16,128]{1,0:T(8,128)S(1)}, u32[]{:S(2)}, u32[]{:S(2)}) collective-permute-start(f32[16,128]{1,0:T(8,128)S(1)} %get-tuple-element.123), channel_id=1, source_target_pairs={{0,8},{1,9},{2,10},{3,11},{4,12},{5,13},{6,14},{7,15},{8,0},{9,1},... | collective-permute-start | bytes 24584 | tf_op jit(solution)/shard_map/ppermute | solution.py:263
  69.4 1.5 %collective-permute-start.31 = (f32[16,128]{1,0:T(8,128)S(1)}, f32[16,128]{1,0:T(8,128)S(1)}, u32[]{:S(2)}, u32[]{:S(2)}) collective-permute-start(f32[16,128]{1,0:T(8,128)S(1)} %get-tuple-element.124), channel_id=1, source_target_pairs={{0,12},{1,13},{2,14},{3,15},{4,8},{5,9},{6,10},{7,11},{8,4},{9,5},... | collective-permute-start | bytes 24584 | tf_op jit(solution)/shard_map/ppermute | solution.py:263
  70.8 1.3 collective-permute-done.30.refs_3_
  72.1 1.6 %collective-permute-done.31.refs_4_ = f32[16,128]{1,0:T(8,128)S(1)} collective-permute-done((f32[16,128]{1,0:T(8,128)S(1)}, f32[16,128]{1,0:T(8,128)S(1)}, u32[]{:S(2)}, u32[]{:S(2)}) %collective-permute-start.31) | collective-permute-done | bytes 8224 | tf_op jit(solution)/shard_map/ppermute | solution.py:263
  73.7 3.0 %collective-permute-start.33 = (f32[312,128]{1,0:T(8,128)S(1)}, f32[312,128]{1,0:T(8,128)S(1)}, u32[]{:S(2)}, u32[]{:S(2)}) collective-permute-start(f32[312,128]{1,0:T(8,128)S(1)} %get-tuple-element.126), channel_id=1, source_target_pairs={{0,3},{1,2},{2,1},{3,0},{4,7},{5,6},{6,5},{7,4},{8,11},{9,10},{10,... | collective-permute-start | bytes 479240 | tf_op jit(solution)/shard_map/ppermute | solution.py:263
  77.0 2.1 %collective-permute-start.36 = (f32[96,128]{1,0:T(8,128)S(1)}, f32[96,128]{1,0:T(8,128)S(1)}, u32[]{:S(2)}, u32[]{:S(2)}) collective-permute-start(f32[96,128]{1,0:T(8,128)S(1)} %get-tuple-element.129), channel_id=1, source_target_pairs={{0,19},{1,18},{2,17},{3,16},{4,23},{5,22},{6,21},{7,20},{8,27},{9,... | collective-permute-start | bytes 147464 | tf_op jit(solution)/shard_map/ppermute | solution.py:263
  79.3 5.0 %collective-permute-done.35.refs_8_ = f32[32,128]{1,0:T(8,128)S(1)} collective-permute-done((f32[32,128]{1,0:T(8,128)S(1)}, f32[32,128]{1,0:T(8,128)S(1)}, u32[]{:S(2)}, u32[]{:S(2)}) %collective-permute-start.35) | collective-permute-done | bytes 16416 | tf_op jit(solution)/shard_map/ppermute | solution.py:263
  84.2 1.2 shard_map.99
  86.8 3.0 %collective-permute-done.37.refs_2_ = f32[248,128]{1,0:T(8,128)S(1)} collective-permute-done((f32[248,128]{1,0:T(8,128)S(1)}, f32[248,128]{1,0:T(8,128)S(1)}, u32[]{:S(2)}, u32[]{:S(2)}) %collective-permute-start.37) | collective-permute-done | bytes 127008 | tf_op jit(solution)/shard_map/ppermute | solution.py:263
  89.9 1.5 %collective-permute-start.39 = (f32[248,128]{1,0:T(8,128)S(1)}, f32[248,128]{1,0:T(8,128)S(1)}, u32[]{:S(2)}, u32[]{:S(2)}) collective-permute-start(f32[248,128]{1,0:T(8,128)S(1)} %get-tuple-element.137), channel_id=1, source_target_pairs={{0,1},{1,0},{2,3},{3,2},{4,5},{5,4},{6,7},{7,6},{8,9},{9,8},{10,11... | collective-permute-start | bytes 380936 | tf_op jit(solution)/shard_map/ppermute | solution.py:263
  91.4 0.8 collective-permute-start.40
  92.5 2.4 %collective-permute-start.42 = (f32[32,128]{1,0:T(8,128)S(1)}, f32[32,128]{1,0:T(8,128)S(1)}, u32[]{:S(2)}, u32[]{:S(2)}) collective-permute-start(f32[32,128]{1,0:T(8,128)S(1)} %get-tuple-element.140), channel_id=1, source_target_pairs={{0,17},{1,16},{2,19},{3,18},{4,21},{5,20},{6,23},{7,22},{8,25},{9,... | collective-permute-start | bytes 49160 | tf_op jit(solution)/shard_map/ppermute | solution.py:263
  95.4 2.5 %collective-permute-done.42.refs_7_ = f32[32,128]{1,0:T(8,128)S(1)} collective-permute-done((f32[32,128]{1,0:T(8,128)S(1)}, f32[32,128]{1,0:T(8,128)S(1)}, u32[]{:S(2)}, u32[]{:S(2)}) %collective-permute-start.42) | collective-permute-done | bytes 16416 | tf_op jit(solution)/shard_map/ppermute | solution.py:263
  97.9 1.2 collective-permute-done.43.refs_8_
  99.6 1.0 shard_map.103.refs_0_
  100.8 0.7 collective-permute-start.45
  101.9 1.6 %collective-permute-start.47 = (f32[16,128]{1,0:T(8,128)S(1)}, f32[16,128]{1,0:T(8,128)S(1)}, u32[]{:S(2)}, u32[]{:S(2)}) collective-permute-start(f32[16,128]{1,0:T(8,128)S(1)} %get-tuple-element.147), channel_id=1, source_target_pairs={{0,8},{1,9},{2,10},{3,11},{4,12},{5,13},{6,14},{7,15},{8,0},{9,1},... | collective-permute-start | bytes 24584 | tf_op jit(solution)/shard_map/ppermute | solution.py:263
  103.5 1.4 %collective-permute-start.48 = (f32[16,128]{1,0:T(8,128)S(1)}, f32[16,128]{1,0:T(8,128)S(1)}, u32[]{:S(2)}, u32[]{:S(2)}) collective-permute-start(f32[16,128]{1,0:T(8,128)S(1)} %get-tuple-element.148), channel_id=1, source_target_pairs={{0,12},{1,13},{2,14},{3,15},{4,8},{5,9},{6,10},{7,11},{8,4},{9,5},... | collective-permute-start | bytes 24584 | tf_op jit(solution)/shard_map/ppermute | solution.py:263
  104.9 1.4 %collective-permute-done.47.refs_3_ = f32[16,128]{1,0:T(8,128)S(1)} collective-permute-done((f32[16,128]{1,0:T(8,128)S(1)}, f32[16,128]{1,0:T(8,128)S(1)}, u32[]{:S(2)}, u32[]{:S(2)}) %collective-permute-start.47) | collective-permute-done | bytes 8224 | tf_op jit(solution)/shard_map/ppermute | solution.py:263
  106.2 1.5 %collective-permute-done.48.refs_4_ = f32[16,128]{1,0:T(8,128)S(1)} collective-permute-done((f32[16,128]{1,0:T(8,128)S(1)}, f32[16,128]{1,0:T(8,128)S(1)}, u32[]{:S(2)}, u32[]{:S(2)}) %collective-permute-start.48) | collective-permute-done | bytes 8224 | tf_op jit(solution)/shard_map/ppermute | solution.py:263
  107.8 2.8 %collective-permute-start.50 = (f32[312,128]{1,0:T(8,128)S(1)}, f32[312,128]{1,0:T(8,128)S(1)}, u32[]{:S(2)}, u32[]{:S(2)}) collective-permute-start(f32[312,128]{1,0:T(8,128)S(1)} %get-tuple-element.150), channel_id=1, source_target_pairs={{0,3},{1,2},{2,1},{3,0},{4,7},{5,6},{6,5},{7,4},{8,11},{9,10},{10,... | collective-permute-start | bytes 479240 | tf_op jit(solution)/shard_map/ppermute | solution.py:263
  110.9 2.4 %collective-permute-start.53 = (f32[96,128]{1,0:T(8,128)S(1)}, f32[96,128]{1,0:T(8,128)S(1)}, u32[]{:S(2)}, u32[]{:S(2)}) collective-permute-start(f32[96,128]{1,0:T(8,128)S(1)} %get-tuple-element.153), channel_id=1, source_target_pairs={{0,19},{1,18},{2,17},{3,16},{4,23},{5,22},{6,21},{7,20},{8,27},{9,... | collective-permute-start | bytes 147464 | tf_op jit(solution)/shard_map/ppermute | solution.py:263
  113.3 4.8 %collective-permute-done.52.refs_8_ = f32[32,128]{1,0:T(8,128)S(1)} collective-permute-done((f32[32,128]{1,0:T(8,128)S(1)}, f32[32,128]{1,0:T(8,128)S(1)}, u32[]{:S(2)}, u32[]{:S(2)}) %collective-permute-start.52) | collective-permute-done | bytes 16416 | tf_op jit(solution)/shard_map/ppermute | solution.py:263
  118.2 1.2 shard_map.106
  120.7 3.1 %collective-permute-done.54.refs_2_.refs_0_ = f32[248,128]{1,0:T(8,128)S(1)} collective-permute-done((f32[248,128]{1,0:T(8,128)S(1)}, f32[248,128]{1,0:T(8,128)S(1)}, u32[]{:S(2)}, u32[]{:S(2)}) %collective-permute-start.54) | collective-permute-done | bytes 127008 | tf_op jit(solution)/shard_map/ppermute | solution.py:263
  123.9 1.5 %collective-permute-start.56 = (f32[248,128]{1,0:T(8,128)S(1)}, f32[248,128]{1,0:T(8,128)S(1)}, u32[]{:S(2)}, u32[]{:S(2)}) collective-permute-start(f32[248,128]{1,0:T(8,128)S(1)} %get-tuple-element.162), channel_id=1, source_target_pairs={{0,1},{1,0},{2,3},{3,2},{4,5},{5,4},{6,7},{7,6},{8,9},{9,8},{10,11... | collective-permute-start | bytes 380936 | tf_op jit(solution)/shard_map/ppermute | solution.py:263
  126.2 2.6 %collective-permute-start.59 = (f32[32,128]{1,0:T(8,128)S(1)}, f32[32,128]{1,0:T(8,128)S(1)}, u32[]{:S(2)}, u32[]{:S(2)}) collective-permute-start(f32[32,128]{1,0:T(8,128)S(1)} %get-tuple-element.165), channel_id=1, source_target_pairs={{0,17},{1,16},{2,19},{3,18},{4,21},{5,20},{6,23},{7,22},{8,25},{9,... | collective-permute-start | bytes 49160 | tf_op jit(solution)/shard_map/ppermute | solution.py:263
  129.2 2.5 %shard_map.108 = f32[1158,1,128]{2,1,0:T(1,128)} custom-call(s32[1,1158]{1,0:T(1,128)S(1)} %bitcast.17, f32[1280,128]{1,0:T(8,128)S(1)} %get-tuple-element.157.acc), custom_call_target="tpu_custom_call" | custom-call | bytes 1252888 | tf_op jit(solution)/shard_map/pallas_call | solution.py:276
  131.9 1.0 collective-permute-done.60.refs_6_
  132.9 2.5 %shard_map.110 = f32[1158,1,128]{2,1,0:T(1,128)} custom-call(s32[1,1158]{1,0:T(1,128)S(1)} %bitcast.18, f32[576,128]{1,0:T(8,128)S(1)} %get-tuple-element.158.refs_0_.early, f32[704,128]{1,0:T(8,128)S(1)} %get-tuple-element.159.refs_1_.late, f32[248,128]{1,0:T(8,128)S(1)} %collective-permute-done.54.refs_2_.refs_0_, ...), custom_call_target="tpu_custom_call" | custom-call | bytes 2575896 | tf_op jit(solution)/shard_map/pallas_call | solution.py:276
  (105 shorter events, 13.0 us)
Async XLA Ops:
  1.5 8.0 %collective-permute-start = (f32[16,128]{1,0:T(8,128)S(1)}, f32[16,128]{1,0:T(8,128)S(1)}, u32[]{:S(2)}, u32[]{:S(2)}) collective-permute-start(f32[16,128]{1,0:T(8,128)S(1)} %shard_map.83.refs_1_.refs_4_), channel_id=1, source_target_pairs={{0,1},{1,0},{2,3},{3,2},{4,5},{5,4},{6,7},{7,6},{8,9},{9,8},{10,11... | collective-permute-start | bytes 24584 | tf_op jit(solution)/shard_map/ppermute | solution.py:263
  1.6 7.9 %collective-permute-start.1 = (f32[16,128]{1,0:T(8,128)S(1)}, f32[16,128]{1,0:T(8,128)S(1)}, u32[]{:S(2)}, u32[]{:S(2)}) collective-permute-start(f32[16,128]{1,0:T(8,128)S(1)} %shard_map.83.refs_1_.refs_4_), channel_id=1, source_target_pairs={{0,8},{1,9},{2,10},{3,11},{4,12},{5,13},{6,14},{7,15},{8,0},{9,1},... | collective-permute-start | bytes 24584 | tf_op jit(solution)/shard_map/ppermute | solution.py:263
  5.3 4.2 %collective-permute-start.2 = (f32[16,128]{1,0:T(8,128)S(1)}, f32[16,128]{1,0:T(8,128)S(1)}, u32[]{:S(2)}, u32[]{:S(2)}) collective-permute-start(f32[16,128]{1,0:T(8,128)S(1)} %shard_map.83.refs_1_.refs_4_), channel_id=1, source_target_pairs={{0,9},{1,8},{2,11},{3,10},{4,13},{5,12},{6,15},{7,14},{8,1},{9,0},... | collective-permute-start | bytes 24584 | tf_op jit(solution)/shard_map/ppermute | solution.py:263
  6.3 2.1 %copy-start.2 = (bf16[1,1,1,6,1158]{4,3,2,1,0:T(8,128)(2,1)S(1)}, bf16[1,1,1,6,1158]{4,3,2,1,0:T(8,128)(2,1)}, u32[]{:S(2)}) copy-start(bf16[1,1,1,6,1158]{4,3,2,1,0:T(8,128)(2,1)} %param.9) | copy-start | bytes 41692
  7.1 4.6 %copy-start.4 = (bf16[1,1,1,1158,1158]{4,3,2,1,0:T(8,128)(2,1)S(1)}, bf16[1,1,1,1158,1158]{4,3,2,1,0:T(8,128)(2,1)}, u32[]{:S(2)}) copy-start(bf16[1,1,1,1158,1158]{4,3,2,1,0:T(8,128)(2,1)} %param.8) | copy-start | bytes 8045788
  9.7 7.7 %collective-permute-start.3 = (f32[336,128]{1,0:T(8,128)S(1)}, f32[336,128]{1,0:T(8,128)S(1)}, u32[]{:S(2)}, u32[]{:S(2)}) collective-permute-start(f32[336,128]{1,0:T(8,128)S(1)} %get-tuple-element.89), channel_id=1, source_target_pairs={{0,4},{1,5},{2,6},{3,7},{4,0},{5,1},{6,2},{7,3},{8,12},{9,13},{10,... | collective-permute-start | bytes 516104 | tf_op jit(solution)/shard_map/ppermute | solution.py:263
  11.2 6.1 %collective-permute-start.4 = (f32[272,128]{1,0:T(8,128)S(1)}, f32[272,128]{1,0:T(8,128)S(1)}, u32[]{:S(2)}, u32[]{:S(2)}) collective-permute-start(f32[272,128]{1,0:T(8,128)S(1)} %get-tuple-element.90), channel_id=1, source_target_pairs={{0,1},{1,0},{2,3},{3,2},{4,8},{5,9},{6,10},{7,11},{8,4},{9,5},{10,... | collective-permute-start | bytes 417800 | tf_op jit(solution)/shard_map/ppermute | solution.py:263
  11.7 10.6 %copy-start.5 = (bf16[1,1,1,1158,1158]{4,3,2,1,0:T(8,128)(2,1)S(1)}, bf16[1,1,1,1158,1158]{4,3,2,1,0:T(8,128)(2,1)}, u32[]{:S(2)}) copy-start(bf16[1,1,1,1158,1158]{4,3,2,1,0:T(8,128)(2,1)} %param.7) | copy-start | bytes 8045788
  17.7 11.8 %collective-permute-start.5 = (f32[272,128]{1,0:T(8,128)S(1)}, f32[272,128]{1,0:T(8,128)S(1)}, u32[]{:S(2)}, u32[]{:S(2)}) collective-permute-start(f32[272,128]{1,0:T(8,128)S(1)} %get-tuple-element.91), channel_id=1, source_target_pairs={{0,1},{1,0},{2,3},{3,2},{4,5},{5,4},{6,7},{7,6},{8,9},{9,8},{10,11... | collective-permute-start | bytes 417800 | tf_op jit(solution)/shard_map/ppermute | solution.py:263
  17.8 11.7 %collective-permute-start.6 = (f32[400,128]{1,0:T(8,128)S(1)}, f32[400,128]{1,0:T(8,128)S(1)}, u32[]{:S(2)}, u32[]{:S(2)}) collective-permute-start(f32[400,128]{1,0:T(8,128)S(1)} %get-tuple-element.92), channel_id=1, source_target_pairs={{0,3},{1,2},{2,1},{3,0},{4,7},{5,6},{6,5},{7,4},{8,11},{9,10},{10,... | collective-permute-start | bytes 614408 | tf_op jit(solution)/shard_map/ppermute | solution.py:263
  19.4 10.1 %collective-permute-start.7 = (f32[400,128]{1,0:T(8,128)S(1)}, f32[400,128]{1,0:T(8,128)S(1)}, u32[]{:S(2)}, u32[]{:S(2)}) collective-permute-start(f32[400,128]{1,0:T(8,128)S(1)} %get-tuple-element.93), channel_id=1, source_target_pairs={{0,16},{1,17},{2,18},{3,19},{4,20},{5,21},{6,22},{7,23},{8,24},{9,... | collective-permute-start | bytes 614408 | tf_op jit(solution)/shard_map/ppermute | solution.py:263
  20.7 8.8 %collective-permute-start.8 = (f32[56,128]{1,0:T(8,128)S(1)}, f32[56,128]{1,0:T(8,128)S(1)}, u32[]{:S(2)}, u32[]{:S(2)}) collective-permute-start(f32[56,128]{1,0:T(8,128)S(1)} %get-tuple-element.94), channel_id=1, source_target_pairs={{0,17},{1,16},{2,19},{3,18},{4,21},{5,20},{6,23},{7,22},{8,25},{9,... | collective-permute-start | bytes 86024 | tf_op jit(solution)/shard_map/ppermute | solution.py:263
  21.1 8.3 %collective-permute-start.9 = (f32[184,128]{1,0:T(8,128)S(1)}, f32[184,128]{1,0:T(8,128)S(1)}, u32[]{:S(2)}, u32[]{:S(2)}) collective-permute-start(f32[184,128]{1,0:T(8,128)S(1)} %get-tuple-element.95), channel_id=1, source_target_pairs={{0,19},{1,18},{2,17},{3,16},{4,23},{5,22},{6,21},{7,20},{8,27},{9,... | collective-permute-start | bytes 282632 | tf_op jit(solution)/shard_map/ppermute | solution.py:263
  29.9 1.4 %collective-permute-start.10 = (f32[8,128]{1,0:T(8,128)S(1)}, f32[8,128]{1,0:T(8,128)S(1)}, u32[]{:S(2)}, u32[]{:S(2)}) collective-permute-start(f32[8,128]{1,0:T(8,128)S(1)} %get-tuple-element.97.refs_1_.refs_6_.refs_12_), channel_id=1, source_target_pairs={{0,1},{1,0},{2,3},{3,2},{4,5},{5,4},{6,7},{7,6},{8,9},{9,8},{10,11... | collective-permute-start | bytes 12296 | tf_op jit(solution)/shard_map/ppermute | solution.py:263
  31.3 8.5 %collective-permute-start.11 = (f32[264,128]{1,0:T(8,128)S(1)}, f32[264,128]{1,0:T(8,128)S(1)}, u32[]{:S(2)}, u32[]{:S(2)}) collective-permute-start(f32[264,128]{1,0:T(8,128)S(1)} %get-tuple-element.98), channel_id=1, source_target_pairs={{0,4},{1,5},{2,6},{3,7},{4,0},{5,1},{6,2},{7,3},{8,12},{9,13},{10,... | collective-permute-start | bytes 405512 | tf_op jit(solution)/shard_map/ppermute | solution.py:263
  34.2 5.6 %collective-permute-start.12 = (f32[248,128]{1,0:T(8,128)S(1)}, f32[248,128]{1,0:T(8,128)S(1)}, u32[]{:S(2)}, u32[]{:S(2)}) collective-permute-start(f32[248,128]{1,0:T(8,128)S(1)} %get-tuple-element.99), channel_id=1, source_target_pairs={{0,1},{1,0},{2,3},{3,2},{4,8},{5,9},{6,10},{7,11},{8,4},{9,5},{10,... | collective-permute-start | bytes 380936 | tf_op jit(solution)/shard_map/ppermute | solution.py:263
  34.6 4.5 %collective-permute-start.13 = (f32[16,128]{1,0:T(8,128)S(1)}, f32[16,128]{1,0:T(8,128)S(1)}, u32[]{:S(2)}, u32[]{:S(2)}) collective-permute-start(f32[16,128]{1,0:T(8,128)S(1)} %get-tuple-element.100), channel_id=1, source_target_pairs={{0,8},{1,9},{2,10},{3,11},{4,12},{5,13},{6,14},{7,15},{8,0},{9,1},... | collective-permute-start | bytes 24584 | tf_op jit(solution)/shard_map/ppermute | solution.py:263
  35.4 4.3 %collective-permute-start.14 = (f32[16,128]{1,0:T(8,128)S(1)}, f32[16,128]{1,0:T(8,128)S(1)}, u32[]{:S(2)}, u32[]{:S(2)}) collective-permute-start(f32[16,128]{1,0:T(8,128)S(1)} %get-tuple-element.101), channel_id=1, source_target_pairs={{0,12},{1,13},{2,14},{3,15},{4,8},{5,9},{6,10},{7,11},{8,4},{9,5},... | collective-permute-start | bytes 24584 | tf_op jit(solution)/shard_map/ppermute | solution.py:263
  39.8 10.3 %collective-permute-start.15 = (f32[248,128]{1,0:T(8,128)S(1)}, f32[248,128]{1,0:T(8,128)S(1)}, u32[]{:S(2)}, u32[]{:S(2)}) collective-permute-start(f32[248,128]{1,0:T(8,128)S(1)} %get-tuple-element.102), channel_id=1, source_target_pairs={{0,1},{1,0},{2,3},{3,2},{4,5},{5,4},{6,7},{7,6},{8,9},{9,8},{10,11... | collective-permute-start | bytes 380936 | tf_op jit(solution)/shard_map/ppermute | solution.py:263
  41.7 8.4 %collective-permute-start.16 = (f32[312,128]{1,0:T(8,128)S(1)}, f32[312,128]{1,0:T(8,128)S(1)}, u32[]{:S(2)}, u32[]{:S(2)}) collective-permute-start(f32[312,128]{1,0:T(8,128)S(1)} %get-tuple-element.103), channel_id=1, source_target_pairs={{0,3},{1,2},{2,1},{3,0},{4,7},{5,6},{6,5},{7,4},{8,11},{9,10},{10,... | collective-permute-start | bytes 479240 | tf_op jit(solution)/shard_map/ppermute | solution.py:263
  42.9 7.2 %collective-permute-start.17 = (f32[312,128]{1,0:T(8,128)S(1)}, f32[312,128]{1,0:T(8,128)S(1)}, u32[]{:S(2)}, u32[]{:S(2)}) collective-permute-start(f32[312,128]{1,0:T(8,128)S(1)} %get-tuple-element.104), channel_id=1, source_target_pairs={{0,16},{1,17},{2,18},{3,19},{4,20},{5,21},{6,22},{7,23},{8,24},{9,... | collective-permute-start | bytes 479240 | tf_op jit(solution)/shard_map/ppermute | solution.py:263
  43.2 6.6 %collective-permute-start.18 = (f32[32,128]{1,0:T(8,128)S(1)}, f32[32,128]{1,0:T(8,128)S(1)}, u32[]{:S(2)}, u32[]{:S(2)}) collective-permute-start(f32[32,128]{1,0:T(8,128)S(1)} %get-tuple-element.105), channel_id=1, source_target_pairs={{0,17},{1,16},{2,19},{3,18},{4,21},{5,20},{6,23},{7,22},{8,25},{9,... | collective-permute-start | bytes 49160 | tf_op jit(solution)/shard_map/ppermute | solution.py:263
  45.0 5.1 %collective-permute-start.19 = (f32[96,128]{1,0:T(8,128)S(1)}, f32[96,128]{1,0:T(8,128)S(1)}, u32[]{:S(2)}, u32[]{:S(2)}) collective-permute-start(f32[96,128]{1,0:T(8,128)S(1)} %get-tuple-element.106), channel_id=1, source_target_pairs={{0,19},{1,18},{2,17},{3,16},{4,23},{5,22},{6,21},{7,20},{8,27},{9,... | collective-permute-start | bytes 147464 | tf_op jit(solution)/shard_map/ppermute | solution.py:263
  51.3 5.1 %collective-permute-start.20 = (f32[248,128]{1,0:T(8,128)S(1)}, f32[248,128]{1,0:T(8,128)S(1)}, u32[]{:S(2)}, u32[]{:S(2)}) collective-permute-start(f32[248,128]{1,0:T(8,128)S(1)} %get-tuple-element.111), channel_id=1, source_target_pairs={{0,4},{1,5},{2,6},{3,7},{4,0},{5,1},{6,2},{7,3},{8,12},{9,13},{10,... | collective-permute-start | bytes 380936 | tf_op jit(solution)/shard_map/ppermute | solution.py:263
  51.4 5.0 %collective-permute-start.21 = (f32[248,128]{1,0:T(8,128)S(1)}, f32[248,128]{1,0:T(8,128)S(1)}, u32[]{:S(2)}, u32[]{:S(2)}) collective-permute-start(f32[248,128]{1,0:T(8,128)S(1)} %get-tuple-element.112), channel_id=1, source_target_pairs={{0,1},{1,0},{2,3},{3,2},{4,8},{5,9},{6,10},{7,11},{8,4},{9,5},{10,... | collective-permute-start | bytes 380936 | tf_op jit(solution)/shard_map/ppermute | solution.py:263
  56.5 8.6 %collective-permute-start.22 = (f32[248,128]{1,0:T(8,128)S(1)}, f32[248,128]{1,0:T(8,128)S(1)}, u32[]{:S(2)}, u32[]{:S(2)}) collective-permute-start(f32[248,128]{1,0:T(8,128)S(1)} %get-tuple-element.113), channel_id=1, source_target_pairs={{0,1},{1,0},{2,3},{3,2},{4,5},{5,4},{6,7},{7,6},{8,9},{9,8},{10,11... | collective-permute-start | bytes 380936 | tf_op jit(solution)/shard_map/ppermute | solution.py:263
  57.3 7.7 %collective-permute-start.23 = (f32[248,128]{1,0:T(8,128)S(1)}, f32[248,128]{1,0:T(8,128)S(1)}, u32[]{:S(2)}, u32[]{:S(2)}) collective-permute-start(f32[248,128]{1,0:T(8,128)S(1)} %get-tuple-element.114), channel_id=1, source_target_pairs={{0,4},{1,2},{2,1},{3,7},{4,0},{5,6},{6,5},{7,3},{8,12},{9,10},{10,... | collective-permute-start | bytes 380936 | tf_op jit(solution)/shard_map/ppermute | solution.py:263
  58.5 6.5 %collective-permute-start.24 = (f32[248,128]{1,0:T(8,128)S(1)}, f32[248,128]{1,0:T(8,128)S(1)}, u32[]{:S(2)}, u32[]{:S(2)}) collective-permute-start(f32[248,128]{1,0:T(8,128)S(1)} %get-tuple-element.115), channel_id=1, source_target_pairs={{0,16},{1,17},{2,18},{3,19},{4,20},{5,21},{6,22},{7,23},{8,24},{9,... | collective-permute-start | bytes 380936 | tf_op jit(solution)/shard_map/ppermute | solution.py:263
  58.8 5.3 %collective-permute-start.25 = (f32[32,128]{1,0:T(8,128)S(1)}, f32[32,128]{1,0:T(8,128)S(1)}, u32[]{:S(2)}, u32[]{:S(2)}) collective-permute-start(f32[32,128]{1,0:T(8,128)S(1)} %get-tuple-element.116), channel_id=1, source_target_pairs={{0,17},{1,16},{2,19},{3,18},{4,21},{5,20},{6,23},{7,22},{8,25},{9,... | collective-permute-start | bytes 49160 | tf_op jit(solution)/shard_map/ppermute | solution.py:263
  60.8 4.2 %collective-permute-start.26 = (f32[32,128]{1,0:T(8,128)S(1)}, f32[32,128]{1,0:T(8,128)S(1)}, u32[]{:S(2)}, u32[]{:S(2)}) collective-permute-start(f32[32,128]{1,0:T(8,128)S(1)} %get-tuple-element.117), channel_id=1, source_target_pairs={{0,4},{1,18},{2,17},{3,7},{4,0},{5,22},{6,21},{7,3},{8,12},{9,26},... | collective-permute-start | bytes 49160 | tf_op jit(solution)/shard_map/ppermute | solution.py:263
  65.5 1.2 collective-permute-start.27
  66.7 7.0 %collective-permute-start.28 = (f32[264,128]{1,0:T(8,128)S(1)}, f32[264,128]{1,0:T(8,128)S(1)}, u32[]{:S(2)}, u32[]{:S(2)}) collective-permute-start(f32[264,128]{1,0:T(8,128)S(1)} %get-tuple-element.121), channel_id=1, source_target_pairs={{0,4},{1,5},{2,6},{3,7},{4,0},{5,1},{6,2},{7,3},{8,12},{9,13},{10,... | collective-permute-start | bytes 405512 | tf_op jit(solution)/shard_map/ppermute | solution.py:263
  67.4 6.3 %collective-permute-start.29 = (f32[248,128]{1,0:T(8,128)S(1)}, f32[248,128]{1,0:T(8,128)S(1)}, u32[]{:S(2)}, u32[]{:S(2)}) collective-permute-start(f32[248,128]{1,0:T(8,128)S(1)} %get-tuple-element.122), channel_id=1, source_target_pairs={{0,1},{1,0},{2,3},{3,2},{4,8},{5,9},{6,10},{7,11},{8,4},{9,5},{10,... | collective-permute-start | bytes 380936 | tf_op jit(solution)/shard_map/ppermute | solution.py:263
  67.8 4.3 %collective-permute-start.30 = (f32[16,128]{1,0:T(8,128)S(1)}, f32[16,128]{1,0:T(8,128)S(1)}, u32[]{:S(2)}, u32[]{:S(2)}) collective-permute-start(f32[16,128]{1,0:T(8,128)S(1)} %get-tuple-element.123), channel_id=1, source_target_pairs={{0,8},{1,9},{2,10},{3,11},{4,12},{5,13},{6,14},{7,15},{8,0},{9,1},... | collective-permute-start | bytes 24584 | tf_op jit(solution)/shard_map/ppermute | solution.py:263
  69.4 4.3 %collective-permute-start.31 = (f32[16,128]{1,0:T(8,128)S(1)}, f32[16,128]{1,0:T(8,128)S(1)}, u32[]{:S(2)}, u32[]{:S(2)}) collective-permute-start(f32[16,128]{1,0:T(8,128)S(1)} %get-tuple-element.124), channel_id=1, source_target_pairs={{0,12},{1,13},{2,14},{3,15},{4,8},{5,9},{6,10},{7,11},{8,4},{9,5},... | collective-permute-start | bytes 24584 | tf_op jit(solution)/shard_map/ppermute | solution.py:263
  73.7 10.5 %collective-permute-start.33 = (f32[312,128]{1,0:T(8,128)S(1)}, f32[312,128]{1,0:T(8,128)S(1)}, u32[]{:S(2)}, u32[]{:S(2)}) collective-permute-start(f32[312,128]{1,0:T(8,128)S(1)} %get-tuple-element.126), channel_id=1, source_target_pairs={{0,3},{1,2},{2,1},{3,0},{4,7},{5,6},{6,5},{7,4},{8,11},{9,10},{10,... | collective-permute-start | bytes 479240 | tf_op jit(solution)/shard_map/ppermute | solution.py:263
  76.7 7.5 %collective-permute-start.34 = (f32[312,128]{1,0:T(8,128)S(1)}, f32[312,128]{1,0:T(8,128)S(1)}, u32[]{:S(2)}, u32[]{:S(2)}) collective-permute-start(f32[312,128]{1,0:T(8,128)S(1)} %get-tuple-element.127), channel_id=1, source_target_pairs={{0,16},{1,17},{2,18},{3,19},{4,20},{5,21},{6,22},{7,23},{8,24},{9,... | collective-permute-start | bytes 479240 | tf_op jit(solution)/shard_map/ppermute | solution.py:263
  77.0 7.2 %collective-permute-start.32 = (f32[248,128]{1,0:T(8,128)S(1)}, f32[248,128]{1,0:T(8,128)S(1)}, u32[]{:S(2)}, u32[]{:S(2)}) collective-permute-start(f32[248,128]{1,0:T(8,128)S(1)} %get-tuple-element.125), channel_id=1, source_target_pairs={{0,1},{1,0},{2,3},{3,2},{4,5},{5,4},{6,7},{7,6},{8,9},{9,8},{10,11... | collective-permute-start | bytes 380936 | tf_op jit(solution)/shard_map/ppermute | solution.py:263
  77.0 7.2 %collective-permute-start.36 = (f32[96,128]{1,0:T(8,128)S(1)}, f32[96,128]{1,0:T(8,128)S(1)}, u32[]{:S(2)}, u32[]{:S(2)}) collective-permute-start(f32[96,128]{1,0:T(8,128)S(1)} %get-tuple-element.129), channel_id=1, source_target_pairs={{0,19},{1,18},{2,17},{3,16},{4,23},{5,22},{6,21},{7,20},{8,27},{9,... | collective-permute-start | bytes 147464 | tf_op jit(solution)/shard_map/ppermute | solution.py:263
  79.1 5.1 %collective-permute-start.35 = (f32[32,128]{1,0:T(8,128)S(1)}, f32[32,128]{1,0:T(8,128)S(1)}, u32[]{:S(2)}, u32[]{:S(2)}) collective-permute-start(f32[32,128]{1,0:T(8,128)S(1)} %get-tuple-element.128), channel_id=1, source_target_pairs={{0,17},{1,16},{2,19},{3,18},{4,21},{5,20},{6,23},{7,22},{8,25},{9,... | collective-permute-start | bytes 49160 | tf_op jit(solution)/shard_map/ppermute | solution.py:263
  85.4 4.4 %collective-permute-start.37 = (f32[248,128]{1,0:T(8,128)S(1)}, f32[248,128]{1,0:T(8,128)S(1)}, u32[]{:S(2)}, u32[]{:S(2)}) collective-permute-start(f32[248,128]{1,0:T(8,128)S(1)} %get-tuple-element.135), channel_id=1, source_target_pairs={{0,4},{1,5},{2,6},{3,7},{4,0},{5,1},{6,2},{7,3},{8,12},{9,13},{10,... | collective-permute-start | bytes 380936 | tf_op jit(solution)/shard_map/ppermute | solution.py:263
  85.5 4.4 %collective-permute-start.38 = (f32[248,128]{1,0:T(8,128)S(1)}, f32[248,128]{1,0:T(8,128)S(1)}, u32[]{:S(2)}, u32[]{:S(2)}) collective-permute-start(f32[248,128]{1,0:T(8,128)S(1)} %get-tuple-element.136), channel_id=1, source_target_pairs={{0,1},{1,0},{2,3},{3,2},{4,8},{5,9},{6,10},{7,11},{8,4},{9,5},{10,... | collective-permute-start | bytes 380936 | tf_op jit(solution)/shard_map/ppermute | solution.py:263
  89.9 9.2 %collective-permute-start.39 = (f32[248,128]{1,0:T(8,128)S(1)}, f32[248,128]{1,0:T(8,128)S(1)}, u32[]{:S(2)}, u32[]{:S(2)}) collective-permute-start(f32[248,128]{1,0:T(8,128)S(1)} %get-tuple-element.137), channel_id=1, source_target_pairs={{0,1},{1,0},{2,3},{3,2},{4,5},{5,4},{6,7},{7,6},{8,9},{9,8},{10,11... | collective-permute-start | bytes 380936 | tf_op jit(solution)/shard_map/ppermute | solution.py:263
  91.4 7.7 %collective-permute-start.40 = (f32[248,128]{1,0:T(8,128)S(1)}, f32[248,128]{1,0:T(8,128)S(1)}, u32[]{:S(2)}, u32[]{:S(2)}) collective-permute-start(f32[248,128]{1,0:T(8,128)S(1)} %get-tuple-element.138), channel_id=1, source_target_pairs={{0,4},{1,2},{2,1},{3,7},{4,0},{5,6},{6,5},{7,3},{8,12},{9,10},{10,... | collective-permute-start | bytes 380936 | tf_op jit(solution)/shard_map/ppermute | solution.py:263
  92.2 6.9 %collective-permute-start.41 = (f32[248,128]{1,0:T(8,128)S(1)}, f32[248,128]{1,0:T(8,128)S(1)}, u32[]{:S(2)}, u32[]{:S(2)}) collective-permute-start(f32[248,128]{1,0:T(8,128)S(1)} %get-tuple-element.139), channel_id=1, source_target_pairs={{0,16},{1,17},{2,18},{3,19},{4,20},{5,21},{6,22},{7,23},{8,24},{9,... | collective-permute-start | bytes 380936 | tf_op jit(solution)/shard_map/ppermute | solution.py:263
  92.5 5.5 %collective-permute-start.42 = (f32[32,128]{1,0:T(8,128)S(1)}, f32[32,128]{1,0:T(8,128)S(1)}, u32[]{:S(2)}, u32[]{:S(2)}) collective-permute-start(f32[32,128]{1,0:T(8,128)S(1)} %get-tuple-element.140), channel_id=1, source_target_pairs={{0,17},{1,16},{2,19},{3,18},{4,21},{5,20},{6,23},{7,22},{8,25},{9,... | collective-permute-start | bytes 49160 | tf_op jit(solution)/shard_map/ppermute | solution.py:263
  94.9 4.2 %collective-permute-start.43 = (f32[32,128]{1,0:T(8,128)S(1)}, f32[32,128]{1,0:T(8,128)S(1)}, u32[]{:S(2)}, u32[]{:S(2)}) collective-permute-start(f32[32,128]{1,0:T(8,128)S(1)} %get-tuple-element.141), channel_id=1, source_target_pairs={{0,4},{1,18},{2,17},{3,7},{4,0},{5,22},{6,21},{7,3},{8,12},{9,26},... | collective-permute-start | bytes 49160 | tf_op jit(solution)/shard_map/ppermute | solution.py:263
  99.6 1.2 collective-permute-start.44
  100.8 7.0 %collective-permute-start.45 = (f32[264,128]{1,0:T(8,128)S(1)}, f32[264,128]{1,0:T(8,128)S(1)}, u32[]{:S(2)}, u32[]{:S(2)}) collective-permute-start(f32[264,128]{1,0:T(8,128)S(1)} %get-tuple-element.145), channel_id=1, source_target_pairs={{0,4},{1,5},{2,6},{3,7},{4,0},{5,1},{6,2},{7,3},{8,12},{9,13},{10,... | collective-permute-start | bytes 405512 | tf_op jit(solution)/shard_map/ppermute | solution.py:263
  101.4 6.3 %collective-permute-start.46 = (f32[248,128]{1,0:T(8,128)S(1)}, f32[248,128]{1,0:T(8,128)S(1)}, u32[]{:S(2)}, u32[]{:S(2)}) collective-permute-start(f32[248,128]{1,0:T(8,128)S(1)} %get-tuple-element.146), channel_id=1, source_target_pairs={{0,1},{1,0},{2,3},{3,2},{4,8},{5,9},{6,10},{7,11},{8,4},{9,5},{10,... | collective-permute-start | bytes 380936 | tf_op jit(solution)/shard_map/ppermute | solution.py:263
  101.9 4.4 %collective-permute-start.47 = (f32[16,128]{1,0:T(8,128)S(1)}, f32[16,128]{1,0:T(8,128)S(1)}, u32[]{:S(2)}, u32[]{:S(2)}) collective-permute-start(f32[16,128]{1,0:T(8,128)S(1)} %get-tuple-element.147), channel_id=1, source_target_pairs={{0,8},{1,9},{2,10},{3,11},{4,12},{5,13},{6,14},{7,15},{8,0},{9,1},... | collective-permute-start | bytes 24584 | tf_op jit(solution)/shard_map/ppermute | solution.py:263
  103.5 4.3 %collective-permute-start.48 = (f32[16,128]{1,0:T(8,128)S(1)}, f32[16,128]{1,0:T(8,128)S(1)}, u32[]{:S(2)}, u32[]{:S(2)}) collective-permute-start(f32[16,128]{1,0:T(8,128)S(1)} %get-tuple-element.148), channel_id=1, source_target_pairs={{0,12},{1,13},{2,14},{3,15},{4,8},{5,9},{6,10},{7,11},{8,4},{9,5},... | collective-permute-start | bytes 24584 | tf_op jit(solution)/shard_map/ppermute | solution.py:263
  107.8 10.3 %collective-permute-start.50 = (f32[312,128]{1,0:T(8,128)S(1)}, f32[312,128]{1,0:T(8,128)S(1)}, u32[]{:S(2)}, u32[]{:S(2)}) collective-permute-start(f32[312,128]{1,0:T(8,128)S(1)} %get-tuple-element.150), channel_id=1, source_target_pairs={{0,3},{1,2},{2,1},{3,0},{4,7},{5,6},{6,5},{7,4},{8,11},{9,10},{10,... | collective-permute-start | bytes 479240 | tf_op jit(solution)/shard_map/ppermute | solution.py:263
  110.6 7.6 %collective-permute-start.51 = (f32[312,128]{1,0:T(8,128)S(1)}, f32[312,128]{1,0:T(8,128)S(1)}, u32[]{:S(2)}, u32[]{:S(2)}) collective-permute-start(f32[312,128]{1,0:T(8,128)S(1)} %get-tuple-element.151), channel_id=1, source_target_pairs={{0,16},{1,17},{2,18},{3,19},{4,20},{5,21},{6,22},{7,23},{8,24},{9,... | collective-permute-start | bytes 479240 | tf_op jit(solution)/shard_map/ppermute | solution.py:263
  110.8 7.3 %collective-permute-start.49 = (f32[248,128]{1,0:T(8,128)S(1)}, f32[248,128]{1,0:T(8,128)S(1)}, u32[]{:S(2)}, u32[]{:S(2)}) collective-permute-start(f32[248,128]{1,0:T(8,128)S(1)} %get-tuple-element.149), channel_id=1, source_target_pairs={{0,1},{1,0},{2,3},{3,2},{4,5},{5,4},{6,7},{7,6},{8,9},{9,8},{10,11... | collective-permute-start | bytes 380936 | tf_op jit(solution)/shard_map/ppermute | solution.py:263
  110.9 7.3 %collective-permute-start.53 = (f32[96,128]{1,0:T(8,128)S(1)}, f32[96,128]{1,0:T(8,128)S(1)}, u32[]{:S(2)}, u32[]{:S(2)}) collective-permute-start(f32[96,128]{1,0:T(8,128)S(1)} %get-tuple-element.153), channel_id=1, source_target_pairs={{0,19},{1,18},{2,17},{3,16},{4,23},{5,22},{6,21},{7,20},{8,27},{9,... | collective-permute-start | bytes 147464 | tf_op jit(solution)/shard_map/ppermute | solution.py:263
  113.2 4.9 %collective-permute-start.52 = (f32[32,128]{1,0:T(8,128)S(1)}, f32[32,128]{1,0:T(8,128)S(1)}, u32[]{:S(2)}, u32[]{:S(2)}) collective-permute-start(f32[32,128]{1,0:T(8,128)S(1)} %get-tuple-element.152), channel_id=1, source_target_pairs={{0,17},{1,16},{2,19},{3,18},{4,21},{5,20},{6,23},{7,22},{8,25},{9,... | collective-permute-start | bytes 49160 | tf_op jit(solution)/shard_map/ppermute | solution.py:263
  119.3 4.5 %collective-permute-start.54 = (f32[248,128]{1,0:T(8,128)S(1)}, f32[248,128]{1,0:T(8,128)S(1)}, u32[]{:S(2)}, u32[]{:S(2)}) collective-permute-start(f32[248,128]{1,0:T(8,128)S(1)} %get-tuple-element.160), channel_id=1, source_target_pairs={{0,4},{1,5},{2,6},{3,7},{4,0},{5,1},{6,2},{7,3},{8,12},{9,13},{10,... | collective-permute-start | bytes 380936 | tf_op jit(solution)/shard_map/ppermute | solution.py:263
  119.4 4.4 %collective-permute-start.55 = (f32[248,128]{1,0:T(8,128)S(1)}, f32[248,128]{1,0:T(8,128)S(1)}, u32[]{:S(2)}, u32[]{:S(2)}) collective-permute-start(f32[248,128]{1,0:T(8,128)S(1)} %get-tuple-element.161), channel_id=1, source_target_pairs={{0,1},{1,0},{2,3},{3,2},{4,8},{5,9},{6,10},{7,11},{8,4},{9,5},{10,... | collective-permute-start | bytes 380936 | tf_op jit(solution)/shard_map/ppermute | solution.py:263
  123.9 9.0 %collective-permute-start.56 = (f32[248,128]{1,0:T(8,128)S(1)}, f32[248,128]{1,0:T(8,128)S(1)}, u32[]{:S(2)}, u32[]{:S(2)}) collective-permute-start(f32[248,128]{1,0:T(8,128)S(1)} %get-tuple-element.162), channel_id=1, source_target_pairs={{0,1},{1,0},{2,3},{3,2},{4,5},{5,4},{6,7},{7,6},{8,9},{9,8},{10,11... | collective-permute-start | bytes 380936 | tf_op jit(solution)/shard_map/ppermute | solution.py:263
  125.4 7.5 %collective-permute-start.57 = (f32[248,128]{1,0:T(8,128)S(1)}, f32[248,128]{1,0:T(8,128)S(1)}, u32[]{:S(2)}, u32[]{:S(2)}) collective-permute-start(f32[248,128]{1,0:T(8,128)S(1)} %get-tuple-element.163), channel_id=1, source_target_pairs={{0,4},{1,2},{2,1},{3,7},{4,0},{5,6},{6,5},{7,3},{8,12},{9,10},{10,... | collective-permute-start | bytes 380936 | tf_op jit(solution)/shard_map/ppermute | solution.py:263
  126.0 6.9 %collective-permute-start.58 = (f32[248,128]{1,0:T(8,128)S(1)}, f32[248,128]{1,0:T(8,128)S(1)}, u32[]{:S(2)}, u32[]{:S(2)}) collective-permute-start(f32[248,128]{1,0:T(8,128)S(1)} %get-tuple-element.164), channel_id=1, source_target_pairs={{0,16},{1,17},{2,18},{3,19},{4,20},{5,21},{6,22},{7,23},{8,24},{9,... | collective-permute-start | bytes 380936 | tf_op jit(solution)/shard_map/ppermute | solution.py:263
  126.2 5.6 %collective-permute-start.59 = (f32[32,128]{1,0:T(8,128)S(1)}, f32[32,128]{1,0:T(8,128)S(1)}, u32[]{:S(2)}, u32[]{:S(2)}) collective-permute-start(f32[32,128]{1,0:T(8,128)S(1)} %get-tuple-element.165), channel_id=1, source_target_pairs={{0,17},{1,16},{2,19},{3,18},{4,21},{5,20},{6,23},{7,22},{8,25},{9,... | collective-permute-start | bytes 49160 | tf_op jit(solution)/shard_map/ppermute | solution.py:263
  128.8 4.1 %collective-permute-start.60 = (f32[32,128]{1,0:T(8,128)S(1)}, f32[32,128]{1,0:T(8,128)S(1)}, u32[]{:S(2)}, u32[]{:S(2)}) collective-permute-start(f32[32,128]{1,0:T(8,128)S(1)} %get-tuple-element.166), channel_id=1, source_target_pairs={{0,4},{1,18},{2,17},{3,7},{4,0},{5,22},{6,21},{7,3},{8,12},{9,26},... | collective-permute-start | bytes 49160 | tf_op jit(solution)/shard_map/ppermute | solution.py:263
  (3 other events, 2.8 us)

commit v6 on v5

--- a/solution.py
+++ b/solution.py
@@ -49,6 +49,9 @@
 COARSE_AT = _lay(EARLY, 0)
 SPLIT = -(-(COARSE_AT + 16) // 16) * 16
 ROWS = -(-_lay(LATE, SPLIT) // TILE) * TILE
+TILES = ROWS // TILE
+CUT_INVERSE = 3
+CUT_SCHUR = 2
 PARTS = {"all": (0, ROWS), "early": (0, SPLIT), "late": (SPLIT, ROWS)}
 
 
@@ -381,25 +384,31 @@
     turned[:, :6] = dot_last(one[...], basis[...]) * weight[:, :6]
 
 
-def left_kernel(one, matrix, basis, mid, few):
-    for t in range(0, ROWS, TILE):
-        mid[t : t + TILE, :] = dot(one[t : t + TILE, :], matrix[...]).astype(BF16)
-    if basis is not None:
-        few[...] = jnp.zeros(few.shape, F32)
-        few[:6, :] = basis[...].astype(F32)
-        mid[COARSE_AT : COARSE_AT + 16, :] = few[...].astype(BF16)
-
-
-def right_left_kernel(one, mid, weight, other, out, mid_other):
-    right(one, mid, weight, out)
-    left_kernel(one, other, None, mid_other, None)
-
-
-def right_kernel(one, mid, out):
-    right(one, mid, None, out)
-
-
-def right(one, mid, weight, out):
+def left_tiles(one, matrix, start, stop, out):
+    for t in range(start, stop):
+        at = (t - start) * TILE
+        out[at : at + TILE, :] = dot(one[t * TILE : (t + 1) * TILE, :], matrix[...]).astype(BF16)
+
+
+def inverse_left_kernel(one, matrix, basis, mid, few):
+    left_tiles(one, matrix, 0, CUT_INVERSE, mid)
+    few[...] = jnp.zeros(few.shape, F32)
+    few[:6, :] = basis[...].astype(F32)
+    mid[COARSE_AT : COARSE_AT + 16, :] = few[...].astype(BF16)
+
+
+def inverse_right_kernel(one, mid, matrix, weight, schur, out, schur_mid, more):
+    left_tiles(one, matrix, CUT_INVERSE, TILES, more)
+    right(one, (mid, more), weight, out)
+    left_tiles(one, schur, 0, CUT_SCHUR, schur_mid)
+
+
+def schur_right_kernel(one, mid, matrix, out, more):
+    left_tiles(one, matrix, CUT_SCHUR, TILES, more)
+    right(one, (mid, more), None, out)
+
+
+def right(one, mids, weight, out):
     order = sorted(range(ROWS // TILE), key=lambda t: (t != COARSE_AT // TILE, t))
 
     def put(value, i, j):
@@ -413,8 +422,10 @@
         out[i * TILE : (i + 1) * TILE, j * TILE : (j + 1) * TILE] = value.astype(BF16)
 
     for a, i in enumerate(order):
+        cut = mids[0].shape[0] // TILE
+        mid, at = (mids[0], i * TILE) if i < cut else (mids[1], (i - cut) * TILE)
         for j in order[a:]:
-            value = dot_last(mid[i * TILE : (i + 1) * TILE, :], one[j * TILE : (j + 1) * TILE, :])
+            value = dot_last(mid[at : at + TILE, :], one[j * TILE : (j + 1) * TILE, :])
             put(value, i, j)
             if i != j:
                 put(value.T, j, i)
@@ -670,17 +681,23 @@
         functools.partial(gather_kernel, LATE, SPLIT), [shape(late_rows, 128)], [canon, load], specs=[smem, vm()]
     )
     flops = 2 * ROWS * IFACE * IFACE
-    middle_shape, square = shape(ROWS, IFACE, BF16), shape(ROWS, ROWS, BF16)
-
+    square = shape(ROWS, ROWS, BF16)
+
+    matrix, other = local_inverse[0, 0, 0], schur_matrix[0, 0, 0]
     (half,) = call(
-        left_kernel,
-        [middle_shape],
-        [one, local_inverse[0, 0, 0], basis],
+        inverse_left_kernel,
+        [shape(CUT_INVERSE * TILE, IFACE, BF16)],
+        [one, matrix, basis],
         scratch=[pltpu.VMEM((16, IFACE), F32)],
         flops=flops,
     )
     inverse, half = call(
-        right_left_kernel, [square, middle_shape], [one, half, weight, schur_matrix[0, 0, 0]], flops=2 * flops
+        inverse_right_kernel,
+        [square, shape(CUT_SCHUR * TILE, IFACE, BF16)],
+        [one, half, matrix, weight, other],
+        scratch=[pltpu.VMEM(((TILES - CUT_INVERSE) * TILE, IFACE), BF16)],
+        limit=24,
+        flops=2 * flops,
     )
     blocks = []
     if plan.ride:
@@ -702,7 +719,13 @@
             scratch=[pltpu.VMEM((plan.wide, plan.wide), F32), pltpu.VMEM((ROWS, plan.wide), F32), pieces],
             flops=2 * ROWS * 3 * plan.wide * plan.wide,
         )
-    (schur,) = call(right_kernel, [square], [one, half], flops=flops)
+    (schur,) = call(
+        schur_right_kernel,
+        [square],
+        [one, half, other],
+        scratch=[pltpu.VMEM(((TILES - CUT_SCHUR) * TILE, IFACE), BF16)],
+        flops=flops,
+    )
     sol = residual = None
     flops = 2 * ROWS * ROWS * 128
     for iteration in range(ITERS):

time: 136 us -> 135 us (level)
  waiting for transfers between devices: 37.3 us -> 30.1 us
  starting transfers between devices: 58.4 us -> 64.9 us
    ppermute x61, waiting for transfers between devices: 37.3 us -> 30.1 us  [transfer(): lax.ppermute(p, AXES, m.pairs())]
    ppermute x61, starting transfers between devices: 58.4 us -> 64.9 us  [transfer(): lax.ppermute(p, AXES, m.pairs())]
  transfers between devices with their start and end apart: 61 -> 61, of which waited for: 20 -> 17; matrix products, arithmetic and copies ran while one was open for 1% -> 1% of each run, Pallas kernels for 21% -> 21%
where the time goes in v6:
time: 135 us
  starting transfers between devices  64.9 us (48%)
  Pallas kernels  36.8 us (27%)
  waiting for transfers between devices  30.1 us (22%)
  local copies, waits for them, and re-layouts  1.91 us (1%)
    ppermute x61, starting transfers between devices, transfer(): lax.ppermute(p, AXES, m.pairs())  64.9 us
    pallas_call x34, Pallas kernels, call(): pl.pallas_call(kernel, out_shape=tuple(outs), in_specs=specs or [vm()] *...  36.8 us
    ppermute x61, waiting for transfers between devices, transfer(): lax.ppermute(p, AXES, m.pairs())  30.1 us
  transfers between devices with their start and end apart: 61, of which 17 were waited for; matrix products, arithmetic and copies ran while one was open for 1% of the time, Pallas kernels for 21%

profile of v6, /device:TPU:1, one launch (start us, length us, event | category | flops | bytes accessed | tf_op | source)
XLA Modules:
  0.0 134.8 jit_solution(9251124634980903400)
XLA Ops:
  0.6 0.7 copy-done.3
  1.6 3.8 %collective-permute-start.1 = (f32[16,128]{1,0:T(8,128)S(1)}, f32[16,128]{1,0:T(8,128)S(1)}, u32[]{:S(2)}, u32[]{:S(2)}) collective-permute-start(f32[16,128]{1,0:T(8,128)S(1)} %shard_map.83.refs_1_.refs_4_), channel_id=1, source_target_pairs={{0,8},{1,9},{2,10},{3,11},{4,12},{5,13},{6,14},{7,15},{8,0},{9,1},... | collective-permute-start | bytes 24584 | tf_op jit(solution)/shard_map/ppermute | solution.py:266
  5.3 0.9 copy.10.canon
  6.3 0.8 shard_map.77
  7.4 1.0 shard_map.81.refs_0_
  8.4 1.1 shard_map.84.refs_5_.refs_8_.refs_0_
  9.7 1.6 %collective-permute-start.3 = (f32[336,128]{1,0:T(8,128)S(1)}, f32[336,128]{1,0:T(8,128)S(1)}, u32[]{:S(2)}, u32[]{:S(2)}) collective-permute-start(f32[336,128]{1,0:T(8,128)S(1)} %get-tuple-element.89), channel_id=1, source_target_pairs={{0,4},{1,5},{2,6},{3,7},{4,0},{5,1},{6,2},{7,3},{8,12},{9,13},{10,... | collective-permute-start | bytes 516104 | tf_op jit(solution)/shard_map/ppermute | solution.py:266
  11.7 2.7 %shard_map.78.mid = bf16[768,1158]{1,0:T(8,128)(2,1)S(1)} custom-call(bf16[1280,1158]{1,0:T(8,128)(2,1)S(1)} %get-tuple-element.85.one, bf16[1158,1158]{1,0:T(8,128)(2,1)S(1)} %bitcast.21, bf16[6,1158]{1,0:T(8,128)(2,1)S(1)} %bitcast.20), custom_call_target="tpu_custom_call" | custom-call | flops 3432867840 | bytes 7438992 | tf_op jit(solution)/shard_map/pallas_call | solution.py:279
  14.5 1.2 shard_map.82.refs_1_
  16.0 1.0 collective-permute-start.5
  17.0 1.4 %collective-permute-start.6 = (f32[400,128]{1,0:T(8,128)S(1)}, f32[400,128]{1,0:T(8,128)S(1)}, u32[]{:S(2)}, u32[]{:S(2)}) collective-permute-start(f32[400,128]{1,0:T(8,128)S(1)} %get-tuple-element.92), channel_id=1, source_target_pairs={{0,3},{1,2},{2,1},{3,0},{4,7},{5,6},{6,5},{7,4},{8,11},{9,10},{10,... | collective-permute-start | bytes 614408 | tf_op jit(solution)/shard_map/ppermute | solution.py:266
  18.4 1.2 collective-permute-start.7
  19.6 0.9 collective-permute-start.8
  20.4 0.8 collective-permute-start.9
  21.3 6.3 %shard_map.79 = (bf16[1280,1280]{1,0:T(8,128)(2,1)S(1)}, bf16[512,1158]{1,0:T(8,128)(2,1)S(1)}) custom-call(bf16[1280,1158]{1,0:T(8,128)(2,1)S(1)} %get-tuple-element.85.one, bf16[768,1158]{1,0:T(8,128)(2,1)S(1)} %shard_map.78.mid, bf16[1158,1158]{1,0:T(8,128)(2,1)S(1)} %bitcast.22, f32[1280,128]{1,0:T(8,128)S(1)} %get-tuple-element.86.weight.refs_10_, ...), custom_call_target="tpu_custom_call" | custom-call | flops 6865735680 | bytes 15224976 | tf_op jit(solution)/shard_map/pallas_call | solution.py:279
  27.9 0.7 collective-permute-start.10
  28.7 1.0 shard_map.88.refs_0_
  29.7 1.9 %collective-permute-start.11 = (f32[264,128]{1,0:T(8,128)S(1)}, f32[264,128]{1,0:T(8,128)S(1)}, u32[]{:S(2)}, u32[]{:S(2)}) collective-permute-start(f32[264,128]{1,0:T(8,128)S(1)} %get-tuple-element.98), channel_id=1, source_target_pairs={{0,4},{1,5},{2,6},{3,7},{4,0},{5,1},{6,2},{7,3},{8,12},{9,13},{10,... | collective-permute-start | bytes 405512 | tf_op jit(solution)/shard_map/ppermute | solution.py:266
  32.0 1.4 %collective-permute-start.13 = (f32[16,128]{1,0:T(8,128)S(1)}, f32[16,128]{1,0:T(8,128)S(1)}, u32[]{:S(2)}, u32[]{:S(2)}) collective-permute-start(f32[16,128]{1,0:T(8,128)S(1)} %get-tuple-element.100), channel_id=1, source_target_pairs={{0,8},{1,9},{2,10},{3,11},{4,12},{5,13},{6,14},{7,15},{8,0},{9,1},... | collective-permute-start | bytes 24584 | tf_op jit(solution)/shard_map/ppermute | solution.py:266
  33.4 2.4 %collective-permute-start.14 = (f32[16,128]{1,0:T(8,128)S(1)}, f32[16,128]{1,0:T(8,128)S(1)}, u32[]{:S(2)}, u32[]{:S(2)}) collective-permute-start(f32[16,128]{1,0:T(8,128)S(1)} %get-tuple-element.101), channel_id=1, source_target_pairs={{0,12},{1,13},{2,14},{3,15},{4,8},{5,9},{6,10},{7,11},{8,4},{9,5},... | collective-permute-start | bytes 24584 | tf_op jit(solution)/shard_map/ppermute | solution.py:266
  35.8 2.4 %shard_map.90.refs_1_.refs_11_ = bf16[1280,768]{1,0:T(8,128)(2,1)S(1)} custom-call(f32[1280,128]{1,0:T(8,128)S(1)} %shard_map.84.refs_5_.refs_8_.refs_0_, f32[16,128]{1,0:T(8,128)S(1)} %shard_map.83.refs_1_.refs_4_, f32[16,128]{1,0:T(8,128)S(1)} %collective-permute-done.refs_2_.refs_5_, f32[16,128]{1,0:T(8,128)S(1)} %collective-permute-done.1.refs_3_.refs_6_, ...), custom_call_target="tpu_custom_call" | custom-call | flops 503316480 | bytes 3637248 | tf_op jit(solution)/shard_map/pallas_call | solution.py:279
  38.3 1.4 %collective-permute-start.15 = (f32[248,128]{1,0:T(8,128)S(1)}, f32[248,128]{1,0:T(8,128)S(1)}, u32[]{:S(2)}, u32[]{:S(2)}) collective-permute-start(f32[248,128]{1,0:T(8,128)S(1)} %get-tuple-element.102), channel_id=1, source_target_pairs={{0,1},{1,0},{2,3},{3,2},{4,5},{5,4},{6,7},{7,6},{8,9},{9,8},{10,11... | collective-permute-start | bytes 380936 | tf_op jit(solution)/shard_map/ppermute | solution.py:266
  39.7 1.2 collective-permute-start.16
  40.9 1.0 collective-permute-start.17
  41.9 1.1 collective-permute-start.18
  43.6 5.3 %shard_map.80.refs_10_.matrix = bf16[1280,1280]{1,0:T(8,128)(2,1)S(1)} custom-call(bf16[1280,1158]{1,0:T(8,128)(2,1)S(1)} %get-tuple-element.85.one, bf16[512,1158]{1,0:T(8,128)(2,1)S(1)} %get-tuple-element.87.mid, bf16[1158,1158]{1,0:T(8,128)(2,1)S(1)} %bitcast.24), custom_call_target="tpu_custom_call" | custom-call | flops 3432867840 | bytes 10109000 | tf_op jit(solution)/shard_map/pallas_call | solution.py:279
  49.0 1.2 shard_map.92
  50.3 0.8 collective-permute-start.21
  51.7 2.8 %collective-permute-done.20.refs_2_ = f32[248,128]{1,0:T(8,128)S(1)} collective-permute-done((f32[248,128]{1,0:T(8,128)S(1)}, f32[248,128]{1,0:T(8,128)S(1)}, u32[]{:S(2)}, u32[]{:S(2)}) %collective-permute-start.20) | collective-permute-done | bytes 127008 | tf_op jit(solution)/shard_map/ppermute | solution.py:266
  54.6 1.7 %collective-permute-start.22 = (f32[248,128]{1,0:T(8,128)S(1)}, f32[248,128]{1,0:T(8,128)S(1)}, u32[]{:S(2)}, u32[]{:S(2)}) collective-permute-start(f32[248,128]{1,0:T(8,128)S(1)} %get-tuple-element.113), channel_id=1, source_target_pairs={{0,1},{1,0},{2,3},{3,2},{4,5},{5,4},{6,7},{7,6},{8,9},{9,8},{10,11... | collective-permute-start | bytes 380936 | tf_op jit(solution)/shard_map/ppermute | solution.py:266
  56.2 1.2 collective-permute-start.23
  57.9 2.1 %collective-permute-start.25 = (f32[32,128]{1,0:T(8,128)S(1)}, f32[32,128]{1,0:T(8,128)S(1)}, u32[]{:S(2)}, u32[]{:S(2)}) collective-permute-start(f32[32,128]{1,0:T(8,128)S(1)} %get-tuple-element.116), channel_id=1, source_target_pairs={{0,17},{1,16},{2,19},{3,18},{4,21},{5,20},{6,23},{7,22},{8,25},{9,... | collective-permute-start | bytes 49160 | tf_op jit(solution)/shard_map/ppermute | solution.py:266
  60.0 1.2 collective-permute-start.26
  61.1 1.9 %collective-permute-done.25.refs_7_ = f32[32,128]{1,0:T(8,128)S(1)} collective-permute-done((f32[32,128]{1,0:T(8,128)S(1)}, f32[32,128]{1,0:T(8,128)S(1)}, u32[]{:S(2)}, u32[]{:S(2)}) %collective-permute-start.25) | collective-permute-done | bytes 16416 | tf_op jit(solution)/shard_map/ppermute | solution.py:266
  63.0 1.0 collective-permute-done.26.refs_8_
  64.4 1.0 shard_map.96.refs_0_
  66.9 1.6 %collective-permute-start.30 = (f32[16,128]{1,0:T(8,128)S(1)}, f32[16,128]{1,0:T(8,128)S(1)}, u32[]{:S(2)}, u32[]{:S(2)}) collective-permute-start(f32[16,128]{1,0:T(8,128)S(1)} %get-tuple-element.123), channel_id=1, source_target_pairs={{0,8},{1,9},{2,10},{3,11},{4,12},{5,13},{6,14},{7,15},{8,0},{9,1},... | collective-permute-start | bytes 24584 | tf_op jit(solution)/shard_map/ppermute | solution.py:266
  68.5 2.4 %collective-permute-start.31 = (f32[16,128]{1,0:T(8,128)S(1)}, f32[16,128]{1,0:T(8,128)S(1)}, u32[]{:S(2)}, u32[]{:S(2)}) collective-permute-start(f32[16,128]{1,0:T(8,128)S(1)} %get-tuple-element.124), channel_id=1, source_target_pairs={{0,12},{1,13},{2,14},{3,15},{4,8},{5,9},{6,10},{7,11},{8,4},{9,5},... | collective-permute-start | bytes 24584 | tf_op jit(solution)/shard_map/ppermute | solution.py:266
  71.5 1.4 %collective-permute-done.31.refs_4_ = f32[16,128]{1,0:T(8,128)S(1)} collective-permute-done((f32[16,128]{1,0:T(8,128)S(1)}, f32[16,128]{1,0:T(8,128)S(1)}, u32[]{:S(2)}, u32[]{:S(2)}) %collective-permute-start.31) | collective-permute-done | bytes 8224 | tf_op jit(solution)/shard_map/ppermute | solution.py:266
  73.0 2.8 %collective-permute-start.33 = (f32[312,128]{1,0:T(8,128)S(1)}, f32[312,128]{1,0:T(8,128)S(1)}, u32[]{:S(2)}, u32[]{:S(2)}) collective-permute-start(f32[312,128]{1,0:T(8,128)S(1)} %get-tuple-element.126), channel_id=1, source_target_pairs={{0,3},{1,2},{2,1},{3,0},{4,7},{5,6},{6,5},{7,4},{8,11},{9,10},{10,... | collective-permute-start | bytes 479240 | tf_op jit(solution)/shard_map/ppermute | solution.py:266
  76.2 1.8 %collective-permute-start.36 = (f32[96,128]{1,0:T(8,128)S(1)}, f32[96,128]{1,0:T(8,128)S(1)}, u32[]{:S(2)}, u32[]{:S(2)}) collective-permute-start(f32[96,128]{1,0:T(8,128)S(1)} %get-tuple-element.129), channel_id=1, source_target_pairs={{0,19},{1,18},{2,17},{3,16},{4,23},{5,22},{6,21},{7,20},{8,27},{9,... | collective-permute-start | bytes 147464 | tf_op jit(solution)/shard_map/ppermute | solution.py:266
  78.4 4.7 %collective-permute-done.35.refs_8_ = f32[32,128]{1,0:T(8,128)S(1)} collective-permute-done((f32[32,128]{1,0:T(8,128)S(1)}, f32[32,128]{1,0:T(8,128)S(1)}, u32[]{:S(2)}, u32[]{:S(2)}) %collective-permute-start.35) | collective-permute-done | bytes 16416 | tf_op jit(solution)/shard_map/ppermute | solution.py:266
  83.3 1.2 shard_map.99
  85.8 3.2 %collective-permute-done.37.refs_2_ = f32[248,128]{1,0:T(8,128)S(1)} collective-permute-done((f32[248,128]{1,0:T(8,128)S(1)}, f32[248,128]{1,0:T(8,128)S(1)}, u32[]{:S(2)}, u32[]{:S(2)}) %collective-permute-start.37) | collective-permute-done | bytes 127008 | tf_op jit(solution)/shard_map/ppermute | solution.py:266
  89.0 1.4 %collective-permute-start.39 = (f32[248,128]{1,0:T(8,128)S(1)}, f32[248,128]{1,0:T(8,128)S(1)}, u32[]{:S(2)}, u32[]{:S(2)}) collective-permute-start(f32[248,128]{1,0:T(8,128)S(1)} %get-tuple-element.137), channel_id=1, source_target_pairs={{0,1},{1,0},{2,3},{3,2},{4,5},{5,4},{6,7},{7,6},{8,9},{9,8},{10,11... | collective-permute-start | bytes 380936 | tf_op jit(solution)/shard_map/ppermute | solution.py:266
  91.6 2.5 %collective-permute-start.42 = (f32[32,128]{1,0:T(8,128)S(1)}, f32[32,128]{1,0:T(8,128)S(1)}, u32[]{:S(2)}, u32[]{:S(2)}) collective-permute-start(f32[32,128]{1,0:T(8,128)S(1)} %get-tuple-element.140), channel_id=1, source_target_pairs={{0,17},{1,16},{2,19},{3,18},{4,21},{5,20},{6,23},{7,22},{8,25},{9,... | collective-permute-start | bytes 49160 | tf_op jit(solution)/shard_map/ppermute | solution.py:266
  94.0 0.7 collective-permute-start.43
  94.8 2.4 %collective-permute-done.42.refs_7_ = f32[32,128]{1,0:T(8,128)S(1)} collective-permute-done((f32[32,128]{1,0:T(8,128)S(1)}, f32[32,128]{1,0:T(8,128)S(1)}, u32[]{:S(2)}, u32[]{:S(2)}) %collective-permute-start.42) | collective-permute-done | bytes 16416 | tf_op jit(solution)/shard_map/ppermute | solution.py:266
  97.2 1.0 collective-permute-done.43.refs_8_
  98.6 1.0 shard_map.103.refs_0_
  99.8 0.7 collective-permute-start.45
  100.9 1.7 %collective-permute-start.47 = (f32[16,128]{1,0:T(8,128)S(1)}, f32[16,128]{1,0:T(8,128)S(1)}, u32[]{:S(2)}, u32[]{:S(2)}) collective-permute-start(f32[16,128]{1,0:T(8,128)S(1)} %get-tuple-element.147), channel_id=1, source_target_pairs={{0,8},{1,9},{2,10},{3,11},{4,12},{5,13},{6,14},{7,15},{8,0},{9,1},... | collective-permute-start | bytes 24584 | tf_op jit(solution)/shard_map/ppermute | solution.py:266
  102.6 2.4 %collective-permute-start.48 = (f32[16,128]{1,0:T(8,128)S(1)}, f32[16,128]{1,0:T(8,128)S(1)}, u32[]{:S(2)}, u32[]{:S(2)}) collective-permute-start(f32[16,128]{1,0:T(8,128)S(1)} %get-tuple-element.148), channel_id=1, source_target_pairs={{0,12},{1,13},{2,14},{3,15},{4,8},{5,9},{6,10},{7,11},{8,4},{9,5},... | collective-permute-start | bytes 24584 | tf_op jit(solution)/shard_map/ppermute | solution.py:266
  105.4 1.5 %collective-permute-done.48.refs_4_ = f32[16,128]{1,0:T(8,128)S(1)} collective-permute-done((f32[16,128]{1,0:T(8,128)S(1)}, f32[16,128]{1,0:T(8,128)S(1)}, u32[]{:S(2)}, u32[]{:S(2)}) %collective-permute-start.48) | collective-permute-done | bytes 8224 | tf_op jit(solution)/shard_map/ppermute | solution.py:266
  107.0 2.7 %collective-permute-start.50 = (f32[312,128]{1,0:T(8,128)S(1)}, f32[312,128]{1,0:T(8,128)S(1)}, u32[]{:S(2)}, u32[]{:S(2)}) collective-permute-start(f32[312,128]{1,0:T(8,128)S(1)} %get-tuple-element.150), channel_id=1, source_target_pairs={{0,3},{1,2},{2,1},{3,0},{4,7},{5,6},{6,5},{7,4},{8,11},{9,10},{10,... | collective-permute-start | bytes 479240 | tf_op jit(solution)/shard_map/ppermute | solution.py:266
  110.2 2.1 %collective-permute-start.53 = (f32[96,128]{1,0:T(8,128)S(1)}, f32[96,128]{1,0:T(8,128)S(1)}, u32[]{:S(2)}, u32[]{:S(2)}) collective-permute-start(f32[96,128]{1,0:T(8,128)S(1)} %get-tuple-element.153), channel_id=1, source_target_pairs={{0,19},{1,18},{2,17},{3,16},{4,23},{5,22},{6,21},{7,20},{8,27},{9,... | collective-permute-start | bytes 147464 | tf_op jit(solution)/shard_map/ppermute | solution.py:266
  112.6 4.6 %collective-permute-done.52.refs_8_ = f32[32,128]{1,0:T(8,128)S(1)} collective-permute-done((f32[32,128]{1,0:T(8,128)S(1)}, f32[32,128]{1,0:T(8,128)S(1)}, u32[]{:S(2)}, u32[]{:S(2)}) %collective-permute-start.52) | collective-permute-done | bytes 16416 | tf_op jit(solution)/shard_map/ppermute | solution.py:266
  117.2 1.4 %shard_map.106 = (f32[1280,128]{1,0:T(8,128)S(1)}, bf16[1280,128]{1,0:T(8,128)(2,1)S(1)}, f32[576,128]{1,0:T(8,128)S(1)}, f32[248,128]{1,0:T(8,128)S(1)}, f32[248,128]{1,0:T(8,128)S(1)}) custom-call(f32[1280,128]{1,0:T(8,128)S(1)} %shard_map.103.refs_0_, f32[264,128]{1,0:T(8,128)S(1)} %collective-permute-done.45.refs_1_, ...), custom_call_target="tpu_custom_call" | custom-call | flops 419430400 | bytes 8228864 | tf_op jit(solution)/shard_map/pallas_call | solution.py:279
  120.0 3.1 %collective-permute-done.54.refs_2_.refs_0_ = f32[248,128]{1,0:T(8,128)S(1)} collective-permute-done((f32[248,128]{1,0:T(8,128)S(1)}, f32[248,128]{1,0:T(8,128)S(1)}, u32[]{:S(2)}, u32[]{:S(2)}) %collective-permute-start.54) | collective-permute-done | bytes 127008 | tf_op jit(solution)/shard_map/ppermute | solution.py:266
  123.2 1.5 %collective-permute-start.56 = (f32[248,128]{1,0:T(8,128)S(1)}, f32[248,128]{1,0:T(8,128)S(1)}, u32[]{:S(2)}, u32[]{:S(2)}) collective-permute-start(f32[248,128]{1,0:T(8,128)S(1)} %get-tuple-element.162), channel_id=1, source_target_pairs={{0,1},{1,0},{2,3},{3,2},{4,5},{5,4},{6,7},{7,6},{8,9},{9,8},{10,11... | collective-permute-start | bytes 380936 | tf_op jit(solution)/shard_map/ppermute | solution.py:266
  125.8 2.3 %collective-permute-start.59 = (f32[32,128]{1,0:T(8,128)S(1)}, f32[32,128]{1,0:T(8,128)S(1)}, u32[]{:S(2)}, u32[]{:S(2)}) collective-permute-start(f32[32,128]{1,0:T(8,128)S(1)} %get-tuple-element.165), channel_id=1, source_target_pairs={{0,17},{1,16},{2,19},{3,18},{4,21},{5,20},{6,23},{7,22},{8,25},{9,... | collective-permute-start | bytes 49160 | tf_op jit(solution)/shard_map/ppermute | solution.py:266
  128.8 2.5 %shard_map.108 = f32[1158,1,128]{2,1,0:T(1,128)} custom-call(s32[1,1158]{1,0:T(1,128)S(1)} %bitcast.17, f32[1280,128]{1,0:T(8,128)S(1)} %get-tuple-element.157.acc), custom_call_target="tpu_custom_call" | custom-call | bytes 1252888 | tf_op jit(solution)/shard_map/pallas_call | solution.py:279
  131.4 0.9 collective-permute-done.60.refs_6_
  132.2 2.5 %shard_map.110 = f32[1158,1,128]{2,1,0:T(1,128)} custom-call(s32[1,1158]{1,0:T(1,128)S(1)} %bitcast.18, f32[576,128]{1,0:T(8,128)S(1)} %get-tuple-element.158.refs_0_.early, f32[704,128]{1,0:T(8,128)S(1)} %get-tuple-element.159.refs_1_.late, f32[248,128]{1,0:T(8,128)S(1)} %collective-permute-done.54.refs_2_.refs_0_, ...), custom_call_target="tpu_custom_call" | custom-call | bytes 2575896 | tf_op jit(solution)/shard_map/pallas_call | solution.py:279
  (105 shorter events, 15.8 us)
Async XLA Ops:
  1.5 8.0 %collective-permute-start = (f32[16,128]{1,0:T(8,128)S(1)}, f32[16,128]{1,0:T(8,128)S(1)}, u32[]{:S(2)}, u32[]{:S(2)}) collective-permute-start(f32[16,128]{1,0:T(8,128)S(1)} %shard_map.83.refs_1_.refs_4_), channel_id=1, source_target_pairs={{0,1},{1,0},{2,3},{3,2},{4,5},{5,4},{6,7},{7,6},{8,9},{9,8},{10,11... | collective-permute-start | bytes 24584 | tf_op jit(solution)/shard_map/ppermute | solution.py:266
  1.6 7.9 %collective-permute-start.1 = (f32[16,128]{1,0:T(8,128)S(1)}, f32[16,128]{1,0:T(8,128)S(1)}, u32[]{:S(2)}, u32[]{:S(2)}) collective-permute-start(f32[16,128]{1,0:T(8,128)S(1)} %shard_map.83.refs_1_.refs_4_), channel_id=1, source_target_pairs={{0,8},{1,9},{2,10},{3,11},{4,12},{5,13},{6,14},{7,15},{8,0},{9,1},... | collective-permute-start | bytes 24584 | tf_op jit(solution)/shard_map/ppermute | solution.py:266
  5.3 4.2 %collective-permute-start.2 = (f32[16,128]{1,0:T(8,128)S(1)}, f32[16,128]{1,0:T(8,128)S(1)}, u32[]{:S(2)}, u32[]{:S(2)}) collective-permute-start(f32[16,128]{1,0:T(8,128)S(1)} %shard_map.83.refs_1_.refs_4_), channel_id=1, source_target_pairs={{0,9},{1,8},{2,11},{3,10},{4,13},{5,12},{6,15},{7,14},{8,1},{9,0},... | collective-permute-start | bytes 24584 | tf_op jit(solution)/shard_map/ppermute | solution.py:266
  6.3 2.1 %copy-start.2 = (bf16[1,1,1,6,1158]{4,3,2,1,0:T(8,128)(2,1)S(1)}, bf16[1,1,1,6,1158]{4,3,2,1,0:T(8,128)(2,1)}, u32[]{:S(2)}) copy-start(bf16[1,1,1,6,1158]{4,3,2,1,0:T(8,128)(2,1)} %param.9) | copy-start | bytes 41692
  8.4 3.3 %copy-start.4 = (bf16[1,1,1,1158,1158]{4,3,2,1,0:T(8,128)(2,1)S(1)}, bf16[1,1,1,1158,1158]{4,3,2,1,0:T(8,128)(2,1)}, u32[]{:S(2)}) copy-start(bf16[1,1,1,1158,1158]{4,3,2,1,0:T(8,128)(2,1)} %param.8) | copy-start | bytes 8045788
  9.7 6.0 %collective-permute-start.3 = (f32[336,128]{1,0:T(8,128)S(1)}, f32[336,128]{1,0:T(8,128)S(1)}, u32[]{:S(2)}, u32[]{:S(2)}) collective-permute-start(f32[336,128]{1,0:T(8,128)S(1)} %get-tuple-element.89), channel_id=1, source_target_pairs={{0,4},{1,5},{2,6},{3,7},{4,0},{5,1},{6,2},{7,3},{8,12},{9,13},{10,... | collective-permute-start | bytes 516104 | tf_op jit(solution)/shard_map/ppermute | solution.py:266
  11.3 4.4 %collective-permute-start.4 = (f32[272,128]{1,0:T(8,128)S(1)}, f32[272,128]{1,0:T(8,128)S(1)}, u32[]{:S(2)}, u32[]{:S(2)}) collective-permute-start(f32[272,128]{1,0:T(8,128)S(1)} %get-tuple-element.90), channel_id=1, source_target_pairs={{0,1},{1,0},{2,3},{3,2},{4,8},{5,9},{6,10},{7,11},{8,4},{9,5},{10,... | collective-permute-start | bytes 417800 | tf_op jit(solution)/shard_map/ppermute | solution.py:266
  11.7 9.5 %copy-start.5 = (bf16[1,1,1,1158,1158]{4,3,2,1,0:T(8,128)(2,1)S(1)}, bf16[1,1,1,1158,1158]{4,3,2,1,0:T(8,128)(2,1)}, u32[]{:S(2)}) copy-start(bf16[1,1,1,1158,1158]{4,3,2,1,0:T(8,128)(2,1)} %param.7) | copy-start | bytes 8045788
  16.0 11.6 %collective-permute-start.5 = (f32[272,128]{1,0:T(8,128)S(1)}, f32[272,128]{1,0:T(8,128)S(1)}, u32[]{:S(2)}, u32[]{:S(2)}) collective-permute-start(f32[272,128]{1,0:T(8,128)S(1)} %get-tuple-element.91), channel_id=1, source_target_pairs={{0,1},{1,0},{2,3},{3,2},{4,5},{5,4},{6,7},{7,6},{8,9},{9,8},{10,11... | collective-permute-start | bytes 417800 | tf_op jit(solution)/shard_map/ppermute | solution.py:266
  17.0 10.6 %collective-permute-start.6 = (f32[400,128]{1,0:T(8,128)S(1)}, f32[400,128]{1,0:T(8,128)S(1)}, u32[]{:S(2)}, u32[]{:S(2)}) collective-permute-start(f32[400,128]{1,0:T(8,128)S(1)} %get-tuple-element.92), channel_id=1, source_target_pairs={{0,3},{1,2},{2,1},{3,0},{4,7},{5,6},{6,5},{7,4},{8,11},{9,10},{10,... | collective-permute-start | bytes 614408 | tf_op jit(solution)/shard_map/ppermute | solution.py:266
  18.4 9.2 %collective-permute-start.7 = (f32[400,128]{1,0:T(8,128)S(1)}, f32[400,128]{1,0:T(8,128)S(1)}, u32[]{:S(2)}, u32[]{:S(2)}) collective-permute-start(f32[400,128]{1,0:T(8,128)S(1)} %get-tuple-element.93), channel_id=1, source_target_pairs={{0,16},{1,17},{2,18},{3,19},{4,20},{5,21},{6,22},{7,23},{8,24},{9,... | collective-permute-start | bytes 614408 | tf_op jit(solution)/shard_map/ppermute | solution.py:266
  19.6 8.0 %collective-permute-start.8 = (f32[56,128]{1,0:T(8,128)S(1)}, f32[56,128]{1,0:T(8,128)S(1)}, u32[]{:S(2)}, u32[]{:S(2)}) collective-permute-start(f32[56,128]{1,0:T(8,128)S(1)} %get-tuple-element.94), channel_id=1, source_target_pairs={{0,17},{1,16},{2,19},{3,18},{4,21},{5,20},{6,23},{7,22},{8,25},{9,... | collective-permute-start | bytes 86024 | tf_op jit(solution)/shard_map/ppermute | solution.py:266
  20.4 7.1 %collective-permute-start.9 = (f32[184,128]{1,0:T(8,128)S(1)}, f32[184,128]{1,0:T(8,128)S(1)}, u32[]{:S(2)}, u32[]{:S(2)}) collective-permute-start(f32[184,128]{1,0:T(8,128)S(1)} %get-tuple-element.95), channel_id=1, source_target_pairs={{0,19},{1,18},{2,17},{3,16},{4,23},{5,22},{6,21},{7,20},{8,27},{9,... | collective-permute-start | bytes 282632 | tf_op jit(solution)/shard_map/ppermute | solution.py:266
  27.9 1.7 %collective-permute-start.10 = (f32[8,128]{1,0:T(8,128)S(1)}, f32[8,128]{1,0:T(8,128)S(1)}, u32[]{:S(2)}, u32[]{:S(2)}) collective-permute-start(f32[8,128]{1,0:T(8,128)S(1)} %get-tuple-element.97.refs_1_.refs_6_.refs_12_), channel_id=1, source_target_pairs={{0,1},{1,0},{2,3},{3,2},{4,5},{5,4},{6,7},{7,6},{8,9},{9,8},{10,11... | collective-permute-start | bytes 12296 | tf_op jit(solution)/shard_map/ppermute | solution.py:266
  29.7 8.5 %collective-permute-start.11 = (f32[264,128]{1,0:T(8,128)S(1)}, f32[264,128]{1,0:T(8,128)S(1)}, u32[]{:S(2)}, u32[]{:S(2)}) collective-permute-start(f32[264,128]{1,0:T(8,128)S(1)} %get-tuple-element.98), channel_id=1, source_target_pairs={{0,4},{1,5},{2,6},{3,7},{4,0},{5,1},{6,2},{7,3},{8,12},{9,13},{10,... | collective-permute-start | bytes 405512 | tf_op jit(solution)/shard_map/ppermute | solution.py:266
  31.6 6.6 %collective-permute-start.12 = (f32[248,128]{1,0:T(8,128)S(1)}, f32[248,128]{1,0:T(8,128)S(1)}, u32[]{:S(2)}, u32[]{:S(2)}) collective-permute-start(f32[248,128]{1,0:T(8,128)S(1)} %get-tuple-element.99), channel_id=1, source_target_pairs={{0,1},{1,0},{2,3},{3,2},{4,8},{5,9},{6,10},{7,11},{8,4},{9,5},{10,... | collective-permute-start | bytes 380936 | tf_op jit(solution)/shard_map/ppermute | solution.py:266
  32.0 6.2 %collective-permute-start.13 = (f32[16,128]{1,0:T(8,128)S(1)}, f32[16,128]{1,0:T(8,128)S(1)}, u32[]{:S(2)}, u32[]{:S(2)}) collective-permute-start(f32[16,128]{1,0:T(8,128)S(1)} %get-tuple-element.100), channel_id=1, source_target_pairs={{0,8},{1,9},{2,10},{3,11},{4,12},{5,13},{6,14},{7,15},{8,0},{9,1},... | collective-permute-start | bytes 24584 | tf_op jit(solution)/shard_map/ppermute | solution.py:266
  33.4 4.8 %collective-permute-start.14 = (f32[16,128]{1,0:T(8,128)S(1)}, f32[16,128]{1,0:T(8,128)S(1)}, u32[]{:S(2)}, u32[]{:S(2)}) collective-permute-start(f32[16,128]{1,0:T(8,128)S(1)} %get-tuple-element.101), channel_id=1, source_target_pairs={{0,12},{1,13},{2,14},{3,15},{4,8},{5,9},{6,10},{7,11},{8,4},{9,5},... | collective-permute-start | bytes 24584 | tf_op jit(solution)/shard_map/ppermute | solution.py:266
  38.3 10.7 %collective-permute-start.15 = (f32[248,128]{1,0:T(8,128)S(1)}, f32[248,128]{1,0:T(8,128)S(1)}, u32[]{:S(2)}, u32[]{:S(2)}) collective-permute-start(f32[248,128]{1,0:T(8,128)S(1)} %get-tuple-element.102), channel_id=1, source_target_pairs={{0,1},{1,0},{2,3},{3,2},{4,5},{5,4},{6,7},{7,6},{8,9},{9,8},{10,11... | collective-permute-start | bytes 380936 | tf_op jit(solution)/shard_map/ppermute | solution.py:266
  39.7 9.3 %collective-permute-start.16 = (f32[312,128]{1,0:T(8,128)S(1)}, f32[312,128]{1,0:T(8,128)S(1)}, u32[]{:S(2)}, u32[]{:S(2)}) collective-permute-start(f32[312,128]{1,0:T(8,128)S(1)} %get-tuple-element.103), channel_id=1, source_target_pairs={{0,3},{1,2},{2,1},{3,0},{4,7},{5,6},{6,5},{7,4},{8,11},{9,10},{10,... | collective-permute-start | bytes 479240 | tf_op jit(solution)/shard_map/ppermute | solution.py:266
  40.9 8.1 %collective-permute-start.17 = (f32[312,128]{1,0:T(8,128)S(1)}, f32[312,128]{1,0:T(8,128)S(1)}, u32[]{:S(2)}, u32[]{:S(2)}) collective-permute-start(f32[312,128]{1,0:T(8,128)S(1)} %get-tuple-element.104), channel_id=1, source_target_pairs={{0,16},{1,17},{2,18},{3,19},{4,20},{5,21},{6,22},{7,23},{8,24},{9,... | collective-permute-start | bytes 479240 | tf_op jit(solution)/shard_map/ppermute | solution.py:266
  41.9 7.1 %collective-permute-start.18 = (f32[32,128]{1,0:T(8,128)S(1)}, f32[32,128]{1,0:T(8,128)S(1)}, u32[]{:S(2)}, u32[]{:S(2)}) collective-permute-start(f32[32,128]{1,0:T(8,128)S(1)} %get-tuple-element.105), channel_id=1, source_target_pairs={{0,17},{1,16},{2,19},{3,18},{4,21},{5,20},{6,23},{7,22},{8,25},{9,... | collective-permute-start | bytes 49160 | tf_op jit(solution)/shard_map/ppermute | solution.py:266
  43.0 6.0 %collective-permute-start.19 = (f32[96,128]{1,0:T(8,128)S(1)}, f32[96,128]{1,0:T(8,128)S(1)}, u32[]{:S(2)}, u32[]{:S(2)}) collective-permute-start(f32[96,128]{1,0:T(8,128)S(1)} %get-tuple-element.106), channel_id=1, source_target_pairs={{0,19},{1,18},{2,17},{3,16},{4,23},{5,22},{6,21},{7,20},{8,27},{9,... | collective-permute-start | bytes 147464 | tf_op jit(solution)/shard_map/ppermute | solution.py:266
  50.2 4.3 %collective-permute-start.20 = (f32[248,128]{1,0:T(8,128)S(1)}, f32[248,128]{1,0:T(8,128)S(1)}, u32[]{:S(2)}, u32[]{:S(2)}) collective-permute-start(f32[248,128]{1,0:T(8,128)S(1)} %get-tuple-element.111), channel_id=1, source_target_pairs={{0,4},{1,5},{2,6},{3,7},{4,0},{5,1},{6,2},{7,3},{8,12},{9,13},{10,... | collective-permute-start | bytes 380936 | tf_op jit(solution)/shard_map/ppermute | solution.py:266
  50.3 4.2 %collective-permute-start.21 = (f32[248,128]{1,0:T(8,128)S(1)}, f32[248,128]{1,0:T(8,128)S(1)}, u32[]{:S(2)}, u32[]{:S(2)}) collective-permute-start(f32[248,128]{1,0:T(8,128)S(1)} %get-tuple-element.112), channel_id=1, source_target_pairs={{0,1},{1,0},{2,3},{3,2},{4,8},{5,9},{6,10},{7,11},{8,4},{9,5},{10,... | collective-permute-start | bytes 380936 | tf_op jit(solution)/shard_map/ppermute | solution.py:266
  54.6 9.5 %collective-permute-start.22 = (f32[248,128]{1,0:T(8,128)S(1)}, f32[248,128]{1,0:T(8,128)S(1)}, u32[]{:S(2)}, u32[]{:S(2)}) collective-permute-start(f32[248,128]{1,0:T(8,128)S(1)} %get-tuple-element.113), channel_id=1, source_target_pairs={{0,1},{1,0},{2,3},{3,2},{4,5},{5,4},{6,7},{7,6},{8,9},{9,8},{10,11... | collective-permute-start | bytes 380936 | tf_op jit(solution)/shard_map/ppermute | solution.py:266
  56.2 7.8 %collective-permute-start.23 = (f32[248,128]{1,0:T(8,128)S(1)}, f32[248,128]{1,0:T(8,128)S(1)}, u32[]{:S(2)}, u32[]{:S(2)}) collective-permute-start(f32[248,128]{1,0:T(8,128)S(1)} %get-tuple-element.114), channel_id=1, source_target_pairs={{0,4},{1,2},{2,1},{3,7},{4,0},{5,6},{6,5},{7,3},{8,12},{9,10},{10,... | collective-permute-start | bytes 380936 | tf_op jit(solution)/shard_map/ppermute | solution.py:266
  57.4 6.6 %collective-permute-start.24 = (f32[248,128]{1,0:T(8,128)S(1)}, f32[248,128]{1,0:T(8,128)S(1)}, u32[]{:S(2)}, u32[]{:S(2)}) collective-permute-start(f32[248,128]{1,0:T(8,128)S(1)} %get-tuple-element.115), channel_id=1, source_target_pairs={{0,16},{1,17},{2,18},{3,19},{4,20},{5,21},{6,22},{7,23},{8,24},{9,... | collective-permute-start | bytes 380936 | tf_op jit(solution)/shard_map/ppermute | solution.py:266
  57.9 5.1 %collective-permute-start.25 = (f32[32,128]{1,0:T(8,128)S(1)}, f32[32,128]{1,0:T(8,128)S(1)}, u32[]{:S(2)}, u32[]{:S(2)}) collective-permute-start(f32[32,128]{1,0:T(8,128)S(1)} %get-tuple-element.116), channel_id=1, source_target_pairs={{0,17},{1,16},{2,19},{3,18},{4,21},{5,20},{6,23},{7,22},{8,25},{9,... | collective-permute-start | bytes 49160 | tf_op jit(solution)/shard_map/ppermute | solution.py:266
  60.0 4.1 %collective-permute-start.26 = (f32[32,128]{1,0:T(8,128)S(1)}, f32[32,128]{1,0:T(8,128)S(1)}, u32[]{:S(2)}, u32[]{:S(2)}) collective-permute-start(f32[32,128]{1,0:T(8,128)S(1)} %get-tuple-element.117), channel_id=1, source_target_pairs={{0,4},{1,18},{2,17},{3,7},{4,0},{5,22},{6,21},{7,3},{8,12},{9,26},... | collective-permute-start | bytes 49160 | tf_op jit(solution)/shard_map/ppermute | solution.py:266
  64.4 1.2 collective-permute-start.27
  65.6 7.3 %collective-permute-start.28 = (f32[264,128]{1,0:T(8,128)S(1)}, f32[264,128]{1,0:T(8,128)S(1)}, u32[]{:S(2)}, u32[]{:S(2)}) collective-permute-start(f32[264,128]{1,0:T(8,128)S(1)} %get-tuple-element.121), channel_id=1, source_target_pairs={{0,4},{1,5},{2,6},{3,7},{4,0},{5,1},{6,2},{7,3},{8,12},{9,13},{10,... | collective-permute-start | bytes 405512 | tf_op jit(solution)/shard_map/ppermute | solution.py:266
  66.3 6.6 %collective-permute-start.29 = (f32[248,128]{1,0:T(8,128)S(1)}, f32[248,128]{1,0:T(8,128)S(1)}, u32[]{:S(2)}, u32[]{:S(2)}) collective-permute-start(f32[248,128]{1,0:T(8,128)S(1)} %get-tuple-element.122), channel_id=1, source_target_pairs={{0,1},{1,0},{2,3},{3,2},{4,8},{5,9},{6,10},{7,11},{8,4},{9,5},{10,... | collective-permute-start | bytes 380936 | tf_op jit(solution)/shard_map/ppermute | solution.py:266
  66.9 4.6 %collective-permute-start.30 = (f32[16,128]{1,0:T(8,128)S(1)}, f32[16,128]{1,0:T(8,128)S(1)}, u32[]{:S(2)}, u32[]{:S(2)}) collective-permute-start(f32[16,128]{1,0:T(8,128)S(1)} %get-tuple-element.123), channel_id=1, source_target_pairs={{0,8},{1,9},{2,10},{3,11},{4,12},{5,13},{6,14},{7,15},{8,0},{9,1},... | collective-permute-start | bytes 24584 | tf_op jit(solution)/shard_map/ppermute | solution.py:266
  68.5 4.4 %collective-permute-start.31 = (f32[16,128]{1,0:T(8,128)S(1)}, f32[16,128]{1,0:T(8,128)S(1)}, u32[]{:S(2)}, u32[]{:S(2)}) collective-permute-start(f32[16,128]{1,0:T(8,128)S(1)} %get-tuple-element.124), channel_id=1, source_target_pairs={{0,12},{1,13},{2,14},{3,15},{4,8},{5,9},{6,10},{7,11},{8,4},{9,5},... | collective-permute-start | bytes 24584 | tf_op jit(solution)/shard_map/ppermute | solution.py:266
  73.0 10.3 %collective-permute-start.33 = (f32[312,128]{1,0:T(8,128)S(1)}, f32[312,128]{1,0:T(8,128)S(1)}, u32[]{:S(2)}, u32[]{:S(2)}) collective-permute-start(f32[312,128]{1,0:T(8,128)S(1)} %get-tuple-element.126), channel_id=1, source_target_pairs={{0,3},{1,2},{2,1},{3,0},{4,7},{5,6},{6,5},{7,4},{8,11},{9,10},{10,... | collective-permute-start | bytes 479240 | tf_op jit(solution)/shard_map/ppermute | solution.py:266
  75.8 7.5 %collective-permute-start.34 = (f32[312,128]{1,0:T(8,128)S(1)}, f32[312,128]{1,0:T(8,128)S(1)}, u32[]{:S(2)}, u32[]{:S(2)}) collective-permute-start(f32[312,128]{1,0:T(8,128)S(1)} %get-tuple-element.127), channel_id=1, source_target_pairs={{0,16},{1,17},{2,18},{3,19},{4,20},{5,21},{6,22},{7,23},{8,24},{9,... | collective-permute-start | bytes 479240 | tf_op jit(solution)/shard_map/ppermute | solution.py:266
  76.2 7.0 %collective-permute-start.32 = (f32[248,128]{1,0:T(8,128)S(1)}, f32[248,128]{1,0:T(8,128)S(1)}, u32[]{:S(2)}, u32[]{:S(2)}) collective-permute-start(f32[248,128]{1,0:T(8,128)S(1)} %get-tuple-element.125), channel_id=1, source_target_pairs={{0,1},{1,0},{2,3},{3,2},{4,5},{5,4},{6,7},{7,6},{8,9},{9,8},{10,11... | collective-permute-start | bytes 380936 | tf_op jit(solution)/shard_map/ppermute | solution.py:266
  76.2 7.0 %collective-permute-start.36 = (f32[96,128]{1,0:T(8,128)S(1)}, f32[96,128]{1,0:T(8,128)S(1)}, u32[]{:S(2)}, u32[]{:S(2)}) collective-permute-start(f32[96,128]{1,0:T(8,128)S(1)} %get-tuple-element.129), channel_id=1, source_target_pairs={{0,19},{1,18},{2,17},{3,16},{4,23},{5,22},{6,21},{7,20},{8,27},{9,... | collective-permute-start | bytes 147464 | tf_op jit(solution)/shard_map/ppermute | solution.py:266
  78.1 5.0 %collective-permute-start.35 = (f32[32,128]{1,0:T(8,128)S(1)}, f32[32,128]{1,0:T(8,128)S(1)}, u32[]{:S(2)}, u32[]{:S(2)}) collective-permute-start(f32[32,128]{1,0:T(8,128)S(1)} %get-tuple-element.128), channel_id=1, source_target_pairs={{0,17},{1,16},{2,19},{3,18},{4,21},{5,20},{6,23},{7,22},{8,25},{9,... | collective-permute-start | bytes 49160 | tf_op jit(solution)/shard_map/ppermute | solution.py:266
  84.4 4.5 %collective-permute-start.37 = (f32[248,128]{1,0:T(8,128)S(1)}, f32[248,128]{1,0:T(8,128)S(1)}, u32[]{:S(2)}, u32[]{:S(2)}) collective-permute-start(f32[248,128]{1,0:T(8,128)S(1)} %get-tuple-element.135), channel_id=1, source_target_pairs={{0,4},{1,5},{2,6},{3,7},{4,0},{5,1},{6,2},{7,3},{8,12},{9,13},{10,... | collective-permute-start | bytes 380936 | tf_op jit(solution)/shard_map/ppermute | solution.py:266
  84.5 4.4 %collective-permute-start.38 = (f32[248,128]{1,0:T(8,128)S(1)}, f32[248,128]{1,0:T(8,128)S(1)}, u32[]{:S(2)}, u32[]{:S(2)}) collective-permute-start(f32[248,128]{1,0:T(8,128)S(1)} %get-tuple-element.136), channel_id=1, source_target_pairs={{0,1},{1,0},{2,3},{3,2},{4,8},{5,9},{6,10},{7,11},{8,4},{9,5},{10,... | collective-permute-start | bytes 380936 | tf_op jit(solution)/shard_map/ppermute | solution.py:266
  89.0 9.1 %collective-permute-start.39 = (f32[248,128]{1,0:T(8,128)S(1)}, f32[248,128]{1,0:T(8,128)S(1)}, u32[]{:S(2)}, u32[]{:S(2)}) collective-permute-start(f32[248,128]{1,0:T(8,128)S(1)} %get-tuple-element.137), channel_id=1, source_target_pairs={{0,1},{1,0},{2,3},{3,2},{4,5},{5,4},{6,7},{7,6},{8,9},{9,8},{10,11... | collective-permute-start | bytes 380936 | tf_op jit(solution)/shard_map/ppermute | solution.py:266
  90.5 7.7 %collective-permute-start.40 = (f32[248,128]{1,0:T(8,128)S(1)}, f32[248,128]{1,0:T(8,128)S(1)}, u32[]{:S(2)}, u32[]{:S(2)}) collective-permute-start(f32[248,128]{1,0:T(8,128)S(1)} %get-tuple-element.138), channel_id=1, source_target_pairs={{0,4},{1,2},{2,1},{3,7},{4,0},{5,6},{6,5},{7,3},{8,12},{9,10},{10,... | collective-permute-start | bytes 380936 | tf_op jit(solution)/shard_map/ppermute | solution.py:266
  91.1 7.1 %collective-permute-start.41 = (f32[248,128]{1,0:T(8,128)S(1)}, f32[248,128]{1,0:T(8,128)S(1)}, u32[]{:S(2)}, u32[]{:S(2)}) collective-permute-start(f32[248,128]{1,0:T(8,128)S(1)} %get-tuple-element.139), channel_id=1, source_target_pairs={{0,16},{1,17},{2,18},{3,19},{4,20},{5,21},{6,22},{7,23},{8,24},{9,... | collective-permute-start | bytes 380936 | tf_op jit(solution)/shard_map/ppermute | solution.py:266
  91.6 5.6 %collective-permute-start.42 = (f32[32,128]{1,0:T(8,128)S(1)}, f32[32,128]{1,0:T(8,128)S(1)}, u32[]{:S(2)}, u32[]{:S(2)}) collective-permute-start(f32[32,128]{1,0:T(8,128)S(1)} %get-tuple-element.140), channel_id=1, source_target_pairs={{0,17},{1,16},{2,19},{3,18},{4,21},{5,20},{6,23},{7,22},{8,25},{9,... | collective-permute-start | bytes 49160 | tf_op jit(solution)/shard_map/ppermute | solution.py:266
  94.0 4.1 %collective-permute-start.43 = (f32[32,128]{1,0:T(8,128)S(1)}, f32[32,128]{1,0:T(8,128)S(1)}, u32[]{:S(2)}, u32[]{:S(2)}) collective-permute-start(f32[32,128]{1,0:T(8,128)S(1)} %get-tuple-element.141), channel_id=1, source_target_pairs={{0,4},{1,18},{2,17},{3,7},{4,0},{5,22},{6,21},{7,3},{8,12},{9,26},... | collective-permute-start | bytes 49160 | tf_op jit(solution)/shard_map/ppermute | solution.py:266
  98.6 1.2 collective-permute-start.44
  99.8 7.1 %collective-permute-start.45 = (f32[264,128]{1,0:T(8,128)S(1)}, f32[264,128]{1,0:T(8,128)S(1)}, u32[]{:S(2)}, u32[]{:S(2)}) collective-permute-start(f32[264,128]{1,0:T(8,128)S(1)} %get-tuple-element.145), channel_id=1, source_target_pairs={{0,4},{1,5},{2,6},{3,7},{4,0},{5,1},{6,2},{7,3},{8,12},{9,13},{10,... | collective-permute-start | bytes 405512 | tf_op jit(solution)/shard_map/ppermute | solution.py:266
  100.5 6.4 %collective-permute-start.46 = (f32[248,128]{1,0:T(8,128)S(1)}, f32[248,128]{1,0:T(8,128)S(1)}, u32[]{:S(2)}, u32[]{:S(2)}) collective-permute-start(f32[248,128]{1,0:T(8,128)S(1)} %get-tuple-element.146), channel_id=1, source_target_pairs={{0,1},{1,0},{2,3},{3,2},{4,8},{5,9},{6,10},{7,11},{8,4},{9,5},{10,... | collective-permute-start | bytes 380936 | tf_op jit(solution)/shard_map/ppermute | solution.py:266
  100.9 4.4 %collective-permute-start.47 = (f32[16,128]{1,0:T(8,128)S(1)}, f32[16,128]{1,0:T(8,128)S(1)}, u32[]{:S(2)}, u32[]{:S(2)}) collective-permute-start(f32[16,128]{1,0:T(8,128)S(1)} %get-tuple-element.147), channel_id=1, source_target_pairs={{0,8},{1,9},{2,10},{3,11},{4,12},{5,13},{6,14},{7,15},{8,0},{9,1},... | collective-permute-start | bytes 24584 | tf_op jit(solution)/shard_map/ppermute | solution.py:266
  102.6 4.3 %collective-permute-start.48 = (f32[16,128]{1,0:T(8,128)S(1)}, f32[16,128]{1,0:T(8,128)S(1)}, u32[]{:S(2)}, u32[]{:S(2)}) collective-permute-start(f32[16,128]{1,0:T(8,128)S(1)} %get-tuple-element.148), channel_id=1, source_target_pairs={{0,12},{1,13},{2,14},{3,15},{4,8},{5,9},{6,10},{7,11},{8,4},{9,5},... | collective-permute-start | bytes 24584 | tf_op jit(solution)/shard_map/ppermute | solution.py:266
  107.0 10.3 %collective-permute-start.50 = (f32[312,128]{1,0:T(8,128)S(1)}, f32[312,128]{1,0:T(8,128)S(1)}, u32[]{:S(2)}, u32[]{:S(2)}) collective-permute-start(f32[312,128]{1,0:T(8,128)S(1)} %get-tuple-element.150), channel_id=1, source_target_pairs={{0,3},{1,2},{2,1},{3,0},{4,7},{5,6},{6,5},{7,4},{8,11},{9,10},{10,... | collective-permute-start | bytes 479240 | tf_op jit(solution)/shard_map/ppermute | solution.py:266
  109.7 7.6 %collective-permute-start.51 = (f32[312,128]{1,0:T(8,128)S(1)}, f32[312,128]{1,0:T(8,128)S(1)}, u32[]{:S(2)}, u32[]{:S(2)}) collective-permute-start(f32[312,128]{1,0:T(8,128)S(1)} %get-tuple-element.151), channel_id=1, source_target_pairs={{0,16},{1,17},{2,18},{3,19},{4,20},{5,21},{6,22},{7,23},{8,24},{9,... | collective-permute-start | bytes 479240 | tf_op jit(solution)/shard_map/ppermute | solution.py:266
  110.2 7.1 %collective-permute-start.49 = (f32[248,128]{1,0:T(8,128)S(1)}, f32[248,128]{1,0:T(8,128)S(1)}, u32[]{:S(2)}, u32[]{:S(2)}) collective-permute-start(f32[248,128]{1,0:T(8,128)S(1)} %get-tuple-element.149), channel_id=1, source_target_pairs={{0,1},{1,0},{2,3},{3,2},{4,5},{5,4},{6,7},{7,6},{8,9},{9,8},{10,11... | collective-permute-start | bytes 380936 | tf_op jit(solution)/shard_map/ppermute | solution.py:266
  110.2 7.1 %collective-permute-start.53 = (f32[96,128]{1,0:T(8,128)S(1)}, f32[96,128]{1,0:T(8,128)S(1)}, u32[]{:S(2)}, u32[]{:S(2)}) collective-permute-start(f32[96,128]{1,0:T(8,128)S(1)} %get-tuple-element.153), channel_id=1, source_target_pairs={{0,19},{1,18},{2,17},{3,16},{4,23},{5,22},{6,21},{7,20},{8,27},{9,... | collective-permute-start | bytes 147464 | tf_op jit(solution)/shard_map/ppermute | solution.py:266
  112.2 5.0 %collective-permute-start.52 = (f32[32,128]{1,0:T(8,128)S(1)}, f32[32,128]{1,0:T(8,128)S(1)}, u32[]{:S(2)}, u32[]{:S(2)}) collective-permute-start(f32[32,128]{1,0:T(8,128)S(1)} %get-tuple-element.152), channel_id=1, source_target_pairs={{0,17},{1,16},{2,19},{3,18},{4,21},{5,20},{6,23},{7,22},{8,25},{9,... | collective-permute-start | bytes 49160 | tf_op jit(solution)/shard_map/ppermute | solution.py:266
  118.7 4.5 %collective-permute-start.54 = (f32[248,128]{1,0:T(8,128)S(1)}, f32[248,128]{1,0:T(8,128)S(1)}, u32[]{:S(2)}, u32[]{:S(2)}) collective-permute-start(f32[248,128]{1,0:T(8,128)S(1)} %get-tuple-element.160), channel_id=1, source_target_pairs={{0,4},{1,5},{2,6},{3,7},{4,0},{5,1},{6,2},{7,3},{8,12},{9,13},{10,... | collective-permute-start | bytes 380936 | tf_op jit(solution)/shard_map/ppermute | solution.py:266
  118.7 4.4 %collective-permute-start.55 = (f32[248,128]{1,0:T(8,128)S(1)}, f32[248,128]{1,0:T(8,128)S(1)}, u32[]{:S(2)}, u32[]{:S(2)}) collective-permute-start(f32[248,128]{1,0:T(8,128)S(1)} %get-tuple-element.161), channel_id=1, source_target_pairs={{0,1},{1,0},{2,3},{3,2},{4,8},{5,9},{6,10},{7,11},{8,4},{9,5},{10,... | collective-permute-start | bytes 380936 | tf_op jit(solution)/shard_map/ppermute | solution.py:266
  123.2 9.0 %collective-permute-start.56 = (f32[248,128]{1,0:T(8,128)S(1)}, f32[248,128]{1,0:T(8,128)S(1)}, u32[]{:S(2)}, u32[]{:S(2)}) collective-permute-start(f32[248,128]{1,0:T(8,128)S(1)} %get-tuple-element.162), channel_id=1, source_target_pairs={{0,1},{1,0},{2,3},{3,2},{4,5},{5,4},{6,7},{7,6},{8,9},{9,8},{10,11... | collective-permute-start | bytes 380936 | tf_op jit(solution)/shard_map/ppermute | solution.py:266
  124.7 7.5 %collective-permute-start.57 = (f32[248,128]{1,0:T(8,128)S(1)}, f32[248,128]{1,0:T(8,128)S(1)}, u32[]{:S(2)}, u32[]{:S(2)}) collective-permute-start(f32[248,128]{1,0:T(8,128)S(1)} %get-tuple-element.163), channel_id=1, source_target_pairs={{0,4},{1,2},{2,1},{3,7},{4,0},{5,6},{6,5},{7,3},{8,12},{9,10},{10,... | collective-permute-start | bytes 380936 | tf_op jit(solution)/shard_map/ppermute | solution.py:266
  125.3 6.9 %collective-permute-start.58 = (f32[248,128]{1,0:T(8,128)S(1)}, f32[248,128]{1,0:T(8,128)S(1)}, u32[]{:S(2)}, u32[]{:S(2)}) collective-permute-start(f32[248,128]{1,0:T(8,128)S(1)} %get-tuple-element.164), channel_id=1, source_target_pairs={{0,16},{1,17},{2,18},{3,19},{4,20},{5,21},{6,22},{7,23},{8,24},{9,... | collective-permute-start | bytes 380936 | tf_op jit(solution)/shard_map/ppermute | solution.py:266
  125.8 5.5 %collective-permute-start.59 = (f32[32,128]{1,0:T(8,128)S(1)}, f32[32,128]{1,0:T(8,128)S(1)}, u32[]{:S(2)}, u32[]{:S(2)}) collective-permute-start(f32[32,128]{1,0:T(8,128)S(1)} %get-tuple-element.165), channel_id=1, source_target_pairs={{0,17},{1,16},{2,19},{3,18},{4,21},{5,20},{6,23},{7,22},{8,25},{9,... | collective-permute-start | bytes 49160 | tf_op jit(solution)/shard_map/ppermute | solution.py:266
  128.1 4.1 %collective-permute-start.60 = (f32[32,128]{1,0:T(8,128)S(1)}, f32[32,128]{1,0:T(8,128)S(1)}, u32[]{:S(2)}, u32[]{:S(2)}) collective-permute-start(f32[32,128]{1,0:T(8,128)S(1)} %get-tuple-element.166), channel_id=1, source_target_pairs={{0,4},{1,18},{2,17},{3,7},{4,0},{5,22},{6,21},{7,3},{8,12},{9,26},... | collective-permute-start | bytes 49160 | tf_op jit(solution)/shard_map/ppermute | solution.py:266
  (3 other events, 2.8 us)

commit v7 on v6

--- a/solution.py
+++ b/solution.py
@@ -584,7 +584,7 @@
         basis = many[rows, :].astype(BF16)
         whole = dot(jnp.concatenate([basis] * 3, axis=1), parts)
         high, low = split(whole, 2)
-        out[rows, :] = jnp.concatenate([high, high, low], axis=1)
+        out[rows, :] = jnp.concatenate([high, low], axis=1)
 
     each_tile(body)
 
@@ -604,9 +604,11 @@
     if plan.ride:
         collect(plan, "update", own, swapped + got, 1, 0, stack, 0)
         high, low = split(stack[...], 2)
-        right = jnp.concatenate([high, low, high], axis=0)
+        right = jnp.concatenate([high, low], axis=1)
         for t in range(0, ROWS, 320):
-            value = acc[t : t + 320, :] + dot(lift[t : t + 320, :], right)
+            both_parts = dot(lift[t : t + 320, : plan.wide], right)
+            value = dot(lift[t : t + 320, plan.wide :], high) + both_parts[:, 128:]
+            value = acc[t : t + 320, :] + (both_parts[:, :128] + value)
             update[t : t + 320, :] = value
             rounded[t : t + 320, :] = value.astype(BF16)
     else:
@@ -714,7 +716,7 @@
     if plan.ride:
         (lift,) = call(
             functools.partial(lifting_kernel, plan),
-            [shape(ROWS, 3 * plan.wide, BF16)],
+            [shape(ROWS, 2 * plan.wide, BF16)],
             [turned] + blocks + got,
             scratch=[pltpu.VMEM((plan.wide, plan.wide), F32), pltpu.VMEM((ROWS, plan.wide), F32), pieces],
             flops=2 * ROWS * 3 * plan.wide * plan.wide,

time: 135 us -> 135 us (level)
  no operation moved by 1% of the time
where the time goes in v7:
time: 135 us; the launch traced here: 134 us
  starting transfers between devices  65.1 us (48%)
  Pallas kernels  36.1 us (27%)
  waiting for transfers between devices  30.1 us (22%)
  local copies, waits for them, and re-layouts  1.91 us (1%)
    ppermute x61, starting transfers between devices, transfer(): lax.ppermute(p, AXES, m.pairs())  65.1 us
    pallas_call x34, Pallas kernels, call(): pl.pallas_call(kernel, out_shape=tuple(outs), in_specs=specs or [vm()] *...  36.1 us
    ppermute x61, waiting for transfers between devices, transfer(): lax.ppermute(p, AXES, m.pairs())  30.1 us
  transfers between devices with their start and end apart: 61, of which 17 were waited for; matrix products, arithmetic and copies ran while one was open for 1% of the time, Pallas kernels for 21%

profile of v7, /device:TPU:1, one launch (start us, length us, event | category | flops | bytes accessed | tf_op | source)
XLA Modules:
  0.0 134.3 jit_solution(7202066105865770770)
XLA Ops:
  0.6 0.7 copy-done.3
  1.6 3.8 %collective-permute-start.1 = (f32[16,128]{1,0:T(8,128)S(1)}, f32[16,128]{1,0:T(8,128)S(1)}, u32[]{:S(2)}, u32[]{:S(2)}) collective-permute-start(f32[16,128]{1,0:T(8,128)S(1)} %shard_map.83.refs_1_.refs_4_), channel_id=1, source_target_pairs={{0,8},{1,9},{2,10},{3,11},{4,12},{5,13},{6,14},{7,15},{8,0},{9,1},... | collective-permute-start | bytes 24584 | tf_op jit(solution)/shard_map/ppermute | solution.py:266
  5.3 0.9 copy.10.canon
  6.3 0.8 shard_map.77
  7.4 1.0 shard_map.81.refs_0_
  8.4 1.1 shard_map.84.refs_5_.refs_8_.refs_0_
  9.7 1.6 %collective-permute-start.3 = (f32[336,128]{1,0:T(8,128)S(1)}, f32[336,128]{1,0:T(8,128)S(1)}, u32[]{:S(2)}, u32[]{:S(2)}) collective-permute-start(f32[336,128]{1,0:T(8,128)S(1)} %get-tuple-element.89), channel_id=1, source_target_pairs={{0,4},{1,5},{2,6},{3,7},{4,0},{5,1},{6,2},{7,3},{8,12},{9,13},{10,... | collective-permute-start | bytes 516104 | tf_op jit(solution)/shard_map/ppermute | solution.py:266
  11.7 2.7 %shard_map.78.mid = bf16[768,1158]{1,0:T(8,128)(2,1)S(1)} custom-call(bf16[1280,1158]{1,0:T(8,128)(2,1)S(1)} %get-tuple-element.85.one, bf16[1158,1158]{1,0:T(8,128)(2,1)S(1)} %bitcast.21, bf16[6,1158]{1,0:T(8,128)(2,1)S(1)} %bitcast.20), custom_call_target="tpu_custom_call" | custom-call | flops 3432867840 | bytes 7438992 | tf_op jit(solution)/shard_map/pallas_call | solution.py:279
  14.5 1.2 shard_map.82.refs_1_
  16.0 1.0 collective-permute-start.5
  17.0 1.4 %collective-permute-start.6 = (f32[400,128]{1,0:T(8,128)S(1)}, f32[400,128]{1,0:T(8,128)S(1)}, u32[]{:S(2)}, u32[]{:S(2)}) collective-permute-start(f32[400,128]{1,0:T(8,128)S(1)} %get-tuple-element.92), channel_id=1, source_target_pairs={{0,3},{1,2},{2,1},{3,0},{4,7},{5,6},{6,5},{7,4},{8,11},{9,10},{10,... | collective-permute-start | bytes 614408 | tf_op jit(solution)/shard_map/ppermute | solution.py:266
  18.4 1.2 collective-permute-start.7
  19.6 0.9 collective-permute-start.8
  20.4 0.8 collective-permute-start.9
  21.3 6.3 %shard_map.79 = (bf16[1280,1280]{1,0:T(8,128)(2,1)S(1)}, bf16[512,1158]{1,0:T(8,128)(2,1)S(1)}) custom-call(bf16[1280,1158]{1,0:T(8,128)(2,1)S(1)} %get-tuple-element.85.one, bf16[768,1158]{1,0:T(8,128)(2,1)S(1)} %shard_map.78.mid, bf16[1158,1158]{1,0:T(8,128)(2,1)S(1)} %bitcast.22, f32[1280,128]{1,0:T(8,128)S(1)} %get-tuple-element.86.weight.refs_10_, ...), custom_call_target="tpu_custom_call" | custom-call | flops 6865735680 | bytes 15224976 | tf_op jit(solution)/shard_map/pallas_call | solution.py:279
  27.9 0.7 collective-permute-start.10
  28.7 1.0 shard_map.88.refs_0_
  29.7 1.9 %collective-permute-start.11 = (f32[264,128]{1,0:T(8,128)S(1)}, f32[264,128]{1,0:T(8,128)S(1)}, u32[]{:S(2)}, u32[]{:S(2)}) collective-permute-start(f32[264,128]{1,0:T(8,128)S(1)} %get-tuple-element.98), channel_id=1, source_target_pairs={{0,4},{1,5},{2,6},{3,7},{4,0},{5,1},{6,2},{7,3},{8,12},{9,13},{10,... | collective-permute-start | bytes 405512 | tf_op jit(solution)/shard_map/ppermute | solution.py:266
  32.0 1.4 %collective-permute-start.13 = (f32[16,128]{1,0:T(8,128)S(1)}, f32[16,128]{1,0:T(8,128)S(1)}, u32[]{:S(2)}, u32[]{:S(2)}) collective-permute-start(f32[16,128]{1,0:T(8,128)S(1)} %get-tuple-element.100), channel_id=1, source_target_pairs={{0,8},{1,9},{2,10},{3,11},{4,12},{5,13},{6,14},{7,15},{8,0},{9,1},... | collective-permute-start | bytes 24584 | tf_op jit(solution)/shard_map/ppermute | solution.py:266
  33.4 2.4 %collective-permute-start.14 = (f32[16,128]{1,0:T(8,128)S(1)}, f32[16,128]{1,0:T(8,128)S(1)}, u32[]{:S(2)}, u32[]{:S(2)}) collective-permute-start(f32[16,128]{1,0:T(8,128)S(1)} %get-tuple-element.101), channel_id=1, source_target_pairs={{0,12},{1,13},{2,14},{3,15},{4,8},{5,9},{6,10},{7,11},{8,4},{9,5},... | collective-permute-start | bytes 24584 | tf_op jit(solution)/shard_map/ppermute | solution.py:266
  35.8 2.4 %shard_map.90.refs_1_.refs_11_ = bf16[1280,512]{1,0:T(8,128)(2,1)S(1)} custom-call(f32[1280,128]{1,0:T(8,128)S(1)} %shard_map.84.refs_5_.refs_8_.refs_0_, f32[16,128]{1,0:T(8,128)S(1)} %shard_map.83.refs_1_.refs_4_, f32[16,128]{1,0:T(8,128)S(1)} %collective-permute-done.refs_2_.refs_5_, f32[16,128]{1,0:T(8,128)S(1)} %collective-permute-done.1.refs_3_.refs_6_, ...), custom_call_target="tpu_custom_call" | custom-call | flops 503316480 | bytes 2981888 | tf_op jit(solution)/shard_map/pallas_call | solution.py:279
  38.3 1.4 %collective-permute-start.15 = (f32[248,128]{1,0:T(8,128)S(1)}, f32[248,128]{1,0:T(8,128)S(1)}, u32[]{:S(2)}, u32[]{:S(2)}) collective-permute-start(f32[248,128]{1,0:T(8,128)S(1)} %get-tuple-element.102), channel_id=1, source_target_pairs={{0,1},{1,0},{2,3},{3,2},{4,5},{5,4},{6,7},{7,6},{8,9},{9,8},{10,11... | collective-permute-start | bytes 380936 | tf_op jit(solution)/shard_map/ppermute | solution.py:266
  39.7 1.2 collective-permute-start.16
  40.9 1.0 collective-permute-start.17
  41.9 1.1 collective-permute-start.18
  43.6 5.3 %shard_map.80.refs_10_.matrix = bf16[1280,1280]{1,0:T(8,128)(2,1)S(1)} custom-call(bf16[1280,1158]{1,0:T(8,128)(2,1)S(1)} %get-tuple-element.85.one, bf16[512,1158]{1,0:T(8,128)(2,1)S(1)} %get-tuple-element.87.mid, bf16[1158,1158]{1,0:T(8,128)(2,1)S(1)} %bitcast.24), custom_call_target="tpu_custom_call" | custom-call | flops 3432867840 | bytes 10109000 | tf_op jit(solution)/shard_map/pallas_call | solution.py:279
  49.0 1.0 shard_map.92
  50.1 0.8 collective-permute-start.21
  51.6 2.8 %collective-permute-done.20.refs_2_ = f32[248,128]{1,0:T(8,128)S(1)} collective-permute-done((f32[248,128]{1,0:T(8,128)S(1)}, f32[248,128]{1,0:T(8,128)S(1)}, u32[]{:S(2)}, u32[]{:S(2)}) %collective-permute-start.20) | collective-permute-done | bytes 127008 | tf_op jit(solution)/shard_map/ppermute | solution.py:266
  54.4 1.7 %collective-permute-start.22 = (f32[248,128]{1,0:T(8,128)S(1)}, f32[248,128]{1,0:T(8,128)S(1)}, u32[]{:S(2)}, u32[]{:S(2)}) collective-permute-start(f32[248,128]{1,0:T(8,128)S(1)} %get-tuple-element.113), channel_id=1, source_target_pairs={{0,1},{1,0},{2,3},{3,2},{4,5},{5,4},{6,7},{7,6},{8,9},{9,8},{10,11... | collective-permute-start | bytes 380936 | tf_op jit(solution)/shard_map/ppermute | solution.py:266
  56.1 1.2 collective-permute-start.23
  57.7 2.1 %collective-permute-start.25 = (f32[32,128]{1,0:T(8,128)S(1)}, f32[32,128]{1,0:T(8,128)S(1)}, u32[]{:S(2)}, u32[]{:S(2)}) collective-permute-start(f32[32,128]{1,0:T(8,128)S(1)} %get-tuple-element.116), channel_id=1, source_target_pairs={{0,17},{1,16},{2,19},{3,18},{4,21},{5,20},{6,23},{7,22},{8,25},{9,... | collective-permute-start | bytes 49160 | tf_op jit(solution)/shard_map/ppermute | solution.py:266
  59.8 1.2 collective-permute-start.26
  61.0 1.9 %collective-permute-done.25.refs_7_ = f32[32,128]{1,0:T(8,128)S(1)} collective-permute-done((f32[32,128]{1,0:T(8,128)S(1)}, f32[32,128]{1,0:T(8,128)S(1)}, u32[]{:S(2)}, u32[]{:S(2)}) %collective-permute-start.25) | collective-permute-done | bytes 16416 | tf_op jit(solution)/shard_map/ppermute | solution.py:266
  62.9 1.0 collective-permute-done.26.refs_8_
  64.3 1.0 shard_map.96.refs_0_
  66.8 1.6 %collective-permute-start.30 = (f32[16,128]{1,0:T(8,128)S(1)}, f32[16,128]{1,0:T(8,128)S(1)}, u32[]{:S(2)}, u32[]{:S(2)}) collective-permute-start(f32[16,128]{1,0:T(8,128)S(1)} %get-tuple-element.123), channel_id=1, source_target_pairs={{0,8},{1,9},{2,10},{3,11},{4,12},{5,13},{6,14},{7,15},{8,0},{9,1},... | collective-permute-start | bytes 24584 | tf_op jit(solution)/shard_map/ppermute | solution.py:266
  68.4 2.4 %collective-permute-start.31 = (f32[16,128]{1,0:T(8,128)S(1)}, f32[16,128]{1,0:T(8,128)S(1)}, u32[]{:S(2)}, u32[]{:S(2)}) collective-permute-start(f32[16,128]{1,0:T(8,128)S(1)} %get-tuple-element.124), channel_id=1, source_target_pairs={{0,12},{1,13},{2,14},{3,15},{4,8},{5,9},{6,10},{7,11},{8,4},{9,5},... | collective-permute-start | bytes 24584 | tf_op jit(solution)/shard_map/ppermute | solution.py:266
  71.3 1.4 %collective-permute-done.31.refs_4_ = f32[16,128]{1,0:T(8,128)S(1)} collective-permute-done((f32[16,128]{1,0:T(8,128)S(1)}, f32[16,128]{1,0:T(8,128)S(1)}, u32[]{:S(2)}, u32[]{:S(2)}) %collective-permute-start.31) | collective-permute-done | bytes 8224 | tf_op jit(solution)/shard_map/ppermute | solution.py:266
  72.8 2.8 %collective-permute-start.33 = (f32[312,128]{1,0:T(8,128)S(1)}, f32[312,128]{1,0:T(8,128)S(1)}, u32[]{:S(2)}, u32[]{:S(2)}) collective-permute-start(f32[312,128]{1,0:T(8,128)S(1)} %get-tuple-element.126), channel_id=1, source_target_pairs={{0,3},{1,2},{2,1},{3,0},{4,7},{5,6},{6,5},{7,4},{8,11},{9,10},{10,... | collective-permute-start | bytes 479240 | tf_op jit(solution)/shard_map/ppermute | solution.py:266
  76.1 1.8 %collective-permute-start.36 = (f32[96,128]{1,0:T(8,128)S(1)}, f32[96,128]{1,0:T(8,128)S(1)}, u32[]{:S(2)}, u32[]{:S(2)}) collective-permute-start(f32[96,128]{1,0:T(8,128)S(1)} %get-tuple-element.129), channel_id=1, source_target_pairs={{0,19},{1,18},{2,17},{3,16},{4,23},{5,22},{6,21},{7,20},{8,27},{9,... | collective-permute-start | bytes 147464 | tf_op jit(solution)/shard_map/ppermute | solution.py:266
  78.3 4.7 %collective-permute-done.35.refs_8_ = f32[32,128]{1,0:T(8,128)S(1)} collective-permute-done((f32[32,128]{1,0:T(8,128)S(1)}, f32[32,128]{1,0:T(8,128)S(1)}, u32[]{:S(2)}, u32[]{:S(2)}) %collective-permute-start.35) | collective-permute-done | bytes 16416 | tf_op jit(solution)/shard_map/ppermute | solution.py:266
  83.1 1.0 shard_map.99
  85.5 3.2 %collective-permute-done.37.refs_2_ = f32[248,128]{1,0:T(8,128)S(1)} collective-permute-done((f32[248,128]{1,0:T(8,128)S(1)}, f32[248,128]{1,0:T(8,128)S(1)}, u32[]{:S(2)}, u32[]{:S(2)}) %collective-permute-start.37) | collective-permute-done | bytes 127008 | tf_op jit(solution)/shard_map/ppermute | solution.py:266
  88.7 1.4 %collective-permute-start.39 = (f32[248,128]{1,0:T(8,128)S(1)}, f32[248,128]{1,0:T(8,128)S(1)}, u32[]{:S(2)}, u32[]{:S(2)}) collective-permute-start(f32[248,128]{1,0:T(8,128)S(1)} %get-tuple-element.137), channel_id=1, source_target_pairs={{0,1},{1,0},{2,3},{3,2},{4,5},{5,4},{6,7},{7,6},{8,9},{9,8},{10,11... | collective-permute-start | bytes 380936 | tf_op jit(solution)/shard_map/ppermute | solution.py:266
  91.3 2.5 %collective-permute-start.42 = (f32[32,128]{1,0:T(8,128)S(1)}, f32[32,128]{1,0:T(8,128)S(1)}, u32[]{:S(2)}, u32[]{:S(2)}) collective-permute-start(f32[32,128]{1,0:T(8,128)S(1)} %get-tuple-element.140), channel_id=1, source_target_pairs={{0,17},{1,16},{2,19},{3,18},{4,21},{5,20},{6,23},{7,22},{8,25},{9,... | collective-permute-start | bytes 49160 | tf_op jit(solution)/shard_map/ppermute | solution.py:266
  93.8 0.7 collective-permute-start.43
  94.5 2.4 %collective-permute-done.42.refs_7_ = f32[32,128]{1,0:T(8,128)S(1)} collective-permute-done((f32[32,128]{1,0:T(8,128)S(1)}, f32[32,128]{1,0:T(8,128)S(1)}, u32[]{:S(2)}, u32[]{:S(2)}) %collective-permute-start.42) | collective-permute-done | bytes 16416 | tf_op jit(solution)/shard_map/ppermute | solution.py:266
  96.9 1.0 collective-permute-done.43.refs_8_
  98.3 1.0 shard_map.103.refs_0_
  99.5 0.7 collective-permute-start.45
  100.6 1.7 %collective-permute-start.47 = (f32[16,128]{1,0:T(8,128)S(1)}, f32[16,128]{1,0:T(8,128)S(1)}, u32[]{:S(2)}, u32[]{:S(2)}) collective-permute-start(f32[16,128]{1,0:T(8,128)S(1)} %get-tuple-element.147), channel_id=1, source_target_pairs={{0,8},{1,9},{2,10},{3,11},{4,12},{5,13},{6,14},{7,15},{8,0},{9,1},... | collective-permute-start | bytes 24584 | tf_op jit(solution)/shard_map/ppermute | solution.py:266
  102.3 2.4 %collective-permute-start.48 = (f32[16,128]{1,0:T(8,128)S(1)}, f32[16,128]{1,0:T(8,128)S(1)}, u32[]{:S(2)}, u32[]{:S(2)}) collective-permute-start(f32[16,128]{1,0:T(8,128)S(1)} %get-tuple-element.148), channel_id=1, source_target_pairs={{0,12},{1,13},{2,14},{3,15},{4,8},{5,9},{6,10},{7,11},{8,4},{9,5},... | collective-permute-start | bytes 24584 | tf_op jit(solution)/shard_map/ppermute | solution.py:266
  105.1 1.5 %collective-permute-done.48.refs_4_ = f32[16,128]{1,0:T(8,128)S(1)} collective-permute-done((f32[16,128]{1,0:T(8,128)S(1)}, f32[16,128]{1,0:T(8,128)S(1)}, u32[]{:S(2)}, u32[]{:S(2)}) %collective-permute-start.48) | collective-permute-done | bytes 8224 | tf_op jit(solution)/shard_map/ppermute | solution.py:266
  106.7 2.7 %collective-permute-start.50 = (f32[312,128]{1,0:T(8,128)S(1)}, f32[312,128]{1,0:T(8,128)S(1)}, u32[]{:S(2)}, u32[]{:S(2)}) collective-permute-start(f32[312,128]{1,0:T(8,128)S(1)} %get-tuple-element.150), channel_id=1, source_target_pairs={{0,3},{1,2},{2,1},{3,0},{4,7},{5,6},{6,5},{7,4},{8,11},{9,10},{10,... | collective-permute-start | bytes 479240 | tf_op jit(solution)/shard_map/ppermute | solution.py:266
  109.9 2.1 %collective-permute-start.53 = (f32[96,128]{1,0:T(8,128)S(1)}, f32[96,128]{1,0:T(8,128)S(1)}, u32[]{:S(2)}, u32[]{:S(2)}) collective-permute-start(f32[96,128]{1,0:T(8,128)S(1)} %get-tuple-element.153), channel_id=1, source_target_pairs={{0,19},{1,18},{2,17},{3,16},{4,23},{5,22},{6,21},{7,20},{8,27},{9,... | collective-permute-start | bytes 147464 | tf_op jit(solution)/shard_map/ppermute | solution.py:266
  112.3 4.6 %collective-permute-done.52.refs_8_ = f32[32,128]{1,0:T(8,128)S(1)} collective-permute-done((f32[32,128]{1,0:T(8,128)S(1)}, f32[32,128]{1,0:T(8,128)S(1)}, u32[]{:S(2)}, u32[]{:S(2)}) %collective-permute-start.52) | collective-permute-done | bytes 16416 | tf_op jit(solution)/shard_map/ppermute | solution.py:266
  117.0 1.0 shard_map.106
  119.6 3.1 %collective-permute-done.54.refs_2_.refs_0_ = f32[248,128]{1,0:T(8,128)S(1)} collective-permute-done((f32[248,128]{1,0:T(8,128)S(1)}, f32[248,128]{1,0:T(8,128)S(1)}, u32[]{:S(2)}, u32[]{:S(2)}) %collective-permute-start.54) | collective-permute-done | bytes 127008 | tf_op jit(solution)/shard_map/ppermute | solution.py:266
  122.7 1.5 %collective-permute-start.56 = (f32[248,128]{1,0:T(8,128)S(1)}, f32[248,128]{1,0:T(8,128)S(1)}, u32[]{:S(2)}, u32[]{:S(2)}) collective-permute-start(f32[248,128]{1,0:T(8,128)S(1)} %get-tuple-element.162), channel_id=1, source_target_pairs={{0,1},{1,0},{2,3},{3,2},{4,5},{5,4},{6,7},{7,6},{8,9},{9,8},{10,11... | collective-permute-start | bytes 380936 | tf_op jit(solution)/shard_map/ppermute | solution.py:266
  125.3 2.4 %collective-permute-start.59 = (f32[32,128]{1,0:T(8,128)S(1)}, f32[32,128]{1,0:T(8,128)S(1)}, u32[]{:S(2)}, u32[]{:S(2)}) collective-permute-start(f32[32,128]{1,0:T(8,128)S(1)} %get-tuple-element.165), channel_id=1, source_target_pairs={{0,17},{1,16},{2,19},{3,18},{4,21},{5,20},{6,23},{7,22},{8,25},{9,... | collective-permute-start | bytes 49160 | tf_op jit(solution)/shard_map/ppermute | solution.py:266
  128.3 2.5 %shard_map.108 = f32[1158,1,128]{2,1,0:T(1,128)} custom-call(s32[1,1158]{1,0:T(1,128)S(1)} %bitcast.17, f32[1280,128]{1,0:T(8,128)S(1)} %get-tuple-element.157.acc), custom_call_target="tpu_custom_call" | custom-call | bytes 1252888 | tf_op jit(solution)/shard_map/pallas_call | solution.py:279
  130.9 0.9 collective-permute-done.60.refs_6_
  131.8 2.5 %shard_map.110 = f32[1158,1,128]{2,1,0:T(1,128)} custom-call(s32[1,1158]{1,0:T(1,128)S(1)} %bitcast.18, f32[576,128]{1,0:T(8,128)S(1)} %get-tuple-element.158.refs_0_.early, f32[704,128]{1,0:T(8,128)S(1)} %get-tuple-element.159.refs_1_.late, f32[248,128]{1,0:T(8,128)S(1)} %collective-permute-done.54.refs_2_.refs_0_, ...), custom_call_target="tpu_custom_call" | custom-call | bytes 2575896 | tf_op jit(solution)/shard_map/pallas_call | solution.py:279
  (105 shorter events, 16.0 us)
Async XLA Ops:
  1.5 8.0 %collective-permute-start = (f32[16,128]{1,0:T(8,128)S(1)}, f32[16,128]{1,0:T(8,128)S(1)}, u32[]{:S(2)}, u32[]{:S(2)}) collective-permute-start(f32[16,128]{1,0:T(8,128)S(1)} %shard_map.83.refs_1_.refs_4_), channel_id=1, source_target_pairs={{0,1},{1,0},{2,3},{3,2},{4,5},{5,4},{6,7},{7,6},{8,9},{9,8},{10,11... | collective-permute-start | bytes 24584 | tf_op jit(solution)/shard_map/ppermute | solution.py:266
  1.6 7.9 %collective-permute-start.1 = (f32[16,128]{1,0:T(8,128)S(1)}, f32[16,128]{1,0:T(8,128)S(1)}, u32[]{:S(2)}, u32[]{:S(2)}) collective-permute-start(f32[16,128]{1,0:T(8,128)S(1)} %shard_map.83.refs_1_.refs_4_), channel_id=1, source_target_pairs={{0,8},{1,9},{2,10},{3,11},{4,12},{5,13},{6,14},{7,15},{8,0},{9,1},... | collective-permute-start | bytes 24584 | tf_op jit(solution)/shard_map/ppermute | solution.py:266
  5.3 4.2 %collective-permute-start.2 = (f32[16,128]{1,0:T(8,128)S(1)}, f32[16,128]{1,0:T(8,128)S(1)}, u32[]{:S(2)}, u32[]{:S(2)}) collective-permute-start(f32[16,128]{1,0:T(8,128)S(1)} %shard_map.83.refs_1_.refs_4_), channel_id=1, source_target_pairs={{0,9},{1,8},{2,11},{3,10},{4,13},{5,12},{6,15},{7,14},{8,1},{9,0},... | collective-permute-start | bytes 24584 | tf_op jit(solution)/shard_map/ppermute | solution.py:266
  6.3 2.1 %copy-start.2 = (bf16[1,1,1,6,1158]{4,3,2,1,0:T(8,128)(2,1)S(1)}, bf16[1,1,1,6,1158]{4,3,2,1,0:T(8,128)(2,1)}, u32[]{:S(2)}) copy-start(bf16[1,1,1,6,1158]{4,3,2,1,0:T(8,128)(2,1)} %param.9) | copy-start | bytes 41692
  8.4 3.3 %copy-start.4 = (bf16[1,1,1,1158,1158]{4,3,2,1,0:T(8,128)(2,1)S(1)}, bf16[1,1,1,1158,1158]{4,3,2,1,0:T(8,128)(2,1)}, u32[]{:S(2)}) copy-start(bf16[1,1,1,1158,1158]{4,3,2,1,0:T(8,128)(2,1)} %param.8) | copy-start | bytes 8045788
  9.7 6.0 %collective-permute-start.3 = (f32[336,128]{1,0:T(8,128)S(1)}, f32[336,128]{1,0:T(8,128)S(1)}, u32[]{:S(2)}, u32[]{:S(2)}) collective-permute-start(f32[336,128]{1,0:T(8,128)S(1)} %get-tuple-element.89), channel_id=1, source_target_pairs={{0,4},{1,5},{2,6},{3,7},{4,0},{5,1},{6,2},{7,3},{8,12},{9,13},{10,... | collective-permute-start | bytes 516104 | tf_op jit(solution)/shard_map/ppermute | solution.py:266
  11.3 4.4 %collective-permute-start.4 = (f32[272,128]{1,0:T(8,128)S(1)}, f32[272,128]{1,0:T(8,128)S(1)}, u32[]{:S(2)}, u32[]{:S(2)}) collective-permute-start(f32[272,128]{1,0:T(8,128)S(1)} %get-tuple-element.90), channel_id=1, source_target_pairs={{0,1},{1,0},{2,3},{3,2},{4,8},{5,9},{6,10},{7,11},{8,4},{9,5},{10,... | collective-permute-start | bytes 417800 | tf_op jit(solution)/shard_map/ppermute | solution.py:266
  11.7 9.5 %copy-start.5 = (bf16[1,1,1,1158,1158]{4,3,2,1,0:T(8,128)(2,1)S(1)}, bf16[1,1,1,1158,1158]{4,3,2,1,0:T(8,128)(2,1)}, u32[]{:S(2)}) copy-start(bf16[1,1,1,1158,1158]{4,3,2,1,0:T(8,128)(2,1)} %param.7) | copy-start | bytes 8045788
  16.0 11.6 %collective-permute-start.5 = (f32[272,128]{1,0:T(8,128)S(1)}, f32[272,128]{1,0:T(8,128)S(1)}, u32[]{:S(2)}, u32[]{:S(2)}) collective-permute-start(f32[272,128]{1,0:T(8,128)S(1)} %get-tuple-element.91), channel_id=1, source_target_pairs={{0,1},{1,0},{2,3},{3,2},{4,5},{5,4},{6,7},{7,6},{8,9},{9,8},{10,11... | collective-permute-start | bytes 417800 | tf_op jit(solution)/shard_map/ppermute | solution.py:266
  17.0 10.6 %collective-permute-start.6 = (f32[400,128]{1,0:T(8,128)S(1)}, f32[400,128]{1,0:T(8,128)S(1)}, u32[]{:S(2)}, u32[]{:S(2)}) collective-permute-start(f32[400,128]{1,0:T(8,128)S(1)} %get-tuple-element.92), channel_id=1, source_target_pairs={{0,3},{1,2},{2,1},{3,0},{4,7},{5,6},{6,5},{7,4},{8,11},{9,10},{10,... | collective-permute-start | bytes 614408 | tf_op jit(solution)/shard_map/ppermute | solution.py:266
  18.4 9.2 %collective-permute-start.7 = (f32[400,128]{1,0:T(8,128)S(1)}, f32[400,128]{1,0:T(8,128)S(1)}, u32[]{:S(2)}, u32[]{:S(2)}) collective-permute-start(f32[400,128]{1,0:T(8,128)S(1)} %get-tuple-element.93), channel_id=1, source_target_pairs={{0,16},{1,17},{2,18},{3,19},{4,20},{5,21},{6,22},{7,23},{8,24},{9,... | collective-permute-start | bytes 614408 | tf_op jit(solution)/shard_map/ppermute | solution.py:266
  19.6 8.0 %collective-permute-start.8 = (f32[56,128]{1,0:T(8,128)S(1)}, f32[56,128]{1,0:T(8,128)S(1)}, u32[]{:S(2)}, u32[]{:S(2)}) collective-permute-start(f32[56,128]{1,0:T(8,128)S(1)} %get-tuple-element.94), channel_id=1, source_target_pairs={{0,17},{1,16},{2,19},{3,18},{4,21},{5,20},{6,23},{7,22},{8,25},{9,... | collective-permute-start | bytes 86024 | tf_op jit(solution)/shard_map/ppermute | solution.py:266
  20.4 7.1 %collective-permute-start.9 = (f32[184,128]{1,0:T(8,128)S(1)}, f32[184,128]{1,0:T(8,128)S(1)}, u32[]{:S(2)}, u32[]{:S(2)}) collective-permute-start(f32[184,128]{1,0:T(8,128)S(1)} %get-tuple-element.95), channel_id=1, source_target_pairs={{0,19},{1,18},{2,17},{3,16},{4,23},{5,22},{6,21},{7,20},{8,27},{9,... | collective-permute-start | bytes 282632 | tf_op jit(solution)/shard_map/ppermute | solution.py:266
  27.9 1.7 %collective-permute-start.10 = (f32[8,128]{1,0:T(8,128)S(1)}, f32[8,128]{1,0:T(8,128)S(1)}, u32[]{:S(2)}, u32[]{:S(2)}) collective-permute-start(f32[8,128]{1,0:T(8,128)S(1)} %get-tuple-element.97.refs_1_.refs_6_.refs_12_), channel_id=1, source_target_pairs={{0,1},{1,0},{2,3},{3,2},{4,5},{5,4},{6,7},{7,6},{8,9},{9,8},{10,11... | collective-permute-start | bytes 12296 | tf_op jit(solution)/shard_map/ppermute | solution.py:266
  29.7 8.5 %collective-permute-start.11 = (f32[264,128]{1,0:T(8,128)S(1)}, f32[264,128]{1,0:T(8,128)S(1)}, u32[]{:S(2)}, u32[]{:S(2)}) collective-permute-start(f32[264,128]{1,0:T(8,128)S(1)} %get-tuple-element.98), channel_id=1, source_target_pairs={{0,4},{1,5},{2,6},{3,7},{4,0},{5,1},{6,2},{7,3},{8,12},{9,13},{10,... | collective-permute-start | bytes 405512 | tf_op jit(solution)/shard_map/ppermute | solution.py:266
  31.6 6.6 %collective-permute-start.12 = (f32[248,128]{1,0:T(8,128)S(1)}, f32[248,128]{1,0:T(8,128)S(1)}, u32[]{:S(2)}, u32[]{:S(2)}) collective-permute-start(f32[248,128]{1,0:T(8,128)S(1)} %get-tuple-element.99), channel_id=1, source_target_pairs={{0,1},{1,0},{2,3},{3,2},{4,8},{5,9},{6,10},{7,11},{8,4},{9,5},{10,... | collective-permute-start | bytes 380936 | tf_op jit(solution)/shard_map/ppermute | solution.py:266
  32.0 6.2 %collective-permute-start.13 = (f32[16,128]{1,0:T(8,128)S(1)}, f32[16,128]{1,0:T(8,128)S(1)}, u32[]{:S(2)}, u32[]{:S(2)}) collective-permute-start(f32[16,128]{1,0:T(8,128)S(1)} %get-tuple-element.100), channel_id=1, source_target_pairs={{0,8},{1,9},{2,10},{3,11},{4,12},{5,13},{6,14},{7,15},{8,0},{9,1},... | collective-permute-start | bytes 24584 | tf_op jit(solution)/shard_map/ppermute | solution.py:266
  33.4 4.8 %collective-permute-start.14 = (f32[16,128]{1,0:T(8,128)S(1)}, f32[16,128]{1,0:T(8,128)S(1)}, u32[]{:S(2)}, u32[]{:S(2)}) collective-permute-start(f32[16,128]{1,0:T(8,128)S(1)} %get-tuple-element.101), channel_id=1, source_target_pairs={{0,12},{1,13},{2,14},{3,15},{4,8},{5,9},{6,10},{7,11},{8,4},{9,5},... | collective-permute-start | bytes 24584 | tf_op jit(solution)/shard_map/ppermute | solution.py:266
  38.3 10.6 %collective-permute-start.15 = (f32[248,128]{1,0:T(8,128)S(1)}, f32[248,128]{1,0:T(8,128)S(1)}, u32[]{:S(2)}, u32[]{:S(2)}) collective-permute-start(f32[248,128]{1,0:T(8,128)S(1)} %get-tuple-element.102), channel_id=1, source_target_pairs={{0,1},{1,0},{2,3},{3,2},{4,5},{5,4},{6,7},{7,6},{8,9},{9,8},{10,11... | collective-permute-start | bytes 380936 | tf_op jit(solution)/shard_map/ppermute | solution.py:266
  39.7 9.3 %collective-permute-start.16 = (f32[312,128]{1,0:T(8,128)S(1)}, f32[312,128]{1,0:T(8,128)S(1)}, u32[]{:S(2)}, u32[]{:S(2)}) collective-permute-start(f32[312,128]{1,0:T(8,128)S(1)} %get-tuple-element.103), channel_id=1, source_target_pairs={{0,3},{1,2},{2,1},{3,0},{4,7},{5,6},{6,5},{7,4},{8,11},{9,10},{10,... | collective-permute-start | bytes 479240 | tf_op jit(solution)/shard_map/ppermute | solution.py:266
  40.9 8.1 %collective-permute-start.17 = (f32[312,128]{1,0:T(8,128)S(1)}, f32[312,128]{1,0:T(8,128)S(1)}, u32[]{:S(2)}, u32[]{:S(2)}) collective-permute-start(f32[312,128]{1,0:T(8,128)S(1)} %get-tuple-element.104), channel_id=1, source_target_pairs={{0,16},{1,17},{2,18},{3,19},{4,20},{5,21},{6,22},{7,23},{8,24},{9,... | collective-permute-start | bytes 479240 | tf_op jit(solution)/shard_map/ppermute | solution.py:266
  41.9 7.1 %collective-permute-start.18 = (f32[32,128]{1,0:T(8,128)S(1)}, f32[32,128]{1,0:T(8,128)S(1)}, u32[]{:S(2)}, u32[]{:S(2)}) collective-permute-start(f32[32,128]{1,0:T(8,128)S(1)} %get-tuple-element.105), channel_id=1, source_target_pairs={{0,17},{1,16},{2,19},{3,18},{4,21},{5,20},{6,23},{7,22},{8,25},{9,... | collective-permute-start | bytes 49160 | tf_op jit(solution)/shard_map/ppermute | solution.py:266
  43.0 6.0 %collective-permute-start.19 = (f32[96,128]{1,0:T(8,128)S(1)}, f32[96,128]{1,0:T(8,128)S(1)}, u32[]{:S(2)}, u32[]{:S(2)}) collective-permute-start(f32[96,128]{1,0:T(8,128)S(1)} %get-tuple-element.106), channel_id=1, source_target_pairs={{0,19},{1,18},{2,17},{3,16},{4,23},{5,22},{6,21},{7,20},{8,27},{9,... | collective-permute-start | bytes 147464 | tf_op jit(solution)/shard_map/ppermute | solution.py:266
  50.1 4.3 %collective-permute-start.20 = (f32[248,128]{1,0:T(8,128)S(1)}, f32[248,128]{1,0:T(8,128)S(1)}, u32[]{:S(2)}, u32[]{:S(2)}) collective-permute-start(f32[248,128]{1,0:T(8,128)S(1)} %get-tuple-element.111), channel_id=1, source_target_pairs={{0,4},{1,5},{2,6},{3,7},{4,0},{5,1},{6,2},{7,3},{8,12},{9,13},{10,... | collective-permute-start | bytes 380936 | tf_op jit(solution)/shard_map/ppermute | solution.py:266
  50.1 4.2 %collective-permute-start.21 = (f32[248,128]{1,0:T(8,128)S(1)}, f32[248,128]{1,0:T(8,128)S(1)}, u32[]{:S(2)}, u32[]{:S(2)}) collective-permute-start(f32[248,128]{1,0:T(8,128)S(1)} %get-tuple-element.112), channel_id=1, source_target_pairs={{0,1},{1,0},{2,3},{3,2},{4,8},{5,9},{6,10},{7,11},{8,4},{9,5},{10,... | collective-permute-start | bytes 380936 | tf_op jit(solution)/shard_map/ppermute | solution.py:266
  54.4 9.5 %collective-permute-start.22 = (f32[248,128]{1,0:T(8,128)S(1)}, f32[248,128]{1,0:T(8,128)S(1)}, u32[]{:S(2)}, u32[]{:S(2)}) collective-permute-start(f32[248,128]{1,0:T(8,128)S(1)} %get-tuple-element.113), channel_id=1, source_target_pairs={{0,1},{1,0},{2,3},{3,2},{4,5},{5,4},{6,7},{7,6},{8,9},{9,8},{10,11... | collective-permute-start | bytes 380936 | tf_op jit(solution)/shard_map/ppermute | solution.py:266
  56.1 7.8 %collective-permute-start.23 = (f32[248,128]{1,0:T(8,128)S(1)}, f32[248,128]{1,0:T(8,128)S(1)}, u32[]{:S(2)}, u32[]{:S(2)}) collective-permute-start(f32[248,128]{1,0:T(8,128)S(1)} %get-tuple-element.114), channel_id=1, source_target_pairs={{0,4},{1,2},{2,1},{3,7},{4,0},{5,6},{6,5},{7,3},{8,12},{9,10},{10,... | collective-permute-start | bytes 380936 | tf_op jit(solution)/shard_map/ppermute | solution.py:266
  57.3 6.6 %collective-permute-start.24 = (f32[248,128]{1,0:T(8,128)S(1)}, f32[248,128]{1,0:T(8,128)S(1)}, u32[]{:S(2)}, u32[]{:S(2)}) collective-permute-start(f32[248,128]{1,0:T(8,128)S(1)} %get-tuple-element.115), channel_id=1, source_target_pairs={{0,16},{1,17},{2,18},{3,19},{4,20},{5,21},{6,22},{7,23},{8,24},{9,... | collective-permute-start | bytes 380936 | tf_op jit(solution)/shard_map/ppermute | solution.py:266
  57.7 5.1 %collective-permute-start.25 = (f32[32,128]{1,0:T(8,128)S(1)}, f32[32,128]{1,0:T(8,128)S(1)}, u32[]{:S(2)}, u32[]{:S(2)}) collective-permute-start(f32[32,128]{1,0:T(8,128)S(1)} %get-tuple-element.116), channel_id=1, source_target_pairs={{0,17},{1,16},{2,19},{3,18},{4,21},{5,20},{6,23},{7,22},{8,25},{9,... | collective-permute-start | bytes 49160 | tf_op jit(solution)/shard_map/ppermute | solution.py:266
  59.8 4.1 %collective-permute-start.26 = (f32[32,128]{1,0:T(8,128)S(1)}, f32[32,128]{1,0:T(8,128)S(1)}, u32[]{:S(2)}, u32[]{:S(2)}) collective-permute-start(f32[32,128]{1,0:T(8,128)S(1)} %get-tuple-element.117), channel_id=1, source_target_pairs={{0,4},{1,18},{2,17},{3,7},{4,0},{5,22},{6,21},{7,3},{8,12},{9,26},... | collective-permute-start | bytes 49160 | tf_op jit(solution)/shard_map/ppermute | solution.py:266
  64.3 1.2 collective-permute-start.27
  65.5 7.3 %collective-permute-start.28 = (f32[264,128]{1,0:T(8,128)S(1)}, f32[264,128]{1,0:T(8,128)S(1)}, u32[]{:S(2)}, u32[]{:S(2)}) collective-permute-start(f32[264,128]{1,0:T(8,128)S(1)} %get-tuple-element.121), channel_id=1, source_target_pairs={{0,4},{1,5},{2,6},{3,7},{4,0},{5,1},{6,2},{7,3},{8,12},{9,13},{10,... | collective-permute-start | bytes 405512 | tf_op jit(solution)/shard_map/ppermute | solution.py:266
  66.2 6.6 %collective-permute-start.29 = (f32[248,128]{1,0:T(8,128)S(1)}, f32[248,128]{1,0:T(8,128)S(1)}, u32[]{:S(2)}, u32[]{:S(2)}) collective-permute-start(f32[248,128]{1,0:T(8,128)S(1)} %get-tuple-element.122), channel_id=1, source_target_pairs={{0,1},{1,0},{2,3},{3,2},{4,8},{5,9},{6,10},{7,11},{8,4},{9,5},{10,... | collective-permute-start | bytes 380936 | tf_op jit(solution)/shard_map/ppermute | solution.py:266
  66.8 4.5 %collective-permute-start.30 = (f32[16,128]{1,0:T(8,128)S(1)}, f32[16,128]{1,0:T(8,128)S(1)}, u32[]{:S(2)}, u32[]{:S(2)}) collective-permute-start(f32[16,128]{1,0:T(8,128)S(1)} %get-tuple-element.123), channel_id=1, source_target_pairs={{0,8},{1,9},{2,10},{3,11},{4,12},{5,13},{6,14},{7,15},{8,0},{9,1},... | collective-permute-start | bytes 24584 | tf_op jit(solution)/shard_map/ppermute | solution.py:266
  68.4 4.4 %collective-permute-start.31 = (f32[16,128]{1,0:T(8,128)S(1)}, f32[16,128]{1,0:T(8,128)S(1)}, u32[]{:S(2)}, u32[]{:S(2)}) collective-permute-start(f32[16,128]{1,0:T(8,128)S(1)} %get-tuple-element.124), channel_id=1, source_target_pairs={{0,12},{1,13},{2,14},{3,15},{4,8},{5,9},{6,10},{7,11},{8,4},{9,5},... | collective-permute-start | bytes 24584 | tf_op jit(solution)/shard_map/ppermute | solution.py:266
  72.8 10.3 %collective-permute-start.33 = (f32[312,128]{1,0:T(8,128)S(1)}, f32[312,128]{1,0:T(8,128)S(1)}, u32[]{:S(2)}, u32[]{:S(2)}) collective-permute-start(f32[312,128]{1,0:T(8,128)S(1)} %get-tuple-element.126), channel_id=1, source_target_pairs={{0,3},{1,2},{2,1},{3,0},{4,7},{5,6},{6,5},{7,4},{8,11},{9,10},{10,... | collective-permute-start | bytes 479240 | tf_op jit(solution)/shard_map/ppermute | solution.py:266
  75.6 7.5 %collective-permute-start.34 = (f32[312,128]{1,0:T(8,128)S(1)}, f32[312,128]{1,0:T(8,128)S(1)}, u32[]{:S(2)}, u32[]{:S(2)}) collective-permute-start(f32[312,128]{1,0:T(8,128)S(1)} %get-tuple-element.127), channel_id=1, source_target_pairs={{0,16},{1,17},{2,18},{3,19},{4,20},{5,21},{6,22},{7,23},{8,24},{9,... | collective-permute-start | bytes 479240 | tf_op jit(solution)/shard_map/ppermute | solution.py:266
  76.1 7.0 %collective-permute-start.32 = (f32[248,128]{1,0:T(8,128)S(1)}, f32[248,128]{1,0:T(8,128)S(1)}, u32[]{:S(2)}, u32[]{:S(2)}) collective-permute-start(f32[248,128]{1,0:T(8,128)S(1)} %get-tuple-element.125), channel_id=1, source_target_pairs={{0,1},{1,0},{2,3},{3,2},{4,5},{5,4},{6,7},{7,6},{8,9},{9,8},{10,11... | collective-permute-start | bytes 380936 | tf_op jit(solution)/shard_map/ppermute | solution.py:266
  76.1 7.0 %collective-permute-start.36 = (f32[96,128]{1,0:T(8,128)S(1)}, f32[96,128]{1,0:T(8,128)S(1)}, u32[]{:S(2)}, u32[]{:S(2)}) collective-permute-start(f32[96,128]{1,0:T(8,128)S(1)} %get-tuple-element.129), channel_id=1, source_target_pairs={{0,19},{1,18},{2,17},{3,16},{4,23},{5,22},{6,21},{7,20},{8,27},{9,... | collective-permute-start | bytes 147464 | tf_op jit(solution)/shard_map/ppermute | solution.py:266
  77.9 5.1 %collective-permute-start.35 = (f32[32,128]{1,0:T(8,128)S(1)}, f32[32,128]{1,0:T(8,128)S(1)}, u32[]{:S(2)}, u32[]{:S(2)}) collective-permute-start(f32[32,128]{1,0:T(8,128)S(1)} %get-tuple-element.128), channel_id=1, source_target_pairs={{0,17},{1,16},{2,19},{3,18},{4,21},{5,20},{6,23},{7,22},{8,25},{9,... | collective-permute-start | bytes 49160 | tf_op jit(solution)/shard_map/ppermute | solution.py:266
  84.2 4.5 %collective-permute-start.37 = (f32[248,128]{1,0:T(8,128)S(1)}, f32[248,128]{1,0:T(8,128)S(1)}, u32[]{:S(2)}, u32[]{:S(2)}) collective-permute-start(f32[248,128]{1,0:T(8,128)S(1)} %get-tuple-element.135), channel_id=1, source_target_pairs={{0,4},{1,5},{2,6},{3,7},{4,0},{5,1},{6,2},{7,3},{8,12},{9,13},{10,... | collective-permute-start | bytes 380936 | tf_op jit(solution)/shard_map/ppermute | solution.py:266
  84.2 4.4 %collective-permute-start.38 = (f32[248,128]{1,0:T(8,128)S(1)}, f32[248,128]{1,0:T(8,128)S(1)}, u32[]{:S(2)}, u32[]{:S(2)}) collective-permute-start(f32[248,128]{1,0:T(8,128)S(1)} %get-tuple-element.136), channel_id=1, source_target_pairs={{0,1},{1,0},{2,3},{3,2},{4,8},{5,9},{6,10},{7,11},{8,4},{9,5},{10,... | collective-permute-start | bytes 380936 | tf_op jit(solution)/shard_map/ppermute | solution.py:266
  88.7 9.1 %collective-permute-start.39 = (f32[248,128]{1,0:T(8,128)S(1)}, f32[248,128]{1,0:T(8,128)S(1)}, u32[]{:S(2)}, u32[]{:S(2)}) collective-permute-start(f32[248,128]{1,0:T(8,128)S(1)} %get-tuple-element.137), channel_id=1, source_target_pairs={{0,1},{1,0},{2,3},{3,2},{4,5},{5,4},{6,7},{7,6},{8,9},{9,8},{10,11... | collective-permute-start | bytes 380936 | tf_op jit(solution)/shard_map/ppermute | solution.py:266
  90.2 7.7 %collective-permute-start.40 = (f32[248,128]{1,0:T(8,128)S(1)}, f32[248,128]{1,0:T(8,128)S(1)}, u32[]{:S(2)}, u32[]{:S(2)}) collective-permute-start(f32[248,128]{1,0:T(8,128)S(1)} %get-tuple-element.138), channel_id=1, source_target_pairs={{0,4},{1,2},{2,1},{3,7},{4,0},{5,6},{6,5},{7,3},{8,12},{9,10},{10,... | collective-permute-start | bytes 380936 | tf_op jit(solution)/shard_map/ppermute | solution.py:266
  90.8 7.0 %collective-permute-start.41 = (f32[248,128]{1,0:T(8,128)S(1)}, f32[248,128]{1,0:T(8,128)S(1)}, u32[]{:S(2)}, u32[]{:S(2)}) collective-permute-start(f32[248,128]{1,0:T(8,128)S(1)} %get-tuple-element.139), channel_id=1, source_target_pairs={{0,16},{1,17},{2,18},{3,19},{4,20},{5,21},{6,22},{7,23},{8,24},{9,... | collective-permute-start | bytes 380936 | tf_op jit(solution)/shard_map/ppermute | solution.py:266
  91.3 5.6 %collective-permute-start.42 = (f32[32,128]{1,0:T(8,128)S(1)}, f32[32,128]{1,0:T(8,128)S(1)}, u32[]{:S(2)}, u32[]{:S(2)}) collective-permute-start(f32[32,128]{1,0:T(8,128)S(1)} %get-tuple-element.140), channel_id=1, source_target_pairs={{0,17},{1,16},{2,19},{3,18},{4,21},{5,20},{6,23},{7,22},{8,25},{9,... | collective-permute-start | bytes 49160 | tf_op jit(solution)/shard_map/ppermute | solution.py:266
  93.8 4.1 %collective-permute-start.43 = (f32[32,128]{1,0:T(8,128)S(1)}, f32[32,128]{1,0:T(8,128)S(1)}, u32[]{:S(2)}, u32[]{:S(2)}) collective-permute-start(f32[32,128]{1,0:T(8,128)S(1)} %get-tuple-element.141), channel_id=1, source_target_pairs={{0,4},{1,18},{2,17},{3,7},{4,0},{5,22},{6,21},{7,3},{8,12},{9,26},... | collective-permute-start | bytes 49160 | tf_op jit(solution)/shard_map/ppermute | solution.py:266
  98.3 1.2 collective-permute-start.44
  99.5 7.1 %collective-permute-start.45 = (f32[264,128]{1,0:T(8,128)S(1)}, f32[264,128]{1,0:T(8,128)S(1)}, u32[]{:S(2)}, u32[]{:S(2)}) collective-permute-start(f32[264,128]{1,0:T(8,128)S(1)} %get-tuple-element.145), channel_id=1, source_target_pairs={{0,4},{1,5},{2,6},{3,7},{4,0},{5,1},{6,2},{7,3},{8,12},{9,13},{10,... | collective-permute-start | bytes 405512 | tf_op jit(solution)/shard_map/ppermute | solution.py:266
  100.2 6.4 %collective-permute-start.46 = (f32[248,128]{1,0:T(8,128)S(1)}, f32[248,128]{1,0:T(8,128)S(1)}, u32[]{:S(2)}, u32[]{:S(2)}) collective-permute-start(f32[248,128]{1,0:T(8,128)S(1)} %get-tuple-element.146), channel_id=1, source_target_pairs={{0,1},{1,0},{2,3},{3,2},{4,8},{5,9},{6,10},{7,11},{8,4},{9,5},{10,... | collective-permute-start | bytes 380936 | tf_op jit(solution)/shard_map/ppermute | solution.py:266
  100.6 4.5 %collective-permute-start.47 = (f32[16,128]{1,0:T(8,128)S(1)}, f32[16,128]{1,0:T(8,128)S(1)}, u32[]{:S(2)}, u32[]{:S(2)}) collective-permute-start(f32[16,128]{1,0:T(8,128)S(1)} %get-tuple-element.147), channel_id=1, source_target_pairs={{0,8},{1,9},{2,10},{3,11},{4,12},{5,13},{6,14},{7,15},{8,0},{9,1},... | collective-permute-start | bytes 24584 | tf_op jit(solution)/shard_map/ppermute | solution.py:266
  102.3 4.3 %collective-permute-start.48 = (f32[16,128]{1,0:T(8,128)S(1)}, f32[16,128]{1,0:T(8,128)S(1)}, u32[]{:S(2)}, u32[]{:S(2)}) collective-permute-start(f32[16,128]{1,0:T(8,128)S(1)} %get-tuple-element.148), channel_id=1, source_target_pairs={{0,12},{1,13},{2,14},{3,15},{4,8},{5,9},{6,10},{7,11},{8,4},{9,5},... | collective-permute-start | bytes 24584 | tf_op jit(solution)/shard_map/ppermute | solution.py:266
  106.7 10.3 %collective-permute-start.50 = (f32[312,128]{1,0:T(8,128)S(1)}, f32[312,128]{1,0:T(8,128)S(1)}, u32[]{:S(2)}, u32[]{:S(2)}) collective-permute-start(f32[312,128]{1,0:T(8,128)S(1)} %get-tuple-element.150), channel_id=1, source_target_pairs={{0,3},{1,2},{2,1},{3,0},{4,7},{5,6},{6,5},{7,4},{8,11},{9,10},{10,... | collective-permute-start | bytes 479240 | tf_op jit(solution)/shard_map/ppermute | solution.py:266
  109.4 7.6 %collective-permute-start.51 = (f32[312,128]{1,0:T(8,128)S(1)}, f32[312,128]{1,0:T(8,128)S(1)}, u32[]{:S(2)}, u32[]{:S(2)}) collective-permute-start(f32[312,128]{1,0:T(8,128)S(1)} %get-tuple-element.151), channel_id=1, source_target_pairs={{0,16},{1,17},{2,18},{3,19},{4,20},{5,21},{6,22},{7,23},{8,24},{9,... | collective-permute-start | bytes 479240 | tf_op jit(solution)/shard_map/ppermute | solution.py:266
  109.9 7.1 %collective-permute-start.49 = (f32[248,128]{1,0:T(8,128)S(1)}, f32[248,128]{1,0:T(8,128)S(1)}, u32[]{:S(2)}, u32[]{:S(2)}) collective-permute-start(f32[248,128]{1,0:T(8,128)S(1)} %get-tuple-element.149), channel_id=1, source_target_pairs={{0,1},{1,0},{2,3},{3,2},{4,5},{5,4},{6,7},{7,6},{8,9},{9,8},{10,11... | collective-permute-start | bytes 380936 | tf_op jit(solution)/shard_map/ppermute | solution.py:266
  109.9 7.1 %collective-permute-start.53 = (f32[96,128]{1,0:T(8,128)S(1)}, f32[96,128]{1,0:T(8,128)S(1)}, u32[]{:S(2)}, u32[]{:S(2)}) collective-permute-start(f32[96,128]{1,0:T(8,128)S(1)} %get-tuple-element.153), channel_id=1, source_target_pairs={{0,19},{1,18},{2,17},{3,16},{4,23},{5,22},{6,21},{7,20},{8,27},{9,... | collective-permute-start | bytes 147464 | tf_op jit(solution)/shard_map/ppermute | solution.py:266
  111.9 5.0 %collective-permute-start.52 = (f32[32,128]{1,0:T(8,128)S(1)}, f32[32,128]{1,0:T(8,128)S(1)}, u32[]{:S(2)}, u32[]{:S(2)}) collective-permute-start(f32[32,128]{1,0:T(8,128)S(1)} %get-tuple-element.152), channel_id=1, source_target_pairs={{0,17},{1,16},{2,19},{3,18},{4,21},{5,20},{6,23},{7,22},{8,25},{9,... | collective-permute-start | bytes 49160 | tf_op jit(solution)/shard_map/ppermute | solution.py:266
  118.0 4.7 %collective-permute-start.54 = (f32[248,128]{1,0:T(8,128)S(1)}, f32[248,128]{1,0:T(8,128)S(1)}, u32[]{:S(2)}, u32[]{:S(2)}) collective-permute-start(f32[248,128]{1,0:T(8,128)S(1)} %get-tuple-element.160), channel_id=1, source_target_pairs={{0,4},{1,5},{2,6},{3,7},{4,0},{5,1},{6,2},{7,3},{8,12},{9,13},{10,... | collective-permute-start | bytes 380936 | tf_op jit(solution)/shard_map/ppermute | solution.py:266
  118.3 4.4 %collective-permute-start.55 = (f32[248,128]{1,0:T(8,128)S(1)}, f32[248,128]{1,0:T(8,128)S(1)}, u32[]{:S(2)}, u32[]{:S(2)}) collective-permute-start(f32[248,128]{1,0:T(8,128)S(1)} %get-tuple-element.161), channel_id=1, source_target_pairs={{0,1},{1,0},{2,3},{3,2},{4,8},{5,9},{6,10},{7,11},{8,4},{9,5},{10,... | collective-permute-start | bytes 380936 | tf_op jit(solution)/shard_map/ppermute | solution.py:266
  122.7 9.0 %collective-permute-start.56 = (f32[248,128]{1,0:T(8,128)S(1)}, f32[248,128]{1,0:T(8,128)S(1)}, u32[]{:S(2)}, u32[]{:S(2)}) collective-permute-start(f32[248,128]{1,0:T(8,128)S(1)} %get-tuple-element.162), channel_id=1, source_target_pairs={{0,1},{1,0},{2,3},{3,2},{4,5},{5,4},{6,7},{7,6},{8,9},{9,8},{10,11... | collective-permute-start | bytes 380936 | tf_op jit(solution)/shard_map/ppermute | solution.py:266
  124.2 7.5 %collective-permute-start.57 = (f32[248,128]{1,0:T(8,128)S(1)}, f32[248,128]{1,0:T(8,128)S(1)}, u32[]{:S(2)}, u32[]{:S(2)}) collective-permute-start(f32[248,128]{1,0:T(8,128)S(1)} %get-tuple-element.163), channel_id=1, source_target_pairs={{0,4},{1,2},{2,1},{3,7},{4,0},{5,6},{6,5},{7,3},{8,12},{9,10},{10,... | collective-permute-start | bytes 380936 | tf_op jit(solution)/shard_map/ppermute | solution.py:266
  124.9 6.9 %collective-permute-start.58 = (f32[248,128]{1,0:T(8,128)S(1)}, f32[248,128]{1,0:T(8,128)S(1)}, u32[]{:S(2)}, u32[]{:S(2)}) collective-permute-start(f32[248,128]{1,0:T(8,128)S(1)} %get-tuple-element.164), channel_id=1, source_target_pairs={{0,16},{1,17},{2,18},{3,19},{4,20},{5,21},{6,22},{7,23},{8,24},{9,... | collective-permute-start | bytes 380936 | tf_op jit(solution)/shard_map/ppermute | solution.py:266
  125.3 5.6 %collective-permute-start.59 = (f32[32,128]{1,0:T(8,128)S(1)}, f32[32,128]{1,0:T(8,128)S(1)}, u32[]{:S(2)}, u32[]{:S(2)}) collective-permute-start(f32[32,128]{1,0:T(8,128)S(1)} %get-tuple-element.165), channel_id=1, source_target_pairs={{0,17},{1,16},{2,19},{3,18},{4,21},{5,20},{6,23},{7,22},{8,25},{9,... | collective-permute-start | bytes 49160 | tf_op jit(solution)/shard_map/ppermute | solution.py:266
  127.7 4.1 %collective-permute-start.60 = (f32[32,128]{1,0:T(8,128)S(1)}, f32[32,128]{1,0:T(8,128)S(1)}, u32[]{:S(2)}, u32[]{:S(2)}) collective-permute-start(f32[32,128]{1,0:T(8,128)S(1)} %get-tuple-element.166), channel_id=1, source_target_pairs={{0,4},{1,18},{2,17},{3,7},{4,0},{5,22},{6,21},{7,3},{8,12},{9,26},... | collective-permute-start | bytes 49160 | tf_op jit(solution)/shard_map/ppermute | solution.py:266
  (3 other events, 2.8 us)
